TPU v7x, 32 devices: a whole 2x2x4 slice. The times are simulated.
32 devices in a mesh: mod: 4 (over y, x), slab: 4 (over z), sub: 2 (over core).
Axes of the slice: x: 2, y: 2, z: 4, core: 2. Of those that a mesh axis runs over, the one named last changes fastest.
Arguments:
- design: float32 [8, 128, 128], P('slab', 'sub'), may hold values from 0.1 to 1
- fixed_mask: int32 [3, 32, 128, 128], P(None, ('mod', 'slab'), 'sub'), may hold values from 0 to 1, as said below
- load_mask: int32 [3, 32, 128, 128], P(None, ('mod', 'slab'), 'sub'), may hold values from 0 to 1, as said below
Outputs:
- displacement: float32 [3, 32, 128, 128], P(None, ('mod', 'slab'), 'sub')
- gradient: float32 [8, 128, 128], P('slab', 'sub')
Inputs may be any that keep to these rules, and one draw needn't show every extreme that they name: `fixed_mask`: 1 marks a supported degree of freedom. `load_mask`: 1 marks a loaded degree of freedom, carrying a unit force.
All inputs are finite; a program needn't handle non-finite values.
Results may differ from a plain program's by a relative error of at most 0.013.
Values sent between devices are 32-bit elements; how exact they have to be, the bound alone decides.
No kernel may reach another device: no remote copies, remote signals or barrier semaphores. Data moves between devices by JAX's collectives and lax.ppermute only.
A program may use at most 64 MiB of HBM per device.

v0:
```python
import math

import jax
import jax.numpy as jnp
import numpy as np
from jax import lax
from jax.sharding import PartitionSpec as P

ITERS = 3


stiff_floor = 0.01
penalty = 3.0
sharpness = 4.0
threshold = 0.5
filter_reach = 1.8


def passed_along(value, axis, steps):
    count = lax.axis_size(axis)
    first, last = (max(0, -steps), min(count, count - steps))
    return lax.ppermute(value, axis, [(source, source + steps) for source in range(first, last)])


def extended_2(block, sides, width, periodic):
    for axis, dim in sides:
        count = lax.axis_size(axis)
        forward = [(i, i + 1) for i in range(count - 1)]
        if periodic:
            forward.append((count - 1, 0))
        backward = [(target, source) for source, target in forward]
        low = lax.ppermute(
            lax.slice_in_dim(block, block.shape[dim] - width, None, axis=dim), axis, forward
        )
        high = lax.ppermute(lax.slice_in_dim(block, 0, width, axis=dim), axis, backward)
        block = jnp.concatenate([low, block, high], axis=dim)
    return block


def stiffness_table():
    poisson = 0.3
    lame_first = poisson / ((1.0 + poisson) * (1.0 - 2.0 * poisson))
    shear_modulus = 1.0 / (2.0 * (1.0 + poisson))
    elastic = np.zeros((6, 6))
    elastic[:3, :3] = lame_first
    for axis_id in range(3):
        elastic[axis_id, axis_id] += 2.0 * shear_modulus
        elastic[axis_id + 3, axis_id + 3] = shear_modulus
    offset = 0.5 / math.sqrt(3.0)
    points = [0.5 - offset, 0.5 + offset]
    stiffness = np.zeros((24, 24))
    for point_x in points:
        for point_y in points:
            for point_z in points:
                strain = np.zeros((6, 24))
                for corner in range(8):
                    bit_x, bit_y, bit_z = (corner >> 2 & 1, corner >> 1 & 1, corner & 1)
                    along_x = point_x if bit_x else 1.0 - point_x
                    along_y = point_y if bit_y else 1.0 - point_y
                    along_z = point_z if bit_z else 1.0 - point_z
                    sign_x = 1.0 if bit_x else -1.0
                    sign_y = 1.0 if bit_y else -1.0
                    sign_z = 1.0 if bit_z else -1.0
                    grad_x = sign_x * along_y * along_z
                    grad_y = along_x * sign_y * along_z
                    grad_z = along_x * along_y * sign_z
                    column = 3 * corner
                    strain[0, column] = grad_x
                    strain[1, column + 1] = grad_y
                    strain[2, column + 2] = grad_z
                    strain[3, column] = grad_y
                    strain[3, column + 1] = grad_x
                    strain[4, column + 1] = grad_z
                    strain[4, column + 2] = grad_y
                    strain[5, column] = grad_z
                    strain[5, column + 2] = grad_x
                stiffness += strain.T @ elastic @ strain / 8.0
    return jnp.asarray(stiffness, dtype=jnp.float32)


def stencil_weights():
    entries = []
    for shift_x in (-1, 0, 1):
        for shift_y in (-1, 0, 1):
            for shift_z in (-1, 0, 1):
                weight = filter_reach - math.sqrt(
                    shift_x * shift_x + shift_y * shift_y + shift_z * shift_z
                )
                entries.append((shift_x, shift_y, shift_z, weight))
    return entries


def smooth_sum(padded, count_x, count_y, depth_cells):
    running = jnp.zeros((count_x, count_y, depth_cells), jnp.float32)
    for shift_x, shift_y, shift_z, weight in stencil_weights():
        running = (
            running
            + weight
            * padded[
                1 + shift_x : 1 + shift_x + count_x,
                1 + shift_y : 1 + shift_y + count_y,
                1 + shift_z : 1 + shift_z + depth_cells,
            ]
        )
    return running


def project(values):
    lower_end = math.tanh(sharpness * threshold)
    upper_end = math.tanh(sharpness * (1.0 - threshold))
    return (lower_end + jnp.tanh(sharpness * (values - threshold))) / (lower_end + upper_end)


def project_slope(values):
    lower_end = math.tanh(sharpness * threshold)
    upper_end = math.tanh(sharpness * (1.0 - threshold))
    hyper = jnp.tanh(sharpness * (values - threshold))
    return sharpness * (1.0 - hyper * hyper) / (lower_end + upper_end)


def gather_corners(extended, count_x, count_y):
    depth_cells = extended.shape[3]
    shifted_z = jnp.pad(extended[..., 1:], ((0, 0), (0, 0), (0, 0), (0, 1)))
    columns = []
    for corner in range(8):
        bit_x, bit_y, bit_z = (corner >> 2 & 1, corner >> 1 & 1, corner & 1)
        source = shifted_z if bit_z else extended
        columns.append(source[:, bit_x : bit_x + count_x, bit_y : bit_y + count_y, :])
    return jnp.stack(columns).reshape(24, count_x * count_y * depth_cells)


def element_forces(extended, moduli):
    count_x, count_y, depth_cells = moduli.shape
    values = gather_corners(extended, count_x, count_y)
    forces = jnp.dot(stiffness_table(), values, precision=lax.Precision.HIGHEST) * moduli.reshape(
        1, -1
    )
    forces = forces.reshape(8, 3, count_x, count_y, depth_cells)
    result = jnp.zeros((3, count_x + 1, count_y + 1, depth_cells), forces.dtype)
    for corner in range(8):
        bit_x, bit_y, bit_z = (corner >> 2 & 1, corner >> 1 & 1, corner & 1)
        portion = forces[corner]
        if bit_z:
            portion = jnp.pad(portion[..., :-1], ((0, 0), (0, 0), (0, 0), (1, 0)))
        result = result.at[:, bit_x : bit_x + count_x, bit_y : bit_y + count_y, :].add(portion)
    return result


def element_energy(extended):
    count_x = extended.shape[1] - 1
    count_y = extended.shape[2] - 1
    depth_cells = extended.shape[3]
    values = gather_corners(extended, count_x, count_y)
    product = jnp.dot(stiffness_table(), values, precision=lax.Precision.HIGHEST)
    return jnp.sum(values * product, axis=0).reshape(count_x, count_y, depth_cells)


def extend_upper(field):
    next_deck = passed_along(field[:, :1], ("mod", "slab"), -1)
    widened = jnp.concatenate([field, next_deck], axis=1)
    next_across = passed_along(widened[:, :, :1], "sub", -1)
    return jnp.concatenate([widened, next_across], axis=2)


def apply_operator(field, free_dofs, moduli_lower, moduli_own):
    masked = free_dofs * field
    count_x, count_y, depth_cells = moduli_own.shape
    padded = extended_2(masked, ((("mod", "slab"), 1), ("sub", 2)), 1, False)
    forces = element_forces(padded, moduli_lower)
    result = forces[:, 1 : count_x + 1, 1 : count_y + 1]
    return free_dofs * result


def squares(residual):
    return lax.psum(jnp.sum(residual * residual), ("mod", "slab", "sub"))


def local(design, fixed_mask, load_mask):
    count_x, count_y, depth_cells = design.shape
    grid_y = count_y * lax.axis_size("sub")
    row_y = lax.axis_index("sub") * count_y + jnp.arange(-2, count_y + 2, dtype=jnp.int32)
    inside_y = ((row_y >= 0) & (row_y < grid_y)).astype(jnp.float32)
    padded = extended_2(design, (("slab", 0), ("sub", 1)), 2, True)
    padded = jnp.pad(padded * inside_y[None, :, None], ((0, 0), (0, 0), (1, 1)))
    valid = jnp.broadcast_to(inside_y[None, :, None], (count_x + 4, count_y + 4, depth_cells))
    valid = jnp.pad(valid, ((0, 0), (0, 0), (1, 1)))
    weight_sum = smooth_sum(valid, count_x + 2, count_y + 2, depth_cells)
    filtered = smooth_sum(padded, count_x + 2, count_y + 2, depth_cells) / weight_sum
    projected = project(filtered)
    moduli = stiff_floor + (1.0 - stiff_floor) * projected**3
    at_start = (lax.axis_index("mod") == 0) & (lax.axis_index("slab") == 0)
    keep_x = jnp.where(at_start & (jnp.arange(count_x + 1, dtype=jnp.int32) == 0), 0.0, 1.0).astype(
        jnp.float32
    )
    keep_y = inside_y[1 : count_y + 2]
    moduli_lower = (
        moduli[: count_x + 1, : count_y + 1] * keep_x[:, None, None] * keep_y[None, :, None]
    )
    moduli_own = moduli[1 : count_x + 1, 1 : count_y + 1]
    filtered_own = filtered[1 : count_x + 1, 1 : count_y + 1]
    projected_own = projected[1 : count_x + 1, 1 : count_y + 1]
    weight_own = weight_sum[1 : count_x + 1, 1 : count_y + 1]
    free_dofs = (1 - fixed_mask).astype(jnp.float32)
    right_side = free_dofs * load_mask.astype(jnp.float32)
    displacement = jnp.zeros_like(right_side)
    residual = right_side
    direction = right_side
    norm_now = squares(residual)
    for step in range(ITERS):
        image = apply_operator(direction, free_dofs, moduli_lower, moduli_own)
        step_size = norm_now / lax.psum(jnp.sum(direction * image), ("mod", "slab", "sub"))
        displacement = displacement + step_size * direction
        if step + 1 < ITERS:
            residual = residual - step_size * image
            norm_next = squares(residual)
            direction = residual + norm_next / norm_now * direction
            norm_now = norm_next
    energy = element_energy(extend_upper(displacement))
    slope = -penalty * (1.0 - stiff_floor) * projected_own * projected_own * energy
    module_sens = lax.psum(slope, "mod")
    scaled = module_sens * project_slope(filtered_own) / weight_own
    scaled_pad = extended_2(scaled, (("slab", 0), ("sub", 1)), 1, True)
    scaled_pad = scaled_pad * inside_y[1 : count_y + 3][None, :, None]
    scaled_pad = jnp.pad(scaled_pad, ((0, 0), (0, 0), (1, 1)))
    gradient = smooth_sum(scaled_pad, count_x, count_y, depth_cells)
    return (displacement, gradient)


def solution(mesh):
    placed = (
        P("slab", "sub", None),
        P(None, ("mod", "slab"), "sub", None),
        P(None, ("mod", "slab"), "sub", None),
    )
    return jax.shard_map(
        local,
        mesh=mesh,
        in_specs=placed,
        out_specs=(P(None, ("mod", "slab"), "sub", None), P("slab", "sub", None)),
        check_vma=False,
    )
```

profile of v0, /device:TPU:0, one launch (start us, length us, event | category | flops | bytes accessed | tf_op | source)
XLA Modules:
  0.0 446.0 jit_solution(13329795043386357759)
XLA Ops:
  7.2 3.1 collective-permute-start.4
  10.3 2.1 collective-permute-start.5
  13.5 1.8 collective-permute-start
  19.8 2.9 add_multiply_fusion
  24.7 3.0 collective-permute-start.2
  34.8 1.9 reshape.1023
  36.8 2.2 fusion
  46.6 1.7 scatter-add.64
  48.3 1.5 pad_add_fusion.7
  49.9 1.7 scatter-add.65
  53.4 43.1 %all-reduce.22 = (f32[]{:T(128)}, f32[]{:T(128)}) all-reduce(f32[]{:T(128)} %get-tuple-element.291, f32[]{:T(128)} %get-tuple-element.290), channel_id=1, replica_groups=mesh['mod'=4,'slab'=4,'sub'=2] {'mod','slab','sub'}, use_global_device_ids=true, to_apply=%region_1.2 | all-reduce | flops 2 | bytes 16 | tf_op jit(solution)/shard_map/psum | solution.py:175
  98.5 42.8 %psum.51 = f32[]{:T(128)} all-reduce(f32[]{:T(128)} %get-tuple-element.306), channel_id=1, replica_groups=mesh['mod'=4,'slab'=4,'sub'=2] {'mod','slab','sub'}, use_global_device_ids=true, to_apply=%region_5.6 | all-reduce | flops 1 | bytes 8 | tf_op jit(solution)/shard_map/psum | solution.py:175
  142.6 1.8 collective-permute-start.8
  146.7 4.5 %collective-permute-done.9 = f32[3,1,64,128]{3,2,1,0:T(8,128)S(1)} collective-permute-done((f32[3,1,64,128]{3,2,1,0:T(8,128)S(1)}, f32[3,1,64,128]{3,2,1,0:T(8,128)S(1)}, u32[]{:S(2)}, u32[]{:S(2)}) %collective-permute-start.9) | collective-permute-done | bytes 98336 | tf_op jit(solution)/shard_map/ppermute | solution.py:35
  152.5 3.2 collective-permute-start.10
  162.6 1.9 reshape.1029
  164.5 2.2 fusion.1
  166.8 1.4 fusion.198
  168.1 1.9 reshape.1031
  171.2 1.9 squeeze.55
  178.2 1.7 scatter-add.74
  179.9 1.5 pad_add_fusion.4
  181.4 1.7 scatter-add.75
  184.9 44.6 %psum.52 = f32[]{:T(128)} all-reduce(f32[]{:T(128)} %get-tuple-element.300), channel_id=1, replica_groups=mesh['mod'=4,'slab'=4,'sub'=2] {'mod','slab','sub'}, use_global_device_ids=true, to_apply=%region_7.8 | all-reduce | flops 1 | bytes 8 | tf_op jit(solution)/shard_map/psum | solution.py:211
  231.5 42.1 %psum.53 = f32[]{:T(128)} all-reduce(f32[]{:T(128)} %multiply_reduce_fusion), channel_id=1, replica_groups=mesh['mod'=4,'slab'=4,'sub'=2] {'mod','slab','sub'}, use_global_device_ids=true, to_apply=%region_9.10 | all-reduce | flops 1 | bytes 8 | tf_op jit(solution)/shard_map/psum | solution.py:175
  274.8 1.8 collective-permute-start.12
  278.8 4.4 collective-permute-done.13
  284.5 3.2 collective-permute-start.14
  294.7 1.9 reshape.1033
  296.6 2.2 fusion.2
  298.8 1.4 fusion.197
  300.2 1.9 reshape.1035
  303.2 1.9 squeeze.59
  307.4 1.9 pad_add_fusion.2
  312.0 1.7 scatter-add.84
  313.7 1.4 pad_add_fusion.1
  315.1 1.7 scatter-add.85
  317.9 1.7 fusion.47
  319.5 44.7 %psum.54 = f32[]{:T(128)} all-reduce(f32[]{:T(128)} %fusion.47), channel_id=1, replica_groups=mesh['mod'=4,'slab'=4,'sub'=2] {'mod','slab','sub'}, use_global_device_ids=true, to_apply=%region_11.12 | all-reduce | flops 1 | bytes 8 | tf_op jit(solution)/shard_map/psum | solution.py:211
  367.5 5.3 %collective-permute-done.16 = f32[3,1,64,128]{3,2,1,0:T(8,128)S(1)} collective-permute-done((f32[3,1,64,128]{3,2,1,0:T(8,128)S(1)}, f32[3,1,64,128]{3,2,1,0:T(8,128)S(1)}, u32[]{:S(2)}, u32[]{:S(2)}) %collective-permute-start.16) | collective-permute-done | bytes 98336 | tf_op jit(solution)/shard_map/ppermute | solution.py:22
  374.1 1.8 collective-permute-done.17
  380.9 1.6 reshape.1037
  382.5 1.6 fusion.3
  384.1 1.5 fusion.143
  385.6 44.2 %all-reduce.25.cloned.1.call-done = f32[2,64,128]{2,1,0:T(8,128)} async-done(((f32[2,64,128]{2,1,0:T(8,128)}), f32[2,64,128]{2,1,0:T(8,128)}) %all-reduce.25.cloned.1.call-update) | async-done | bytes 65552 | tf_op jit(solution)/shard_map/psum | solution.py:220
  430.8 1.5 collective-permute-start.18
  432.4 2.3 collective-permute-start.19
  434.7 2.0 collective-permute-done.18
  (175 shorter events, 73.1 us)
Async XLA Ops:
  7.2 422.7 %all-reduce.25.cloned.1.call-start = ((), (), s32[]{:S(2)}) async-start(), calls=%async_computation | async-start | bytes 131072 | tf_op jit(solution)/shard_map/psum | solution.py:220
  7.2 10.1 %collective-permute-start.4 = (f32[2,64,128]{2,1,0:T(8,128)}, f32[2,64,128]{2,1,0:T(8,128)S(1)}, u32[]{:S(2)}, u32[]{:S(2)}) collective-permute-start(f32[2,64,128]{2,1,0:T(8,128)} %param.55), channel_id=1, source_target_pairs={{0,2},{2,4},{4,6},{6,0},{1,3},{3,5},{5,7},{7,1},{8,10},{10,12},{12... | collective-permute-start | bytes 196616 | tf_op jit(solution)/shard_map/ppermute | solution.py:32
  10.3 7.9 %collective-permute-start.5 = (f32[2,64,128]{2,1,0:T(8,128)}, f32[2,64,128]{2,1,0:T(8,128)S(1)}, u32[]{:S(2)}, u32[]{:S(2)}) collective-permute-start(f32[2,64,128]{2,1,0:T(8,128)} %param.55), channel_id=1, source_target_pairs={{2,0},{4,2},{6,4},{0,6},{3,1},{5,3},{7,5},{1,7},{10,8},{12,10},{14... | collective-permute-start | bytes 196616 | tf_op jit(solution)/shard_map/ppermute | solution.py:35
  13.5 9.2 %collective-permute-start = (f32[3,1,64,128]{3,2,1,0:T(8,128)S(1)}, f32[3,1,64,128]{3,2,1,0:T(8,128)S(1)}, u32[]{:S(2)}, u32[]{:S(2)}) collective-permute-start(f32[3,1,64,128]{3,2,1,0:T(8,128)S(1)} %get-tuple-element.358), channel_id=1, source_target_pairs={{0,2},{2,4},{4,6},{6,8},{8,10},{10,12},{12,14},{14,16},{16,18},{18... | collective-permute-start | bytes 294920 | tf_op jit(solution)/shard_map/ppermute | solution.py:32
  15.3 8.0 %collective-permute-start.1 = (f32[3,1,64,128]{3,2,1,0:T(8,128)S(1)}, f32[3,1,64,128]{3,2,1,0:T(8,128)S(1)}, u32[]{:S(2)}, u32[]{:S(2)}) collective-permute-start(f32[3,1,64,128]{3,2,1,0:T(8,128)S(1)} %get-tuple-element.359), channel_id=1, source_target_pairs={{2,0},{4,2},{6,4},{8,6},{10,8},{12,10},{14,12},{16,14},{18,16},{20... | collective-permute-start | bytes 294920 | tf_op jit(solution)/shard_map/ppermute | solution.py:35
  18.2 1.2 collective-permute-start.6
  18.3 1.3 collective-permute-start.7
  22.7 5.0 %copy-start.10 = (f32[4,66,128]{2,1,0:T(8,128)}, f32[4,66,128]{2,1,0:T(8,128)S(1)}, u32[]{:S(2)}) copy-start(f32[4,66,128]{2,1,0:T(8,128)S(1)} %get-tuple-element.311) | copy-start | bytes 405508
  23.4 4.5 collective-permute-start.3
  24.7 3.8 collective-permute-start.2
  34.8 1.9 copy-start.11
  44.7 6.9 %copy-start.3 = (f32[3,3,65,128]{3,2,1,0:T(8,128)S(1)}, f32[3,3,65,128]{3,2,1,0:T(8,128)}, u32[]{:S(2)}) copy-start(f32[3,3,65,128]{3,2,1,0:T(8,128)} %reshape.1027) | copy-start | bytes 898564
  48.3 4.2 copy-start
  48.3 4.2 copy-start.6
  48.3 4.2 copy-start.9
  142.6 4.0 collective-permute-start.8
  144.5 6.7 %collective-permute-start.9 = (f32[3,1,64,128]{3,2,1,0:T(8,128)S(1)}, f32[3,1,64,128]{3,2,1,0:T(8,128)S(1)}, u32[]{:S(2)}, u32[]{:S(2)}) collective-permute-start(f32[3,1,64,128]{3,2,1,0:T(8,128)S(1)} %get-tuple-element.355), channel_id=1, source_target_pairs={{2,0},{4,2},{6,4},{8,6},{10,8},{12,10},{14,12},{16,14},{18,16},{20... | collective-permute-start | bytes 294920 | tf_op jit(solution)/shard_map/ppermute | solution.py:35
  151.2 4.5 %collective-permute-start.11 = (f32[3,4,1,128]{3,2,1,0:T(1,128)S(1)}, f32[3,4,1,128]{3,2,1,0:T(1,128)S(1)}, u32[]{:S(2)}, u32[]{:S(2)}) collective-permute-start(f32[3,4,1,128]{3,2,1,0:T(1,128)S(1)} %get-tuple-element.345), channel_id=1, source_target_pairs={{1,0},{3,2},{5,4},{7,6},{9,8},{11,10},{13,12},{15,14},{17,16},{19,... | collective-permute-start | bytes 18440 | tf_op jit(solution)/shard_map/ppermute | solution.py:35
  152.5 3.8 collective-permute-start.10
  174.6 8.5 %copy-start.4 = (f32[3,3,65,128]{3,2,1,0:T(8,128)S(1)}, f32[3,3,65,128]{3,2,1,0:T(8,128)}, u32[]{:S(2)}) copy-start(f32[3,3,65,128]{3,2,1,0:T(8,128)} %reshape.1031) | copy-start | bytes 898564
  179.9 4.2 copy-start.7
  181.4 2.7 copy-start.8
  274.8 4.0 collective-permute-start.12
  276.6 6.5 %collective-permute-start.13 = (f32[3,1,64,128]{3,2,1,0:T(8,128)S(1)}, f32[3,1,64,128]{3,2,1,0:T(8,128)S(1)}, u32[]{:S(2)}, u32[]{:S(2)}) collective-permute-start(f32[3,1,64,128]{3,2,1,0:T(8,128)S(1)} %get-tuple-element.353), channel_id=1, source_target_pairs={{2,0},{4,2},{6,4},{8,6},{10,8},{12,10},{14,12},{16,14},{18,16},{20... | collective-permute-start | bytes 294920 | tf_op jit(solution)/shard_map/ppermute | solution.py:35
  283.2 4.6 %collective-permute-start.15 = (f32[3,4,1,128]{3,2,1,0:T(1,128)S(1)}, f32[3,4,1,128]{3,2,1,0:T(1,128)S(1)}, u32[]{:S(2)}, u32[]{:S(2)}) collective-permute-start(f32[3,4,1,128]{3,2,1,0:T(1,128)S(1)} %get-tuple-element.341), channel_id=1, source_target_pairs={{1,0},{3,2},{5,4},{7,6},{9,8},{11,10},{13,12},{15,14},{17,16},{19,... | collective-permute-start | bytes 18440 | tf_op jit(solution)/shard_map/ppermute | solution.py:35
  284.5 3.8 collective-permute-start.14
  307.4 9.5 %copy-start.2 = (f32[3,3,65,128]{3,2,1,0:T(8,128)S(1)}, f32[3,3,65,128]{3,2,1,0:T(8,128)}, u32[]{:S(2)}) copy-start(f32[3,3,65,128]{3,2,1,0:T(8,128)} %reshape.1035) | copy-start | bytes 898564
  315.1 2.7 copy-start.5
  366.2 16.3 %copy-start.1 = (f32[3,2,64,128]{3,2,1,0:T(8,128)}, f32[3,2,64,128]{3,2,1,0:T(8,128)S(1)}, u32[]{:S(2)}) copy-start(f32[3,2,64,128]{3,2,1,0:T(8,128)S(1)} %get-tuple-element.295) | copy-start | bytes 589828
  366.2 6.6 %collective-permute-start.16 = (f32[3,1,64,128]{3,2,1,0:T(8,128)S(1)}, f32[3,1,64,128]{3,2,1,0:T(8,128)S(1)}, u32[]{:S(2)}, u32[]{:S(2)}) collective-permute-start(f32[3,1,64,128]{3,2,1,0:T(8,128)S(1)} %slice.1645), channel_id=1, source_target_pairs={{2,0},{4,2},{6,4},{8,6},{10,8},{12,10},{14,12},{16,14},{18,16},{20... | collective-permute-start | bytes 294920 | tf_op jit(solution)/shard_map/ppermute | solution.py:22
  372.8 3.0 collective-permute-start.17
  430.8 5.9 %collective-permute-start.18 = (f32[1,64,128]{2,1,0:T(8,128)S(1)}, f32[1,64,128]{2,1,0:T(8,128)S(1)}, u32[]{:S(2)}, u32[]{:S(2)}) collective-permute-start(f32[1,64,128]{2,1,0:T(8,128)S(1)} %get-tuple-element.362), channel_id=1, source_target_pairs={{0,2},{2,4},{4,6},{6,0},{1,3},{3,5},{5,7},{7,1},{8,10},{10,12},{12... | collective-permute-start | bytes 98312 | tf_op jit(solution)/shard_map/ppermute | solution.py:32
  432.4 4.3 collective-permute-start.19
  436.7 1.2 collective-permute-start.20
  436.8 1.3 collective-permute-start.21
Sparse Core Ops, SparseCore 0:
  385.7 44.0 all-reduce.24
where the time goes:
time: 448 us; the launch traced here: 446 us
  blocking collectives  217 us (48%)
  local copies, waits for them, and re-layouts  69 us (15%)
  waiting for transfers between devices  67.9 us (15%)
  starting transfers between devices  35.5 us (8%)
  other arithmetic  26.9 us (6%)
  between operations  21.2 us (5%)
  matrix products  8.23 us (2%)
    psum x3, blocking collectives, squares(): return lax.psum(jnp.sum(residual * residual), ('mod', 'slab', 'sub'))  128 us
    psum x2, blocking collectives, local(): lax.psum(jnp.sum(direction * image), ('mod', 'slab', 'sub'))  89.4 us
    psum x1, waiting for transfers between devices, local(): module_sens = lax.psum(slope, 'mod')  44.2 us
    unnamed x52, local copies, waits for them, and re-layouts  20.3 us
    ppermute x10, starting transfers between devices, extended_2(): lax.ppermute(lax.slice_in_dim(block, block.shape[dim] - width, None, axis...  19.7 us
    scatter-add x18, local copies, waits for them, and re-layouts, element_forces(): result.at[:, bit_x:bit_x + count_x, bit_y:bit_y + count_y, :].add(portion)  15.4 us
    ppermute x10, starting transfers between devices, extended_2(): lax.ppermute(lax.slice_in_dim(block, 0, width, axis=dim), axis, backward)  13.2 us
    add x12, other arithmetic, element_forces(): result.at[:, bit_x:bit_x + count_x, bit_y:bit_y + count_y, :].add(portion)  12 us
  transfers between devices with their start and end apart: 23, of which 16 were waited for; matrix products, arithmetic and copies ran while one was open for 1% of the time, Pallas kernels for 0%

commit v1 on v0

v1 whole, which is shorter than its diff:
```python
import math

import jax
import jax.numpy as jnp
import numpy as np
from jax import lax
from jax.experimental import pallas as pl
from jax.experimental.pallas import tpu as pltpu
from jax.sharding import PartitionSpec as P

stiff_floor = 0.01
penalty = 3.0
sharpness = 4.0
threshold = 0.5
filter_reach = 1.8

AXES = ("mod", "slab", "sub")
ROWS = 8
FACE = filter_reach - 1.0
EDGE = filter_reach - math.sqrt(2.0)
CORNER = filter_reach - math.sqrt(3.0)
LOWER = math.tanh(sharpness * threshold)
UPPER = math.tanh(sharpness * (1.0 - threshold))


def stiffness_modes():
    poisson = 0.3
    lame = poisson / ((1.0 + poisson) * (1.0 - 2.0 * poisson))
    shear = 1.0 / (2.0 * (1.0 + poisson))
    elastic = np.zeros((6, 6))
    elastic[:3, :3] = lame
    for axis in range(3):
        elastic[axis, axis] += 2.0 * shear
        elastic[axis + 3, axis + 3] = shear
    offset = 0.5 / math.sqrt(3.0)
    points = [0.5 - offset, 0.5 + offset]
    stiffness = np.zeros((24, 24))
    for point in ((a, b, c) for a in points for b in points for c in points):
        strain = np.zeros((6, 24))
        for corner in range(8):
            bits = (corner >> 2 & 1, corner >> 1 & 1, corner & 1)
            along = [point[a] if bits[a] else 1.0 - point[a] for a in range(3)]
            sign = [1.0 if bits[a] else -1.0 for a in range(3)]
            gx = sign[0] * along[1] * along[2]
            gy = along[0] * sign[1] * along[2]
            gz = along[0] * along[1] * sign[2]
            col = 3 * corner
            strain[0, col] = gx
            strain[1, col + 1] = gy
            strain[2, col + 2] = gz
            strain[3, col], strain[3, col + 1] = gy, gx
            strain[4, col + 1], strain[4, col + 2] = gz, gy
            strain[5, col], strain[5, col + 2] = gz, gx
        stiffness += strain.T @ elastic @ strain / 8.0
    basis = np.zeros((24, 24))
    for mode in range(8):
        for corner in range(8):
            value = 1.0
            for bit in range(3):
                if mode >> bit & 1 and not corner >> bit & 1:
                    value = -value
            for k in range(3):
                basis[3 * mode + k, 3 * corner + k] = value
    table = basis @ stiffness @ basis.T / 64.0
    table[np.abs(table) < 1e-9] = 0.0
    return table


TABLE = stiffness_modes()


def lanes(shape):
    return lax.broadcasted_iota(jnp.int32, shape, 1)


def rows(shape):
    return lax.broadcasted_iota(jnp.int32, shape, 0)


def z_up(x):
    return jnp.where(lanes(x.shape) < x.shape[1] - 1, pltpu.roll(x, x.shape[1] - 1, 1), 0.0)


def z_down(x):
    return jnp.where(lanes(x.shape) > 0, pltpu.roll(x, 1, 1), 0.0)


def y_up(x):
    return jnp.where(rows(x.shape) < x.shape[0] - 1, pltpu.roll(x, x.shape[0] - 1, 0), 0.0)


def y_down(x):
    return jnp.where(rows(x.shape) > 0, pltpu.roll(x, 1, 0), 0.0)


def two_rows(read, y0, count):
    here = read(y0)
    above = y_up(here) if y0 + ROWS == count else read(y0 + 1)
    return here, above


def face_modes(here, above):
    out = []
    for part in (here + above, above - here):
        shifted = z_up(part)
        out += [part + shifted, shifted - part]
    return out


def element_modes(low, high):
    sums = [[high[k][m] + low[k][m] for m in range(4)] for k in range(3)]
    diffs = [[high[k][m] - low[k][m] for m in range(4)] for k in range(3)]
    return [sums[k] + diffs[k] for k in range(3)]


def mode_forces(q):
    made = {}

    def scaled(j, value):
        key = (j, round(value, 12))
        if key not in made:
            made[key] = q[j % 3][j // 3] * np.float32(value)
        return made[key]

    out = [[None] * 8 for _ in range(3)]
    for i in range(24):
        total = None
        for j in np.nonzero(TABLE[i])[0]:
            term = scaled(int(j), float(TABLE[i, j]))
            total = term if total is None else total + term
        out[i % 3][i // 3] = total
    return out


def element_energy(q):
    r = mode_forces(q)
    total = None
    for k in range(3):
        for m in range(1, 8):
            term = q[k][m] * r[k][m]
            total = term if total is None else total + term
    return total


def apply_rows(low, own, high, mod_low, mod_own):
    r_low = mode_forces(element_modes(low, own))
    r_own = mode_forces(element_modes(own, high))
    here, above = [], []
    for k in range(3):
        field = []
        for m in range(4):
            a, b = r_low[k][m], r_low[k][m + 4]
            c, d = r_own[k][m], r_own[k][m + 4]
            from_low = b if a is None else a + b
            from_own = -d if c is None else c - d
            field.append(mod_low * from_low + mod_own * from_own)
        part = []
        for py in range(2):
            s, d = field[2 * py], field[2 * py + 1]
            part.append((s - d) + z_down(s + d))
        here.append(part[0] - part[1])
        above.append(part[0] + part[1])
    return here, above


def operator_loop(count, read_low, read_own, read_high, read_free, mod_low_ref, mod_own_ref, out_ref):
    shape = (ROWS, out_ref.shape[2])
    square = jnp.zeros(shape, jnp.float32)
    cross = jnp.zeros(shape, jnp.float32)
    norm = jnp.zeros(shape, jnp.float32)
    carry = [jnp.zeros(shape, jnp.float32)] * 3
    first = rows(shape) == 0
    for y0 in range(0, count, ROWS):
        layers = []
        owns = []
        for read in (read_low, read_own, read_high):
            layer = []
            for k in range(3):
                here, up = two_rows(lambda y, k=k, read=read: read(k, y), y0, count)
                layer.append(face_modes(here, up))
                if read is read_own:
                    owns.append(here)
            layers.append(layer)
        here, above = apply_rows(
            *layers, mod_low_ref[pl.ds(y0, ROWS), :], mod_own_ref[pl.ds(y0, ROWS), :]
        )
        for k in range(3):
            rolled = pltpu.roll(above[k], 1, 0)
            force = here[k] + jnp.where(first, carry[k], rolled)
            carry[k] = rolled
            image = read_free(k, y0) * force
            out_ref[k, pl.ds(y0, ROWS), :] = image
            square += image * image
            cross += owns[k] * image
            norm += owns[k] * owns[k]
    return norm, cross, square


def energy_loop(count, read_own, read_high, use):
    for y0 in range(0, count, ROWS):
        layers = []
        for read in (read_own, read_high):
            layers.append(
                [
                    face_modes(*two_rows(lambda y, k=k, read=read: read(k, y), y0, count))
                    for k in range(3)
                ]
            )
        use(y0, element_energy(element_modes(*layers)))


def line(tile):
    return jnp.sum(tile, axis=0, keepdims=True)


def prepare_kernel(design, fixed, load, swap, first, second):
    sub = lax.axis_index("sub")

    def right_side(k, layer):
        return (1 - fixed[k, layer]).astype(jnp.float32) * load[k, layer].astype(jnp.float32)

    for k in range(3):
        values = [right_side(k, 0), right_side(k, 1)]
        for layer in range(2):
            swap[2 * k + layer] = values[layer]
        swap[6 + k] = (1 - fixed[k, 1 - sub]).astype(jnp.float32)

        @pl.when(sub == 0)
        def _(k=k, values=values):
            first[k] = values[1]
            second[k] = values[0]

        @pl.when(sub == 1)
        def _(k=k, values=values):
            first[k] = values[0]
            second[k] = values[1]

    swap[9] = design[0]
    swap[10] = design[1]
    first[3] = design[0]
    second[3] = design[0]
    first[4] = design[1]
    second[4] = design[1]


def filter_planes(low, mid, high):
    both = low + high

    def faces(p):
        across = y_up(p) + y_down(p)
        return across + z_up(p) + z_down(p), z_up(across) + z_down(across)

    mid_face, mid_diag = faces(mid)
    both_face, both_diag = faces(both)
    return (
        filter_reach * mid
        + FACE * (both + mid_face)
        + EDGE * (both_face + mid_diag)
        + CORNER * both_diag
    )


def weight_plane(shape, row_offset, count):
    row = rows(shape) + row_offset
    lane = lanes(shape)

    def neighbours(index, size):
        return jnp.where(index > 0, 1.0, 0.0) + jnp.where(index < size - 1, 1.0, 0.0)

    ry = neighbours(row, count)
    rz = neighbours(lane, shape[1])
    face, diag = ry + rz, ry * rz
    return (
        filter_reach
        + FACE * (2.0 + face)
        + EDGE * (2.0 * face + diag)
        + (2.0 * CORNER) * diag
    )


def start_kernel(
    mods, slabs,
    design, fixed, load, swap, first, second, third, fourth,
    v0, v0_high, v1, free, mod_low, mod_own, slope_factor, chain_factor, moments,
    v0_low, layers,
):
    mod, slab, sub = (lax.axis_index(a) for a in AXES)
    half = design.shape[1]
    count = 2 * half
    mine = pl.ds(pl.multiple_of(sub * half, half), half)
    other = pl.ds(pl.multiple_of((1 - sub) * half, half), half)
    for layer in range(2):
        layers[2 - sub + layer, mine, :] = design[layer]
        layers[2 - sub + layer, other, :] = swap[9 + layer]
    for source, part in ((first, mine), (second, other)):

        @pl.when(sub == 0)
        def _(source=source, part=part):
            layers[0, part, :] = source[3]
            layers[1, part, :] = source[4]

        @pl.when(sub == 1)
        def _(source=source, part=part):
            layers[3, part, :] = source[3]

    @pl.when(sub == 1)
    def _():
        layers[0, pl.ds(0, half), :] = third[...]
        layers[0, pl.ds(half, half), :] = fourth[...]

    weight = weight_plane((count, design.shape[2]), 0, count)
    starts = (mod == 0) & (slab == 0) & (sub == 0)
    filtered = filter_planes(layers[0], layers[1], layers[2]) / weight
    hyper = jnp.tanh(sharpness * (filtered - threshold))
    projected = (LOWER + hyper) * (1.0 / (LOWER + UPPER))
    below = stiff_floor + (1.0 - stiff_floor) * projected * projected * projected
    mod_low[...] = below * jnp.where(starts, 0.0, 1.0)
    filtered = filter_planes(layers[1], layers[2], layers[3]) / weight
    hyper = jnp.tanh(sharpness * (filtered - threshold))
    projected = (LOWER + hyper) * (1.0 / (LOWER + UPPER))
    squared = projected * projected
    mod_own[...] = stiff_floor + (1.0 - stiff_floor) * squared * projected
    slope_factor[...] = (-penalty * (1.0 - stiff_floor)) * squared
    chain_factor[...] = (sharpness / (LOWER + UPPER)) * (1.0 - hyper * hyper) / weight

    ends = (mod == mods - 1) & (slab == slabs - 1) & (sub == 1)
    inside = jnp.where(ends, 0.0, 1.0)
    for k in range(3):
        own_half = (1 - fixed[k, sub]).astype(jnp.float32)
        free[k, mine, :] = own_half
        free[k, other, :] = swap[6 + k]
        v0[k, mine, :] = own_half * load[k, sub].astype(jnp.float32)
        v0[k, other, :] = swap[2 * k + sub]
        inner = (1 - fixed[k, 1 - sub]).astype(jnp.float32) * load[k, 1 - sub].astype(jnp.float32)

        @pl.when(sub == 0)
        def _(k=k, inner=inner):
            v0_high[k, mine, :] = inner
            v0_high[k, other, :] = swap[2 * k + 1]
            v0_low[k, mine, :] = first[k]
            v0_low[k, other, :] = second[k]

        @pl.when(sub == 1)
        def _(k=k, inner=inner):
            v0_low[k, mine, :] = inner
            v0_low[k, other, :] = swap[2 * k]
            v0_high[k, mine, :] = first[k] * inside
            v0_high[k, other, :] = second[k] * inside

    norm, cross, square = operator_loop(
        count,
        lambda k, y: v0_low[k, pl.ds(y, ROWS), :],
        lambda k, y: v0[k, pl.ds(y, ROWS), :],
        lambda k, y: v0_high[k, pl.ds(y, ROWS), :],
        lambda k, y: free[k, pl.ds(y, ROWS), :],
        mod_low,
        mod_own,
        v1,
    )
    moments[...] = jnp.concatenate(
        [line(norm), line(cross), line(square), jnp.zeros((5, norm.shape[1]), jnp.float32)], axis=0
    )


def second_kernel(v1, inner, outer, free, mod_low, mod_own, before, v2, v1_high, moments):
    sub = lax.axis_index("sub")
    count = v1.shape[1]
    even = sub == 0
    for k in range(3):
        v1_high[k] = jnp.where(even, inner[k], outer[k])

    def read_low(k, y):
        return jnp.where(even, outer[k, pl.ds(y, ROWS), :], inner[k, pl.ds(y, ROWS), :])

    _, cross, square = operator_loop(
        count,
        read_low,
        lambda k, y: v1[k, pl.ds(y, ROWS), :],
        lambda k, y: v1_high[k, pl.ds(y, ROWS), :],
        lambda k, y: free[k, pl.ds(y, ROWS), :],
        mod_low,
        mod_own,
        v2,
    )
    zero = jnp.zeros((3, cross.shape[1]), jnp.float32)
    moments[...] = before[...] + jnp.concatenate(
        [zero, line(cross), line(square), zero], axis=0
    )


def third_kernel(v2, v2_high, mod_own, before, moments):
    count = v2.shape[1]
    total = [jnp.zeros((ROWS, v2.shape[2]), jnp.float32)]

    def use(y0, energy):
        total[0] += energy * mod_own[pl.ds(y0, ROWS), :]

    energy_loop(
        count,
        lambda k, y: v2[k, pl.ds(y, ROWS), :],
        lambda k, y: v2_high[k, pl.ds(y, ROWS), :],
        use,
    )
    width = v2.shape[2]
    moments[...] = before[...] + jnp.concatenate(
        [
            jnp.zeros((5, width), jnp.float32),
            line(total[0]),
            jnp.zeros((2, width), jnp.float32),
        ],
        axis=0,
    )


def coefficients(m):
    step = m[0] / m[1]
    x0 = step
    r1 = -step
    norm = m[0] + 2.0 * r1 * m[1] + r1 * r1 * m[2]
    ratio = norm / m[0]
    p0, p1 = 1.0 + ratio, r1
    step = norm / (p0 * p0 * m[1] + 2.0 * p0 * p1 * m[2] + p1 * p1 * m[3])
    x0, x1 = x0 + step * p0, step * p1
    r1, r2 = r1 - step * p0, -step * p1
    after = (
        m[0]
        + 2.0 * r1 * m[1]
        + (r1 * r1 + 2.0 * r2) * m[2]
        + 2.0 * r1 * r2 * m[3]
        + r2 * r2 * m[4]
    )
    ratio = after / norm
    p0, p1, p2 = 1.0 + ratio * p0, r1 + ratio * p1, r2
    step = after / (
        p0 * p0 * m[1]
        + 2.0 * p0 * p1 * m[2]
        + (p1 * p1 + 2.0 * p0 * p2) * m[3]
        + 2.0 * p1 * p2 * m[4]
        + p2 * p2 * m[5]
    )
    return x0 + step * p0, x1 + step * p1, step * p2


def combine_kernel(
    gathered, v0, v0_high, v1, v1_high, v2, v2_high, slope_factor,
    slope, keep, send,
    own, high,
):
    sub = lax.axis_index("sub")
    count = v0.shape[1]
    half = count // 2
    total = jnp.sum(gathered[...], axis=0)
    sums = jnp.sum(total, axis=1, keepdims=True)
    c0, c1, c2 = coefficients([sums[k : k + 1] for k in range(6)])
    for k in range(3):
        own[k] = c0 * v0[k] + c1 * v1[k] + c2 * v2[k]
        high[k] = c0 * v0_high[k] + c1 * v1_high[k] + c2 * v2_high[k]

    mine = pl.ds(pl.multiple_of(sub * half, half), half)
    other = pl.ds(pl.multiple_of((1 - sub) * half, half), half)
    for k in range(3):
        keep[k] = own[k, mine, :]
        send[k] = own[k, other, :]

    def use(y0, energy):
        slope[pl.ds(y0, ROWS), :] = slope_factor[pl.ds(y0, ROWS), :] * energy

    energy_loop(
        count,
        lambda k, y: own[k, pl.ds(y, ROWS), :],
        lambda k, y: high[k, pl.ds(y, ROWS), :],
        use,
    )


def scale_kernel(*refs):
    slopes, (chain_factor, scaled, same, cross) = refs[:-4], refs[-4:]
    sub = lax.axis_index("sub")
    total = slopes[0][...]
    for other in slopes[1:]:
        total = total + other[...]
    scaled[...] = total * chain_factor[...]
    window = same.shape[0]
    shift = scaled.shape[0] - window
    same[...] = scaled[pl.ds(pl.multiple_of(sub * shift, 8), window), :]
    cross[...] = scaled[pl.ds(pl.multiple_of((1 - sub) * shift, 8), window), :]


def gradient_kernel(scaled, partner, outer, far, gradient, planes, sums):
    sub = lax.axis_index("sub")
    window = partner.shape[0]
    shift = scaled.shape[0] - window
    mine = scaled[pl.ds(pl.multiple_of(sub * shift, 8), window), :]

    @pl.when(sub == 0)
    def _():
        planes[0] = outer[...]
        planes[1] = mine
        planes[2] = partner[...]
        planes[3] = far[...]

    @pl.when(sub == 1)
    def _():
        planes[0] = far[...]
        planes[1] = partner[...]
        planes[2] = mine
        planes[3] = outer[...]

    half = gradient.shape[1]
    part = pl.ds(pl.multiple_of(sub * (window - half), 8), half)
    for layer in range(2):
        sums[...] = filter_planes(planes[layer], planes[layer + 1], planes[layer + 2])
        gradient[layer] = sums[part, :]


def call(body, outs, scratch=(), name=None):
    return pl.pallas_call(
        body,
        out_shape=[jax.ShapeDtypeStruct(shape, jnp.float32) for shape in outs],
        scratch_shapes=[pltpu.VMEM(shape, jnp.float32) for shape in scratch],
        compiler_params=pltpu.CompilerParams(vmem_limit_bytes=16 * 2**20),
        name=name,
    )


def routes(mods, slabs):
    chips = mods * slabs

    def at(chip, sub):
        return 2 * chip + sub

    def beside(chip, steps, cyclic):
        target = chip + steps
        if cyclic:
            return target % chips
        return target if 0 <= target < chips else None

    def built(moves, cyclic):
        pairs = []
        for chip in range(chips):
            for sub, steps, to in moves:
                target = beside(chip, steps, cyclic)
                if target is not None:
                    pairs.append((at(chip, sub), at(target, to)))
        return pairs

    def in_module(moves):
        pairs = []
        for chip in range(chips):
            mod, slab = divmod(chip, slabs)
            for sub, steps, to in moves:
                pairs.append((at(chip, sub), at(mod * slabs + (slab + steps) % slabs, to)))
        return pairs

    return dict(
        swap=built([(0, 0, 1), (1, 0, 0)], True),
        first=built([(0, 1, 0), (1, -1, 1)], True),
        second=built([(1, 1, 0), (0, -1, 1)], True),
        third=built([(0, 1, 1)], True),
        fourth=built([(1, 1, 1)], True),
        outer=built([(1, 1, 0), (0, -1, 1)], False),
        down=built([(1, 0, 0), (0, -1, 1)], False),
        halo_cross=in_module([(1, 1, 0), (0, -1, 1)]),
        halo_same=in_module([(0, -1, 0), (1, 1, 1)]),
    )


def module_routes(mods):
    if mods & (mods - 1) == 0:
        return [[(m, m ^ s) for m in range(mods)] for s in range(1, mods)]
    return [[(m, (m + s) % mods) for m in range(mods)] for s in range(1, mods)]


def local(mods, slabs, design, fixed, load):
    half, width = design.shape[1:]
    count = 2 * half
    path = routes(mods, slabs)

    def move(value, name):
        return lax.ppermute(value, AXES, path[name])

    plane = (count, width)
    layer = (3, count, width)
    swap, first, second = call(
        prepare_kernel, [(11, half, width), (5, half, width), (5, half, width)], name="prepare"
    )(design, fixed, load)
    first = move(first, "first")
    second = move(second, "second")
    third = move(design[1], "third")
    fourth = move(design[1], "fourth")
    swap = move(swap, "swap")

    def start_body(*refs):
        start_kernel(mods, slabs, *refs)

    v0, v0_high, v1, free, mod_low, mod_own, slope_factor, chain_factor, moments = call(
        start_body,
        [layer, layer, layer, layer, plane, plane, plane, plane, (8, width)],
        [layer, (4,) + plane],
        name="start",
    )(design, fixed, load, swap, first, second, third, fourth)
    outer = move(v1, "outer")
    inner = move(v1, "swap")
    v2, v1_high, moments = call(second_kernel, [layer, layer, (8, width)], name="second")(
        v1, inner, outer, free, mod_low, mod_own, moments
    )
    v2_high = move(v2, "down")
    (moments,) = call(third_kernel, [(8, width)], name="third")(v2, v2_high, mod_own, moments)
    devices = 2 * mods * slabs
    gathered = lax.all_to_all(
        jnp.broadcast_to(moments, (devices, 8, width)), AXES, 0, 0, tiled=True
    )
    slope, keep, send = call(
        combine_kernel, [plane, (3, half, width), (3, half, width)], [layer, layer], name="combine"
    )(gathered, v0, v0_high, v1, v1_high, v2, v2_high, slope_factor)
    slopes = [slope] + [lax.ppermute(slope, "mod", pairs) for pairs in module_routes(mods)]
    received = move(send, "swap")
    window = half + 8
    scaled, same, cross = call(
        scale_kernel, [plane, (window, width), (window, width)], name="scale"
    )(*slopes, chain_factor)
    outer = move(cross, "halo_cross")
    far = move(same, "halo_same")
    partner = move(cross, "swap")
    even = lax.axis_index("sub") == 0
    displacement = jnp.stack(
        [jnp.where(even, keep, received), jnp.where(even, received, keep)], axis=1
    )
    (gradient,) = call(
        gradient_kernel, [(2, half, width)], [(4, window, width), (window, width)], name="gradient"
    )(scaled, partner, outer, far)
    return displacement, gradient


def solution(mesh):
    mods, slabs = mesh.shape["mod"], mesh.shape["slab"]
    assert mesh.shape["sub"] == 2
    deck = P(None, ("mod", "slab"), "sub", None)

    def body(design, fixed_mask, load_mask):
        return local(mods, slabs, design, fixed_mask, load_mask)

    return jax.shard_map(
        body,
        mesh=mesh,
        in_specs=(P("slab", "sub", None), deck, deck),
        out_specs=(deck, P("slab", "sub", None)),
        check_vma=False,
    )
```

time: 448 us -> 68.6 us (0.15)
  blocking collectives: 217 us -> 18.1 us
  local copies, waits for them, and re-layouts: 69 us -> 3.39 us
  waiting for transfers between devices: 67.9 us -> 22.2 us
  other arithmetic: 26.9 us -> 0.03 us
  between operations: 21.2 us -> 0.73 us
  starting transfers between devices: 35.5 us -> 18.5 us
  matrix products: 8.23 us -> 0 us
  Pallas kernels: 0 us -> 5.44 us
    psum x5 -> x0, blocking collectives: 217 us -> none  [the longest x3 128 us: squares(): return lax.psum(jnp.sum(residual * residual), ('mod', 'slab', 'sub'))]
    psum x1 -> x0, waiting for transfers between devices: 44.2 us -> none  [local(): module_sens = lax.psum(slope, 'mod')]
    all_to_all x0 -> x1, blocking collectives: none -> 18.1 us  [local(): lax.all_to_all(jnp.broadcast_to(moments, (devices, 8, width)), AXES, 0, 0...]
    ppermute x22 -> x15, starting transfers between devices: 35.5 us -> 18.5 us  [the longest x12 15 us: move(): return lax.ppermute(value, AXES, path[name])]
    unnamed x52 -> x7, local copies, waits for them, and re-layouts: 20.3 us -> 3.38 us
    scatter-add x18 -> x0, local copies, waits for them, and re-layouts: 15.4 us -> none  [element_forces(): result.at[:, bit_x:bit_x + count_x, bit_y:bit_y + count_y, :].add(portion)]
    add x13 -> x0, other arithmetic: 13 us -> none  [the longest x12 12 us: element_forces(): result.at[:, bit_x:bit_x + count_x, bit_y:bit_y + count_y, :].add(portion)]
    another operation x18 -> x0, local copies, waits for them, and re-layouts: 11.5 us -> none
  transfers between devices with their start and end apart: 23 -> 15, of which waited for: 16 -> 8; matrix products, arithmetic and copies ran while one was open for 1% -> 1% of each run, Pallas kernels for 0% -> 0%
where the time goes in v1:
time: 68.6 us; the launch traced here: 68.3 us
  waiting for transfers between devices  22.2 us (32%)
  starting transfers between devices  18.5 us (27%)
  blocking collectives  18.1 us (26%)
  Pallas kernels  5.44 us (8%)
  local copies, waits for them, and re-layouts  3.39 us (5%)
  between operations  0.73 us (1%)
    ppermute x12, waiting for transfers between devices, move(): return lax.ppermute(value, AXES, path[name])  18.9 us
    all_to_all x1, blocking collectives, local(): lax.all_to_all(jnp.broadcast_to(moments, (devices, 8, width)), AXES, 0, 0...  18.1 us
    ppermute x12, starting transfers between devices, move(): return lax.ppermute(value, AXES, path[name])  15 us
    ppermute x3, starting transfers between devices, local(): lax.ppermute(slope, 'mod', pairs)  3.49 us
    unnamed x7, local copies, waits for them, and re-layouts  3.38 us
    ppermute x3, waiting for transfers between devices, local(): lax.ppermute(slope, 'mod', pairs)  3.29 us
    pallas_call x1, Pallas kernels, local(): call(start_body, [layer, layer, layer, layer, plane, plane, plane, plane,...  1.96 us
    pallas_call x1, Pallas kernels, local(): call(second_kernel, [layer, layer, (8, width)], name='second')  1.37 us
  transfers between devices with their start and end apart: 15, of which 8 were waited for; matrix products, arithmetic and copies ran while one was open for 1% of the time, Pallas kernels for 0%

profile of v1, /device:TPU:0, one launch (start us, length us, event | category | flops | bytes accessed | tf_op | source)
XLA Modules:
  0.0 68.3 jit_solution(16875552006784328644)
XLA Ops:
  0.6 0.0 copy-start
  0.6 0.9 %copy-done = s32[3,2,64,128]{3,2,1,0:T(8,128)S(1)} copy-done((s32[3,2,64,128]{3,2,1,0:T(8,128)S(1)}, s32[3,2,64,128]{3,2,1,0:T(8,128)}, u32[]{:S(2)}) %copy-start) | copy-done | bytes 196632
  1.6 0.0 copy-start.1
  1.6 0.9 %copy-done.1 = s32[3,2,64,128]{3,2,1,0:T(8,128)S(1)} copy-done((s32[3,2,64,128]{3,2,1,0:T(8,128)S(1)}, s32[3,2,64,128]{3,2,1,0:T(8,128)}, u32[]{:S(2)}) %copy-start.1) | copy-done | bytes 196632
  2.5 0.0 copy-start.2
  2.5 0.8 %copy-done.2 = f32[2,64,128]{2,1,0:T(8,128)S(1)} copy-done((f32[2,64,128]{2,1,0:T(8,128)S(1)}, f32[2,64,128]{2,1,0:T(8,128)}, u32[]{:S(2)}) %copy-start.2) | copy-done | bytes 65560
  3.3 0.1 prepare.1
  3.4 0.5 collective-permute-start
  3.9 2.6 %collective-permute-start.1 = (f32[5,64,128]{2,1,0:T(8,128)S(1)}, f32[5,64,128]{2,1,0:T(8,128)S(1)}, u32[]{:S(2)}, u32[]{:S(2)}) collective-permute-start(f32[5,64,128]{2,1,0:T(8,128)S(1)} %get-tuple-element.24), channel_id=1, source_target_pairs={{0,2},{1,31},{2,4},{3,1},{4,6},{5,3},{6,8},{7,5},{8,10},{9,7},{10,... | collective-permute-start | bytes 491528 | tf_op jit(solution)/shard_map/ppermute | solution.py:580
  6.6 4.1 %collective-permute-start.2 = (f32[5,64,128]{2,1,0:T(8,128)S(1)}, f32[5,64,128]{2,1,0:T(8,128)S(1)}, u32[]{:S(2)}, u32[]{:S(2)}) collective-permute-start(f32[5,64,128]{2,1,0:T(8,128)S(1)} %get-tuple-element.25), channel_id=1, source_target_pairs={{1,2},{0,31},{3,4},{2,1},{5,6},{4,3},{7,8},{6,5},{9,10},{8,7},{11,... | collective-permute-start | bytes 491528 | tf_op jit(solution)/shard_map/ppermute | solution.py:580
  10.7 1.3 %collective-permute-start.3 = (f32[64,128]{1,0:T(8,128)S(1)}, f32[64,128]{1,0:T(8,128)S(1)}, u32[]{:S(2)}, u32[]{:S(2)}) collective-permute-start(f32[64,128]{1,0:T(8,128)S(1)} %slice_bitcast_fusion), channel_id=1, source_target_pairs={{0,3},{2,5},{4,7},{6,9},{8,11},{10,13},{12,15},{14,17},{16,19},{18... | collective-permute-start | bytes 98312 | tf_op jit(solution)/shard_map/ppermute | solution.py:580
  12.0 0.7 collective-permute-start.4
  12.6 3.3 %collective-permute-done.3.refs_6_ = f32[64,128]{1,0:T(8,128)S(1)} collective-permute-done((f32[64,128]{1,0:T(8,128)S(1)}, f32[64,128]{1,0:T(8,128)S(1)}, u32[]{:S(2)}, u32[]{:S(2)}) %collective-permute-start.3) | collective-permute-done | bytes 32800 | tf_op jit(solution)/shard_map/ppermute | solution.py:580
  16.0 0.0 collective-permute-done.4.refs_7_
  16.0 0.0 collective-permute-done.1.refs_4_
  16.0 2.9 %collective-permute-done.2.refs_5_ = f32[5,64,128]{2,1,0:T(8,128)S(1)} collective-permute-done((f32[5,64,128]{2,1,0:T(8,128)S(1)}, f32[5,64,128]{2,1,0:T(8,128)S(1)}, u32[]{:S(2)}, u32[]{:S(2)}) %collective-permute-start.2) | collective-permute-done | bytes 163872 | tf_op jit(solution)/shard_map/ppermute | solution.py:580
  18.9 0.0 collective-permute-done.refs_3_
  18.9 2.0 %start.1 = (f32[3,128,128]{2,1,0:T(8,128)S(1)}, f32[3,128,128]{2,1,0:T(8,128)S(1)}, f32[3,128,128]{2,1,0:T(8,128)S(1)}, f32[3,128,128]{2,1,0:T(8,128)S(1)}, f32[...) custom-call(f32[2,64,128]{2,1,0:T(8,128)S(1)} %copy-done.2, ...), custom_call_target="tpu_custom_call" | custom-call | tf_op jit(solution)/shard_map/start/pallas_call | solution.py:596
  20.8 1.4 %collective-permute-start.5 = (f32[3,128,128]{2,1,0:T(8,128)S(1)}, f32[3,128,128]{2,1,0:T(8,128)S(1)}, u32[]{:S(2)}, u32[]{:S(2)}) collective-permute-start(f32[3,128,128]{2,1,0:T(8,128)S(1)} %get-tuple-element.26.v1), channel_id=1, source_target_pairs={{0,1},{1,0},{2,3},{3,2},{4,5},{5,4},{6,7},{7,6},{8,9},{9,8},{10,11... | collective-permute-start | bytes 589832 | tf_op jit(solution)/shard_map/ppermute | solution.py:580
  22.2 0.7 collective-permute-start.6
  22.9 0.4 collective-permute-done.5.inner
  23.3 0.0 collective-permute-done.6.outer
  23.3 1.4 %second.1 = (f32[3,128,128]{2,1,0:T(8,128)S(1)}, f32[3,128,128]{2,1,0:T(8,128)S(1)}, f32[8,128]{1,0:T(8,128)S(1)}) custom-call(f32[3,128,128]{2,1,0:T(8,128)S(1)} %get-tuple-element.26.v1, f32[3,128,128]{2,1,0:T(8,128)S(1)} %collective-permute-done.5.inner, f32[3,128,128]{2,1,0:T(8,128)S(1)} %collective-permute-done.6.outer, ...), custom_call_target="tpu_custom_call" | custom-call | tf_op jit(solution)/shard_map/second/pallas_call | solution.py:604
  24.7 1.3 %collective-permute-start.7 = (f32[3,128,128]{2,1,0:T(8,128)S(1)}, f32[3,128,128]{2,1,0:T(8,128)S(1)}, u32[]{:S(2)}, u32[]{:S(2)}) collective-permute-start(f32[3,128,128]{2,1,0:T(8,128)S(1)} %get-tuple-element.31.v2), channel_id=1, source_target_pairs={{1,0},{3,2},{2,1},{5,4},{4,3},{7,6},{6,5},{9,8},{8,7},{11,10},{10,... | collective-permute-start | bytes 589832 | tf_op jit(solution)/shard_map/ppermute | solution.py:580
  26.0 9.6 %collective-permute-done.7.v2_high = f32[3,128,128]{2,1,0:T(8,128)S(1)} collective-permute-done((f32[3,128,128]{2,1,0:T(8,128)S(1)}, f32[3,128,128]{2,1,0:T(8,128)S(1)}, u32[]{:S(2)}, u32[]{:S(2)}) %collective-permute-start.7) | collective-permute-done | bytes 196640 | tf_op jit(solution)/shard_map/ppermute | solution.py:580
  35.6 0.4 third.1
  36.0 18.1 %all_to_all.5.gathered = f32[32,8,128]{2,1,0:T(8,128)S(1)} all-to-all(f32[32,8,128]{2,1,0:T(8,128)S(1)} %broadcast_in_dim.3), channel_id=1, replica_groups=mesh['mod'=4,'slab'=4,'sub'=2] {'mod','slab','sub'}, dimensions={0} | all-to-all | bytes 262144 | tf_op jit(solution)/shard_map/all_to_all | solution.py:610
  54.1 0.7 %combine.1 = (f32[128,128]{1,0:T(8,128)S(1)}, f32[3,64,128]{2,1,0:T(8,128)S(1)}, f32[3,64,128]{2,1,0:T(8,128)S(1)}) custom-call(f32[32,8,128]{2,1,0:T(8,128)S(1)} %all_to_all.5.gathered, f32[3,128,128]{2,1,0:T(8,128)S(1)} %get-tuple-element.33.v0, f32[3,128,128]{2,1,0:T(8,128)S(1)} %get-tuple-element.34.v0_high, f32[3,128,128]{2,1,0:T(8,128)S(1)} %get-tuple-element.26.v1, ...), custom_call_target="tpu_custom_call" | custom-call | tf_op jit(solution)/shard_map/combine/pallas_call | solution.py:613
  54.8 0.4 collective-permute-start.8
  55.2 0.6 collective-permute-start.10
  55.8 1.4 %collective-permute-start.11 = (f32[128,128]{1,0:T(8,128)S(1)}, f32[128,128]{1,0:T(8,128)S(1)}, u32[]{:S(2)}, u32[]{:S(2)}) collective-permute-start(f32[128,128]{1,0:T(8,128)S(1)} %get-tuple-element.39.refs_0_), channel_id=1, source_target_pairs={{0,24},{8,16},{16,8},{24,0},{1,25},{9,17},{17,9},{25,1},{2,26},{10... | collective-permute-start | bytes 196616 | tf_op jit(solution)/shard_map/ppermute | solution.py:616
  57.2 1.4 %collective-permute-start.9 = (f32[128,128]{1,0:T(8,128)S(1)}, f32[128,128]{1,0:T(8,128)S(1)}, u32[]{:S(2)}, u32[]{:S(2)}) collective-permute-start(f32[128,128]{1,0:T(8,128)S(1)} %get-tuple-element.39.refs_0_), channel_id=1, source_target_pairs={{0,8},{8,0},{16,24},{24,16},{1,9},{9,1},{17,25},{25,17},{2,10},{10... | collective-permute-start | bytes 196616 | tf_op jit(solution)/shard_map/ppermute | solution.py:616
  58.6 0.8 %collective-permute-done.10.refs_2_ = f32[128,128]{1,0:T(8,128)S(1)} collective-permute-done((f32[128,128]{1,0:T(8,128)S(1)}, f32[128,128]{1,0:T(8,128)S(1)}, u32[]{:S(2)}, u32[]{:S(2)}) %collective-permute-start.10) | collective-permute-done | bytes 65568 | tf_op jit(solution)/shard_map/ppermute | solution.py:616
  59.4 2.1 %collective-permute-done.11.refs_3_ = f32[128,128]{1,0:T(8,128)S(1)} collective-permute-done((f32[128,128]{1,0:T(8,128)S(1)}, f32[128,128]{1,0:T(8,128)S(1)}, u32[]{:S(2)}, u32[]{:S(2)}) %collective-permute-start.11) | collective-permute-done | bytes 65568 | tf_op jit(solution)/shard_map/ppermute | solution.py:616
  61.5 0.4 collective-permute-done.9.refs_1_
  62.0 0.1 collective-permute-start.12
  62.0 1.0 %collective-permute-start.13 = (f32[72,128]{1,0:T(8,128)S(1)}, f32[72,128]{1,0:T(8,128)S(1)}, u32[]{:S(2)}, u32[]{:S(2)}) collective-permute-start(f32[72,128]{1,0:T(8,128)S(1)} %get-tuple-element.42), channel_id=1, source_target_pairs={{1,2},{0,7},{3,4},{2,1},{5,6},{4,3},{7,0},{6,5},{9,10},{8,15},{11,... | collective-permute-start | bytes 110600 | tf_op jit(solution)/shard_map/ppermute | solution.py:580
  63.1 1.0 %collective-permute-start.14 = (f32[72,128]{1,0:T(8,128)S(1)}, f32[72,128]{1,0:T(8,128)S(1)}, u32[]{:S(2)}, u32[]{:S(2)}) collective-permute-start(f32[72,128]{1,0:T(8,128)S(1)} %get-tuple-element.43), channel_id=1, source_target_pairs={{0,6},{1,3},{2,0},{3,5},{4,2},{5,7},{6,4},{7,1},{8,14},{9,11},{10,... | collective-permute-start | bytes 110600 | tf_op jit(solution)/shard_map/ppermute | solution.py:580
  64.0 0.0 collective-permute-done.8
  64.1 0.7 %copy.5 = f32[3,2,64,128]{3,2,1,0:T(8,128)} copy(f32[3,2,64,128]{3,2,0,1:T(8,128)S(1)} %pad_maximum_fusion) | data formatting | bytes 393216
  64.7 0.0 collective-permute-done.12.partner
  64.7 2.7 %collective-permute-done.13.outer = f32[72,128]{1,0:T(8,128)S(1)} collective-permute-done((f32[72,128]{1,0:T(8,128)S(1)}, f32[72,128]{1,0:T(8,128)S(1)}, u32[]{:S(2)}, u32[]{:S(2)}) %collective-permute-start.13) | collective-permute-done | bytes 36896 | tf_op jit(solution)/shard_map/ppermute | solution.py:580
  67.4 0.0 collective-permute-done.14.far
  67.4 0.9 %gradient.1 = f32[2,64,128]{2,1,0:T(8,128)} custom-call(f32[128,128]{1,0:T(8,128)S(1)} %get-tuple-element.41.scaled, f32[72,128]{1,0:T(8,128)S(1)} %collective-permute-done.12.partner, f32[72,128]{1,0:T(8,128)S(1)} %collective-permute-done.13.outer, f32[72,128]{1,0:T(8,128)S(1)} %collective-permute-done.14.far), custom_call_target="tpu_custom_call" | custom-call | tf_op jit(solution)/shard_map/gradient/pallas_call | solution.py:629
  (5 shorter events, 0.1 us)
Async XLA Ops:
  0.6 0.9 %copy-start = (s32[3,2,64,128]{3,2,1,0:T(8,128)S(1)}, s32[3,2,64,128]{3,2,1,0:T(8,128)}, u32[]{:S(2)}) copy-start(s32[3,2,64,128]{3,2,1,0:T(8,128)} %refs_1_.1) | copy-start | bytes 589828
  1.6 0.9 %copy-start.1 = (s32[3,2,64,128]{3,2,1,0:T(8,128)S(1)}, s32[3,2,64,128]{3,2,1,0:T(8,128)}, u32[]{:S(2)}) copy-start(s32[3,2,64,128]{3,2,1,0:T(8,128)} %refs_2_.1) | copy-start | bytes 589828
  2.5 0.8 %copy-start.2 = (f32[2,64,128]{2,1,0:T(8,128)S(1)}, f32[2,64,128]{2,1,0:T(8,128)}, u32[]{:S(2)}) copy-start(f32[2,64,128]{2,1,0:T(8,128)} %refs_0_.1) | copy-start | bytes 196612
  3.4 15.5 %collective-permute-start = (f32[11,64,128]{2,1,0:T(8,128)S(1)}, f32[11,64,128]{2,1,0:T(8,128)S(1)}, u32[]{:S(2)}, u32[]{:S(2)}) collective-permute-start(f32[11,64,128]{2,1,0:T(8,128)S(1)} %get-tuple-element.23), channel_id=1, source_target_pairs={{0,1},{1,0},{2,3},{3,2},{4,5},{5,4},{6,7},{7,6},{8,9},{9,8},{10,11... | collective-permute-start | bytes 1081352 | tf_op jit(solution)/shard_map/ppermute | solution.py:580
  3.9 12.1 %collective-permute-start.1 = (f32[5,64,128]{2,1,0:T(8,128)S(1)}, f32[5,64,128]{2,1,0:T(8,128)S(1)}, u32[]{:S(2)}, u32[]{:S(2)}) collective-permute-start(f32[5,64,128]{2,1,0:T(8,128)S(1)} %get-tuple-element.24), channel_id=1, source_target_pairs={{0,2},{1,31},{2,4},{3,1},{4,6},{5,3},{6,8},{7,5},{8,10},{9,7},{10,... | collective-permute-start | bytes 491528 | tf_op jit(solution)/shard_map/ppermute | solution.py:580
  6.6 12.3 %collective-permute-start.2 = (f32[5,64,128]{2,1,0:T(8,128)S(1)}, f32[5,64,128]{2,1,0:T(8,128)S(1)}, u32[]{:S(2)}, u32[]{:S(2)}) collective-permute-start(f32[5,64,128]{2,1,0:T(8,128)S(1)} %get-tuple-element.25), channel_id=1, source_target_pairs={{1,2},{0,31},{3,4},{2,1},{5,6},{4,3},{7,8},{6,5},{9,10},{8,7},{11,... | collective-permute-start | bytes 491528 | tf_op jit(solution)/shard_map/ppermute | solution.py:580
  10.7 5.3 %collective-permute-start.3 = (f32[64,128]{1,0:T(8,128)S(1)}, f32[64,128]{1,0:T(8,128)S(1)}, u32[]{:S(2)}, u32[]{:S(2)}) collective-permute-start(f32[64,128]{1,0:T(8,128)S(1)} %slice_bitcast_fusion), channel_id=1, source_target_pairs={{0,3},{2,5},{4,7},{6,9},{8,11},{10,13},{12,15},{14,17},{16,19},{18... | collective-permute-start | bytes 98312 | tf_op jit(solution)/shard_map/ppermute | solution.py:580
  12.0 4.0 %collective-permute-start.4 = (f32[64,128]{1,0:T(8,128)S(1)}, f32[64,128]{1,0:T(8,128)S(1)}, u32[]{:S(2)}, u32[]{:S(2)}) collective-permute-start(f32[64,128]{1,0:T(8,128)S(1)} %slice_bitcast_fusion), channel_id=1, source_target_pairs={{1,3},{3,5},{5,7},{7,9},{9,11},{11,13},{13,15},{15,17},{17,19},{19... | collective-permute-start | bytes 98312 | tf_op jit(solution)/shard_map/ppermute | solution.py:580
  20.8 2.5 %collective-permute-start.5 = (f32[3,128,128]{2,1,0:T(8,128)S(1)}, f32[3,128,128]{2,1,0:T(8,128)S(1)}, u32[]{:S(2)}, u32[]{:S(2)}) collective-permute-start(f32[3,128,128]{2,1,0:T(8,128)S(1)} %get-tuple-element.26.v1), channel_id=1, source_target_pairs={{0,1},{1,0},{2,3},{3,2},{4,5},{5,4},{6,7},{7,6},{8,9},{9,8},{10,11... | collective-permute-start | bytes 589832 | tf_op jit(solution)/shard_map/ppermute | solution.py:580
  22.2 1.1 %collective-permute-start.6 = (f32[3,128,128]{2,1,0:T(8,128)S(1)}, f32[3,128,128]{2,1,0:T(8,128)S(1)}, u32[]{:S(2)}, u32[]{:S(2)}) collective-permute-start(f32[3,128,128]{2,1,0:T(8,128)S(1)} %get-tuple-element.26.v1), channel_id=1, source_target_pairs={{1,2},{3,4},{2,1},{5,6},{4,3},{7,8},{6,5},{9,10},{8,7},{11,12},{10... | collective-permute-start | bytes 589832 | tf_op jit(solution)/shard_map/ppermute | solution.py:580
  24.7 10.9 %collective-permute-start.7 = (f32[3,128,128]{2,1,0:T(8,128)S(1)}, f32[3,128,128]{2,1,0:T(8,128)S(1)}, u32[]{:S(2)}, u32[]{:S(2)}) collective-permute-start(f32[3,128,128]{2,1,0:T(8,128)S(1)} %get-tuple-element.31.v2), channel_id=1, source_target_pairs={{1,0},{3,2},{2,1},{5,4},{4,3},{7,6},{6,5},{9,8},{8,7},{11,10},{10,... | collective-permute-start | bytes 589832 | tf_op jit(solution)/shard_map/ppermute | solution.py:580
  54.8 9.2 %collective-permute-start.8 = (f32[3,64,128]{2,1,0:T(8,128)S(1)}, f32[3,64,128]{2,1,0:T(8,128)S(1)}, u32[]{:S(2)}, u32[]{:S(2)}) collective-permute-start(f32[3,64,128]{2,1,0:T(8,128)S(1)} %get-tuple-element.38), channel_id=1, source_target_pairs={{0,1},{1,0},{2,3},{3,2},{4,5},{5,4},{6,7},{7,6},{8,9},{9,8},{10,11... | collective-permute-start | bytes 294920 | tf_op jit(solution)/shard_map/ppermute | solution.py:580
  55.2 4.3 %collective-permute-start.10 = (f32[128,128]{1,0:T(8,128)S(1)}, f32[128,128]{1,0:T(8,128)S(1)}, u32[]{:S(2)}, u32[]{:S(2)}) collective-permute-start(f32[128,128]{1,0:T(8,128)S(1)} %get-tuple-element.39.refs_0_), channel_id=1, source_target_pairs={{0,16},{8,24},{16,0},{24,8},{1,17},{9,25},{17,1},{25,9},{2,18},{10... | collective-permute-start | bytes 196616 | tf_op jit(solution)/shard_map/ppermute | solution.py:616
  55.8 5.8 %collective-permute-start.11 = (f32[128,128]{1,0:T(8,128)S(1)}, f32[128,128]{1,0:T(8,128)S(1)}, u32[]{:S(2)}, u32[]{:S(2)}) collective-permute-start(f32[128,128]{1,0:T(8,128)S(1)} %get-tuple-element.39.refs_0_), channel_id=1, source_target_pairs={{0,24},{8,16},{16,8},{24,0},{1,25},{9,17},{17,9},{25,1},{2,26},{10... | collective-permute-start | bytes 196616 | tf_op jit(solution)/shard_map/ppermute | solution.py:616
  57.2 4.7 %collective-permute-start.9 = (f32[128,128]{1,0:T(8,128)S(1)}, f32[128,128]{1,0:T(8,128)S(1)}, u32[]{:S(2)}, u32[]{:S(2)}) collective-permute-start(f32[128,128]{1,0:T(8,128)S(1)} %get-tuple-element.39.refs_0_), channel_id=1, source_target_pairs={{0,8},{8,0},{16,24},{24,16},{1,9},{9,1},{17,25},{25,17},{2,10},{10... | collective-permute-start | bytes 196616 | tf_op jit(solution)/shard_map/ppermute | solution.py:616
  62.0 2.8 %collective-permute-start.12 = (f32[72,128]{1,0:T(8,128)S(1)}, f32[72,128]{1,0:T(8,128)S(1)}, u32[]{:S(2)}, u32[]{:S(2)}) collective-permute-start(f32[72,128]{1,0:T(8,128)S(1)} %get-tuple-element.42), channel_id=1, source_target_pairs={{0,1},{1,0},{2,3},{3,2},{4,5},{5,4},{6,7},{7,6},{8,9},{9,8},{10,11... | collective-permute-start | bytes 110600 | tf_op jit(solution)/shard_map/ppermute | solution.py:580
  62.0 5.4 %collective-permute-start.13 = (f32[72,128]{1,0:T(8,128)S(1)}, f32[72,128]{1,0:T(8,128)S(1)}, u32[]{:S(2)}, u32[]{:S(2)}) collective-permute-start(f32[72,128]{1,0:T(8,128)S(1)} %get-tuple-element.42), channel_id=1, source_target_pairs={{1,2},{0,7},{3,4},{2,1},{5,6},{4,3},{7,0},{6,5},{9,10},{8,15},{11,... | collective-permute-start | bytes 110600 | tf_op jit(solution)/shard_map/ppermute | solution.py:580
  63.1 4.4 %collective-permute-start.14 = (f32[72,128]{1,0:T(8,128)S(1)}, f32[72,128]{1,0:T(8,128)S(1)}, u32[]{:S(2)}, u32[]{:S(2)}) collective-permute-start(f32[72,128]{1,0:T(8,128)S(1)} %get-tuple-element.43), channel_id=1, source_target_pairs={{0,6},{1,3},{2,0},{3,5},{4,2},{5,7},{6,4},{7,1},{8,14},{9,11},{10,... | collective-permute-start | bytes 110600 | tf_op jit(solution)/shard_map/ppermute | solution.py:580

commit v2 on v1

--- a/solution.py
+++ b/solution.py
@@ -213,34 +213,40 @@
     return jnp.sum(tile, axis=0, keepdims=True)
 
 
-def prepare_kernel(design, fixed, load, swap, first, second):
+def prepare_kernel(design_hbm, fixed_hbm, load_hbm, swap, first, second, third, fourth, own, design, fixed, load, sems):
     sub = lax.axis_index("sub")
-
-    def right_side(k, layer):
-        return (1 - fixed[k, layer]).astype(jnp.float32) * load[k, layer].astype(jnp.float32)
+    copies = [
+        pltpu.make_async_copy(source, target, sems.at[n])
+        for n, (source, target) in enumerate(
+            ((fixed_hbm, fixed), (load_hbm, load), (design_hbm, design))
+        )
+    ]
+    for copy in copies:
+        copy.start()
+    for copy in copies:
+        copy.wait()
 
     for k in range(3):
-        values = [right_side(k, 0), right_side(k, 1)]
+        frees = [(1 - fixed[k, layer]).astype(jnp.float32) for layer in range(2)]
+        values = [frees[layer] * load[k, layer].astype(jnp.float32) for layer in range(2)]
         for layer in range(2):
             swap[2 * k + layer] = values[layer]
-        swap[6 + k] = (1 - fixed[k, 1 - sub]).astype(jnp.float32)
-
-        @pl.when(sub == 0)
-        def _(k=k, values=values):
-            first[k] = values[1]
-            second[k] = values[0]
-
-        @pl.when(sub == 1)
-        def _(k=k, values=values):
-            first[k] = values[0]
-            second[k] = values[1]
-
-    swap[9] = design[0]
-    swap[10] = design[1]
-    first[3] = design[0]
-    second[3] = design[0]
-    first[4] = design[1]
-    second[4] = design[1]
+            own[2 * k + layer] = values[layer]
+        low = sub == 0
+        swap[6 + k] = jnp.where(low, frees[1], frees[0])
+        own[6 + k] = jnp.where(low, frees[0], frees[1])
+        first[k] = jnp.where(low, values[1], values[0])
+        second[k] = jnp.where(low, values[0], values[1])
+    low = sub == 0
+    for layer in range(2):
+        swap[9 + layer] = design[layer]
+        own[9 + layer] = design[layer]
+    later = jnp.where(low, design[1], design[0])
+    sooner = jnp.where(low, design[0], design[1])
+    first[3] = later
+    third[...] = later
+    second[3] = sooner
+    fourth[...] = sooner
 
 
 def filter_planes(low, mid, high):
@@ -280,35 +286,31 @@
 
 def start_kernel(
     mods, slabs,
-    design, fixed, load, swap, first, second, third, fourth,
+    own, first, second, third, fourth, swap,
     v0, v0_high, v1, free, mod_low, mod_own, slope_factor, chain_factor, moments,
     v0_low, layers,
 ):
     mod, slab, sub = (lax.axis_index(a) for a in AXES)
-    half = design.shape[1]
+    half = third.shape[0]
     count = 2 * half
     mine = pl.ds(pl.multiple_of(sub * half, half), half)
     other = pl.ds(pl.multiple_of((1 - sub) * half, half), half)
     for layer in range(2):
-        layers[2 - sub + layer, mine, :] = design[layer]
+        layers[2 - sub + layer, mine, :] = own[9 + layer]
         layers[2 - sub + layer, other, :] = swap[9 + layer]
-    for source, part in ((first, mine), (second, other)):
+    for near, deep, part in ((first, fourth, mine), (second, third, other)):
 
         @pl.when(sub == 0)
-        def _(source=source, part=part):
-            layers[0, part, :] = source[3]
-            layers[1, part, :] = source[4]
+        def _(near=near, deep=deep, part=part):
+            layers[0, part, :] = deep[...]
+            layers[1, part, :] = near[3]
 
         @pl.when(sub == 1)
-        def _(source=source, part=part):
-            layers[3, part, :] = source[3]
-
-    @pl.when(sub == 1)
-    def _():
-        layers[0, pl.ds(0, half), :] = third[...]
-        layers[0, pl.ds(half, half), :] = fourth[...]
-
-    weight = weight_plane((count, design.shape[2]), 0, count)
+        def _(near=near, deep=deep, part=part):
+            layers[3, part, :] = near[3]
+            layers[0, part, :] = deep[...]
+
+    weight = weight_plane((count, third.shape[1]), 0, count)
     starts = (mod == 0) & (slab == 0) & (sub == 0)
     filtered = filter_planes(layers[0], layers[1], layers[2]) / weight
     hyper = jnp.tanh(sharpness * (filtered - threshold))
@@ -326,23 +328,21 @@
     ends = (mod == mods - 1) & (slab == slabs - 1) & (sub == 1)
     inside = jnp.where(ends, 0.0, 1.0)
     for k in range(3):
-        own_half = (1 - fixed[k, sub]).astype(jnp.float32)
-        free[k, mine, :] = own_half
+        free[k, mine, :] = own[6 + k]
         free[k, other, :] = swap[6 + k]
-        v0[k, mine, :] = own_half * load[k, sub].astype(jnp.float32)
+        v0[k, mine, :] = own[2 * k + sub]
         v0[k, other, :] = swap[2 * k + sub]
-        inner = (1 - fixed[k, 1 - sub]).astype(jnp.float32) * load[k, 1 - sub].astype(jnp.float32)
 
         @pl.when(sub == 0)
-        def _(k=k, inner=inner):
-            v0_high[k, mine, :] = inner
+        def _(k=k):
+            v0_high[k, mine, :] = own[2 * k + 1]
             v0_high[k, other, :] = swap[2 * k + 1]
             v0_low[k, mine, :] = first[k]
             v0_low[k, other, :] = second[k]
 
         @pl.when(sub == 1)
-        def _(k=k, inner=inner):
-            v0_low[k, mine, :] = inner
+        def _(k=k):
+            v0_low[k, mine, :] = own[2 * k]
             v0_low[k, other, :] = swap[2 * k]
             v0_high[k, mine, :] = first[k] * inside
             v0_high[k, other, :] = second[k] * inside
@@ -362,7 +362,7 @@
     )
 
 
-def second_kernel(v1, inner, outer, free, mod_low, mod_own, before, v2, v1_high, moments):
+def second_kernel(v1, outer, inner, free, mod_low, mod_own, before, v2, v1_high, moments):
     sub = lax.axis_index("sub")
     count = v1.shape[1]
     even = sub == 0
@@ -473,20 +473,16 @@
     )
 
 
-def scale_kernel(*refs):
-    slopes, (chain_factor, scaled, same, cross) = refs[:-4], refs[-4:]
+def scale_kernel(slopes, chain_factor, scaled, same, cross):
     sub = lax.axis_index("sub")
-    total = slopes[0][...]
-    for other in slopes[1:]:
-        total = total + other[...]
-    scaled[...] = total * chain_factor[...]
+    scaled[...] = jnp.sum(slopes[...], axis=0) * chain_factor[...]
     window = same.shape[0]
     shift = scaled.shape[0] - window
     same[...] = scaled[pl.ds(pl.multiple_of(sub * shift, 8), window), :]
     cross[...] = scaled[pl.ds(pl.multiple_of((1 - sub) * shift, 8), window), :]
 
 
-def gradient_kernel(scaled, partner, outer, far, gradient, planes, sums):
+def gradient_kernel(scaled, outer, far, partner, gradient, planes, sums):
     sub = lax.axis_index("sub")
     window = partner.shape[0]
     shift = scaled.shape[0] - window
@@ -556,8 +552,8 @@
         swap=built([(0, 0, 1), (1, 0, 0)], True),
         first=built([(0, 1, 0), (1, -1, 1)], True),
         second=built([(1, 1, 0), (0, -1, 1)], True),
-        third=built([(0, 1, 1)], True),
-        fourth=built([(1, 1, 1)], True),
+        third=built([(0, 1, 1), (1, 1, 0)], True),
+        fourth=built([(0, 1, 0), (1, 1, 1)], True),
         outer=built([(1, 1, 0), (0, -1, 1)], False),
         down=built([(1, 0, 0), (0, -1, 1)], False),
         halo_cross=in_module([(1, 1, 0), (0, -1, 1)]),
@@ -565,12 +561,6 @@
     )
 
 
-def module_routes(mods):
-    if mods & (mods - 1) == 0:
-        return [[(m, m ^ s) for m in range(mods)] for s in range(1, mods)]
-    return [[(m, (m + s) % mods) for m in range(mods)] for s in range(1, mods)]
-
-
 def local(mods, slabs, design, fixed, load):
     half, width = design.shape[1:]
     count = 2 * half
@@ -581,13 +571,27 @@
 
     plane = (count, width)
     layer = (3, count, width)
-    swap, first, second = call(
-        prepare_kernel, [(11, half, width), (5, half, width), (5, half, width)], name="prepare"
+    block = (half, width)
+    swap, first, second, third, fourth, own = pl.pallas_call(
+        prepare_kernel,
+        out_shape=[
+            jax.ShapeDtypeStruct(shape, jnp.float32)
+            for shape in ((11,) + block, (4,) + block, (4,) + block, block, block, (11,) + block)
+        ],
+        in_specs=[pl.BlockSpec(memory_space=pltpu.HBM)] * 3,
+        scratch_shapes=[
+            pltpu.VMEM(design.shape, jnp.float32),
+            pltpu.VMEM(fixed.shape, jnp.int32),
+            pltpu.VMEM(load.shape, jnp.int32),
+            pltpu.SemaphoreType.DMA((3,)),
+        ],
+        compiler_params=pltpu.CompilerParams(vmem_limit_bytes=16 * 2**20),
+        name="prepare",
     )(design, fixed, load)
     first = move(first, "first")
     second = move(second, "second")
-    third = move(design[1], "third")
-    fourth = move(design[1], "fourth")
+    third = move(third, "third")
+    fourth = move(fourth, "fourth")
     swap = move(swap, "swap")
 
     def start_body(*refs):
@@ -598,27 +602,29 @@
         [layer, layer, layer, layer, plane, plane, plane, plane, (8, width)],
         [layer, (4,) + plane],
         name="start",
-    )(design, fixed, load, swap, first, second, third, fourth)
+    )(own, first, second, third, fourth, swap)
     outer = move(v1, "outer")
     inner = move(v1, "swap")
     v2, v1_high, moments = call(second_kernel, [layer, layer, (8, width)], name="second")(
-        v1, inner, outer, free, mod_low, mod_own, moments
+        v1, outer, inner, free, mod_low, mod_own, moments
     )
     v2_high = move(v2, "down")
     (moments,) = call(third_kernel, [(8, width)], name="third")(v2, v2_high, mod_own, moments)
-    devices = 2 * mods * slabs
-    gathered = lax.all_to_all(
-        jnp.broadcast_to(moments, (devices, 8, width)), AXES, 0, 0, tiled=True
-    )
+    def shared(value, axes, parts):
+        copies = jnp.broadcast_to(value, (parts,) + value.shape)
+        return lax.all_to_all(copies, axes, 0, 0, tiled=True)
+
+    moments = jnp.sum(shared(moments, ("slab", "sub"), 2 * slabs), axis=0)
+    gathered = shared(moments, "mod", mods)
     slope, keep, send = call(
         combine_kernel, [plane, (3, half, width), (3, half, width)], [layer, layer], name="combine"
     )(gathered, v0, v0_high, v1, v1_high, v2, v2_high, slope_factor)
-    slopes = [slope] + [lax.ppermute(slope, "mod", pairs) for pairs in module_routes(mods)]
+    slopes = shared(slope, "mod", mods)
     received = move(send, "swap")
     window = half + 8
     scaled, same, cross = call(
         scale_kernel, [plane, (window, width), (window, width)], name="scale"
-    )(*slopes, chain_factor)
+    )(slopes, chain_factor)
     outer = move(cross, "halo_cross")
     far = move(same, "halo_same")
     partner = move(cross, "swap")
@@ -628,7 +634,7 @@
     )
     (gradient,) = call(
         gradient_kernel, [(2, half, width)], [(4, window, width), (window, width)], name="gradient"
-    )(scaled, partner, outer, far)
+    )(scaled, outer, far, partner)
     return displacement, gradient
 
 

time: 68.6 us -> 76 us (1.11)
  blocking collectives: 18.1 us -> 23.1 us
  waiting for transfers between devices: 22.2 us -> 23.4 us
    all_to_all x0 -> x1, waiting for transfers between devices: none -> 6.07 us  [shared(): return lax.all_to_all(copies, axes, 0, 0, tiled=True)]
    all_to_all x1 -> x2, blocking collectives: 18.1 us -> 23.1 us  [shared(): return lax.all_to_all(copies, axes, 0, 0, tiled=True)]
    ppermute x3 -> x0, starting transfers between devices: 3.49 us -> none  [local(): lax.ppermute(slope, 'mod', pairs)]
    all_to_all x0 -> x1, starting transfers between devices: none -> 3.4 us  [shared(): return lax.all_to_all(copies, axes, 0, 0, tiled=True)]
    ppermute x3 -> x0, waiting for transfers between devices: 3.29 us -> none  [local(): lax.ppermute(slope, 'mod', pairs)]
    ppermute x12, waiting for transfers between devices: 18.9 us -> 17.4 us  [move(): return lax.ppermute(value, AXES, path[name])]
  transfers between devices with their start and end apart: 15 -> 13, of which waited for: 8 -> 7; matrix products, arithmetic and copies ran while one was open for 1% -> 2% of each run, Pallas kernels for 0% -> 0%
where the time goes in v2:
time: 76 us; the launch traced here: 75.6 us
  waiting for transfers between devices  23.4 us (31%)
  blocking collectives  23.1 us (30%)
  starting transfers between devices  18.1 us (24%)
  Pallas kernels  5.97 us (8%)
  local copies, waits for them, and re-layouts  4.11 us (5%)
    all_to_all x2, blocking collectives, shared(): return lax.all_to_all(copies, axes, 0, 0, tiled=True)  23.1 us
    ppermute x12, waiting for transfers between devices, move(): return lax.ppermute(value, AXES, path[name])  17.4 us
    ppermute x12, starting transfers between devices, move(): return lax.ppermute(value, AXES, path[name])  14.7 us
    all_to_all x1, waiting for transfers between devices, shared(): return lax.all_to_all(copies, axes, 0, 0, tiled=True)  6.07 us
    all_to_all x1, starting transfers between devices, shared(): return lax.all_to_all(copies, axes, 0, 0, tiled=True)  3.4 us
    unnamed x7, local copies, waits for them, and re-layouts  3.38 us
    pallas_call x1, Pallas kernels, local(): call(start_body, [layer, layer, layer, layer, plane, plane, plane, plane,...  1.95 us
  transfers between devices with their start and end apart: 13, of which 7 were waited for; matrix products, arithmetic and copies ran while one was open for 2% of the time, Pallas kernels for 0%

profile of v2, /device:TPU:0, one launch (start us, length us, event | category | flops | bytes accessed | tf_op | source)
XLA Modules:
  0.0 75.6 jit_solution(3306814482640003005)
XLA Ops:
  0.6 0.0 copy-start
  0.6 0.9 %copy-done = s32[3,2,64,128]{3,2,1,0:T(8,128)S(1)} copy-done((s32[3,2,64,128]{3,2,1,0:T(8,128)S(1)}, s32[3,2,64,128]{3,2,1,0:T(8,128)}, u32[]{:S(2)}) %copy-start) | copy-done | bytes 196632
  1.6 0.0 copy-start.1
  1.6 0.9 %copy-done.1 = s32[3,2,64,128]{3,2,1,0:T(8,128)S(1)} copy-done((s32[3,2,64,128]{3,2,1,0:T(8,128)S(1)}, s32[3,2,64,128]{3,2,1,0:T(8,128)}, u32[]{:S(2)}) %copy-start.1) | copy-done | bytes 196632
  2.5 0.0 copy-start.2
  2.5 0.8 %copy-done.2 = f32[2,64,128]{2,1,0:T(8,128)S(1)} copy-done((f32[2,64,128]{2,1,0:T(8,128)S(1)}, f32[2,64,128]{2,1,0:T(8,128)}, u32[]{:S(2)}) %copy-start.2) | copy-done | bytes 65560
  3.3 0.7 prepare.1
  4.0 0.5 collective-permute-start.4
  4.5 2.6 %collective-permute-start = (f32[4,64,128]{2,1,0:T(8,128)S(1)}, f32[4,64,128]{2,1,0:T(8,128)S(1)}, u32[]{:S(2)}, u32[]{:S(2)}) collective-permute-start(f32[4,64,128]{2,1,0:T(8,128)S(1)} %get-tuple-element.27), channel_id=1, source_target_pairs={{0,2},{1,31},{2,4},{3,1},{4,6},{5,3},{6,8},{7,5},{8,10},{9,7},{10,... | collective-permute-start | bytes 393224 | tf_op jit(solution)/shard_map/ppermute | solution.py:570
  7.1 4.1 %collective-permute-start.1 = (f32[4,64,128]{2,1,0:T(8,128)S(1)}, f32[4,64,128]{2,1,0:T(8,128)S(1)}, u32[]{:S(2)}, u32[]{:S(2)}) collective-permute-start(f32[4,64,128]{2,1,0:T(8,128)S(1)} %get-tuple-element.28), channel_id=1, source_target_pairs={{1,2},{0,31},{3,4},{2,1},{5,6},{4,3},{7,8},{6,5},{9,10},{8,7},{11,... | collective-permute-start | bytes 393224 | tf_op jit(solution)/shard_map/ppermute | solution.py:570
  11.3 0.0 collective-permute-start.2
  11.3 1.6 %collective-permute-start.3 = (f32[64,128]{1,0:T(8,128)S(1)}, f32[64,128]{1,0:T(8,128)S(1)}, u32[]{:S(2)}, u32[]{:S(2)}) collective-permute-start(f32[64,128]{1,0:T(8,128)S(1)} %get-tuple-element.30), channel_id=1, source_target_pairs={{0,2},{1,3},{2,4},{3,5},{4,6},{5,7},{6,8},{7,9},{8,10},{9,11},{10,... | collective-permute-start | bytes 98312 | tf_op jit(solution)/shard_map/ppermute | solution.py:570
  12.9 5.9 %collective-permute-done.2.refs_3_ = f32[64,128]{1,0:T(8,128)S(1)} collective-permute-done((f32[64,128]{1,0:T(8,128)S(1)}, f32[64,128]{1,0:T(8,128)S(1)}, u32[]{:S(2)}, u32[]{:S(2)}) %collective-permute-start.2) | collective-permute-done | bytes 32800 | tf_op jit(solution)/shard_map/ppermute | solution.py:570
  18.8 0.4 collective-permute-done.3.refs_4_
  19.2 0.0 collective-permute-done.refs_1_
  19.2 0.0 collective-permute-done.1.refs_2_
  19.2 0.0 collective-permute-done.4.refs_5_
  19.2 2.0 %start.1 = (f32[3,128,128]{2,1,0:T(8,128)S(1)}, f32[3,128,128]{2,1,0:T(8,128)S(1)}, f32[3,128,128]{2,1,0:T(8,128)S(1)}, f32[3,128,128]{2,1,0:T(8,128)S(1)}, f32[...) custom-call(f32[11,64,128]{2,1,0:T(8,128)S(1)} %get-tuple-element.26, ...), custom_call_target="tpu_custom_call" | custom-call | tf_op jit(solution)/shard_map/start/pallas_call | solution.py:600
  21.2 0.7 collective-permute-start.5
  21.8 1.6 %collective-permute-start.6 = (f32[3,128,128]{2,1,0:T(8,128)S(1)}, f32[3,128,128]{2,1,0:T(8,128)S(1)}, u32[]{:S(2)}, u32[]{:S(2)}) collective-permute-start(f32[3,128,128]{2,1,0:T(8,128)S(1)} %get-tuple-element.32.v1), channel_id=1, source_target_pairs={{0,1},{1,0},{2,3},{3,2},{4,5},{5,4},{6,7},{7,6},{8,9},{9,8},{10,11... | collective-permute-start | bytes 589832 | tf_op jit(solution)/shard_map/ppermute | solution.py:570
  23.5 0.0 collective-permute-done.5.outer
  23.5 1.1 %collective-permute-done.6.inner = f32[3,128,128]{2,1,0:T(8,128)S(1)} collective-permute-done((f32[3,128,128]{2,1,0:T(8,128)S(1)}, f32[3,128,128]{2,1,0:T(8,128)S(1)}, u32[]{:S(2)}, u32[]{:S(2)}) %collective-permute-start.6) | collective-permute-done | bytes 196640 | tf_op jit(solution)/shard_map/ppermute | solution.py:570
  24.5 1.4 %second.1 = (f32[3,128,128]{2,1,0:T(8,128)S(1)}, f32[3,128,128]{2,1,0:T(8,128)S(1)}, f32[8,128]{1,0:T(8,128)S(1)}) custom-call(f32[3,128,128]{2,1,0:T(8,128)S(1)} %get-tuple-element.32.v1, f32[3,128,128]{2,1,0:T(8,128)S(1)} %collective-permute-done.5.outer, f32[3,128,128]{2,1,0:T(8,128)S(1)} %collective-permute-done.6.inner, ...), custom_call_target="tpu_custom_call" | custom-call | tf_op jit(solution)/shard_map/second/pallas_call | solution.py:608
  25.9 1.3 %collective-permute-start.7 = (f32[3,128,128]{2,1,0:T(8,128)S(1)}, f32[3,128,128]{2,1,0:T(8,128)S(1)}, u32[]{:S(2)}, u32[]{:S(2)}) collective-permute-start(f32[3,128,128]{2,1,0:T(8,128)S(1)} %get-tuple-element.37.v2), channel_id=1, source_target_pairs={{1,0},{3,2},{2,1},{5,4},{4,3},{7,6},{6,5},{9,8},{8,7},{11,10},{10,... | collective-permute-start | bytes 589832 | tf_op jit(solution)/shard_map/ppermute | solution.py:570
  27.2 7.4 %collective-permute-done.7.v2_high = f32[3,128,128]{2,1,0:T(8,128)S(1)} collective-permute-done((f32[3,128,128]{2,1,0:T(8,128)S(1)}, f32[3,128,128]{2,1,0:T(8,128)S(1)}, u32[]{:S(2)}, u32[]{:S(2)}) %collective-permute-start.7) | collective-permute-done | bytes 196640 | tf_op jit(solution)/shard_map/ppermute | solution.py:570
  34.6 0.4 third.1
  35.1 14.2 %all_to_all.15 = f32[8,8,128]{2,1,0:T(8,128)S(1)} all-to-all(f32[8,8,128]{2,1,0:T(8,128)S(1)} %broadcast_in_dim.9), channel_id=1, replica_groups=mesh['mod'=4,'slab'=4,'sub'=2] {'slab','sub'}, dimensions={0} | all-to-all | bytes 65536 | tf_op jit(solution)/shard_map/all_to_all | solution.py:615
  49.3 8.9 %all_to_all.16.gathered = f32[4,8,128]{2,1,0:T(8,128)S(1)} all-to-all(f32[4,8,128]{2,1,0:T(8,128)S(1)} %broadcast_in_dim.10), channel_id=1, replica_groups=mesh['mod'=4,'slab'=4,'sub'=2] {'mod'}, dimensions={0} | all-to-all | bytes 32768 | tf_op jit(solution)/shard_map/all_to_all | solution.py:615
  58.2 0.7 combine.1
  58.9 0.1 collective-permute-start.8
  59.0 0.7 broadcast_in_dim.11
  59.7 3.4 %all-to-all-start.2 = ((f32[4,128,128]{2,1,0:T(8,128)}), f32[4,128,128]{2,1,0:T(8,128)S(1)}, u32[]{:S(2)}, u32[]{:S(2)}) async-start(f32[4,128,128]{2,1,0:T(8,128)} %broadcast_in_dim.11), calls=%async_computation.2 | async-start | bytes 524288 | tf_op jit(solution)/shard_map/all_to_all | solution.py:615
  63.1 0.0 collective-permute-done.8
  63.2 6.1 %all-to-all-done.2.slopes = f32[4,128,128]{2,1,0:T(8,128)S(1)} async-done(((f32[4,128,128]{2,1,0:T(8,128)}), f32[4,128,128]{2,1,0:T(8,128)S(1)}, u32[]{:S(2)}, u32[]{:S(2)}) %all-to-all-start.2) | async-done | bytes 262176 | tf_op jit(solution)/shard_map/all_to_all | solution.py:615
  69.3 0.1 collective-permute-start.11
  69.3 0.7 collective-permute-start.9
  70.0 1.4 %collective-permute-start.10 = (f32[72,128]{1,0:T(8,128)S(1)}, f32[72,128]{1,0:T(8,128)S(1)}, u32[]{:S(2)}, u32[]{:S(2)}) collective-permute-start(f32[72,128]{1,0:T(8,128)S(1)} %get-tuple-element.49), channel_id=1, source_target_pairs={{0,6},{1,3},{2,0},{3,5},{4,2},{5,7},{6,4},{7,1},{8,14},{9,11},{10,... | collective-permute-start | bytes 110600 | tf_op jit(solution)/shard_map/ppermute | solution.py:570
  71.4 0.7 copy.6
  72.1 1.8 %collective-permute-done.10.far = f32[72,128]{1,0:T(8,128)S(1)} collective-permute-done((f32[72,128]{1,0:T(8,128)S(1)}, f32[72,128]{1,0:T(8,128)S(1)}, u32[]{:S(2)}, u32[]{:S(2)}) %collective-permute-start.10) | collective-permute-done | bytes 36896 | tf_op jit(solution)/shard_map/ppermute | solution.py:570
  74.0 0.0 collective-permute-done.11.partner
  74.0 0.7 collective-permute-done.9.outer
  74.7 0.9 %gradient.1 = f32[2,64,128]{2,1,0:T(8,128)} custom-call(f32[128,128]{1,0:T(8,128)S(1)} %get-tuple-element.47.scaled, f32[72,128]{1,0:T(8,128)S(1)} %collective-permute-done.9.outer, f32[72,128]{1,0:T(8,128)S(1)} %collective-permute-done.10.far, f32[72,128]{1,0:T(8,128)S(1)} %collective-permute-done.11.partner), custom_call_target="tpu_custom_call" | custom-call | tf_op jit(solution)/shard_map/gradient/pallas_call | solution.py:635
  (6 shorter events, 0.1 us)
Async XLA Ops:
  0.6 0.9 %copy-start = (s32[3,2,64,128]{3,2,1,0:T(8,128)S(1)}, s32[3,2,64,128]{3,2,1,0:T(8,128)}, u32[]{:S(2)}) copy-start(s32[3,2,64,128]{3,2,1,0:T(8,128)} %fixed_hbm.1) | copy-start | bytes 589828
  1.6 0.9 %copy-start.1 = (s32[3,2,64,128]{3,2,1,0:T(8,128)S(1)}, s32[3,2,64,128]{3,2,1,0:T(8,128)}, u32[]{:S(2)}) copy-start(s32[3,2,64,128]{3,2,1,0:T(8,128)} %load_hbm.1) | copy-start | bytes 589828
  2.5 0.8 %copy-start.2 = (f32[2,64,128]{2,1,0:T(8,128)S(1)}, f32[2,64,128]{2,1,0:T(8,128)}, u32[]{:S(2)}) copy-start(f32[2,64,128]{2,1,0:T(8,128)} %design_hbm.1) | copy-start | bytes 196612
  4.0 15.2 %collective-permute-start.4 = (f32[11,64,128]{2,1,0:T(8,128)S(1)}, f32[11,64,128]{2,1,0:T(8,128)S(1)}, u32[]{:S(2)}, u32[]{:S(2)}) collective-permute-start(f32[11,64,128]{2,1,0:T(8,128)S(1)} %get-tuple-element.31), channel_id=1, source_target_pairs={{0,1},{1,0},{2,3},{3,2},{4,5},{5,4},{6,7},{7,6},{8,9},{9,8},{10,11... | collective-permute-start | bytes 1081352 | tf_op jit(solution)/shard_map/ppermute | solution.py:570
  4.5 14.7 %collective-permute-start = (f32[4,64,128]{2,1,0:T(8,128)S(1)}, f32[4,64,128]{2,1,0:T(8,128)S(1)}, u32[]{:S(2)}, u32[]{:S(2)}) collective-permute-start(f32[4,64,128]{2,1,0:T(8,128)S(1)} %get-tuple-element.27), channel_id=1, source_target_pairs={{0,2},{1,31},{2,4},{3,1},{4,6},{5,3},{6,8},{7,5},{8,10},{9,7},{10,... | collective-permute-start | bytes 393224 | tf_op jit(solution)/shard_map/ppermute | solution.py:570
  7.1 12.0 %collective-permute-start.1 = (f32[4,64,128]{2,1,0:T(8,128)S(1)}, f32[4,64,128]{2,1,0:T(8,128)S(1)}, u32[]{:S(2)}, u32[]{:S(2)}) collective-permute-start(f32[4,64,128]{2,1,0:T(8,128)S(1)} %get-tuple-element.28), channel_id=1, source_target_pairs={{1,2},{0,31},{3,4},{2,1},{5,6},{4,3},{7,8},{6,5},{9,10},{8,7},{11,... | collective-permute-start | bytes 393224 | tf_op jit(solution)/shard_map/ppermute | solution.py:570
  11.3 7.5 %collective-permute-start.2 = (f32[64,128]{1,0:T(8,128)S(1)}, f32[64,128]{1,0:T(8,128)S(1)}, u32[]{:S(2)}, u32[]{:S(2)}) collective-permute-start(f32[64,128]{1,0:T(8,128)S(1)} %get-tuple-element.29), channel_id=1, source_target_pairs={{0,3},{1,2},{2,5},{3,4},{4,7},{5,6},{6,9},{7,8},{8,11},{9,10},{10,... | collective-permute-start | bytes 98312 | tf_op jit(solution)/shard_map/ppermute | solution.py:570
  11.3 7.9 %collective-permute-start.3 = (f32[64,128]{1,0:T(8,128)S(1)}, f32[64,128]{1,0:T(8,128)S(1)}, u32[]{:S(2)}, u32[]{:S(2)}) collective-permute-start(f32[64,128]{1,0:T(8,128)S(1)} %get-tuple-element.30), channel_id=1, source_target_pairs={{0,2},{1,3},{2,4},{3,5},{4,6},{5,7},{6,8},{7,9},{8,10},{9,11},{10,... | collective-permute-start | bytes 98312 | tf_op jit(solution)/shard_map/ppermute | solution.py:570
  21.2 2.3 %collective-permute-start.5 = (f32[3,128,128]{2,1,0:T(8,128)S(1)}, f32[3,128,128]{2,1,0:T(8,128)S(1)}, u32[]{:S(2)}, u32[]{:S(2)}) collective-permute-start(f32[3,128,128]{2,1,0:T(8,128)S(1)} %get-tuple-element.32.v1), channel_id=1, source_target_pairs={{1,2},{3,4},{2,1},{5,6},{4,3},{7,8},{6,5},{9,10},{8,7},{11,12},{10... | collective-permute-start | bytes 589832 | tf_op jit(solution)/shard_map/ppermute | solution.py:570
  21.8 2.7 %collective-permute-start.6 = (f32[3,128,128]{2,1,0:T(8,128)S(1)}, f32[3,128,128]{2,1,0:T(8,128)S(1)}, u32[]{:S(2)}, u32[]{:S(2)}) collective-permute-start(f32[3,128,128]{2,1,0:T(8,128)S(1)} %get-tuple-element.32.v1), channel_id=1, source_target_pairs={{0,1},{1,0},{2,3},{3,2},{4,5},{5,4},{6,7},{7,6},{8,9},{9,8},{10,11... | collective-permute-start | bytes 589832 | tf_op jit(solution)/shard_map/ppermute | solution.py:570
  25.9 8.7 %collective-permute-start.7 = (f32[3,128,128]{2,1,0:T(8,128)S(1)}, f32[3,128,128]{2,1,0:T(8,128)S(1)}, u32[]{:S(2)}, u32[]{:S(2)}) collective-permute-start(f32[3,128,128]{2,1,0:T(8,128)S(1)} %get-tuple-element.37.v2), channel_id=1, source_target_pairs={{1,0},{3,2},{2,1},{5,4},{4,3},{7,6},{6,5},{9,8},{8,7},{11,10},{10,... | collective-permute-start | bytes 589832 | tf_op jit(solution)/shard_map/ppermute | solution.py:570
  58.9 4.2 %collective-permute-start.8 = (f32[3,64,128]{2,1,0:T(8,128)S(1)}, f32[3,64,128]{2,1,0:T(8,128)S(1)}, u32[]{:S(2)}, u32[]{:S(2)}) collective-permute-start(f32[3,64,128]{2,1,0:T(8,128)S(1)} %get-tuple-element.44), channel_id=1, source_target_pairs={{0,1},{1,0},{2,3},{3,2},{4,5},{5,4},{6,7},{7,6},{8,9},{9,8},{10,11... | collective-permute-start | bytes 294920 | tf_op jit(solution)/shard_map/ppermute | solution.py:570
  59.7 9.5 %all-to-all-start.2 = ((f32[4,128,128]{2,1,0:T(8,128)}), f32[4,128,128]{2,1,0:T(8,128)S(1)}, u32[]{:S(2)}, u32[]{:S(2)}) async-start(f32[4,128,128]{2,1,0:T(8,128)} %broadcast_in_dim.11), calls=%async_computation.2 | async-start | bytes 524288 | tf_op jit(solution)/shard_map/all_to_all | solution.py:615
  69.3 4.7 %collective-permute-start.11 = (f32[72,128]{1,0:T(8,128)S(1)}, f32[72,128]{1,0:T(8,128)S(1)}, u32[]{:S(2)}, u32[]{:S(2)}) collective-permute-start(f32[72,128]{1,0:T(8,128)S(1)} %get-tuple-element.48), channel_id=1, source_target_pairs={{0,1},{1,0},{2,3},{3,2},{4,5},{5,4},{6,7},{7,6},{8,9},{9,8},{10,11... | collective-permute-start | bytes 110600 | tf_op jit(solution)/shard_map/ppermute | solution.py:570
  69.3 5.4 %collective-permute-start.9 = (f32[72,128]{1,0:T(8,128)S(1)}, f32[72,128]{1,0:T(8,128)S(1)}, u32[]{:S(2)}, u32[]{:S(2)}) collective-permute-start(f32[72,128]{1,0:T(8,128)S(1)} %get-tuple-element.48), channel_id=1, source_target_pairs={{1,2},{0,7},{3,4},{2,1},{5,6},{4,3},{7,0},{6,5},{9,10},{8,15},{11,... | collective-permute-start | bytes 110600 | tf_op jit(solution)/shard_map/ppermute | solution.py:570
  70.0 4.0 %collective-permute-start.10 = (f32[72,128]{1,0:T(8,128)S(1)}, f32[72,128]{1,0:T(8,128)S(1)}, u32[]{:S(2)}, u32[]{:S(2)}) collective-permute-start(f32[72,128]{1,0:T(8,128)S(1)} %get-tuple-element.49), channel_id=1, source_target_pairs={{0,6},{1,3},{2,0},{3,5},{4,2},{5,7},{6,4},{7,1},{8,14},{9,11},{10,... | collective-permute-start | bytes 110600 | tf_op jit(solution)/shard_map/ppermute | solution.py:570

commit v3 on v2

--- a/solution.py
+++ b/solution.py
@@ -213,22 +213,11 @@
     return jnp.sum(tile, axis=0, keepdims=True)
 
 
-def prepare_kernel(design_hbm, fixed_hbm, load_hbm, swap, first, second, third, fourth, own, design, fixed, load, sems):
+def prepare_kernel(free, right, design, swap, first, second, third, fourth, own):
     sub = lax.axis_index("sub")
-    copies = [
-        pltpu.make_async_copy(source, target, sems.at[n])
-        for n, (source, target) in enumerate(
-            ((fixed_hbm, fixed), (load_hbm, load), (design_hbm, design))
-        )
-    ]
-    for copy in copies:
-        copy.start()
-    for copy in copies:
-        copy.wait()
-
     for k in range(3):
-        frees = [(1 - fixed[k, layer]).astype(jnp.float32) for layer in range(2)]
-        values = [frees[layer] * load[k, layer].astype(jnp.float32) for layer in range(2)]
+        frees = [free[k, layer] for layer in range(2)]
+        values = [right[k, layer] for layer in range(2)]
         for layer in range(2):
             swap[2 * k + layer] = values[layer]
             own[2 * k + layer] = values[layer]
@@ -442,15 +431,14 @@
 
 
 def combine_kernel(
-    gathered, v0, v0_high, v1, v1_high, v2, v2_high, slope_factor,
+    moments, v0, v0_high, v1, v1_high, v2, v2_high, slope_factor,
     slope, keep, send,
     own, high,
 ):
     sub = lax.axis_index("sub")
     count = v0.shape[1]
     half = count // 2
-    total = jnp.sum(gathered[...], axis=0)
-    sums = jnp.sum(total, axis=1, keepdims=True)
+    sums = jnp.sum(moments[...], axis=1, keepdims=True)
     c0, c1, c2 = coefficients([sums[k : k + 1] for k in range(6)])
     for k in range(3):
         own[k] = c0 * v0[k] + c1 * v1[k] + c2 * v2[k]
@@ -473,9 +461,9 @@
     )
 
 
-def scale_kernel(slopes, chain_factor, scaled, same, cross):
+def scale_kernel(slope, rest, chain_factor, scaled, same, cross):
     sub = lax.axis_index("sub")
-    scaled[...] = jnp.sum(slopes[...], axis=0) * chain_factor[...]
+    scaled[...] = (slope[...] + rest[...]) * chain_factor[...]
     window = same.shape[0]
     shift = scaled.shape[0] - window
     same[...] = scaled[pl.ds(pl.multiple_of(sub * shift, 8), window), :]
@@ -561,6 +549,38 @@
     )
 
 
+def all_sum(value, axis, count):
+    if count & (count - 1) == 0:
+        step = 1
+        while step < count:
+            value = value + lax.ppermute(value, axis, [(i, i ^ step) for i in range(count)])
+            step *= 2
+        return value
+    total = value
+    for step in range(1, count):
+        total = total + lax.ppermute(value, axis, [(i, (i + step) % count) for i in range(count)])
+    return total
+
+
+def module_sum(value, mods, slabs):
+    if mods & (mods - 1):
+        return all_sum(value, "mod", mods), jnp.zeros_like(value)
+    steps = [1 << bit for bit in range(mods.bit_length() - 1)]
+    got = jnp.zeros_like(value)
+    for n, _ in enumerate(steps):
+        pairs = []
+        for mod in range(mods):
+            for slab in range(slabs):
+                for sub in range(2):
+                    step = steps[n] if sub == 0 else steps[-1 - n]
+                    pairs.append(
+                        (2 * (mod * slabs + slab) + sub, 2 * ((mod ^ step) * slabs + slab) + sub)
+                    )
+        value = value + got if n else value
+        got = lax.ppermute(value, AXES, pairs)
+    return value, got
+
+
 def local(mods, slabs, design, fixed, load):
     half, width = design.shape[1:]
     count = 2 * half
@@ -572,22 +592,13 @@
     plane = (count, width)
     layer = (3, count, width)
     block = (half, width)
-    swap, first, second, third, fourth, own = pl.pallas_call(
+    free = (1 - fixed).astype(jnp.float32)
+    right = free * load.astype(jnp.float32)
+    swap, first, second, third, fourth, own = call(
         prepare_kernel,
-        out_shape=[
-            jax.ShapeDtypeStruct(shape, jnp.float32)
-            for shape in ((11,) + block, (4,) + block, (4,) + block, block, block, (11,) + block)
-        ],
-        in_specs=[pl.BlockSpec(memory_space=pltpu.HBM)] * 3,
-        scratch_shapes=[
-            pltpu.VMEM(design.shape, jnp.float32),
-            pltpu.VMEM(fixed.shape, jnp.int32),
-            pltpu.VMEM(load.shape, jnp.int32),
-            pltpu.SemaphoreType.DMA((3,)),
-        ],
-        compiler_params=pltpu.CompilerParams(vmem_limit_bytes=16 * 2**20),
+        [(11,) + block, (4,) + block, (4,) + block, block, block, (11,) + block],
         name="prepare",
-    )(design, fixed, load)
+    )(free, right, design)
     first = move(first, "first")
     second = move(second, "second")
     third = move(third, "third")
@@ -610,21 +621,18 @@
     )
     v2_high = move(v2, "down")
     (moments,) = call(third_kernel, [(8, width)], name="third")(v2, v2_high, mod_own, moments)
-    def shared(value, axes, parts):
-        copies = jnp.broadcast_to(value, (parts,) + value.shape)
-        return lax.all_to_all(copies, axes, 0, 0, tiled=True)
-
-    moments = jnp.sum(shared(moments, ("slab", "sub"), 2 * slabs), axis=0)
-    gathered = shared(moments, "mod", mods)
+    moments = all_sum(moments, "sub", 2)
+    moments = all_sum(moments, "slab", slabs)
+    moments = all_sum(moments, "mod", mods)
     slope, keep, send = call(
         combine_kernel, [plane, (3, half, width), (3, half, width)], [layer, layer], name="combine"
-    )(gathered, v0, v0_high, v1, v1_high, v2, v2_high, slope_factor)
-    slopes = shared(slope, "mod", mods)
+    )(moments, v0, v0_high, v1, v1_high, v2, v2_high, slope_factor)
+    slope, rest = module_sum(slope, mods, slabs)
     received = move(send, "swap")
     window = half + 8
     scaled, same, cross = call(
         scale_kernel, [plane, (window, width), (window, width)], name="scale"
-    )(slopes, chain_factor)
+    )(slope, rest, chain_factor)
     outer = move(cross, "halo_cross")
     far = move(same, "halo_same")
     partner = move(cross, "swap")

time: 76 us -> 72.5 us (0.954)
  blocking collectives: 23.1 us -> 0 us
  starting transfers between devices: 18.1 us -> 31.8 us
  waiting for transfers between devices: 23.4 us -> 30.9 us
  local copies, waits for them, and re-layouts: 4.11 us -> 1.59 us
  other arithmetic: 0.05 us -> 1.08 us
    all_to_all x2 -> x0, blocking collectives: 23.1 us -> none  [shared(): return lax.all_to_all(copies, axes, 0, 0, tiled=True)]
    ppermute x0 -> x7, waiting for transfers between devices: none -> 14.7 us  [the longest x5 9.97 us: all_sum(): lax.ppermute(value, axis, [(i, i ^ step) for i in range(count)])]
    ppermute x0 -> x7, starting transfers between devices: none -> 14.7 us  [the longest x5 10.8 us: all_sum(): lax.ppermute(value, axis, [(i, i ^ step) for i in range(count)])]
    all_to_all x1 -> x0, waiting for transfers between devices: 6.07 us -> none  [shared(): return lax.all_to_all(copies, axes, 0, 0, tiled=True)]
    all_to_all x1 -> x0, starting transfers between devices: 3.4 us -> none  [shared(): return lax.all_to_all(copies, axes, 0, 0, tiled=True)]
    ppermute x12, starting transfers between devices: 14.7 us -> 17.2 us  [move(): return lax.ppermute(value, AXES, path[name])]
    unnamed x7, local copies, waits for them, and re-layouts: 3.38 us -> 1.59 us
    ppermute x12, waiting for transfers between devices: 17.4 us -> 16.2 us  [move(): return lax.ppermute(value, AXES, path[name])]
  transfers between devices with their start and end apart: 13 -> 19, of which waited for: 7 -> 12; matrix products, arithmetic and copies ran while one was open for 2% -> 1% of each run, Pallas kernels for 0% -> 0%
where the time goes in v3:
time: 72.5 us; the launch traced here: 71.6 us
  starting transfers between devices  31.8 us (44%)
  waiting for transfers between devices  30.9 us (43%)
  Pallas kernels  5.42 us (7%)
  local copies, waits for them, and re-layouts  1.59 us (2%)
  other arithmetic  1.08 us (1%)
  between operations  0.74 us (1%)
    ppermute x12, starting transfers between devices, move(): return lax.ppermute(value, AXES, path[name])  17.2 us
    ppermute x12, waiting for transfers between devices, move(): return lax.ppermute(value, AXES, path[name])  16.2 us
    ppermute x5, starting transfers between devices, all_sum(): lax.ppermute(value, axis, [(i, i ^ step) for i in range(count)])  10.8 us
    ppermute x5, waiting for transfers between devices, all_sum(): lax.ppermute(value, axis, [(i, i ^ step) for i in range(count)])  9.97 us
    ppermute x2, waiting for transfers between devices, module_sum(): got = lax.ppermute(value, AXES, pairs)  4.75 us
    ppermute x2, starting transfers between devices, module_sum(): got = lax.ppermute(value, AXES, pairs)  3.89 us
    pallas_call x1, Pallas kernels, local(): call(start_body, [layer, layer, layer, layer, plane, plane, plane, plane,...  1.96 us
    unnamed x7, local copies, waits for them, and re-layouts  1.59 us
  transfers between devices with their start and end apart: 19, of which 12 were waited for; matrix products, arithmetic and copies ran while one was open for 1% of the time, Pallas kernels for 0%

profile of v3, /device:TPU:0, one launch (start us, length us, event | category | flops | bytes accessed | tf_op | source)
XLA Modules:
  0.0 71.6 jit_solution(6528075200070716454)
XLA Ops:
  0.6 1.0 %subtract_convert_fusion.free = f32[3,2,64,128]{3,2,1,0:T(8,128)S(1)} fusion(s32[3,2,64,128]{3,2,1,0:T(8,128)} %param.4), kind=kLoop, calls=%fused_computation.2 | loop fusion | flops 98304 | bytes 393216 | tf_op jit(solution)/shard_map/convert_element_type | solution.py:595
  1.7 0.1 copy-done.2
  1.8 0.8 %copy-done = f32[2,64,128]{2,1,0:T(8,128)S(1)} copy-done((f32[2,64,128]{2,1,0:T(8,128)S(1)}, f32[2,64,128]{2,1,0:T(8,128)}, u32[]{:S(2)}) %copy-start) | copy-done | bytes 65560
  2.6 0.1 prepare.1
  2.7 0.5 collective-permute-start.4
  3.2 2.6 %collective-permute-start = (f32[4,64,128]{2,1,0:T(8,128)S(1)}, f32[4,64,128]{2,1,0:T(8,128)S(1)}, u32[]{:S(2)}, u32[]{:S(2)}) collective-permute-start(f32[4,64,128]{2,1,0:T(8,128)S(1)} %get-tuple-element.27), channel_id=1, source_target_pairs={{0,2},{1,31},{2,4},{3,1},{4,6},{5,3},{6,8},{7,5},{8,10},{9,7},{10,... | collective-permute-start | bytes 393224 | tf_op jit(solution)/shard_map/ppermute | solution.py:590
  5.8 4.1 %collective-permute-start.1 = (f32[4,64,128]{2,1,0:T(8,128)S(1)}, f32[4,64,128]{2,1,0:T(8,128)S(1)}, u32[]{:S(2)}, u32[]{:S(2)}) collective-permute-start(f32[4,64,128]{2,1,0:T(8,128)S(1)} %get-tuple-element.28), channel_id=1, source_target_pairs={{1,2},{0,31},{3,4},{2,1},{5,6},{4,3},{7,8},{6,5},{9,10},{8,7},{11,... | collective-permute-start | bytes 393224 | tf_op jit(solution)/shard_map/ppermute | solution.py:590
  9.9 0.0 collective-permute-start.2
  9.9 1.6 %collective-permute-start.3 = (f32[64,128]{1,0:T(8,128)S(1)}, f32[64,128]{1,0:T(8,128)S(1)}, u32[]{:S(2)}, u32[]{:S(2)}) collective-permute-start(f32[64,128]{1,0:T(8,128)S(1)} %get-tuple-element.30), channel_id=1, source_target_pairs={{0,2},{1,3},{2,4},{3,5},{4,6},{5,7},{6,8},{7,9},{8,10},{9,11},{10,... | collective-permute-start | bytes 98312 | tf_op jit(solution)/shard_map/ppermute | solution.py:590
  11.6 5.9 %collective-permute-done.2.refs_3_ = f32[64,128]{1,0:T(8,128)S(1)} collective-permute-done((f32[64,128]{1,0:T(8,128)S(1)}, f32[64,128]{1,0:T(8,128)S(1)}, u32[]{:S(2)}, u32[]{:S(2)}) %collective-permute-start.2) | collective-permute-done | bytes 32800 | tf_op jit(solution)/shard_map/ppermute | solution.py:590
  17.4 0.4 collective-permute-done.3.refs_4_
  17.9 0.0 collective-permute-done.refs_1_
  17.9 0.0 collective-permute-done.1.refs_2_
  17.9 0.0 collective-permute-done.4.refs_5_
  17.9 2.0 %start.1 = (f32[3,128,128]{2,1,0:T(8,128)S(1)}, f32[3,128,128]{2,1,0:T(8,128)S(1)}, f32[3,128,128]{2,1,0:T(8,128)S(1)}, f32[3,128,128]{2,1,0:T(8,128)S(1)}, f32[...) custom-call(f32[11,64,128]{2,1,0:T(8,128)S(1)} %get-tuple-element.26, ...), custom_call_target="tpu_custom_call" | custom-call | tf_op jit(solution)/shard_map/start/pallas_call | solution.py:611
  19.8 0.7 collective-permute-start.5
  20.5 1.6 %collective-permute-start.6 = (f32[3,128,128]{2,1,0:T(8,128)S(1)}, f32[3,128,128]{2,1,0:T(8,128)S(1)}, u32[]{:S(2)}, u32[]{:S(2)}) collective-permute-start(f32[3,128,128]{2,1,0:T(8,128)S(1)} %get-tuple-element.32.v1), channel_id=1, source_target_pairs={{0,1},{1,0},{2,3},{3,2},{4,5},{5,4},{6,7},{7,6},{8,9},{9,8},{10,11... | collective-permute-start | bytes 589832 | tf_op jit(solution)/shard_map/ppermute | solution.py:590
  22.2 0.0 collective-permute-done.5.outer
  22.2 1.1 %collective-permute-done.6.inner = f32[3,128,128]{2,1,0:T(8,128)S(1)} collective-permute-done((f32[3,128,128]{2,1,0:T(8,128)S(1)}, f32[3,128,128]{2,1,0:T(8,128)S(1)}, u32[]{:S(2)}, u32[]{:S(2)}) %collective-permute-start.6) | collective-permute-done | bytes 196640 | tf_op jit(solution)/shard_map/ppermute | solution.py:590
  23.2 1.4 %second.1 = (f32[3,128,128]{2,1,0:T(8,128)S(1)}, f32[3,128,128]{2,1,0:T(8,128)S(1)}, f32[8,128]{1,0:T(8,128)S(1)}) custom-call(f32[3,128,128]{2,1,0:T(8,128)S(1)} %get-tuple-element.32.v1, f32[3,128,128]{2,1,0:T(8,128)S(1)} %collective-permute-done.5.outer, f32[3,128,128]{2,1,0:T(8,128)S(1)} %collective-permute-done.6.inner, ...), custom_call_target="tpu_custom_call" | custom-call | tf_op jit(solution)/shard_map/second/pallas_call | solution.py:619
  24.6 1.3 %collective-permute-start.7 = (f32[3,128,128]{2,1,0:T(8,128)S(1)}, f32[3,128,128]{2,1,0:T(8,128)S(1)}, u32[]{:S(2)}, u32[]{:S(2)}) collective-permute-start(f32[3,128,128]{2,1,0:T(8,128)S(1)} %get-tuple-element.37.v2), channel_id=1, source_target_pairs={{1,0},{3,2},{2,1},{5,4},{4,3},{7,6},{6,5},{9,8},{8,7},{11,10},{10,... | collective-permute-start | bytes 589832 | tf_op jit(solution)/shard_map/ppermute | solution.py:590
  25.9 7.4 %collective-permute-done.7.v2_high = f32[3,128,128]{2,1,0:T(8,128)S(1)} collective-permute-done((f32[3,128,128]{2,1,0:T(8,128)S(1)}, f32[3,128,128]{2,1,0:T(8,128)S(1)}, u32[]{:S(2)}, u32[]{:S(2)}) %collective-permute-start.7) | collective-permute-done | bytes 196640 | tf_op jit(solution)/shard_map/ppermute | solution.py:590
  33.3 0.4 third.1
  33.8 4.2 %collective-permute-start.8 = (f32[8,128]{1,0:T(8,128)S(1)}, f32[8,128]{1,0:T(8,128)S(1)}, u32[]{:S(2)}, u32[]{:S(2)}) collective-permute-start(f32[8,128]{1,0:T(8,128)S(1)} %third.1), channel_id=1, source_target_pairs={{0,1},{1,0},{2,3},{3,2},{4,5},{5,4},{6,7},{7,6},{8,9},{9,8},{10,11... | collective-permute-start | bytes 12296 | tf_op jit(solution)/shard_map/ppermute | solution.py:556
  38.0 0.8 %collective-permute-done.8 = f32[8,128]{1,0:T(8,128)S(1)} collective-permute-done((f32[8,128]{1,0:T(8,128)S(1)}, f32[8,128]{1,0:T(8,128)S(1)}, u32[]{:S(2)}, u32[]{:S(2)}) %collective-permute-start.8) | collective-permute-done | bytes 4128 | tf_op jit(solution)/shard_map/ppermute | solution.py:556
  38.8 0.2 collective-permute-start.9
  39.0 3.4 %collective-permute-done.9 = f32[8,128]{1,0:T(8,128)S(1)} collective-permute-done((f32[8,128]{1,0:T(8,128)S(1)}, f32[8,128]{1,0:T(8,128)S(1)}, u32[]{:S(2)}, u32[]{:S(2)}) %collective-permute-start.9) | collective-permute-done | bytes 4128 | tf_op jit(solution)/shard_map/ppermute | solution.py:556
  42.4 2.2 %collective-permute-start.10 = (f32[8,128]{1,0:T(8,128)S(1)}, f32[8,128]{1,0:T(8,128)S(1)}, u32[]{:S(2)}, u32[]{:S(2)}) collective-permute-start(f32[8,128]{1,0:T(8,128)S(1)} %add.19), channel_id=1, source_target_pairs={{0,4},{2,6},{4,0},{6,2},{1,5},{3,7},{5,1},{7,3},{8,12},{10,14},{12... | collective-permute-start | bytes 12296 | tf_op jit(solution)/shard_map/ppermute | solution.py:556
  44.6 2.3 %collective-permute-done.10 = f32[8,128]{1,0:T(8,128)S(1)} collective-permute-done((f32[8,128]{1,0:T(8,128)S(1)}, f32[8,128]{1,0:T(8,128)S(1)}, u32[]{:S(2)}, u32[]{:S(2)}) %collective-permute-start.10) | collective-permute-done | bytes 4128 | tf_op jit(solution)/shard_map/ppermute | solution.py:556
  46.9 2.4 %collective-permute-start.11 = (f32[8,128]{1,0:T(8,128)S(1)}, f32[8,128]{1,0:T(8,128)S(1)}, u32[]{:S(2)}, u32[]{:S(2)}) collective-permute-start(f32[8,128]{1,0:T(8,128)S(1)} %add.20), channel_id=1, source_target_pairs={{0,8},{8,0},{16,24},{24,16},{1,9},{9,1},{17,25},{25,17},{2,10},{10... | collective-permute-start | bytes 12296 | tf_op jit(solution)/shard_map/ppermute | solution.py:556
  49.4 1.6 %collective-permute-done.11 = f32[8,128]{1,0:T(8,128)S(1)} collective-permute-done((f32[8,128]{1,0:T(8,128)S(1)}, f32[8,128]{1,0:T(8,128)S(1)}, u32[]{:S(2)}, u32[]{:S(2)}) %collective-permute-start.11) | collective-permute-done | bytes 4128 | tf_op jit(solution)/shard_map/ppermute | solution.py:556
  50.9 1.7 %collective-permute-start.12 = (f32[8,128]{1,0:T(8,128)S(1)}, f32[8,128]{1,0:T(8,128)S(1)}, u32[]{:S(2)}, u32[]{:S(2)}) collective-permute-start(f32[8,128]{1,0:T(8,128)S(1)} %add.21), channel_id=1, source_target_pairs={{0,16},{8,24},{16,0},{24,8},{1,17},{9,25},{17,1},{25,9},{2,18},{10... | collective-permute-start | bytes 12296 | tf_op jit(solution)/shard_map/ppermute | solution.py:556
  52.7 1.9 %collective-permute-done.12 = f32[8,128]{1,0:T(8,128)S(1)} collective-permute-done((f32[8,128]{1,0:T(8,128)S(1)}, f32[8,128]{1,0:T(8,128)S(1)}, u32[]{:S(2)}, u32[]{:S(2)}) %collective-permute-start.12) | collective-permute-done | bytes 4128 | tf_op jit(solution)/shard_map/ppermute | solution.py:556
  54.6 0.7 combine.1
  55.2 0.1 collective-permute-start.13
  55.3 2.1 %collective-permute-start.14 = (f32[128,128]{1,0:T(8,128)S(1)}, f32[128,128]{1,0:T(8,128)S(1)}, u32[]{:S(2)}, u32[]{:S(2)}) collective-permute-start(f32[128,128]{1,0:T(8,128)S(1)} %get-tuple-element.45), channel_id=1, source_target_pairs={{0,8},{1,17},{2,10},{3,19},{4,12},{5,21},{6,14},{7,23},{8,0},{9,25... | collective-permute-start | bytes 196616 | tf_op jit(solution)/shard_map/ppermute | solution.py:580
  57.4 2.2 %collective-permute-done.14 = f32[128,128]{1,0:T(8,128)S(1)} collective-permute-done((f32[128,128]{1,0:T(8,128)S(1)}, f32[128,128]{1,0:T(8,128)S(1)}, u32[]{:S(2)}, u32[]{:S(2)}) %collective-permute-start.14) | collective-permute-done | bytes 65568 | tf_op jit(solution)/shard_map/ppermute | solution.py:580
  59.7 1.8 %collective-permute-start.15 = (f32[128,128]{1,0:T(8,128)S(1)}, f32[128,128]{1,0:T(8,128)S(1)}, u32[]{:S(2)}, u32[]{:S(2)}) collective-permute-start(f32[128,128]{1,0:T(8,128)S(1)} %add.23.slope), channel_id=1, source_target_pairs={{0,16},{1,9},{2,18},{3,11},{4,20},{5,13},{6,22},{7,15},{8,24},{9,1... | collective-permute-start | bytes 196616 | tf_op jit(solution)/shard_map/ppermute | solution.py:580
  61.5 0.0 collective-permute-done.13
  61.5 2.5 %collective-permute-done.15.rest = f32[128,128]{1,0:T(8,128)S(1)} collective-permute-done((f32[128,128]{1,0:T(8,128)S(1)}, f32[128,128]{1,0:T(8,128)S(1)}, u32[]{:S(2)}, u32[]{:S(2)}) %collective-permute-start.15) | collective-permute-done | bytes 65568 | tf_op jit(solution)/shard_map/ppermute | solution.py:580
  64.0 2.8 %collective-permute-start.16 = (f32[72,128]{1,0:T(8,128)S(1)}, f32[72,128]{1,0:T(8,128)S(1)}, u32[]{:S(2)}, u32[]{:S(2)}) collective-permute-start(f32[72,128]{1,0:T(8,128)S(1)} %get-tuple-element.48), channel_id=1, source_target_pairs={{1,2},{0,7},{3,4},{2,1},{5,6},{4,3},{7,0},{6,5},{9,10},{8,15},{11,... | collective-permute-start | bytes 110600 | tf_op jit(solution)/shard_map/ppermute | solution.py:590
  66.8 0.0 collective-permute-start.18
  66.8 1.8 %collective-permute-start.17 = (f32[72,128]{1,0:T(8,128)S(1)}, f32[72,128]{1,0:T(8,128)S(1)}, u32[]{:S(2)}, u32[]{:S(2)}) collective-permute-start(f32[72,128]{1,0:T(8,128)S(1)} %get-tuple-element.49), channel_id=1, source_target_pairs={{0,6},{1,3},{2,0},{3,5},{4,2},{5,7},{6,4},{7,1},{8,14},{9,11},{10,... | collective-permute-start | bytes 110600 | tf_op jit(solution)/shard_map/ppermute | solution.py:590
  68.6 0.7 copy.5
  69.3 0.0 collective-permute-done.16.outer
  69.3 1.4 %collective-permute-done.17.far = f32[72,128]{1,0:T(8,128)S(1)} collective-permute-done((f32[72,128]{1,0:T(8,128)S(1)}, f32[72,128]{1,0:T(8,128)S(1)}, u32[]{:S(2)}, u32[]{:S(2)}) %collective-permute-start.17) | collective-permute-done | bytes 36896 | tf_op jit(solution)/shard_map/ppermute | solution.py:590
  70.7 0.0 collective-permute-done.18.partner
  70.7 0.9 %gradient.1 = f32[2,64,128]{2,1,0:T(8,128)} custom-call(f32[128,128]{1,0:T(8,128)S(1)} %get-tuple-element.47.scaled, f32[72,128]{1,0:T(8,128)S(1)} %collective-permute-done.16.outer, f32[72,128]{1,0:T(8,128)S(1)} %collective-permute-done.17.far, f32[72,128]{1,0:T(8,128)S(1)} %collective-permute-done.18.partner), custom_call_target="tpu_custom_call" | custom-call | tf_op jit(solution)/shard_map/gradient/pallas_call | solution.py:643
  (14 shorter events, 0.1 us)
Async XLA Ops:
  0.6 1.0 %copy-start.1 = (s32[3,2,64,128]{3,2,1,0:T(8,128)S(1)}, s32[3,2,64,128]{3,2,1,0:T(8,128)}, u32[]{:S(2)}) copy-start(s32[3,2,64,128]{3,2,1,0:T(8,128)} %param.4) | copy-start | bytes 589828
  0.6 1.1 %copy-start.2 = (s32[3,2,64,128]{3,2,1,0:T(8,128)S(1)}, s32[3,2,64,128]{3,2,1,0:T(8,128)}, u32[]{:S(2)}) copy-start(s32[3,2,64,128]{3,2,1,0:T(8,128)} %param.5) | copy-start | bytes 589828
  1.7 0.8 %copy-start = (f32[2,64,128]{2,1,0:T(8,128)S(1)}, f32[2,64,128]{2,1,0:T(8,128)}, u32[]{:S(2)}) copy-start(f32[2,64,128]{2,1,0:T(8,128)} %design.1) | copy-start | bytes 196612
  2.7 15.2 %collective-permute-start.4 = (f32[11,64,128]{2,1,0:T(8,128)S(1)}, f32[11,64,128]{2,1,0:T(8,128)S(1)}, u32[]{:S(2)}, u32[]{:S(2)}) collective-permute-start(f32[11,64,128]{2,1,0:T(8,128)S(1)} %get-tuple-element.31), channel_id=1, source_target_pairs={{0,1},{1,0},{2,3},{3,2},{4,5},{5,4},{6,7},{7,6},{8,9},{9,8},{10,11... | collective-permute-start | bytes 1081352 | tf_op jit(solution)/shard_map/ppermute | solution.py:590
  3.2 14.7 %collective-permute-start = (f32[4,64,128]{2,1,0:T(8,128)S(1)}, f32[4,64,128]{2,1,0:T(8,128)S(1)}, u32[]{:S(2)}, u32[]{:S(2)}) collective-permute-start(f32[4,64,128]{2,1,0:T(8,128)S(1)} %get-tuple-element.27), channel_id=1, source_target_pairs={{0,2},{1,31},{2,4},{3,1},{4,6},{5,3},{6,8},{7,5},{8,10},{9,7},{10,... | collective-permute-start | bytes 393224 | tf_op jit(solution)/shard_map/ppermute | solution.py:590
  5.8 12.0 %collective-permute-start.1 = (f32[4,64,128]{2,1,0:T(8,128)S(1)}, f32[4,64,128]{2,1,0:T(8,128)S(1)}, u32[]{:S(2)}, u32[]{:S(2)}) collective-permute-start(f32[4,64,128]{2,1,0:T(8,128)S(1)} %get-tuple-element.28), channel_id=1, source_target_pairs={{1,2},{0,31},{3,4},{2,1},{5,6},{4,3},{7,8},{6,5},{9,10},{8,7},{11,... | collective-permute-start | bytes 393224 | tf_op jit(solution)/shard_map/ppermute | solution.py:590
  9.9 7.5 %collective-permute-start.2 = (f32[64,128]{1,0:T(8,128)S(1)}, f32[64,128]{1,0:T(8,128)S(1)}, u32[]{:S(2)}, u32[]{:S(2)}) collective-permute-start(f32[64,128]{1,0:T(8,128)S(1)} %get-tuple-element.29), channel_id=1, source_target_pairs={{0,3},{1,2},{2,5},{3,4},{4,7},{5,6},{6,9},{7,8},{8,11},{9,10},{10,... | collective-permute-start | bytes 98312 | tf_op jit(solution)/shard_map/ppermute | solution.py:590
  9.9 7.9 %collective-permute-start.3 = (f32[64,128]{1,0:T(8,128)S(1)}, f32[64,128]{1,0:T(8,128)S(1)}, u32[]{:S(2)}, u32[]{:S(2)}) collective-permute-start(f32[64,128]{1,0:T(8,128)S(1)} %get-tuple-element.30), channel_id=1, source_target_pairs={{0,2},{1,3},{2,4},{3,5},{4,6},{5,7},{6,8},{7,9},{8,10},{9,11},{10,... | collective-permute-start | bytes 98312 | tf_op jit(solution)/shard_map/ppermute | solution.py:590
  19.8 2.3 %collective-permute-start.5 = (f32[3,128,128]{2,1,0:T(8,128)S(1)}, f32[3,128,128]{2,1,0:T(8,128)S(1)}, u32[]{:S(2)}, u32[]{:S(2)}) collective-permute-start(f32[3,128,128]{2,1,0:T(8,128)S(1)} %get-tuple-element.32.v1), channel_id=1, source_target_pairs={{1,2},{3,4},{2,1},{5,6},{4,3},{7,8},{6,5},{9,10},{8,7},{11,12},{10... | collective-permute-start | bytes 589832 | tf_op jit(solution)/shard_map/ppermute | solution.py:590
  20.5 2.7 %collective-permute-start.6 = (f32[3,128,128]{2,1,0:T(8,128)S(1)}, f32[3,128,128]{2,1,0:T(8,128)S(1)}, u32[]{:S(2)}, u32[]{:S(2)}) collective-permute-start(f32[3,128,128]{2,1,0:T(8,128)S(1)} %get-tuple-element.32.v1), channel_id=1, source_target_pairs={{0,1},{1,0},{2,3},{3,2},{4,5},{5,4},{6,7},{7,6},{8,9},{9,8},{10,11... | collective-permute-start | bytes 589832 | tf_op jit(solution)/shard_map/ppermute | solution.py:590
  24.6 8.7 %collective-permute-start.7 = (f32[3,128,128]{2,1,0:T(8,128)S(1)}, f32[3,128,128]{2,1,0:T(8,128)S(1)}, u32[]{:S(2)}, u32[]{:S(2)}) collective-permute-start(f32[3,128,128]{2,1,0:T(8,128)S(1)} %get-tuple-element.37.v2), channel_id=1, source_target_pairs={{1,0},{3,2},{2,1},{5,4},{4,3},{7,6},{6,5},{9,8},{8,7},{11,10},{10,... | collective-permute-start | bytes 589832 | tf_op jit(solution)/shard_map/ppermute | solution.py:590
  33.8 5.0 %collective-permute-start.8 = (f32[8,128]{1,0:T(8,128)S(1)}, f32[8,128]{1,0:T(8,128)S(1)}, u32[]{:S(2)}, u32[]{:S(2)}) collective-permute-start(f32[8,128]{1,0:T(8,128)S(1)} %third.1), channel_id=1, source_target_pairs={{0,1},{1,0},{2,3},{3,2},{4,5},{5,4},{6,7},{7,6},{8,9},{9,8},{10,11... | collective-permute-start | bytes 12296 | tf_op jit(solution)/shard_map/ppermute | solution.py:556
  38.8 3.6 %collective-permute-start.9 = (f32[8,128]{1,0:T(8,128)S(1)}, f32[8,128]{1,0:T(8,128)S(1)}, u32[]{:S(2)}, u32[]{:S(2)}) collective-permute-start(f32[8,128]{1,0:T(8,128)S(1)} %add.18), channel_id=1, source_target_pairs={{0,2},{2,0},{4,6},{6,4},{1,3},{3,1},{5,7},{7,5},{8,10},{10,8},{12,... | collective-permute-start | bytes 12296 | tf_op jit(solution)/shard_map/ppermute | solution.py:556
  42.4 4.5 %collective-permute-start.10 = (f32[8,128]{1,0:T(8,128)S(1)}, f32[8,128]{1,0:T(8,128)S(1)}, u32[]{:S(2)}, u32[]{:S(2)}) collective-permute-start(f32[8,128]{1,0:T(8,128)S(1)} %add.19), channel_id=1, source_target_pairs={{0,4},{2,6},{4,0},{6,2},{1,5},{3,7},{5,1},{7,3},{8,12},{10,14},{12... | collective-permute-start | bytes 12296 | tf_op jit(solution)/shard_map/ppermute | solution.py:556
  46.9 4.0 %collective-permute-start.11 = (f32[8,128]{1,0:T(8,128)S(1)}, f32[8,128]{1,0:T(8,128)S(1)}, u32[]{:S(2)}, u32[]{:S(2)}) collective-permute-start(f32[8,128]{1,0:T(8,128)S(1)} %add.20), channel_id=1, source_target_pairs={{0,8},{8,0},{16,24},{24,16},{1,9},{9,1},{17,25},{25,17},{2,10},{10... | collective-permute-start | bytes 12296 | tf_op jit(solution)/shard_map/ppermute | solution.py:556
  50.9 3.6 %collective-permute-start.12 = (f32[8,128]{1,0:T(8,128)S(1)}, f32[8,128]{1,0:T(8,128)S(1)}, u32[]{:S(2)}, u32[]{:S(2)}) collective-permute-start(f32[8,128]{1,0:T(8,128)S(1)} %add.21), channel_id=1, source_target_pairs={{0,16},{8,24},{16,0},{24,8},{1,17},{9,25},{17,1},{25,9},{2,18},{10... | collective-permute-start | bytes 12296 | tf_op jit(solution)/shard_map/ppermute | solution.py:556
  55.2 6.2 %collective-permute-start.13 = (f32[3,64,128]{2,1,0:T(8,128)S(1)}, f32[3,64,128]{2,1,0:T(8,128)S(1)}, u32[]{:S(2)}, u32[]{:S(2)}) collective-permute-start(f32[3,64,128]{2,1,0:T(8,128)S(1)} %get-tuple-element.44), channel_id=1, source_target_pairs={{0,1},{1,0},{2,3},{3,2},{4,5},{5,4},{6,7},{7,6},{8,9},{9,8},{10,11... | collective-permute-start | bytes 294920 | tf_op jit(solution)/shard_map/ppermute | solution.py:590
  55.3 4.3 %collective-permute-start.14 = (f32[128,128]{1,0:T(8,128)S(1)}, f32[128,128]{1,0:T(8,128)S(1)}, u32[]{:S(2)}, u32[]{:S(2)}) collective-permute-start(f32[128,128]{1,0:T(8,128)S(1)} %get-tuple-element.45), channel_id=1, source_target_pairs={{0,8},{1,17},{2,10},{3,19},{4,12},{5,21},{6,14},{7,23},{8,0},{9,25... | collective-permute-start | bytes 196616 | tf_op jit(solution)/shard_map/ppermute | solution.py:580
  59.7 4.3 %collective-permute-start.15 = (f32[128,128]{1,0:T(8,128)S(1)}, f32[128,128]{1,0:T(8,128)S(1)}, u32[]{:S(2)}, u32[]{:S(2)}) collective-permute-start(f32[128,128]{1,0:T(8,128)S(1)} %add.23.slope), channel_id=1, source_target_pairs={{0,16},{1,9},{2,18},{3,11},{4,20},{5,13},{6,22},{7,15},{8,24},{9,1... | collective-permute-start | bytes 196616 | tf_op jit(solution)/shard_map/ppermute | solution.py:580
  64.0 5.3 %collective-permute-start.16 = (f32[72,128]{1,0:T(8,128)S(1)}, f32[72,128]{1,0:T(8,128)S(1)}, u32[]{:S(2)}, u32[]{:S(2)}) collective-permute-start(f32[72,128]{1,0:T(8,128)S(1)} %get-tuple-element.48), channel_id=1, source_target_pairs={{1,2},{0,7},{3,4},{2,1},{5,6},{4,3},{7,0},{6,5},{9,10},{8,15},{11,... | collective-permute-start | bytes 110600 | tf_op jit(solution)/shard_map/ppermute | solution.py:590
  66.8 4.0 %collective-permute-start.18 = (f32[72,128]{1,0:T(8,128)S(1)}, f32[72,128]{1,0:T(8,128)S(1)}, u32[]{:S(2)}, u32[]{:S(2)}) collective-permute-start(f32[72,128]{1,0:T(8,128)S(1)} %get-tuple-element.48), channel_id=1, source_target_pairs={{0,1},{1,0},{2,3},{3,2},{4,5},{5,4},{6,7},{7,6},{8,9},{9,8},{10,11... | collective-permute-start | bytes 110600 | tf_op jit(solution)/shard_map/ppermute | solution.py:590
  66.8 4.0 %collective-permute-start.17 = (f32[72,128]{1,0:T(8,128)S(1)}, f32[72,128]{1,0:T(8,128)S(1)}, u32[]{:S(2)}, u32[]{:S(2)}) collective-permute-start(f32[72,128]{1,0:T(8,128)S(1)} %get-tuple-element.49), channel_id=1, source_target_pairs={{0,6},{1,3},{2,0},{3,5},{4,2},{5,7},{6,4},{7,1},{8,14},{9,11},{10,... | collective-permute-start | bytes 110600 | tf_op jit(solution)/shard_map/ppermute | solution.py:590

commit v4 on v3

--- a/solution.py
+++ b/solution.py
@@ -107,9 +107,9 @@
     return out
 
 
-def element_modes(low, high):
-    sums = [[high[k][m] + low[k][m] for m in range(4)] for k in range(3)]
-    diffs = [[high[k][m] - low[k][m] for m in range(4)] for k in range(3)]
+def element_modes(own, other, side):
+    sums = [[other[k][m] + own[k][m] for m in range(4)] for k in range(3)]
+    diffs = [[(other[k][m] - own[k][m]) * side for m in range(4)] for k in range(3)]
     return [sums[k] + diffs[k] for k in range(3)]
 
 
@@ -142,28 +142,34 @@
     return total
 
 
-def apply_rows(low, own, high, mod_low, mod_own):
-    r_low = mode_forces(element_modes(low, own))
-    r_own = mode_forces(element_modes(own, high))
-    here, above = [], []
-    for k in range(3):
-        field = []
+def own_fields(own, other, side):
+    r = mode_forces(element_modes(own, other, side))
+    fields = []
+    for k in range(3):
         for m in range(4):
-            a, b = r_low[k][m], r_low[k][m + 4]
-            c, d = r_own[k][m], r_own[k][m + 4]
-            from_low = b if a is None else a + b
-            from_own = -d if c is None else c - d
-            field.append(mod_low * from_low + mod_own * from_own)
-        part = []
-        for py in range(2):
-            s, d = field[2 * py], field[2 * py + 1]
-            part.append((s - d) + z_down(s + d))
-        here.append(part[0] - part[1])
-        above.append(part[0] + part[1])
-    return here, above
-
-
-def operator_loop(count, read_low, read_own, read_high, read_free, mod_low_ref, mod_own_ref, out_ref):
+            d = r[k][m + 4] * side
+            fields.append(-d if r[k][m] is None else r[k][m] - d)
+    return fields
+
+
+def layer_modes(read, y0, count):
+    heres, modes = [], []
+    for k in range(3):
+        here, above = two_rows(lambda y, k=k: read(k, y), y0, count)
+        heres.append(here)
+        modes.append(face_modes(here, above))
+    return heres, modes
+
+
+def fields_loop(count, read_own, read_other, side, fields):
+    for y0 in range(0, count, ROWS):
+        _, own = layer_modes(read_own, y0, count)
+        _, other = layer_modes(read_other, y0, count)
+        for n, value in enumerate(own_fields(own, other, side)):
+            fields[n, pl.ds(y0, ROWS), :] = value
+
+
+def operator_loop(count, read_own, read_other, side, fields, mod_inner, mod_outer, free, out_ref):
     shape = (ROWS, out_ref.shape[2])
     square = jnp.zeros(shape, jnp.float32)
     cross = jnp.zeros(shape, jnp.float32)
@@ -171,25 +177,24 @@
     carry = [jnp.zeros(shape, jnp.float32)] * 3
     first = rows(shape) == 0
     for y0 in range(0, count, ROWS):
-        layers = []
-        owns = []
-        for read in (read_low, read_own, read_high):
-            layer = []
-            for k in range(3):
-                here, up = two_rows(lambda y, k=k, read=read: read(k, y), y0, count)
-                layer.append(face_modes(here, up))
-                if read is read_own:
-                    owns.append(here)
-            layers.append(layer)
-        here, above = apply_rows(
-            *layers, mod_low_ref[pl.ds(y0, ROWS), :], mod_own_ref[pl.ds(y0, ROWS), :]
-        )
+        part = pl.ds(y0, ROWS)
+        owns, own = layer_modes(read_own, y0, count)
+        _, other = layer_modes(read_other, y0, count)
+        inner, outer = mod_inner[part, :], mod_outer[part, :]
+        total = [
+            outer * value + inner * fields[n, part, :]
+            for n, value in enumerate(own_fields(own, other, side))
+        ]
         for k in range(3):
-            rolled = pltpu.roll(above[k], 1, 0)
-            force = here[k] + jnp.where(first, carry[k], rolled)
+            faces = []
+            for py in range(2):
+                s, d = total[4 * k + 2 * py], total[4 * k + 2 * py + 1]
+                faces.append((s - d) + z_down(s + d))
+            rolled = pltpu.roll(faces[0] + faces[1], 1, 0)
+            force = (faces[0] - faces[1]) + jnp.where(first, carry[k], rolled)
             carry[k] = rolled
-            image = read_free(k, y0) * force
-            out_ref[k, pl.ds(y0, ROWS), :] = image
+            image = free[k, part, :] * force
+            out_ref[k, part, :] = image
             square += image * image
             cross += owns[k] * image
             norm += owns[k] * owns[k]
@@ -198,15 +203,17 @@
 
 def energy_loop(count, read_own, read_high, use):
     for y0 in range(0, count, ROWS):
-        layers = []
-        for read in (read_own, read_high):
-            layers.append(
-                [
-                    face_modes(*two_rows(lambda y, k=k, read=read: read(k, y), y0, count))
-                    for k in range(3)
-                ]
-            )
-        use(y0, element_energy(element_modes(*layers)))
+        _, own = layer_modes(read_own, y0, count)
+        _, high = layer_modes(read_high, y0, count)
+        use(y0, element_energy(element_modes(own, high, 1.0)))
+
+
+def rows_of(ref):
+    return lambda k, y: ref[k, pl.ds(y, ROWS), :]
+
+
+def inner_side(sub):
+    return jnp.where(sub == 0, 1.0, -1.0).astype(jnp.float32)
 
 
 def line(tile):
@@ -273,103 +280,90 @@
     )
 
 
-def start_kernel(
+def start_inner_kernel(own, swap, v0, v0_inner, free, fields, layers):
+    sub = lax.axis_index("sub")
+    half = own.shape[1]
+    count = 2 * half
+    mine = pl.ds(pl.multiple_of(sub * half, half), half)
+    other = pl.ds(pl.multiple_of((1 - sub) * half, half), half)
+    for layer in range(2):
+        layers[layer, mine, :] = own[9 + layer]
+        layers[layer, other, :] = swap[9 + layer]
+    for k in range(3):
+        free[k, mine, :] = own[6 + k]
+        free[k, other, :] = swap[6 + k]
+        v0[k, mine, :] = own[2 * k + sub]
+        v0[k, other, :] = swap[2 * k + sub]
+        v0_inner[k, mine, :] = own[2 * k + 1 - sub]
+        v0_inner[k, other, :] = swap[2 * k + 1 - sub]
+    fields_loop(count, rows_of(v0), rows_of(v0_inner), inner_side(sub), fields)
+
+
+def start_outer_kernel(
     mods, slabs,
-    own, first, second, third, fourth, swap,
-    v0, v0_high, v1, free, mod_low, mod_own, slope_factor, chain_factor, moments,
-    v0_low, layers,
+    v0, v0_inner, free, fields, layers, first, second, third, fourth,
+    v1, v0_high, mod_inner, mod_outer, mod_own, slope_factor, chain_factor, moments,
+    v0_outer, near, deep,
 ):
     mod, slab, sub = (lax.axis_index(a) for a in AXES)
     half = third.shape[0]
     count = 2 * half
+    even = sub == 0
     mine = pl.ds(pl.multiple_of(sub * half, half), half)
     other = pl.ds(pl.multiple_of((1 - sub) * half, half), half)
-    for layer in range(2):
-        layers[2 - sub + layer, mine, :] = own[9 + layer]
-        layers[2 - sub + layer, other, :] = swap[9 + layer]
-    for near, deep, part in ((first, fourth, mine), (second, third, other)):
-
-        @pl.when(sub == 0)
-        def _(near=near, deep=deep, part=part):
-            layers[0, part, :] = deep[...]
-            layers[1, part, :] = near[3]
-
-        @pl.when(sub == 1)
-        def _(near=near, deep=deep, part=part):
-            layers[3, part, :] = near[3]
-            layers[0, part, :] = deep[...]
-
+    near[mine, :] = first[3]
+    near[other, :] = second[3]
+    deep[mine, :] = fourth[...]
+    deep[other, :] = third[...]
+    starts = (mod == 0) & (slab == 0) & even
+    ends = (mod == mods - 1) & (slab == slabs - 1) & (sub == 1)
+    inside = jnp.where(ends, 0.0, 1.0)
+    for k in range(3):
+        v0_outer[k, mine, :] = first[k] * inside
+        v0_outer[k, other, :] = second[k] * inside
+        v0_high[k] = jnp.where(even, v0_inner[k], v0_outer[k])
+
+    x1 = jnp.where(even, near[...], layers[0])
+    x2 = jnp.where(even, layers[0], layers[1])
+    x3 = jnp.where(even, layers[1], near[...])
     weight = weight_plane((count, third.shape[1]), 0, count)
-    starts = (mod == 0) & (slab == 0) & (sub == 0)
-    filtered = filter_planes(layers[0], layers[1], layers[2]) / weight
+    filtered = filter_planes(deep[...], x1, x2) / weight
     hyper = jnp.tanh(sharpness * (filtered - threshold))
     projected = (LOWER + hyper) * (1.0 / (LOWER + UPPER))
     below = stiff_floor + (1.0 - stiff_floor) * projected * projected * projected
-    mod_low[...] = below * jnp.where(starts, 0.0, 1.0)
-    filtered = filter_planes(layers[1], layers[2], layers[3]) / weight
+    below = below * jnp.where(starts, 0.0, 1.0)
+    filtered = filter_planes(x1, x2, x3) / weight
     hyper = jnp.tanh(sharpness * (filtered - threshold))
     projected = (LOWER + hyper) * (1.0 / (LOWER + UPPER))
     squared = projected * projected
-    mod_own[...] = stiff_floor + (1.0 - stiff_floor) * squared * projected
+    stiff = stiff_floor + (1.0 - stiff_floor) * squared * projected
+    mod_own[...] = stiff
+    mod_inner[...] = jnp.where(even, stiff, below)
+    mod_outer[...] = jnp.where(even, below, stiff)
     slope_factor[...] = (-penalty * (1.0 - stiff_floor)) * squared
     chain_factor[...] = (sharpness / (LOWER + UPPER)) * (1.0 - hyper * hyper) / weight
 
-    ends = (mod == mods - 1) & (slab == slabs - 1) & (sub == 1)
-    inside = jnp.where(ends, 0.0, 1.0)
-    for k in range(3):
-        free[k, mine, :] = own[6 + k]
-        free[k, other, :] = swap[6 + k]
-        v0[k, mine, :] = own[2 * k + sub]
-        v0[k, other, :] = swap[2 * k + sub]
-
-        @pl.when(sub == 0)
-        def _(k=k):
-            v0_high[k, mine, :] = own[2 * k + 1]
-            v0_high[k, other, :] = swap[2 * k + 1]
-            v0_low[k, mine, :] = first[k]
-            v0_low[k, other, :] = second[k]
-
-        @pl.when(sub == 1)
-        def _(k=k):
-            v0_low[k, mine, :] = own[2 * k]
-            v0_low[k, other, :] = swap[2 * k]
-            v0_high[k, mine, :] = first[k] * inside
-            v0_high[k, other, :] = second[k] * inside
-
     norm, cross, square = operator_loop(
-        count,
-        lambda k, y: v0_low[k, pl.ds(y, ROWS), :],
-        lambda k, y: v0[k, pl.ds(y, ROWS), :],
-        lambda k, y: v0_high[k, pl.ds(y, ROWS), :],
-        lambda k, y: free[k, pl.ds(y, ROWS), :],
-        mod_low,
-        mod_own,
-        v1,
+        count, rows_of(v0), rows_of(v0_outer), -inner_side(sub), fields, mod_inner, mod_outer, free, v1
     )
     moments[...] = jnp.concatenate(
         [line(norm), line(cross), line(square), jnp.zeros((5, norm.shape[1]), jnp.float32)], axis=0
     )
 
 
-def second_kernel(v1, outer, inner, free, mod_low, mod_own, before, v2, v1_high, moments):
+def second_inner_kernel(v1, inner, fields):
+    fields_loop(v1.shape[1], rows_of(v1), rows_of(inner), inner_side(lax.axis_index("sub")), fields)
+
+
+def second_outer_kernel(
+    v1, inner, outer, fields, free, mod_inner, mod_outer, before, v2, v1_high, moments
+):
     sub = lax.axis_index("sub")
     count = v1.shape[1]
-    even = sub == 0
-    for k in range(3):
-        v1_high[k] = jnp.where(even, inner[k], outer[k])
-
-    def read_low(k, y):
-        return jnp.where(even, outer[k, pl.ds(y, ROWS), :], inner[k, pl.ds(y, ROWS), :])
-
+    for k in range(3):
+        v1_high[k] = jnp.where(sub == 0, inner[k], outer[k])
     _, cross, square = operator_loop(
-        count,
-        read_low,
-        lambda k, y: v1[k, pl.ds(y, ROWS), :],
-        lambda k, y: v1_high[k, pl.ds(y, ROWS), :],
-        lambda k, y: free[k, pl.ds(y, ROWS), :],
-        mod_low,
-        mod_own,
-        v2,
+        count, rows_of(v1), rows_of(outer), -inner_side(sub), fields, mod_inner, mod_outer, free, v2
     )
     zero = jnp.zeros((3, cross.shape[1]), jnp.float32)
     moments[...] = before[...] + jnp.concatenate(
@@ -431,14 +425,14 @@
 
 
 def combine_kernel(
-    moments, v0, v0_high, v1, v1_high, v2, v2_high, slope_factor,
+    gathered, v0, v0_high, v1, v1_high, v2, v2_high, slope_factor,
     slope, keep, send,
     own, high,
 ):
     sub = lax.axis_index("sub")
     count = v0.shape[1]
     half = count // 2
-    sums = jnp.sum(moments[...], axis=1, keepdims=True)
+    sums = jnp.sum(jnp.sum(gathered[...], axis=0), axis=1, keepdims=True)
     c0, c1, c2 = coefficients([sums[k : k + 1] for k in range(6)])
     for k in range(3):
         own[k] = c0 * v0[k] + c1 * v1[k] + c2 * v2[k]
@@ -461,9 +455,13 @@
     )
 
 
-def scale_kernel(slope, rest, chain_factor, scaled, same, cross):
+def scale_kernel(*refs):
+    slopes, (chain_factor, scaled, same, cross) = refs[:-4], refs[-4:]
     sub = lax.axis_index("sub")
-    scaled[...] = (slope[...] + rest[...]) * chain_factor[...]
+    total = slopes[0][...]
+    for other in slopes[1:]:
+        total = total + other[...]
+    scaled[...] = total * chain_factor[...]
     window = same.shape[0]
     shift = scaled.shape[0] - window
     same[...] = scaled[pl.ds(pl.multiple_of(sub * shift, 8), window), :]
@@ -497,12 +495,14 @@
         gradient[layer] = sums[part, :]
 
 
-def call(body, outs, scratch=(), name=None):
+def call(body, outs, scratch=(), name=None, work=False):
+    cost = pl.CostEstimate(flops=10**7, bytes_accessed=4 * 10**6, transcendentals=0)
     return pl.pallas_call(
         body,
         out_shape=[jax.ShapeDtypeStruct(shape, jnp.float32) for shape in outs],
         scratch_shapes=[pltpu.VMEM(shape, jnp.float32) for shape in scratch],
         compiler_params=pltpu.CompilerParams(vmem_limit_bytes=16 * 2**20),
+        cost_estimate=cost if work else None,
         name=name,
     )
 
@@ -549,36 +549,10 @@
     )
 
 
-def all_sum(value, axis, count):
-    if count & (count - 1) == 0:
-        step = 1
-        while step < count:
-            value = value + lax.ppermute(value, axis, [(i, i ^ step) for i in range(count)])
-            step *= 2
-        return value
-    total = value
-    for step in range(1, count):
-        total = total + lax.ppermute(value, axis, [(i, (i + step) % count) for i in range(count)])
-    return total
-
-
-def module_sum(value, mods, slabs):
-    if mods & (mods - 1):
-        return all_sum(value, "mod", mods), jnp.zeros_like(value)
-    steps = [1 << bit for bit in range(mods.bit_length() - 1)]
-    got = jnp.zeros_like(value)
-    for n, _ in enumerate(steps):
-        pairs = []
-        for mod in range(mods):
-            for slab in range(slabs):
-                for sub in range(2):
-                    step = steps[n] if sub == 0 else steps[-1 - n]
-                    pairs.append(
-                        (2 * (mod * slabs + slab) + sub, 2 * ((mod ^ step) * slabs + slab) + sub)
-                    )
-        value = value + got if n else value
-        got = lax.ppermute(value, AXES, pairs)
-    return value, got
+def module_routes(mods):
+    if mods & (mods - 1) == 0:
+        return [[(m, m ^ s) for m in range(mods)] for s in range(1, mods)]
+    return [[(m, (m + s) % mods) for m in range(mods)] for s in range(1, mods)]
 
 
 def local(mods, slabs, design, fixed, load):
@@ -606,33 +580,41 @@
     swap = move(swap, "swap")
 
     def start_body(*refs):
-        start_kernel(mods, slabs, *refs)
-
-    v0, v0_high, v1, free, mod_low, mod_own, slope_factor, chain_factor, moments = call(
+        start_outer_kernel(mods, slabs, *refs)
+
+    v0, v0_inner, free, fields, layers = call(
+        start_inner_kernel,
+        [layer, layer, layer, (12,) + plane, (2,) + plane],
+        name="start_inner",
+        work=True,
+    )(own, swap)
+    v1, v0_high, mod_inner, mod_outer, mod_own, slope_factor, chain_factor, moments = call(
         start_body,
-        [layer, layer, layer, layer, plane, plane, plane, plane, (8, width)],
-        [layer, (4,) + plane],
-        name="start",
-    )(own, first, second, third, fourth, swap)
+        [layer, layer, plane, plane, plane, plane, plane, (8, width)],
+        [layer, plane, plane],
+        name="start_outer",
+    )(v0, v0_inner, free, fields, layers, first, second, third, fourth)
     outer = move(v1, "outer")
     inner = move(v1, "swap")
-    v2, v1_high, moments = call(second_kernel, [layer, layer, (8, width)], name="second")(
-        v1, outer, inner, free, mod_low, mod_own, moments
-    )
+    (fields,) = call(second_inner_kernel, [(12,) + plane], name="second_inner", work=True)(v1, inner)
+    v2, v1_high, moments = call(
+        second_outer_kernel, [layer, layer, (8, width)], name="second_outer"
+    )(v1, inner, outer, fields, free, mod_inner, mod_outer, moments)
     v2_high = move(v2, "down")
     (moments,) = call(third_kernel, [(8, width)], name="third")(v2, v2_high, mod_own, moments)
-    moments = all_sum(moments, "sub", 2)
-    moments = all_sum(moments, "slab", slabs)
-    moments = all_sum(moments, "mod", mods)
+    devices = 2 * mods * slabs
+    gathered = lax.all_to_all(
+        jnp.broadcast_to(moments, (devices, 8, width)), AXES, 0, 0, tiled=True
+    )
     slope, keep, send = call(
         combine_kernel, [plane, (3, half, width), (3, half, width)], [layer, layer], name="combine"
-    )(moments, v0, v0_high, v1, v1_high, v2, v2_high, slope_factor)
-    slope, rest = module_sum(slope, mods, slabs)
+    )(gathered, v0, v0_high, v1, v1_high, v2, v2_high, slope_factor)
+    slopes = [slope] + [lax.ppermute(slope, "mod", pairs) for pairs in module_routes(mods)]
     received = move(send, "swap")
     window = half + 8
     scaled, same, cross = call(
         scale_kernel, [plane, (window, width), (window, width)], name="scale"
-    )(slope, rest, chain_factor)
+    )(*slopes, chain_factor)
     outer = move(cross, "halo_cross")
     far = move(same, "halo_same")
     partner = move(cross, "swap")

time: 72.5 us -> 66.6 us (0.919)
  blocking collectives: 0 us -> 18.3 us
  starting transfers between devices: 31.8 us -> 19 us
  waiting for transfers between devices: 30.9 us -> 19.9 us
    all_to_all x0 -> x1, blocking collectives: none -> 18.3 us  [local(): lax.all_to_all(jnp.broadcast_to(moments, (devices, 8, width)), AXES, 0, 0...]
    ppermute x7 -> x3, waiting for transfers between devices: 14.7 us -> 3.29 us  [local(): lax.ppermute(slope, 'mod', pairs)]
    ppermute x7 -> x3, starting transfers between devices: 14.7 us -> 3.49 us  [local(): lax.ppermute(slope, 'mod', pairs)]
    ppermute x12, starting transfers between devices: 17.2 us -> 15.5 us  [move(): return lax.ppermute(value, AXES, path[name])]
    pallas_call x2 -> x4, Pallas kernels: 3.34 us -> 3.67 us  [the longest x1 1.69 us: local(): call(start_body, [layer, layer, plane, plane, plane, plane, plane, (8, wi...]
  transfers between devices with their start and end apart: 19 -> 15, of which waited for: 12 -> 9; matrix products, arithmetic and copies ran while one was open for 1% -> 1% of each run, Pallas kernels for 0% -> 1%
where the time goes in v4:
time: 66.6 us; the launch traced here: 66.4 us
  waiting for transfers between devices  19.9 us (30%)
  starting transfers between devices  19 us (29%)
  blocking collectives  18.3 us (27%)
  Pallas kernels  5.79 us (9%)
  local copies, waits for them, and re-layouts  1.6 us (2%)
  other arithmetic  1.06 us (2%)
  between operations  0.76 us (1%)
    all_to_all x1, blocking collectives, local(): lax.all_to_all(jnp.broadcast_to(moments, (devices, 8, width)), AXES, 0, 0...  18.3 us
    ppermute x12, waiting for transfers between devices, move(): return lax.ppermute(value, AXES, path[name])  16.6 us
    ppermute x12, starting transfers between devices, move(): return lax.ppermute(value, AXES, path[name])  15.5 us
    ppermute x3, starting transfers between devices, local(): lax.ppermute(slope, 'mod', pairs)  3.49 us
    ppermute x3, waiting for transfers between devices, local(): lax.ppermute(slope, 'mod', pairs)  3.29 us
    pallas_call x1, Pallas kernels, local(): call(start_body, [layer, layer, plane, plane, plane, plane, plane, (8, wi...  1.69 us
    unnamed x7, local copies, waits for them, and re-layouts  1.59 us
  transfers between devices with their start and end apart: 15, of which 9 were waited for; matrix products, arithmetic and copies ran while one was open for 1% of the time, Pallas kernels for 1%

profile of v4, /device:TPU:0, one launch (start us, length us, event | category | flops | bytes accessed | tf_op | source)
XLA Modules:
  0.0 66.4 jit_solution(4538772202393689717)
XLA Ops:
  0.6 0.0 copy-start.1
  0.6 0.0 copy-start.2
  0.6 1.0 %subtract_convert_fusion.free = f32[3,2,64,128]{3,2,1,0:T(8,128)S(1)} fusion(s32[3,2,64,128]{3,2,1,0:T(8,128)} %param.4), kind=kLoop, calls=%fused_computation.2 | loop fusion | flops 98304 | bytes 393216 | tf_op jit(solution)/shard_map/convert_element_type | solution.py:569
  1.7 0.0 copy-done.1
  1.7 0.1 copy-done.2
  1.7 0.0 copy-start
  1.8 0.8 %copy-done = f32[2,64,128]{2,1,0:T(8,128)S(1)} copy-done((f32[2,64,128]{2,1,0:T(8,128)S(1)}, f32[2,64,128]{2,1,0:T(8,128)}, u32[]{:S(2)}) %copy-start) | copy-done | bytes 65560
  2.6 0.1 prepare.1
  2.7 0.5 collective-permute-start
  3.2 2.6 %collective-permute-start.1 = (f32[4,64,128]{2,1,0:T(8,128)S(1)}, f32[4,64,128]{2,1,0:T(8,128)S(1)}, u32[]{:S(2)}, u32[]{:S(2)}) collective-permute-start(f32[4,64,128]{2,1,0:T(8,128)S(1)} %get-tuple-element.37), channel_id=1, source_target_pairs={{0,2},{1,31},{2,4},{3,1},{4,6},{5,3},{6,8},{7,5},{8,10},{9,7},{10,... | collective-permute-start | bytes 393224 | tf_op jit(solution)/shard_map/ppermute | solution.py:564
  5.8 4.1 %collective-permute-start.2 = (f32[4,64,128]{2,1,0:T(8,128)S(1)}, f32[4,64,128]{2,1,0:T(8,128)S(1)}, u32[]{:S(2)}, u32[]{:S(2)}) collective-permute-start(f32[4,64,128]{2,1,0:T(8,128)S(1)} %get-tuple-element.38), channel_id=1, source_target_pairs={{1,2},{0,31},{3,4},{2,1},{5,6},{4,3},{7,8},{6,5},{9,10},{8,7},{11,... | collective-permute-start | bytes 393224 | tf_op jit(solution)/shard_map/ppermute | solution.py:564
  9.9 0.0 collective-permute-start.3
  9.9 1.6 %collective-permute-start.4 = (f32[64,128]{1,0:T(8,128)S(1)}, f32[64,128]{1,0:T(8,128)S(1)}, u32[]{:S(2)}, u32[]{:S(2)}) collective-permute-start(f32[64,128]{1,0:T(8,128)S(1)} %get-tuple-element.40), channel_id=1, source_target_pairs={{0,2},{1,3},{2,4},{3,5},{4,6},{5,7},{6,8},{7,9},{8,10},{9,11},{10,... | collective-permute-start | bytes 98312 | tf_op jit(solution)/shard_map/ppermute | solution.py:564
  11.6 0.0 collective-permute-done.swap
  11.6 0.5 start_inner.1
  12.0 5.4 %collective-permute-done.3.refs_7_ = f32[64,128]{1,0:T(8,128)S(1)} collective-permute-done((f32[64,128]{1,0:T(8,128)S(1)}, f32[64,128]{1,0:T(8,128)S(1)}, u32[]{:S(2)}, u32[]{:S(2)}) %collective-permute-start.3) | collective-permute-done | bytes 32800 | tf_op jit(solution)/shard_map/ppermute | solution.py:564
  17.4 0.4 collective-permute-done.4.refs_8_
  17.9 0.0 collective-permute-done.1.refs_5_
  17.9 0.0 collective-permute-done.2.refs_6_
  17.9 1.7 %start_outer.1 = (f32[3,128,128]{2,1,0:T(8,128)S(1)}, f32[3,128,128]{2,1,0:T(8,128)S(1)}, f32[128,128]{1,0:T(8,128)S(1)}, f32[128,128]{1,0:T(8,128)S(1)}, f32[12...) custom-call(f32[3,128,128]{2,1,0:T(8,128)S(1)} %get-tuple-element.32.refs_0_.v0, ...), custom_call_target="tpu_custom_call" | custom-call | tf_op jit(solution)/shard_map/start_outer/pallas_call | solution.py:591
  19.6 0.2 collective-permute-start.5
  19.8 0.7 collective-permute-start.6
  20.5 0.6 collective-permute-done.5.inner
  21.1 0.4 second_inner.1.fields
  21.5 0.0 collective-permute-done.6.outer
  21.5 1.1 %second_outer.1 = (f32[3,128,128]{2,1,0:T(8,128)S(1)}, f32[3,128,128]{2,1,0:T(8,128)S(1)}, f32[8,128]{1,0:T(8,128)S(1)}) custom-call(f32[3,128,128]{2,1,0:T(8,128)S(1)} %get-tuple-element.41.v1, f32[3,128,128]{2,1,0:T(8,128)S(1)} %collective-permute-done.5.inner, f32[3,128,128]{2,1,0:T(8,128)S(1)} %collective-permute-done.6.outer, ...), custom_call_target="tpu_custom_call" | custom-call | tf_op jit(solution)/shard_map/second_outer/pallas_call | solution.py:600
  22.6 1.3 %collective-permute-start.7 = (f32[3,128,128]{2,1,0:T(8,128)S(1)}, f32[3,128,128]{2,1,0:T(8,128)S(1)}, u32[]{:S(2)}, u32[]{:S(2)}) collective-permute-start(f32[3,128,128]{2,1,0:T(8,128)S(1)} %get-tuple-element.45.v2), channel_id=1, source_target_pairs={{1,0},{3,2},{2,1},{5,4},{4,3},{7,6},{6,5},{9,8},{8,7},{11,10},{10,... | collective-permute-start | bytes 589832 | tf_op jit(solution)/shard_map/ppermute | solution.py:564
  23.9 9.3 %collective-permute-done.7.v2_high = f32[3,128,128]{2,1,0:T(8,128)S(1)} collective-permute-done((f32[3,128,128]{2,1,0:T(8,128)S(1)}, f32[3,128,128]{2,1,0:T(8,128)S(1)}, u32[]{:S(2)}, u32[]{:S(2)}) %collective-permute-start.7) | collective-permute-done | bytes 196640 | tf_op jit(solution)/shard_map/ppermute | solution.py:564
  33.2 0.4 third.1
  33.6 18.3 %all_to_all.5.gathered = f32[32,8,128]{2,1,0:T(8,128)S(1)} all-to-all(f32[32,8,128]{2,1,0:T(8,128)S(1)} %broadcast_in_dim.3), channel_id=1, replica_groups=mesh['mod'=4,'slab'=4,'sub'=2] {'mod','slab','sub'}, dimensions={0} | all-to-all | bytes 262144 | tf_op jit(solution)/shard_map/all_to_all | solution.py:606
  52.0 0.7 %combine.1 = (f32[128,128]{1,0:T(8,128)S(1)}, f32[3,64,128]{2,1,0:T(8,128)S(1)}, f32[3,64,128]{2,1,0:T(8,128)S(1)}) custom-call(f32[32,8,128]{2,1,0:T(8,128)S(1)} %all_to_all.5.gathered, f32[3,128,128]{2,1,0:T(8,128)S(1)} %get-tuple-element.32.refs_0_.v0, f32[3,128,128]{2,1,0:T(8,128)S(1)} %get-tuple-element.48.v0_high, ...), custom_call_target="tpu_custom_call" | custom-call | tf_op jit(solution)/shard_map/combine/pallas_call | solution.py:609
  52.7 0.4 collective-permute-start.8
  53.1 0.6 collective-permute-start.10
  53.7 1.4 %collective-permute-start.11 = (f32[128,128]{1,0:T(8,128)S(1)}, f32[128,128]{1,0:T(8,128)S(1)}, u32[]{:S(2)}, u32[]{:S(2)}) collective-permute-start(f32[128,128]{1,0:T(8,128)S(1)} %get-tuple-element.53.refs_0_), channel_id=1, source_target_pairs={{0,24},{8,16},{16,8},{24,0},{1,25},{9,17},{17,9},{25,1},{2,26},{10... | collective-permute-start | bytes 196616 | tf_op jit(solution)/shard_map/ppermute | solution.py:612
  55.1 1.4 %collective-permute-start.9 = (f32[128,128]{1,0:T(8,128)S(1)}, f32[128,128]{1,0:T(8,128)S(1)}, u32[]{:S(2)}, u32[]{:S(2)}) collective-permute-start(f32[128,128]{1,0:T(8,128)S(1)} %get-tuple-element.53.refs_0_), channel_id=1, source_target_pairs={{0,8},{8,0},{16,24},{24,16},{1,9},{9,1},{17,25},{25,17},{2,10},{10... | collective-permute-start | bytes 196616 | tf_op jit(solution)/shard_map/ppermute | solution.py:612
  56.5 0.8 %collective-permute-done.10.refs_2_ = f32[128,128]{1,0:T(8,128)S(1)} collective-permute-done((f32[128,128]{1,0:T(8,128)S(1)}, f32[128,128]{1,0:T(8,128)S(1)}, u32[]{:S(2)}, u32[]{:S(2)}) %collective-permute-start.10) | collective-permute-done | bytes 65568 | tf_op jit(solution)/shard_map/ppermute | solution.py:612
  57.3 2.1 %collective-permute-done.11.refs_3_ = f32[128,128]{1,0:T(8,128)S(1)} collective-permute-done((f32[128,128]{1,0:T(8,128)S(1)}, f32[128,128]{1,0:T(8,128)S(1)}, u32[]{:S(2)}, u32[]{:S(2)}) %collective-permute-start.11) | collective-permute-done | bytes 65568 | tf_op jit(solution)/shard_map/ppermute | solution.py:612
  59.4 0.4 collective-permute-done.9.refs_1_
  59.9 0.1 collective-permute-start.12
  59.9 0.7 %collective-permute-start.14 = (f32[72,128]{1,0:T(8,128)S(1)}, f32[72,128]{1,0:T(8,128)S(1)}, u32[]{:S(2)}, u32[]{:S(2)}) collective-permute-start(f32[72,128]{1,0:T(8,128)S(1)} %get-tuple-element.56), channel_id=1, source_target_pairs={{0,1},{1,0},{2,3},{3,2},{4,5},{5,4},{6,7},{7,6},{8,9},{9,8},{10,11... | collective-permute-start | bytes 110600 | tf_op jit(solution)/shard_map/ppermute | solution.py:564
  60.6 3.2 %collective-permute-start.13 = (f32[72,128]{1,0:T(8,128)S(1)}, f32[72,128]{1,0:T(8,128)S(1)}, u32[]{:S(2)}, u32[]{:S(2)}) collective-permute-start(f32[72,128]{1,0:T(8,128)S(1)} %get-tuple-element.57), channel_id=1, source_target_pairs={{0,6},{1,3},{2,0},{3,5},{4,2},{5,7},{6,4},{7,1},{8,14},{9,11},{10,... | collective-permute-start | bytes 110600 | tf_op jit(solution)/shard_map/ppermute | solution.py:564
  63.9 0.0 collective-permute-done.8
  63.9 0.7 %copy.5 = f32[3,2,64,128]{3,2,1,0:T(8,128)} copy(f32[3,2,64,128]{3,2,0,1:T(8,128)S(1)} %pad_maximum_fusion) | data formatting | bytes 393216
  64.6 0.5 collective-permute-done.12.outer
  65.1 0.4 collective-permute-done.13.far
  65.5 0.0 collective-permute-done.14.partner
  65.5 0.9 %gradient.1 = f32[2,64,128]{2,1,0:T(8,128)} custom-call(f32[128,128]{1,0:T(8,128)S(1)} %get-tuple-element.55.scaled, f32[72,128]{1,0:T(8,128)S(1)} %collective-permute-done.12.outer, f32[72,128]{1,0:T(8,128)S(1)} %collective-permute-done.13.far, f32[72,128]{1,0:T(8,128)S(1)} %collective-permute-done.14.partner), custom_call_target="tpu_custom_call" | custom-call | tf_op jit(solution)/shard_map/gradient/pallas_call | solution.py:625
  (5 shorter events, 0.1 us)
Async XLA Ops:
  0.6 1.0 %copy-start.1 = (s32[3,2,64,128]{3,2,1,0:T(8,128)S(1)}, s32[3,2,64,128]{3,2,1,0:T(8,128)}, u32[]{:S(2)}) copy-start(s32[3,2,64,128]{3,2,1,0:T(8,128)} %param.4) | copy-start | bytes 589828
  0.6 1.1 %copy-start.2 = (s32[3,2,64,128]{3,2,1,0:T(8,128)S(1)}, s32[3,2,64,128]{3,2,1,0:T(8,128)}, u32[]{:S(2)}) copy-start(s32[3,2,64,128]{3,2,1,0:T(8,128)} %param.5) | copy-start | bytes 589828
  1.7 0.8 %copy-start = (f32[2,64,128]{2,1,0:T(8,128)S(1)}, f32[2,64,128]{2,1,0:T(8,128)}, u32[]{:S(2)}) copy-start(f32[2,64,128]{2,1,0:T(8,128)} %design.1) | copy-start | bytes 196612
  2.7 8.9 %collective-permute-start = (f32[11,64,128]{2,1,0:T(8,128)S(1)}, f32[11,64,128]{2,1,0:T(8,128)S(1)}, u32[]{:S(2)}, u32[]{:S(2)}) collective-permute-start(f32[11,64,128]{2,1,0:T(8,128)S(1)} %get-tuple-element.31), channel_id=1, source_target_pairs={{0,1},{1,0},{2,3},{3,2},{4,5},{5,4},{6,7},{7,6},{8,9},{9,8},{10,11... | collective-permute-start | bytes 1081352 | tf_op jit(solution)/shard_map/ppermute | solution.py:564
  3.2 14.7 %collective-permute-start.1 = (f32[4,64,128]{2,1,0:T(8,128)S(1)}, f32[4,64,128]{2,1,0:T(8,128)S(1)}, u32[]{:S(2)}, u32[]{:S(2)}) collective-permute-start(f32[4,64,128]{2,1,0:T(8,128)S(1)} %get-tuple-element.37), channel_id=1, source_target_pairs={{0,2},{1,31},{2,4},{3,1},{4,6},{5,3},{6,8},{7,5},{8,10},{9,7},{10,... | collective-permute-start | bytes 393224 | tf_op jit(solution)/shard_map/ppermute | solution.py:564
  5.8 12.0 %collective-permute-start.2 = (f32[4,64,128]{2,1,0:T(8,128)S(1)}, f32[4,64,128]{2,1,0:T(8,128)S(1)}, u32[]{:S(2)}, u32[]{:S(2)}) collective-permute-start(f32[4,64,128]{2,1,0:T(8,128)S(1)} %get-tuple-element.38), channel_id=1, source_target_pairs={{1,2},{0,31},{3,4},{2,1},{5,6},{4,3},{7,8},{6,5},{9,10},{8,7},{11,... | collective-permute-start | bytes 393224 | tf_op jit(solution)/shard_map/ppermute | solution.py:564
  9.9 7.5 %collective-permute-start.3 = (f32[64,128]{1,0:T(8,128)S(1)}, f32[64,128]{1,0:T(8,128)S(1)}, u32[]{:S(2)}, u32[]{:S(2)}) collective-permute-start(f32[64,128]{1,0:T(8,128)S(1)} %get-tuple-element.39), channel_id=1, source_target_pairs={{0,3},{1,2},{2,5},{3,4},{4,7},{5,6},{6,9},{7,8},{8,11},{9,10},{10,... | collective-permute-start | bytes 98312 | tf_op jit(solution)/shard_map/ppermute | solution.py:564
  9.9 7.9 %collective-permute-start.4 = (f32[64,128]{1,0:T(8,128)S(1)}, f32[64,128]{1,0:T(8,128)S(1)}, u32[]{:S(2)}, u32[]{:S(2)}) collective-permute-start(f32[64,128]{1,0:T(8,128)S(1)} %get-tuple-element.40), channel_id=1, source_target_pairs={{0,2},{1,3},{2,4},{3,5},{4,6},{5,7},{6,8},{7,9},{8,10},{9,11},{10,... | collective-permute-start | bytes 98312 | tf_op jit(solution)/shard_map/ppermute | solution.py:564
  19.6 1.5 %collective-permute-start.5 = (f32[3,128,128]{2,1,0:T(8,128)S(1)}, f32[3,128,128]{2,1,0:T(8,128)S(1)}, u32[]{:S(2)}, u32[]{:S(2)}) collective-permute-start(f32[3,128,128]{2,1,0:T(8,128)S(1)} %get-tuple-element.41.v1), channel_id=1, source_target_pairs={{0,1},{1,0},{2,3},{3,2},{4,5},{5,4},{6,7},{7,6},{8,9},{9,8},{10,11... | collective-permute-start | bytes 589832 | tf_op jit(solution)/shard_map/ppermute | solution.py:564
  19.8 1.7 %collective-permute-start.6 = (f32[3,128,128]{2,1,0:T(8,128)S(1)}, f32[3,128,128]{2,1,0:T(8,128)S(1)}, u32[]{:S(2)}, u32[]{:S(2)}) collective-permute-start(f32[3,128,128]{2,1,0:T(8,128)S(1)} %get-tuple-element.41.v1), channel_id=1, source_target_pairs={{1,2},{3,4},{2,1},{5,6},{4,3},{7,8},{6,5},{9,10},{8,7},{11,12},{10... | collective-permute-start | bytes 589832 | tf_op jit(solution)/shard_map/ppermute | solution.py:564
  22.6 10.6 %collective-permute-start.7 = (f32[3,128,128]{2,1,0:T(8,128)S(1)}, f32[3,128,128]{2,1,0:T(8,128)S(1)}, u32[]{:S(2)}, u32[]{:S(2)}) collective-permute-start(f32[3,128,128]{2,1,0:T(8,128)S(1)} %get-tuple-element.45.v2), channel_id=1, source_target_pairs={{1,0},{3,2},{2,1},{5,4},{4,3},{7,6},{6,5},{9,8},{8,7},{11,10},{10,... | collective-permute-start | bytes 589832 | tf_op jit(solution)/shard_map/ppermute | solution.py:564
  52.7 11.2 %collective-permute-start.8 = (f32[3,64,128]{2,1,0:T(8,128)S(1)}, f32[3,64,128]{2,1,0:T(8,128)S(1)}, u32[]{:S(2)}, u32[]{:S(2)}) collective-permute-start(f32[3,64,128]{2,1,0:T(8,128)S(1)} %get-tuple-element.52), channel_id=1, source_target_pairs={{0,1},{1,0},{2,3},{3,2},{4,5},{5,4},{6,7},{7,6},{8,9},{9,8},{10,11... | collective-permute-start | bytes 294920 | tf_op jit(solution)/shard_map/ppermute | solution.py:564
  53.1 4.3 %collective-permute-start.10 = (f32[128,128]{1,0:T(8,128)S(1)}, f32[128,128]{1,0:T(8,128)S(1)}, u32[]{:S(2)}, u32[]{:S(2)}) collective-permute-start(f32[128,128]{1,0:T(8,128)S(1)} %get-tuple-element.53.refs_0_), channel_id=1, source_target_pairs={{0,16},{8,24},{16,0},{24,8},{1,17},{9,25},{17,1},{25,9},{2,18},{10... | collective-permute-start | bytes 196616 | tf_op jit(solution)/shard_map/ppermute | solution.py:612
  53.7 5.8 %collective-permute-start.11 = (f32[128,128]{1,0:T(8,128)S(1)}, f32[128,128]{1,0:T(8,128)S(1)}, u32[]{:S(2)}, u32[]{:S(2)}) collective-permute-start(f32[128,128]{1,0:T(8,128)S(1)} %get-tuple-element.53.refs_0_), channel_id=1, source_target_pairs={{0,24},{8,16},{16,8},{24,0},{1,25},{9,17},{17,9},{25,1},{2,26},{10... | collective-permute-start | bytes 196616 | tf_op jit(solution)/shard_map/ppermute | solution.py:612
  55.1 4.7 %collective-permute-start.9 = (f32[128,128]{1,0:T(8,128)S(1)}, f32[128,128]{1,0:T(8,128)S(1)}, u32[]{:S(2)}, u32[]{:S(2)}) collective-permute-start(f32[128,128]{1,0:T(8,128)S(1)} %get-tuple-element.53.refs_0_), channel_id=1, source_target_pairs={{0,8},{8,0},{16,24},{24,16},{1,9},{9,1},{17,25},{25,17},{2,10},{10... | collective-permute-start | bytes 196616 | tf_op jit(solution)/shard_map/ppermute | solution.py:612
  59.9 5.2 %collective-permute-start.12 = (f32[72,128]{1,0:T(8,128)S(1)}, f32[72,128]{1,0:T(8,128)S(1)}, u32[]{:S(2)}, u32[]{:S(2)}) collective-permute-start(f32[72,128]{1,0:T(8,128)S(1)} %get-tuple-element.56), channel_id=1, source_target_pairs={{1,2},{0,7},{3,4},{2,1},{5,6},{4,3},{7,0},{6,5},{9,10},{8,15},{11,... | collective-permute-start | bytes 110600 | tf_op jit(solution)/shard_map/ppermute | solution.py:564
  59.9 5.6 %collective-permute-start.14 = (f32[72,128]{1,0:T(8,128)S(1)}, f32[72,128]{1,0:T(8,128)S(1)}, u32[]{:S(2)}, u32[]{:S(2)}) collective-permute-start(f32[72,128]{1,0:T(8,128)S(1)} %get-tuple-element.56), channel_id=1, source_target_pairs={{0,1},{1,0},{2,3},{3,2},{4,5},{5,4},{6,7},{7,6},{8,9},{9,8},{10,11... | collective-permute-start | bytes 110600 | tf_op jit(solution)/shard_map/ppermute | solution.py:564
  60.6 4.9 %collective-permute-start.13 = (f32[72,128]{1,0:T(8,128)S(1)}, f32[72,128]{1,0:T(8,128)S(1)}, u32[]{:S(2)}, u32[]{:S(2)}) collective-permute-start(f32[72,128]{1,0:T(8,128)S(1)} %get-tuple-element.57), channel_id=1, source_target_pairs={{0,6},{1,3},{2,0},{3,5},{4,2},{5,7},{6,4},{7,1},{8,14},{9,11},{10,... | collective-permute-start | bytes 110600 | tf_op jit(solution)/shard_map/ppermute | solution.py:564

commit v5 on v4

--- a/solution.py
+++ b/solution.py
@@ -220,11 +220,11 @@
     return jnp.sum(tile, axis=0, keepdims=True)
 
 
-def prepare_kernel(free, right, design, swap, first, second, third, fourth, own):
+def prepare_kernel(free, load, design, swap, first, second, third, fourth, own):
     sub = lax.axis_index("sub")
     for k in range(3):
         frees = [free[k, layer] for layer in range(2)]
-        values = [right[k, layer] for layer in range(2)]
+        values = [frees[layer] * load[k, layer].astype(jnp.float32) for layer in range(2)]
         for layer in range(2):
             swap[2 * k + layer] = values[layer]
             own[2 * k + layer] = values[layer]
@@ -245,21 +245,23 @@
     fourth[...] = sooner
 
 
+def around(p):
+    across = y_up(p) + y_down(p)
+    return across + z_up(p) + z_down(p), z_up(across) + z_down(across)
+
+
+def filter_mid(p):
+    face, diag = around(p)
+    return filter_reach * p + FACE * face + EDGE * diag
+
+
+def filter_side(p):
+    face, diag = around(p)
+    return FACE * p + EDGE * face + CORNER * diag
+
+
 def filter_planes(low, mid, high):
-    both = low + high
-
-    def faces(p):
-        across = y_up(p) + y_down(p)
-        return across + z_up(p) + z_down(p), z_up(across) + z_down(across)
-
-    mid_face, mid_diag = faces(mid)
-    both_face, both_diag = faces(both)
-    return (
-        filter_reach * mid
-        + FACE * (both + mid_face)
-        + EDGE * (both_face + mid_diag)
-        + CORNER * both_diag
-    )
+    return filter_side(low + high) + filter_mid(mid)
 
 
 def weight_plane(shape, row_offset, count):
@@ -280,7 +282,7 @@
     )
 
 
-def start_inner_kernel(own, swap, v0, v0_inner, free, fields, layers):
+def start_inner_kernel(own, swap, v0, v0_inner, free, fields, parts, layers):
     sub = lax.axis_index("sub")
     half = own.shape[1]
     count = 2 * half
@@ -289,6 +291,18 @@
     for layer in range(2):
         layers[layer, mine, :] = own[9 + layer]
         layers[layer, other, :] = swap[9 + layer]
+
+    @pl.when(sub == 0)
+    def _():
+        parts[0] = filter_side(layers[0])
+        parts[1] = filter_mid(layers[0]) + filter_side(layers[1])
+
+    @pl.when(sub == 1)
+    def _():
+        parts[0] = filter_mid(layers[0]) + filter_side(layers[1])
+        parts[1] = filter_side(layers[0]) + filter_mid(layers[1])
+
+    parts[2] = 1.0 / weight_plane((count, own.shape[2]), 0, count)
     for k in range(3):
         free[k, mine, :] = own[6 + k]
         free[k, other, :] = swap[6 + k]
@@ -301,7 +315,7 @@
 
 def start_outer_kernel(
     mods, slabs,
-    v0, v0_inner, free, fields, layers, first, second, third, fourth,
+    first, second, third, fourth, v0, v0_inner, free, fields, parts,
     v1, v0_high, mod_inner, mod_outer, mod_own, slope_factor, chain_factor, moments,
     v0_outer, near, deep,
 ):
@@ -323,16 +337,15 @@
         v0_outer[k, other, :] = second[k] * inside
         v0_high[k] = jnp.where(even, v0_inner[k], v0_outer[k])
 
-    x1 = jnp.where(even, near[...], layers[0])
-    x2 = jnp.where(even, layers[0], layers[1])
-    x3 = jnp.where(even, layers[1], near[...])
-    weight = weight_plane((count, third.shape[1]), 0, count)
-    filtered = filter_planes(deep[...], x1, x2) / weight
+    side = filter_side(near[...])
+    mid = filter_mid(near[...])
+    inverse = parts[2]
+    filtered = (parts[0] + filter_side(deep[...]) + jnp.where(even, mid, 0.0)) * inverse
     hyper = jnp.tanh(sharpness * (filtered - threshold))
     projected = (LOWER + hyper) * (1.0 / (LOWER + UPPER))
     below = stiff_floor + (1.0 - stiff_floor) * projected * projected * projected
     below = below * jnp.where(starts, 0.0, 1.0)
-    filtered = filter_planes(x1, x2, x3) / weight
+    filtered = (parts[1] + side) * inverse
     hyper = jnp.tanh(sharpness * (filtered - threshold))
     projected = (LOWER + hyper) * (1.0 / (LOWER + UPPER))
     squared = projected * projected
@@ -341,7 +354,7 @@
     mod_inner[...] = jnp.where(even, stiff, below)
     mod_outer[...] = jnp.where(even, below, stiff)
     slope_factor[...] = (-penalty * (1.0 - stiff_floor)) * squared
-    chain_factor[...] = (sharpness / (LOWER + UPPER)) * (1.0 - hyper * hyper) / weight
+    chain_factor[...] = (sharpness / (LOWER + UPPER)) * (1.0 - hyper * hyper) * inverse
 
     norm, cross, square = operator_loop(
         count, rows_of(v0), rows_of(v0_outer), -inner_side(sub), fields, mod_inner, mod_outer, free, v1
@@ -356,7 +369,7 @@
 
 
 def second_outer_kernel(
-    v1, inner, outer, fields, free, mod_inner, mod_outer, before, v2, v1_high, moments
+    v1, outer, inner, fields, free, mod_inner, mod_outer, before, v2, v1_high, moments
 ):
     sub = lax.axis_index("sub")
     count = v1.shape[1]
@@ -567,12 +580,11 @@
     layer = (3, count, width)
     block = (half, width)
     free = (1 - fixed).astype(jnp.float32)
-    right = free * load.astype(jnp.float32)
     swap, first, second, third, fourth, own = call(
         prepare_kernel,
         [(11,) + block, (4,) + block, (4,) + block, block, block, (11,) + block],
         name="prepare",
-    )(free, right, design)
+    )(free, load, design)
     first = move(first, "first")
     second = move(second, "second")
     third = move(third, "third")
@@ -582,9 +594,10 @@
     def start_body(*refs):
         start_outer_kernel(mods, slabs, *refs)
 
-    v0, v0_inner, free, fields, layers = call(
+    v0, v0_inner, free, fields, parts = call(
         start_inner_kernel,
-        [layer, layer, layer, (12,) + plane, (2,) + plane],
+        [layer, layer, layer, (12,) + plane, (3,) + plane],
+        [(2,) + plane],
         name="start_inner",
         work=True,
     )(own, swap)
@@ -593,13 +606,13 @@
         [layer, layer, plane, plane, plane, plane, plane, (8, width)],
         [layer, plane, plane],
         name="start_outer",
-    )(v0, v0_inner, free, fields, layers, first, second, third, fourth)
+    )(first, second, third, fourth, v0, v0_inner, free, fields, parts)
     outer = move(v1, "outer")
     inner = move(v1, "swap")
     (fields,) = call(second_inner_kernel, [(12,) + plane], name="second_inner", work=True)(v1, inner)
     v2, v1_high, moments = call(
         second_outer_kernel, [layer, layer, (8, width)], name="second_outer"
-    )(v1, inner, outer, fields, free, mod_inner, mod_outer, moments)
+    )(v1, outer, inner, fields, free, mod_inner, mod_outer, moments)
     v2_high = move(v2, "down")
     (moments,) = call(third_kernel, [(8, width)], name="third")(v2, v2_high, mod_own, moments)
     devices = 2 * mods * slabs

time: 66.6 us -> 65.5 us (0.983)
  local copies, waits for them, and re-layouts: 1.6 us -> 0.75 us
    unnamed x7 -> x5, local copies, waits for them, and re-layouts: 1.59 us -> 0.74 us
  transfers between devices with their start and end apart: 15 -> 15, of which waited for: 9 -> 9; matrix products, arithmetic and copies ran while one was open for 1% -> 1% of each run, Pallas kernels for 1% -> 2%
where the time goes in v5:
time: 65.5 us; the launch traced here: 65.3 us
  waiting for transfers between devices  19.6 us (30%)
  starting transfers between devices  18.9 us (29%)
  blocking collectives  18.3 us (28%)
  Pallas kernels  5.92 us (9%)
  other arithmetic  1.02 us (2%)
  local copies, waits for them, and re-layouts  0.75 us (1%)
  between operations  0.75 us (1%)
    all_to_all x1, blocking collectives, local(): lax.all_to_all(jnp.broadcast_to(moments, (devices, 8, width)), AXES, 0, 0...  18.3 us
    ppermute x12, waiting for transfers between devices, move(): return lax.ppermute(value, AXES, path[name])  16.3 us
    ppermute x12, starting transfers between devices, move(): return lax.ppermute(value, AXES, path[name])  15.5 us
    ppermute x3, starting transfers between devices, local(): lax.ppermute(slope, 'mod', pairs)  3.49 us
    ppermute x3, waiting for transfers between devices, local(): lax.ppermute(slope, 'mod', pairs)  3.29 us
    pallas_call x1, Pallas kernels, local(): call(start_body, [layer, layer, plane, plane, plane, plane, plane, (8, wi...  1.54 us
  transfers between devices with their start and end apart: 15, of which 9 were waited for; matrix products, arithmetic and copies ran while one was open for 1% of the time, Pallas kernels for 2%

profile of v5, /device:TPU:0, one launch (start us, length us, event | category | flops | bytes accessed | tf_op | source)
XLA Modules:
  0.0 65.3 jit_solution(17837463647817422711)
XLA Ops:
  0.6 0.0 copy-start.1
  0.6 0.0 copy-start
  0.6 1.0 %subtract_convert_fusion.free = f32[3,2,64,128]{3,2,1,0:T(8,128)S(1)} fusion(s32[3,2,64,128]{3,2,1,0:T(8,128)} %param.4), kind=kLoop, calls=%fused_computation.1 | loop fusion | flops 98304 | bytes 393216 | tf_op jit(solution)/shard_map/convert_element_type | solution.py:582
  1.6 0.0 copy-done.1
  1.6 0.0 copy-done
  1.7 0.1 prepare.1
  1.8 0.5 collective-permute-start.4
  2.3 2.6 %collective-permute-start = (f32[4,64,128]{2,1,0:T(8,128)S(1)}, f32[4,64,128]{2,1,0:T(8,128)S(1)}, u32[]{:S(2)}, u32[]{:S(2)}) collective-permute-start(f32[4,64,128]{2,1,0:T(8,128)S(1)} %get-tuple-element.30), channel_id=1, source_target_pairs={{0,2},{1,31},{2,4},{3,1},{4,6},{5,3},{6,8},{7,5},{8,10},{9,7},{10,... | collective-permute-start | bytes 393224 | tf_op jit(solution)/shard_map/ppermute | solution.py:577
  4.9 4.1 %collective-permute-start.1 = (f32[4,64,128]{2,1,0:T(8,128)S(1)}, f32[4,64,128]{2,1,0:T(8,128)S(1)}, u32[]{:S(2)}, u32[]{:S(2)}) collective-permute-start(f32[4,64,128]{2,1,0:T(8,128)S(1)} %get-tuple-element.31), channel_id=1, source_target_pairs={{1,2},{0,31},{3,4},{2,1},{5,6},{4,3},{7,8},{6,5},{9,10},{8,7},{11,... | collective-permute-start | bytes 393224 | tf_op jit(solution)/shard_map/ppermute | solution.py:577
  9.0 0.0 collective-permute-start.2
  9.1 1.6 %collective-permute-start.3 = (f32[64,128]{1,0:T(8,128)S(1)}, f32[64,128]{1,0:T(8,128)S(1)}, u32[]{:S(2)}, u32[]{:S(2)}) collective-permute-start(f32[64,128]{1,0:T(8,128)S(1)} %get-tuple-element.33), channel_id=1, source_target_pairs={{0,2},{1,3},{2,4},{3,5},{4,6},{5,7},{6,8},{7,9},{8,10},{9,11},{10,... | collective-permute-start | bytes 98312 | tf_op jit(solution)/shard_map/ppermute | solution.py:577
  10.7 0.0 collective-permute-done.4.swap
  10.7 0.7 %start_inner.1 = (f32[3,128,128]{2,1,0:T(8,128)S(1)}, f32[3,128,128]{2,1,0:T(8,128)S(1)}, f32[3,128,128]{2,1,0:T(8,128)S(1)}, f32[12,128,128]{2,1,0:T(8,128)S(1)}, f32[3,128,128]{2,1,0:T(8,128)S(1)}) custom-call(f32[11,64,128]{2,1,0:T(8,128)S(1)} %get-tuple-element.34.own, f32[11,64,128]{2,1,0:T(8,128)S(1)} %collective-permute-done.4.swap), custom_call_target="tpu_custom_call" | custom-call | flops 10000000 | bytes 4000000 | tf_op jit(solution)/shard_map/start_inner/pallas_call | solution.py:597
  11.4 5.1 %collective-permute-done.2.refs_2_ = f32[64,128]{1,0:T(8,128)S(1)} collective-permute-done((f32[64,128]{1,0:T(8,128)S(1)}, f32[64,128]{1,0:T(8,128)S(1)}, u32[]{:S(2)}, u32[]{:S(2)}) %collective-permute-start.2) | collective-permute-done | bytes 32800 | tf_op jit(solution)/shard_map/ppermute | solution.py:577
  16.5 0.4 collective-permute-done.3.refs_3_
  17.0 0.0 collective-permute-done.refs_0_
  17.0 0.0 collective-permute-done.1.refs_1_
  17.0 1.5 %start_outer.1 = (f32[3,128,128]{2,1,0:T(8,128)S(1)}, f32[3,128,128]{2,1,0:T(8,128)S(1)}, f32[128,128]{1,0:T(8,128)S(1)}, f32[128,128]{1,0:T(8,128)S(1)}, f32[12...) custom-call(f32[4,64,128]{2,1,0:T(8,128)S(1)} %collective-permute-done.refs_0_, ...), custom_call_target="tpu_custom_call" | custom-call | tf_op jit(solution)/shard_map/start_outer/pallas_call | solution.py:604
  18.5 0.2 collective-permute-start.6
  18.7 0.7 %collective-permute-start.5 = (f32[3,128,128]{2,1,0:T(8,128)S(1)}, f32[3,128,128]{2,1,0:T(8,128)S(1)}, u32[]{:S(2)}, u32[]{:S(2)}) collective-permute-start(f32[3,128,128]{2,1,0:T(8,128)S(1)} %get-tuple-element.41.v1), channel_id=1, source_target_pairs={{1,2},{3,4},{2,1},{5,6},{4,3},{7,8},{6,5},{9,10},{8,7},{11,12},{10... | collective-permute-start | bytes 589832 | tf_op jit(solution)/shard_map/ppermute | solution.py:577
  19.4 0.6 collective-permute-done.6.inner
  20.0 0.4 second_inner.1.fields
  20.4 0.0 collective-permute-done.5.outer
  20.4 1.1 %second_outer.1 = (f32[3,128,128]{2,1,0:T(8,128)S(1)}, f32[3,128,128]{2,1,0:T(8,128)S(1)}, f32[8,128]{1,0:T(8,128)S(1)}) custom-call(f32[3,128,128]{2,1,0:T(8,128)S(1)} %get-tuple-element.41.v1, f32[3,128,128]{2,1,0:T(8,128)S(1)} %collective-permute-done.5.outer, f32[3,128,128]{2,1,0:T(8,128)S(1)} %collective-permute-done.6.inner, ...), custom_call_target="tpu_custom_call" | custom-call | tf_op jit(solution)/shard_map/second_outer/pallas_call | solution.py:613
  21.6 1.3 %collective-permute-start.7 = (f32[3,128,128]{2,1,0:T(8,128)S(1)}, f32[3,128,128]{2,1,0:T(8,128)S(1)}, u32[]{:S(2)}, u32[]{:S(2)}) collective-permute-start(f32[3,128,128]{2,1,0:T(8,128)S(1)} %get-tuple-element.45.v2), channel_id=1, source_target_pairs={{1,0},{3,2},{2,1},{5,4},{4,3},{7,6},{6,5},{9,8},{8,7},{11,10},{10,... | collective-permute-start | bytes 589832 | tf_op jit(solution)/shard_map/ppermute | solution.py:577
  22.9 9.3 %collective-permute-done.7.v2_high = f32[3,128,128]{2,1,0:T(8,128)S(1)} collective-permute-done((f32[3,128,128]{2,1,0:T(8,128)S(1)}, f32[3,128,128]{2,1,0:T(8,128)S(1)}, u32[]{:S(2)}, u32[]{:S(2)}) %collective-permute-start.7) | collective-permute-done | bytes 196640 | tf_op jit(solution)/shard_map/ppermute | solution.py:577
  32.1 0.4 third.1
  32.6 18.3 %all_to_all.5.gathered = f32[32,8,128]{2,1,0:T(8,128)S(1)} all-to-all(f32[32,8,128]{2,1,0:T(8,128)S(1)} %broadcast_in_dim.3), channel_id=1, replica_groups=mesh['mod'=4,'slab'=4,'sub'=2] {'mod','slab','sub'}, dimensions={0} | all-to-all | bytes 262144 | tf_op jit(solution)/shard_map/all_to_all | solution.py:619
  50.9 0.7 %combine.1 = (f32[128,128]{1,0:T(8,128)S(1)}, f32[3,64,128]{2,1,0:T(8,128)S(1)}, f32[3,64,128]{2,1,0:T(8,128)S(1)}) custom-call(f32[32,8,128]{2,1,0:T(8,128)S(1)} %all_to_all.5.gathered, f32[3,128,128]{2,1,0:T(8,128)S(1)} %get-tuple-element.36.refs_4_.v0, f32[3,128,128]{2,1,0:T(8,128)S(1)} %get-tuple-element.48.v0_high, ...), custom_call_target="tpu_custom_call" | custom-call | tf_op jit(solution)/shard_map/combine/pallas_call | solution.py:622
  51.6 0.4 collective-permute-start.8
  52.0 0.6 collective-permute-start.10
  52.6 1.4 %collective-permute-start.11 = (f32[128,128]{1,0:T(8,128)S(1)}, f32[128,128]{1,0:T(8,128)S(1)}, u32[]{:S(2)}, u32[]{:S(2)}) collective-permute-start(f32[128,128]{1,0:T(8,128)S(1)} %get-tuple-element.53.refs_0_), channel_id=1, source_target_pairs={{0,24},{8,16},{16,8},{24,0},{1,25},{9,17},{17,9},{25,1},{2,26},{10... | collective-permute-start | bytes 196616 | tf_op jit(solution)/shard_map/ppermute | solution.py:625
  54.1 1.4 %collective-permute-start.9 = (f32[128,128]{1,0:T(8,128)S(1)}, f32[128,128]{1,0:T(8,128)S(1)}, u32[]{:S(2)}, u32[]{:S(2)}) collective-permute-start(f32[128,128]{1,0:T(8,128)S(1)} %get-tuple-element.53.refs_0_), channel_id=1, source_target_pairs={{0,8},{8,0},{16,24},{24,16},{1,9},{9,1},{17,25},{25,17},{2,10},{10... | collective-permute-start | bytes 196616 | tf_op jit(solution)/shard_map/ppermute | solution.py:625
  55.5 0.8 %collective-permute-done.10.refs_2_ = f32[128,128]{1,0:T(8,128)S(1)} collective-permute-done((f32[128,128]{1,0:T(8,128)S(1)}, f32[128,128]{1,0:T(8,128)S(1)}, u32[]{:S(2)}, u32[]{:S(2)}) %collective-permute-start.10) | collective-permute-done | bytes 65568 | tf_op jit(solution)/shard_map/ppermute | solution.py:625
  56.3 2.1 %collective-permute-done.11.refs_3_ = f32[128,128]{1,0:T(8,128)S(1)} collective-permute-done((f32[128,128]{1,0:T(8,128)S(1)}, f32[128,128]{1,0:T(8,128)S(1)}, u32[]{:S(2)}, u32[]{:S(2)}) %collective-permute-start.11) | collective-permute-done | bytes 65568 | tf_op jit(solution)/shard_map/ppermute | solution.py:625
  58.4 0.4 collective-permute-done.9.refs_1_
  58.8 0.1 collective-permute-start.12
  58.9 0.7 %collective-permute-start.14 = (f32[72,128]{1,0:T(8,128)S(1)}, f32[72,128]{1,0:T(8,128)S(1)}, u32[]{:S(2)}, u32[]{:S(2)}) collective-permute-start(f32[72,128]{1,0:T(8,128)S(1)} %get-tuple-element.56), channel_id=1, source_target_pairs={{0,1},{1,0},{2,3},{3,2},{4,5},{5,4},{6,7},{7,6},{8,9},{9,8},{10,11... | collective-permute-start | bytes 110600 | tf_op jit(solution)/shard_map/ppermute | solution.py:577
  59.6 3.2 %collective-permute-start.13 = (f32[72,128]{1,0:T(8,128)S(1)}, f32[72,128]{1,0:T(8,128)S(1)}, u32[]{:S(2)}, u32[]{:S(2)}) collective-permute-start(f32[72,128]{1,0:T(8,128)S(1)} %get-tuple-element.57), channel_id=1, source_target_pairs={{0,6},{1,3},{2,0},{3,5},{4,2},{5,7},{6,4},{7,1},{8,14},{9,11},{10,... | collective-permute-start | bytes 110600 | tf_op jit(solution)/shard_map/ppermute | solution.py:577
  62.8 0.0 collective-permute-done.8
  62.9 0.7 %copy.5 = f32[3,2,64,128]{3,2,1,0:T(8,128)} copy(f32[3,2,64,128]{3,2,0,1:T(8,128)S(1)} %pad_maximum_fusion) | data formatting | bytes 393216
  63.6 0.5 collective-permute-done.12.outer
  64.1 0.4 collective-permute-done.13.far
  64.5 0.0 collective-permute-done.14.partner
  64.5 0.9 %gradient.1 = f32[2,64,128]{2,1,0:T(8,128)} custom-call(f32[128,128]{1,0:T(8,128)S(1)} %get-tuple-element.55.scaled, f32[72,128]{1,0:T(8,128)S(1)} %collective-permute-done.12.outer, f32[72,128]{1,0:T(8,128)S(1)} %collective-permute-done.13.far, f32[72,128]{1,0:T(8,128)S(1)} %collective-permute-done.14.partner), custom_call_target="tpu_custom_call" | custom-call | tf_op jit(solution)/shard_map/gradient/pallas_call | solution.py:638
  (4 shorter events, 0.1 us)
Async XLA Ops:
  0.6 1.0 %copy-start.1 = (f32[2,64,128]{2,1,0:T(8,128)S(1)}, f32[2,64,128]{2,1,0:T(8,128)}, u32[]{:S(2)}) copy-start(f32[2,64,128]{2,1,0:T(8,128)} %design.1) | copy-start | bytes 196612
  0.6 1.1 %copy-start = (s32[3,2,64,128]{3,2,1,0:T(8,128)S(1)}, s32[3,2,64,128]{3,2,1,0:T(8,128)}, u32[]{:S(2)}) copy-start(s32[3,2,64,128]{3,2,1,0:T(8,128)} %load.1) | copy-start | bytes 589828
  1.8 8.9 %collective-permute-start.4 = (f32[11,64,128]{2,1,0:T(8,128)S(1)}, f32[11,64,128]{2,1,0:T(8,128)S(1)}, u32[]{:S(2)}, u32[]{:S(2)}) collective-permute-start(f32[11,64,128]{2,1,0:T(8,128)S(1)} %get-tuple-element.35), channel_id=1, source_target_pairs={{0,1},{1,0},{2,3},{3,2},{4,5},{5,4},{6,7},{7,6},{8,9},{9,8},{10,11... | collective-permute-start | bytes 1081352 | tf_op jit(solution)/shard_map/ppermute | solution.py:577
  2.3 14.7 %collective-permute-start = (f32[4,64,128]{2,1,0:T(8,128)S(1)}, f32[4,64,128]{2,1,0:T(8,128)S(1)}, u32[]{:S(2)}, u32[]{:S(2)}) collective-permute-start(f32[4,64,128]{2,1,0:T(8,128)S(1)} %get-tuple-element.30), channel_id=1, source_target_pairs={{0,2},{1,31},{2,4},{3,1},{4,6},{5,3},{6,8},{7,5},{8,10},{9,7},{10,... | collective-permute-start | bytes 393224 | tf_op jit(solution)/shard_map/ppermute | solution.py:577
  4.9 12.0 %collective-permute-start.1 = (f32[4,64,128]{2,1,0:T(8,128)S(1)}, f32[4,64,128]{2,1,0:T(8,128)S(1)}, u32[]{:S(2)}, u32[]{:S(2)}) collective-permute-start(f32[4,64,128]{2,1,0:T(8,128)S(1)} %get-tuple-element.31), channel_id=1, source_target_pairs={{1,2},{0,31},{3,4},{2,1},{5,6},{4,3},{7,8},{6,5},{9,10},{8,7},{11,... | collective-permute-start | bytes 393224 | tf_op jit(solution)/shard_map/ppermute | solution.py:577
  9.0 7.5 %collective-permute-start.2 = (f32[64,128]{1,0:T(8,128)S(1)}, f32[64,128]{1,0:T(8,128)S(1)}, u32[]{:S(2)}, u32[]{:S(2)}) collective-permute-start(f32[64,128]{1,0:T(8,128)S(1)} %get-tuple-element.32), channel_id=1, source_target_pairs={{0,3},{1,2},{2,5},{3,4},{4,7},{5,6},{6,9},{7,8},{8,11},{9,10},{10,... | collective-permute-start | bytes 98312 | tf_op jit(solution)/shard_map/ppermute | solution.py:577
  9.1 7.9 %collective-permute-start.3 = (f32[64,128]{1,0:T(8,128)S(1)}, f32[64,128]{1,0:T(8,128)S(1)}, u32[]{:S(2)}, u32[]{:S(2)}) collective-permute-start(f32[64,128]{1,0:T(8,128)S(1)} %get-tuple-element.33), channel_id=1, source_target_pairs={{0,2},{1,3},{2,4},{3,5},{4,6},{5,7},{6,8},{7,9},{8,10},{9,11},{10,... | collective-permute-start | bytes 98312 | tf_op jit(solution)/shard_map/ppermute | solution.py:577
  18.5 1.5 %collective-permute-start.6 = (f32[3,128,128]{2,1,0:T(8,128)S(1)}, f32[3,128,128]{2,1,0:T(8,128)S(1)}, u32[]{:S(2)}, u32[]{:S(2)}) collective-permute-start(f32[3,128,128]{2,1,0:T(8,128)S(1)} %get-tuple-element.41.v1), channel_id=1, source_target_pairs={{0,1},{1,0},{2,3},{3,2},{4,5},{5,4},{6,7},{7,6},{8,9},{9,8},{10,11... | collective-permute-start | bytes 589832 | tf_op jit(solution)/shard_map/ppermute | solution.py:577
  18.7 1.7 %collective-permute-start.5 = (f32[3,128,128]{2,1,0:T(8,128)S(1)}, f32[3,128,128]{2,1,0:T(8,128)S(1)}, u32[]{:S(2)}, u32[]{:S(2)}) collective-permute-start(f32[3,128,128]{2,1,0:T(8,128)S(1)} %get-tuple-element.41.v1), channel_id=1, source_target_pairs={{1,2},{3,4},{2,1},{5,6},{4,3},{7,8},{6,5},{9,10},{8,7},{11,12},{10... | collective-permute-start | bytes 589832 | tf_op jit(solution)/shard_map/ppermute | solution.py:577
  21.6 10.6 %collective-permute-start.7 = (f32[3,128,128]{2,1,0:T(8,128)S(1)}, f32[3,128,128]{2,1,0:T(8,128)S(1)}, u32[]{:S(2)}, u32[]{:S(2)}) collective-permute-start(f32[3,128,128]{2,1,0:T(8,128)S(1)} %get-tuple-element.45.v2), channel_id=1, source_target_pairs={{1,0},{3,2},{2,1},{5,4},{4,3},{7,6},{6,5},{9,8},{8,7},{11,10},{10,... | collective-permute-start | bytes 589832 | tf_op jit(solution)/shard_map/ppermute | solution.py:577
  51.6 11.2 %collective-permute-start.8 = (f32[3,64,128]{2,1,0:T(8,128)S(1)}, f32[3,64,128]{2,1,0:T(8,128)S(1)}, u32[]{:S(2)}, u32[]{:S(2)}) collective-permute-start(f32[3,64,128]{2,1,0:T(8,128)S(1)} %get-tuple-element.52), channel_id=1, source_target_pairs={{0,1},{1,0},{2,3},{3,2},{4,5},{5,4},{6,7},{7,6},{8,9},{9,8},{10,11... | collective-permute-start | bytes 294920 | tf_op jit(solution)/shard_map/ppermute | solution.py:577
  52.0 4.3 %collective-permute-start.10 = (f32[128,128]{1,0:T(8,128)S(1)}, f32[128,128]{1,0:T(8,128)S(1)}, u32[]{:S(2)}, u32[]{:S(2)}) collective-permute-start(f32[128,128]{1,0:T(8,128)S(1)} %get-tuple-element.53.refs_0_), channel_id=1, source_target_pairs={{0,16},{8,24},{16,0},{24,8},{1,17},{9,25},{17,1},{25,9},{2,18},{10... | collective-permute-start | bytes 196616 | tf_op jit(solution)/shard_map/ppermute | solution.py:625
  52.6 5.8 %collective-permute-start.11 = (f32[128,128]{1,0:T(8,128)S(1)}, f32[128,128]{1,0:T(8,128)S(1)}, u32[]{:S(2)}, u32[]{:S(2)}) collective-permute-start(f32[128,128]{1,0:T(8,128)S(1)} %get-tuple-element.53.refs_0_), channel_id=1, source_target_pairs={{0,24},{8,16},{16,8},{24,0},{1,25},{9,17},{17,9},{25,1},{2,26},{10... | collective-permute-start | bytes 196616 | tf_op jit(solution)/shard_map/ppermute | solution.py:625
  54.1 4.7 %collective-permute-start.9 = (f32[128,128]{1,0:T(8,128)S(1)}, f32[128,128]{1,0:T(8,128)S(1)}, u32[]{:S(2)}, u32[]{:S(2)}) collective-permute-start(f32[128,128]{1,0:T(8,128)S(1)} %get-tuple-element.53.refs_0_), channel_id=1, source_target_pairs={{0,8},{8,0},{16,24},{24,16},{1,9},{9,1},{17,25},{25,17},{2,10},{10... | collective-permute-start | bytes 196616 | tf_op jit(solution)/shard_map/ppermute | solution.py:625
  58.8 5.2 %collective-permute-start.12 = (f32[72,128]{1,0:T(8,128)S(1)}, f32[72,128]{1,0:T(8,128)S(1)}, u32[]{:S(2)}, u32[]{:S(2)}) collective-permute-start(f32[72,128]{1,0:T(8,128)S(1)} %get-tuple-element.56), channel_id=1, source_target_pairs={{1,2},{0,7},{3,4},{2,1},{5,6},{4,3},{7,0},{6,5},{9,10},{8,15},{11,... | collective-permute-start | bytes 110600 | tf_op jit(solution)/shard_map/ppermute | solution.py:577
  58.9 5.6 %collective-permute-start.14 = (f32[72,128]{1,0:T(8,128)S(1)}, f32[72,128]{1,0:T(8,128)S(1)}, u32[]{:S(2)}, u32[]{:S(2)}) collective-permute-start(f32[72,128]{1,0:T(8,128)S(1)} %get-tuple-element.56), channel_id=1, source_target_pairs={{0,1},{1,0},{2,3},{3,2},{4,5},{5,4},{6,7},{7,6},{8,9},{9,8},{10,11... | collective-permute-start | bytes 110600 | tf_op jit(solution)/shard_map/ppermute | solution.py:577
  59.6 4.9 %collective-permute-start.13 = (f32[72,128]{1,0:T(8,128)S(1)}, f32[72,128]{1,0:T(8,128)S(1)}, u32[]{:S(2)}, u32[]{:S(2)}) collective-permute-start(f32[72,128]{1,0:T(8,128)S(1)} %get-tuple-element.57), channel_id=1, source_target_pairs={{0,6},{1,3},{2,0},{3,5},{4,2},{5,7},{6,4},{7,1},{8,14},{9,11},{10,... | collective-permute-start | bytes 110600 | tf_op jit(solution)/shard_map/ppermute | solution.py:577

commit v6 on v5

--- a/solution.py
+++ b/solution.py
@@ -132,8 +132,7 @@
     return out
 
 
-def element_energy(q):
-    r = mode_forces(q)
+def paired(q, r):
     total = None
     for k in range(3):
         for m in range(1, 8):
@@ -201,11 +200,10 @@
     return norm, cross, square
 
 
-def energy_loop(count, read_own, read_high, use):
-    for y0 in range(0, count, ROWS):
-        _, own = layer_modes(read_own, y0, count)
-        _, high = layer_modes(read_high, y0, count)
-        use(y0, element_energy(element_modes(own, high, 1.0)))
+def element_rows(own, high, y0, count):
+    _, low = layer_modes(rows_of(own), y0, count)
+    _, top = layer_modes(rows_of(high), y0, count)
+    return element_modes(low, top, 1.0)
 
 
 def rows_of(ref):
@@ -384,24 +382,34 @@
     )
 
 
-def third_kernel(v2, v2_high, mod_own, before, moments):
-    count = v2.shape[1]
-    total = [jnp.zeros((ROWS, v2.shape[2]), jnp.float32)]
-
-    def use(y0, energy):
-        total[0] += energy * mod_own[pl.ds(y0, ROWS), :]
-
-    energy_loop(
-        count,
-        lambda k, y: v2[k, pl.ds(y, ROWS), :],
-        lambda k, y: v2_high[k, pl.ds(y, ROWS), :],
-        use,
-    )
-    width = v2.shape[2]
+def early_kernel(v0, v0_high, v1, v1_high, pairs):
+    count = v0.shape[1]
+    for y0 in range(0, count, ROWS):
+        part = pl.ds(y0, ROWS)
+        q0 = element_rows(v0, v0_high, y0, count)
+        q1 = element_rows(v1, v1_high, y0, count)
+        r1 = mode_forces(q1)
+        pairs[0, part, :] = paired(q0, mode_forces(q0))
+        pairs[1, part, :] = paired(q0, r1)
+        pairs[2, part, :] = paired(q1, r1)
+
+
+def third_kernel(v2_high, v2, v0, v0_high, v1, v1_high, mod_own, before, pairs, moments):
+    count, width = v2.shape[1:]
+    total = jnp.zeros((ROWS, width), jnp.float32)
+    for y0 in range(0, count, ROWS):
+        part = pl.ds(y0, ROWS)
+        q2 = element_rows(v2, v2_high, y0, count)
+        r2 = mode_forces(q2)
+        energy = paired(q2, r2)
+        total += energy * mod_own[part, :]
+        pairs[2, part, :] = energy
+        pairs[0, part, :] = paired(element_rows(v0, v0_high, y0, count), r2)
+        pairs[1, part, :] = paired(element_rows(v1, v1_high, y0, count), r2)
     moments[...] = before[...] + jnp.concatenate(
         [
             jnp.zeros((5, width), jnp.float32),
-            line(total[0]),
+            line(total),
             jnp.zeros((2, width), jnp.float32),
         ],
         axis=0,
@@ -437,48 +445,48 @@
     return x0 + step * p0, x1 + step * p1, step * p2
 
 
-def combine_kernel(
-    gathered, v0, v0_high, v1, v1_high, v2, v2_high, slope_factor,
-    slope, keep, send,
-    own, high,
-):
+def combine_kernel(mods, *refs):
+    gathered, v0, v1, v2, slope_factor, chain_factor = refs[:6]
+    early, late = refs[6 : 6 + mods], refs[6 + mods : 6 + 2 * mods]
+    keep, send, scaled, same, cross, own = refs[6 + 2 * mods :]
     sub = lax.axis_index("sub")
     count = v0.shape[1]
     half = count // 2
     sums = jnp.sum(jnp.sum(gathered[...], axis=0), axis=1, keepdims=True)
     c0, c1, c2 = coefficients([sums[k : k + 1] for k in range(6)])
-    for k in range(3):
-        own[k] = c0 * v0[k] + c1 * v1[k] + c2 * v2[k]
-        high[k] = c0 * v0_high[k] + c1 * v1_high[k] + c2 * v2_high[k]
-
+    weights = (
+        (early, (c0 * c0, 2.0 * c0 * c1, c1 * c1)),
+        (late, (2.0 * c0 * c2, 2.0 * c1 * c2, c2 * c2)),
+    )
+    for y0 in range(0, count, ROWS):
+        part = pl.ds(y0, ROWS)
+        energy = None
+        for modules, factors in weights:
+            for n, factor in enumerate(factors):
+                plane = modules[0][n, part, :]
+                for other in modules[1:]:
+                    plane = plane + other[n, part, :]
+                energy = factor * plane if energy is None else energy + factor * plane
+        scaled[part, :] = energy * slope_factor[part, :] * chain_factor[part, :]
+        for k in range(3):
+            own[k, part, :] = c0 * v0[k, part, :] + c1 * v1[k, part, :] + c2 * v2[k, part, :]
+
+    window = same.shape[0]
+    shift = count - window
+    same[...] = scaled[pl.ds(pl.multiple_of(sub * shift, 8), window), :]
+    cross[...] = scaled[pl.ds(pl.multiple_of((1 - sub) * shift, 8), window), :]
     mine = pl.ds(pl.multiple_of(sub * half, half), half)
     other = pl.ds(pl.multiple_of((1 - sub) * half, half), half)
     for k in range(3):
         keep[k] = own[k, mine, :]
         send[k] = own[k, other, :]
 
-    def use(y0, energy):
-        slope[pl.ds(y0, ROWS), :] = slope_factor[pl.ds(y0, ROWS), :] * energy
-
-    energy_loop(
-        count,
-        lambda k, y: own[k, pl.ds(y, ROWS), :],
-        lambda k, y: high[k, pl.ds(y, ROWS), :],
-        use,
-    )
-
-
-def scale_kernel(*refs):
-    slopes, (chain_factor, scaled, same, cross) = refs[:-4], refs[-4:]
+
+def assemble_kernel(keep, received, displacement):
     sub = lax.axis_index("sub")
-    total = slopes[0][...]
-    for other in slopes[1:]:
-        total = total + other[...]
-    scaled[...] = total * chain_factor[...]
-    window = same.shape[0]
-    shift = scaled.shape[0] - window
-    same[...] = scaled[pl.ds(pl.multiple_of(sub * shift, 8), window), :]
-    cross[...] = scaled[pl.ds(pl.multiple_of((1 - sub) * shift, 8), window), :]
+    for k in range(3):
+        displacement[k, sub] = keep[k]
+        displacement[k, 1 - sub] = received[k]
 
 
 def gradient_kernel(scaled, outer, far, partner, gradient, planes, sums):
@@ -614,27 +622,39 @@
         second_outer_kernel, [layer, layer, (8, width)], name="second_outer"
     )(v1, outer, inner, fields, free, mod_inner, mod_outer, moments)
     v2_high = move(v2, "down")
-    (moments,) = call(third_kernel, [(8, width)], name="third")(v2, v2_high, mod_own, moments)
+
+    def modules(pairs):
+        return [pairs] + [lax.ppermute(pairs, "mod", route) for route in module_routes(mods)]
+
+    (early,) = call(early_kernel, [layer], name="early", work=True)(v0, v0_high, v1, v1_high)
+    early = modules(early)
+    late, moments = call(third_kernel, [layer, (8, width)], name="third")(
+        v2_high, v2, v0, v0_high, v1, v1_high, mod_own, moments
+    )
+    late = modules(late)
     devices = 2 * mods * slabs
     gathered = lax.all_to_all(
         jnp.broadcast_to(moments, (devices, 8, width)), AXES, 0, 0, tiled=True
     )
-    slope, keep, send = call(
-        combine_kernel, [plane, (3, half, width), (3, half, width)], [layer, layer], name="combine"
-    )(gathered, v0, v0_high, v1, v1_high, v2, v2_high, slope_factor)
-    slopes = [slope] + [lax.ppermute(slope, "mod", pairs) for pairs in module_routes(mods)]
-    received = move(send, "swap")
+
+    def combine_body(*refs):
+        combine_kernel(mods, *refs)
+
     window = half + 8
-    scaled, same, cross = call(
-        scale_kernel, [plane, (window, width), (window, width)], name="scale"
-    )(*slopes, chain_factor)
+    keep, send, scaled, same, cross = call(
+        combine_body,
+        [(3, half, width), (3, half, width), plane, (window, width), (window, width)],
+        [layer],
+        name="combine",
+    )(gathered, v0, v1, v2, slope_factor, chain_factor, *early, *late)
     outer = move(cross, "halo_cross")
     far = move(same, "halo_same")
     partner = move(cross, "swap")
-    even = lax.axis_index("sub") == 0
-    displacement = jnp.stack(
-        [jnp.where(even, keep, received), jnp.where(even, received, keep)], axis=1
-    )
+    received = move(send, "swap")
+    (displacement,) = call(assemble_kernel, [(3, 2, half, width)], name="assemble", work=True)(
+        keep, received
+    )
+    scaled, displacement = lax.optimization_barrier((scaled, displacement))
     (gradient,) = call(
         gradient_kernel, [(2, half, width)], [(4, window, width), (window, width)], name="gradient"
     )(scaled, outer, far, partner)

time: 65.5 us -> 71.4 us (1.090)
  starting transfers between devices: 18.9 us -> 40.4 us
  blocking collectives: 18.3 us -> 0 us
  Pallas kernels: 5.92 us -> 7.58 us
  waiting for transfers between devices: 19.6 us -> 20.8 us
    all_to_all x1 -> x0, blocking collectives: 18.3 us -> none  [local(): lax.all_to_all(jnp.broadcast_to(moments, (devices, 8, width)), AXES, 0, 0...]
    ppermute x3 -> x6, starting transfers between devices: 3.49 us -> 18.2 us  [modules(): lax.ppermute(pairs, 'mod', route)]
    ppermute x3 -> x6, waiting for transfers between devices: 3.29 us -> 11.1 us  [modules(): lax.ppermute(pairs, 'mod', route)]
    all_to_all x0 -> x1, starting transfers between devices: none -> 7.34 us  [local(): lax.all_to_all(jnp.broadcast_to(moments, (devices, 8, width)), AXES, 0, 0...]
    ppermute x12, waiting for transfers between devices: 16.3 us -> 9.78 us  [move(): return lax.ppermute(value, AXES, path[name])]
    pallas_call x3 -> x4, Pallas kernels: 1.17 us -> 2.82 us  [the longest x1 0.92 us: local(): call(third_kernel, [layer, (8, width)], name='third')]
    unnamed x5 -> x4, local copies, waits for them, and re-layouts: 0.74 us -> 0.02 us
  transfers between devices with their start and end apart: 15 -> 19, of which waited for: 9 -> 10; matrix products, arithmetic and copies ran while one was open for 1% -> 1% of each run, Pallas kernels for 2% -> 5%
where the time goes in v6:
time: 71.4 us; the launch traced here: 71.2 us
  starting transfers between devices  40.4 us (57%)
  waiting for transfers between devices  20.8 us (29%)
  Pallas kernels  7.58 us (11%)
  other arithmetic  0.99 us (1%)
  between operations  0.75 us (1%)
    ppermute x6, starting transfers between devices, modules(): lax.ppermute(pairs, 'mod', route)  18.2 us
    ppermute x12, starting transfers between devices, move(): return lax.ppermute(value, AXES, path[name])  14.9 us
    ppermute x6, waiting for transfers between devices, modules(): lax.ppermute(pairs, 'mod', route)  11.1 us
    ppermute x12, waiting for transfers between devices, move(): return lax.ppermute(value, AXES, path[name])  9.78 us
    all_to_all x1, starting transfers between devices, local(): lax.all_to_all(jnp.broadcast_to(moments, (devices, 8, width)), AXES, 0, 0...  7.34 us
    pallas_call x1, Pallas kernels, local(): call(start_body, [layer, layer, plane, plane, plane, plane, plane, (8, wi...  1.54 us
  transfers between devices with their start and end apart: 19, of which 10 were waited for; matrix products, arithmetic and copies ran while one was open for 1% of the time, Pallas kernels for 5%

profile of v6, /device:TPU:0, one launch (start us, length us, event | category | flops | bytes accessed | tf_op | source)
XLA Modules:
  0.0 71.2 jit_solution(9600422506490718627)
XLA Ops:
  0.6 1.0 %subtract_convert_fusion.free = f32[3,2,64,128]{3,2,1,0:T(8,128)S(1)} fusion(s32[3,2,64,128]{3,2,1,0:T(8,128)} %param.4), kind=kLoop, calls=%fused_computation | loop fusion | flops 98304 | bytes 393216 | tf_op jit(solution)/shard_map/convert_element_type | solution.py:590
  1.6 0.0 copy-done
  1.7 0.0 copy-done.1
  1.7 0.1 prepare.1
  1.7 0.5 collective-permute-start.4
  2.3 2.6 %collective-permute-start = (f32[4,64,128]{2,1,0:T(8,128)S(1)}, f32[4,64,128]{2,1,0:T(8,128)S(1)}, u32[]{:S(2)}, u32[]{:S(2)}) collective-permute-start(f32[4,64,128]{2,1,0:T(8,128)S(1)} %get-tuple-element.33), channel_id=1, source_target_pairs={{0,2},{1,31},{2,4},{3,1},{4,6},{5,3},{6,8},{7,5},{8,10},{9,7},{10,... | collective-permute-start | bytes 393224 | tf_op jit(solution)/shard_map/ppermute | solution.py:585
  4.9 4.1 %collective-permute-start.1 = (f32[4,64,128]{2,1,0:T(8,128)S(1)}, f32[4,64,128]{2,1,0:T(8,128)S(1)}, u32[]{:S(2)}, u32[]{:S(2)}) collective-permute-start(f32[4,64,128]{2,1,0:T(8,128)S(1)} %get-tuple-element.34), channel_id=1, source_target_pairs={{1,2},{0,31},{3,4},{2,1},{5,6},{4,3},{7,8},{6,5},{9,10},{8,7},{11,... | collective-permute-start | bytes 393224 | tf_op jit(solution)/shard_map/ppermute | solution.py:585
  9.0 0.0 collective-permute-start.2
  9.0 1.6 %collective-permute-start.3 = (f32[64,128]{1,0:T(8,128)S(1)}, f32[64,128]{1,0:T(8,128)S(1)}, u32[]{:S(2)}, u32[]{:S(2)}) collective-permute-start(f32[64,128]{1,0:T(8,128)S(1)} %get-tuple-element.36), channel_id=1, source_target_pairs={{0,2},{1,3},{2,4},{3,5},{4,6},{5,7},{6,8},{7,9},{8,10},{9,11},{10,... | collective-permute-start | bytes 98312 | tf_op jit(solution)/shard_map/ppermute | solution.py:585
  10.6 0.0 collective-permute-done.4.swap
  10.6 0.7 %start_inner.1 = (f32[3,128,128]{2,1,0:T(8,128)S(1)}, f32[3,128,128]{2,1,0:T(8,128)S(1)}, f32[3,128,128]{2,1,0:T(8,128)S(1)}, f32[12,128,128]{2,1,0:T(8,128)S(1)}, f32[3,128,128]{2,1,0:T(8,128)S(1)}) custom-call(f32[11,64,128]{2,1,0:T(8,128)S(1)} %get-tuple-element.37.own, f32[11,64,128]{2,1,0:T(8,128)S(1)} %collective-permute-done.4.swap), custom_call_target="tpu_custom_call" | custom-call | flops 10000000 | bytes 4000000 | tf_op jit(solution)/shard_map/start_inner/pallas_call | solution.py:605
  11.4 5.1 %collective-permute-done.2.refs_2_ = f32[64,128]{1,0:T(8,128)S(1)} collective-permute-done((f32[64,128]{1,0:T(8,128)S(1)}, f32[64,128]{1,0:T(8,128)S(1)}, u32[]{:S(2)}, u32[]{:S(2)}) %collective-permute-start.2) | collective-permute-done | bytes 32800 | tf_op jit(solution)/shard_map/ppermute | solution.py:585
  16.5 0.4 collective-permute-done.3.refs_3_
  16.9 0.0 collective-permute-done.refs_0_
  16.9 1.5 %start_outer.1 = (f32[3,128,128]{2,1,0:T(8,128)S(1)}, f32[3,128,128]{2,1,0:T(8,128)S(1)}, f32[128,128]{1,0:T(8,128)S(1)}, f32[128,128]{1,0:T(8,128)S(1)}, f32[12...) custom-call(f32[4,64,128]{2,1,0:T(8,128)S(1)} %collective-permute-done.refs_0_, ...), custom_call_target="tpu_custom_call" | custom-call | tf_op jit(solution)/shard_map/start_outer/pallas_call | solution.py:612
  18.5 0.2 collective-permute-start.6
  18.7 0.7 collective-permute-start.5
  19.4 0.6 collective-permute-done.6.inner
  20.0 0.4 second_inner.1.fields
  20.4 0.0 collective-permute-done.5.outer
  20.4 1.1 %second_outer.1 = (f32[3,128,128]{2,1,0:T(8,128)S(1)}, f32[3,128,128]{2,1,0:T(8,128)S(1)}, f32[8,128]{1,0:T(8,128)S(1)}) custom-call(f32[3,128,128]{2,1,0:T(8,128)S(1)} %get-tuple-element.44.v1.refs_2_, f32[3,128,128]{2,1,0:T(8,128)S(1)} %collective-permute-done.5.outer, f32[3,128,128]{2,1,0:T(8,128)S(1)} %collective-permute-done.6.inner, ...), custom_call_target="tpu_custom_call" | custom-call | tf_op jit(solution)/shard_map/second_outer/pallas_call | solution.py:621
  21.5 1.3 %collective-permute-start.7 = (f32[3,128,128]{2,1,0:T(8,128)S(1)}, f32[3,128,128]{2,1,0:T(8,128)S(1)}, u32[]{:S(2)}, u32[]{:S(2)}) collective-permute-start(f32[3,128,128]{2,1,0:T(8,128)S(1)} %get-tuple-element.48.v2.refs_3_), channel_id=1, source_target_pairs={{1,0},{3,2},{2,1},{5,4},{4,3},{7,6},{6,5},{9,8},{8,7},{11,10},{10,... | collective-permute-start | bytes 589832 | tf_op jit(solution)/shard_map/ppermute | solution.py:585
  22.8 0.9 %early.1.refs_6_ = f32[3,128,128]{2,1,0:T(8,128)S(1)} custom-call(f32[3,128,128]{2,1,0:T(8,128)S(1)} %get-tuple-element.39.refs_4_.v0.refs_1_, f32[3,128,128]{2,1,0:T(8,128)S(1)} %get-tuple-element.49.v0_high, f32[3,128,128]{2,1,0:T(8,128)S(1)} %get-tuple-element.44.v1.refs_2_, f32[3,128,128]{2,1,0:T(8,128)S(1)} %get-tuple-element.50.v1_high), custom_call_target="tpu_custom_call" | custom-call | flops 10000000 | bytes 4000000 | tf_op jit(solution)/shard_map/early/pallas_call | solution.py:629
  23.7 11.4 %collective-permute-start.10 = (f32[3,128,128]{2,1,0:T(8,128)S(1)}, f32[3,128,128]{2,1,0:T(8,128)S(1)}, u32[]{:S(2)}, u32[]{:S(2)}) collective-permute-start(f32[3,128,128]{2,1,0:T(8,128)S(1)} %early.1.refs_6_), channel_id=1, source_target_pairs={{0,24},{8,16},{16,8},{24,0},{1,25},{9,17},{17,9},{25,1},{2,26},{10... | collective-permute-start | bytes 589832 | tf_op jit(solution)/shard_map/ppermute | solution.py:627
  35.1 0.0 collective-permute-done.7.v2_high
  35.1 0.9 %third.1 = (f32[3,128,128]{2,1,0:T(8,128)S(1)}, f32[8,128]{1,0:T(8,128)S(1)}) custom-call(f32[3,128,128]{2,1,0:T(8,128)S(1)} %collective-permute-done.7.v2_high, f32[3,128,128]{2,1,0:T(8,128)S(1)} %get-tuple-element.48.v2.refs_3_, f32[3,128,128]{2,1,0:T(8,128)S(1)} %get-tuple-element.39.refs_4_.v0.refs_1_, f32[3,128,128]{2,1,0:T(8,128)S(1)} %get-tuple-element.49.v0_high, ...), custom_call_target="tpu_custom_call" | custom-call | tf_op jit(solution)/shard_map/third/pallas_call | solution.py:631
  36.0 0.7 broadcast_in_dim.3
  36.7 7.3 %all-to-all-start = ((f32[32,8,128]{2,1,0:T(8,128)}), f32[32,8,128]{2,1,0:T(8,128)S(1)}, u32[]{:S(2)}, u32[]{:S(2)}) async-start(f32[32,8,128]{2,1,0:T(8,128)} %broadcast_in_dim.3), calls=%async_computation | async-start | bytes 262144 | tf_op jit(solution)/shard_map/all_to_all | solution.py:636
  44.1 1.8 %collective-permute-start.9 = (f32[3,128,128]{2,1,0:T(8,128)S(1)}, f32[3,128,128]{2,1,0:T(8,128)S(1)}, u32[]{:S(2)}, u32[]{:S(2)}) collective-permute-start(f32[3,128,128]{2,1,0:T(8,128)S(1)} %early.1.refs_6_), channel_id=1, source_target_pairs={{0,16},{8,24},{16,0},{24,8},{1,17},{9,25},{17,1},{25,9},{2,18},{10... | collective-permute-start | bytes 589832 | tf_op jit(solution)/shard_map/ppermute | solution.py:627
  45.9 1.5 %collective-permute-start.8 = (f32[3,128,128]{2,1,0:T(8,128)S(1)}, f32[3,128,128]{2,1,0:T(8,128)S(1)}, u32[]{:S(2)}, u32[]{:S(2)}) collective-permute-start(f32[3,128,128]{2,1,0:T(8,128)S(1)} %early.1.refs_6_), channel_id=1, source_target_pairs={{0,8},{8,0},{16,24},{24,16},{1,9},{9,1},{17,25},{25,17},{2,10},{10... | collective-permute-start | bytes 589832 | tf_op jit(solution)/shard_map/ppermute | solution.py:627
  47.4 0.3 collective-permute-start.13
  47.6 1.8 %collective-permute-start.12 = (f32[3,128,128]{2,1,0:T(8,128)S(1)}, f32[3,128,128]{2,1,0:T(8,128)S(1)}, u32[]{:S(2)}, u32[]{:S(2)}) collective-permute-start(f32[3,128,128]{2,1,0:T(8,128)S(1)} %get-tuple-element.56.refs_10_), channel_id=1, source_target_pairs={{0,16},{8,24},{16,0},{24,8},{1,17},{9,25},{17,1},{25,9},{2,18},{10... | collective-permute-start | bytes 589832 | tf_op jit(solution)/shard_map/ppermute | solution.py:627
  49.4 1.5 %collective-permute-start.11 = (f32[3,128,128]{2,1,0:T(8,128)S(1)}, f32[3,128,128]{2,1,0:T(8,128)S(1)}, u32[]{:S(2)}, u32[]{:S(2)}) collective-permute-start(f32[3,128,128]{2,1,0:T(8,128)S(1)} %get-tuple-element.56.refs_10_), channel_id=1, source_target_pairs={{0,8},{8,0},{16,24},{24,16},{1,9},{9,1},{17,25},{25,17},{2,10},{10... | collective-permute-start | bytes 589832 | tf_op jit(solution)/shard_map/ppermute | solution.py:627
  50.9 2.4 %collective-permute-done.9.refs_8_ = f32[3,128,128]{2,1,0:T(8,128)S(1)} collective-permute-done((f32[3,128,128]{2,1,0:T(8,128)S(1)}, f32[3,128,128]{2,1,0:T(8,128)S(1)}, u32[]{:S(2)}, u32[]{:S(2)}) %collective-permute-start.9) | collective-permute-done | bytes 196640 | tf_op jit(solution)/shard_map/ppermute | solution.py:627
  53.2 1.0 %collective-permute-done.8.refs_7_ = f32[3,128,128]{2,1,0:T(8,128)S(1)} collective-permute-done((f32[3,128,128]{2,1,0:T(8,128)S(1)}, f32[3,128,128]{2,1,0:T(8,128)S(1)}, u32[]{:S(2)}, u32[]{:S(2)}) %collective-permute-start.8) | collective-permute-done | bytes 196640 | tf_op jit(solution)/shard_map/ppermute | solution.py:627
  54.3 4.2 %collective-permute-done.13.refs_13_ = f32[3,128,128]{2,1,0:T(8,128)S(1)} collective-permute-done((f32[3,128,128]{2,1,0:T(8,128)S(1)}, f32[3,128,128]{2,1,0:T(8,128)S(1)}, u32[]{:S(2)}, u32[]{:S(2)}) %collective-permute-start.13) | collective-permute-done | bytes 196640 | tf_op jit(solution)/shard_map/ppermute | solution.py:627
  58.5 2.6 %collective-permute-done.12.refs_12_ = f32[3,128,128]{2,1,0:T(8,128)S(1)} collective-permute-done((f32[3,128,128]{2,1,0:T(8,128)S(1)}, f32[3,128,128]{2,1,0:T(8,128)S(1)}, u32[]{:S(2)}, u32[]{:S(2)}) %collective-permute-start.12) | collective-permute-done | bytes 196640 | tf_op jit(solution)/shard_map/ppermute | solution.py:627
  61.0 0.9 %collective-permute-done.11.refs_11_ = f32[3,128,128]{2,1,0:T(8,128)S(1)} collective-permute-done((f32[3,128,128]{2,1,0:T(8,128)S(1)}, f32[3,128,128]{2,1,0:T(8,128)S(1)}, u32[]{:S(2)}, u32[]{:S(2)}) %collective-permute-start.11) | collective-permute-done | bytes 196640 | tf_op jit(solution)/shard_map/ppermute | solution.py:627
  61.9 0.3 combine.1
  62.3 0.1 collective-permute-start.14
  62.3 2.8 %collective-permute-start.16 = (f32[72,128]{1,0:T(8,128)S(1)}, f32[72,128]{1,0:T(8,128)S(1)}, u32[]{:S(2)}, u32[]{:S(2)}) collective-permute-start(f32[72,128]{1,0:T(8,128)S(1)} %get-tuple-element.63), channel_id=1, source_target_pairs={{0,6},{1,3},{2,0},{3,5},{4,2},{5,7},{6,4},{7,1},{8,14},{9,11},{10,... | collective-permute-start | bytes 110600 | tf_op jit(solution)/shard_map/ppermute | solution.py:585
  65.2 0.9 %collective-permute-start.15 = (f32[72,128]{1,0:T(8,128)S(1)}, f32[72,128]{1,0:T(8,128)S(1)}, u32[]{:S(2)}, u32[]{:S(2)}) collective-permute-start(f32[72,128]{1,0:T(8,128)S(1)} %get-tuple-element.62), channel_id=1, source_target_pairs={{1,2},{0,7},{3,4},{2,1},{5,6},{4,3},{7,0},{6,5},{9,10},{8,15},{11,... | collective-permute-start | bytes 110600 | tf_op jit(solution)/shard_map/ppermute | solution.py:585
  66.0 0.0 collective-permute-done.14.received
  66.0 0.7 assemble.1
  66.7 0.1 collective-permute-done.16.far
  66.9 0.0 collective-permute-done.17.partner
  66.9 3.5 %collective-permute-done.15.outer = f32[72,128]{1,0:T(8,128)S(1)} collective-permute-done((f32[72,128]{1,0:T(8,128)S(1)}, f32[72,128]{1,0:T(8,128)S(1)}, u32[]{:S(2)}, u32[]{:S(2)}) %collective-permute-start.15) | collective-permute-done | bytes 36896 | tf_op jit(solution)/shard_map/ppermute | solution.py:585
  70.4 0.9 %gradient.1 = f32[2,64,128]{2,1,0:T(8,128)} custom-call(f32[128,128]{1,0:T(8,128)S(1)} %get-tuple-element.61.scaled, f32[72,128]{1,0:T(8,128)S(1)} %collective-permute-done.15.outer, f32[72,128]{1,0:T(8,128)S(1)} %collective-permute-done.16.far, f32[72,128]{1,0:T(8,128)S(1)} %collective-permute-done.17.partner), custom_call_target="tpu_custom_call" | custom-call | tf_op jit(solution)/shard_map/gradient/pallas_call | solution.py:658
  (6 shorter events, 0.0 us)
Async XLA Ops:
  0.6 1.0 %copy-start = (s32[3,2,64,128]{3,2,1,0:T(8,128)S(1)}, s32[3,2,64,128]{3,2,1,0:T(8,128)}, u32[]{:S(2)}) copy-start(s32[3,2,64,128]{3,2,1,0:T(8,128)} %load.1) | copy-start | bytes 589828
  0.6 1.0 %copy-start.1 = (f32[2,64,128]{2,1,0:T(8,128)S(1)}, f32[2,64,128]{2,1,0:T(8,128)}, u32[]{:S(2)}) copy-start(f32[2,64,128]{2,1,0:T(8,128)} %design.1) | copy-start | bytes 196612
  1.7 8.9 %collective-permute-start.4 = (f32[11,64,128]{2,1,0:T(8,128)S(1)}, f32[11,64,128]{2,1,0:T(8,128)S(1)}, u32[]{:S(2)}, u32[]{:S(2)}) collective-permute-start(f32[11,64,128]{2,1,0:T(8,128)S(1)} %get-tuple-element.38), channel_id=1, source_target_pairs={{0,1},{1,0},{2,3},{3,2},{4,5},{5,4},{6,7},{7,6},{8,9},{9,8},{10,11... | collective-permute-start | bytes 1081352 | tf_op jit(solution)/shard_map/ppermute | solution.py:585
  2.3 14.7 %collective-permute-start = (f32[4,64,128]{2,1,0:T(8,128)S(1)}, f32[4,64,128]{2,1,0:T(8,128)S(1)}, u32[]{:S(2)}, u32[]{:S(2)}) collective-permute-start(f32[4,64,128]{2,1,0:T(8,128)S(1)} %get-tuple-element.33), channel_id=1, source_target_pairs={{0,2},{1,31},{2,4},{3,1},{4,6},{5,3},{6,8},{7,5},{8,10},{9,7},{10,... | collective-permute-start | bytes 393224 | tf_op jit(solution)/shard_map/ppermute | solution.py:585
  4.9 12.0 %collective-permute-start.1 = (f32[4,64,128]{2,1,0:T(8,128)S(1)}, f32[4,64,128]{2,1,0:T(8,128)S(1)}, u32[]{:S(2)}, u32[]{:S(2)}) collective-permute-start(f32[4,64,128]{2,1,0:T(8,128)S(1)} %get-tuple-element.34), channel_id=1, source_target_pairs={{1,2},{0,31},{3,4},{2,1},{5,6},{4,3},{7,8},{6,5},{9,10},{8,7},{11,... | collective-permute-start | bytes 393224 | tf_op jit(solution)/shard_map/ppermute | solution.py:585
  9.0 7.5 %collective-permute-start.2 = (f32[64,128]{1,0:T(8,128)S(1)}, f32[64,128]{1,0:T(8,128)S(1)}, u32[]{:S(2)}, u32[]{:S(2)}) collective-permute-start(f32[64,128]{1,0:T(8,128)S(1)} %get-tuple-element.35), channel_id=1, source_target_pairs={{0,3},{1,2},{2,5},{3,4},{4,7},{5,6},{6,9},{7,8},{8,11},{9,10},{10,... | collective-permute-start | bytes 98312 | tf_op jit(solution)/shard_map/ppermute | solution.py:585
  9.0 7.9 %collective-permute-start.3 = (f32[64,128]{1,0:T(8,128)S(1)}, f32[64,128]{1,0:T(8,128)S(1)}, u32[]{:S(2)}, u32[]{:S(2)}) collective-permute-start(f32[64,128]{1,0:T(8,128)S(1)} %get-tuple-element.36), channel_id=1, source_target_pairs={{0,2},{1,3},{2,4},{3,5},{4,6},{5,7},{6,8},{7,9},{8,10},{9,11},{10,... | collective-permute-start | bytes 98312 | tf_op jit(solution)/shard_map/ppermute | solution.py:585
  18.5 1.5 %collective-permute-start.6 = (f32[3,128,128]{2,1,0:T(8,128)S(1)}, f32[3,128,128]{2,1,0:T(8,128)S(1)}, u32[]{:S(2)}, u32[]{:S(2)}) collective-permute-start(f32[3,128,128]{2,1,0:T(8,128)S(1)} %get-tuple-element.44.v1.refs_2_), channel_id=1, source_target_pairs={{0,1},{1,0},{2,3},{3,2},{4,5},{5,4},{6,7},{7,6},{8,9},{9,8},{10,11... | collective-permute-start | bytes 589832 | tf_op jit(solution)/shard_map/ppermute | solution.py:585
  18.7 1.7 %collective-permute-start.5 = (f32[3,128,128]{2,1,0:T(8,128)S(1)}, f32[3,128,128]{2,1,0:T(8,128)S(1)}, u32[]{:S(2)}, u32[]{:S(2)}) collective-permute-start(f32[3,128,128]{2,1,0:T(8,128)S(1)} %get-tuple-element.44.v1.refs_2_), channel_id=1, source_target_pairs={{1,2},{3,4},{2,1},{5,6},{4,3},{7,8},{6,5},{9,10},{8,7},{11,12},{10... | collective-permute-start | bytes 589832 | tf_op jit(solution)/shard_map/ppermute | solution.py:585
  21.5 13.6 %collective-permute-start.7 = (f32[3,128,128]{2,1,0:T(8,128)S(1)}, f32[3,128,128]{2,1,0:T(8,128)S(1)}, u32[]{:S(2)}, u32[]{:S(2)}) collective-permute-start(f32[3,128,128]{2,1,0:T(8,128)S(1)} %get-tuple-element.48.v2.refs_3_), channel_id=1, source_target_pairs={{1,0},{3,2},{2,1},{5,4},{4,3},{7,6},{6,5},{9,8},{8,7},{11,10},{10,... | collective-permute-start | bytes 589832 | tf_op jit(solution)/shard_map/ppermute | solution.py:585
  23.7 25.7 %collective-permute-start.10 = (f32[3,128,128]{2,1,0:T(8,128)S(1)}, f32[3,128,128]{2,1,0:T(8,128)S(1)}, u32[]{:S(2)}, u32[]{:S(2)}) collective-permute-start(f32[3,128,128]{2,1,0:T(8,128)S(1)} %early.1.refs_6_), channel_id=1, source_target_pairs={{0,24},{8,16},{16,8},{24,0},{1,25},{9,17},{17,9},{25,1},{2,26},{10... | collective-permute-start | bytes 589832 | tf_op jit(solution)/shard_map/ppermute | solution.py:627
  36.7 25.2 %all-to-all-start = ((f32[32,8,128]{2,1,0:T(8,128)}), f32[32,8,128]{2,1,0:T(8,128)S(1)}, u32[]{:S(2)}, u32[]{:S(2)}) async-start(f32[32,8,128]{2,1,0:T(8,128)} %broadcast_in_dim.3), calls=%async_computation | async-start | bytes 262144 | tf_op jit(solution)/shard_map/all_to_all | solution.py:636
  44.1 9.1 %collective-permute-start.9 = (f32[3,128,128]{2,1,0:T(8,128)S(1)}, f32[3,128,128]{2,1,0:T(8,128)S(1)}, u32[]{:S(2)}, u32[]{:S(2)}) collective-permute-start(f32[3,128,128]{2,1,0:T(8,128)S(1)} %early.1.refs_6_), channel_id=1, source_target_pairs={{0,16},{8,24},{16,0},{24,8},{1,17},{9,25},{17,1},{25,9},{2,18},{10... | collective-permute-start | bytes 589832 | tf_op jit(solution)/shard_map/ppermute | solution.py:627
  45.9 8.4 %collective-permute-start.8 = (f32[3,128,128]{2,1,0:T(8,128)S(1)}, f32[3,128,128]{2,1,0:T(8,128)S(1)}, u32[]{:S(2)}, u32[]{:S(2)}) collective-permute-start(f32[3,128,128]{2,1,0:T(8,128)S(1)} %early.1.refs_6_), channel_id=1, source_target_pairs={{0,8},{8,0},{16,24},{24,16},{1,9},{9,1},{17,25},{25,17},{2,10},{10... | collective-permute-start | bytes 589832 | tf_op jit(solution)/shard_map/ppermute | solution.py:627
  47.4 11.1 %collective-permute-start.13 = (f32[3,128,128]{2,1,0:T(8,128)S(1)}, f32[3,128,128]{2,1,0:T(8,128)S(1)}, u32[]{:S(2)}, u32[]{:S(2)}) collective-permute-start(f32[3,128,128]{2,1,0:T(8,128)S(1)} %get-tuple-element.56.refs_10_), channel_id=1, source_target_pairs={{0,24},{8,16},{16,8},{24,0},{1,25},{9,17},{17,9},{25,1},{2,26},{10... | collective-permute-start | bytes 589832 | tf_op jit(solution)/shard_map/ppermute | solution.py:627
  47.6 13.4 %collective-permute-start.12 = (f32[3,128,128]{2,1,0:T(8,128)S(1)}, f32[3,128,128]{2,1,0:T(8,128)S(1)}, u32[]{:S(2)}, u32[]{:S(2)}) collective-permute-start(f32[3,128,128]{2,1,0:T(8,128)S(1)} %get-tuple-element.56.refs_10_), channel_id=1, source_target_pairs={{0,16},{8,24},{16,0},{24,8},{1,17},{9,25},{17,1},{25,9},{2,18},{10... | collective-permute-start | bytes 589832 | tf_op jit(solution)/shard_map/ppermute | solution.py:627
  49.4 12.5 %collective-permute-start.11 = (f32[3,128,128]{2,1,0:T(8,128)S(1)}, f32[3,128,128]{2,1,0:T(8,128)S(1)}, u32[]{:S(2)}, u32[]{:S(2)}) collective-permute-start(f32[3,128,128]{2,1,0:T(8,128)S(1)} %get-tuple-element.56.refs_10_), channel_id=1, source_target_pairs={{0,8},{8,0},{16,24},{24,16},{1,9},{9,1},{17,25},{25,17},{2,10},{10... | collective-permute-start | bytes 589832 | tf_op jit(solution)/shard_map/ppermute | solution.py:627
  62.3 3.8 %collective-permute-start.14 = (f32[3,64,128]{2,1,0:T(8,128)S(1)}, f32[3,64,128]{2,1,0:T(8,128)S(1)}, u32[]{:S(2)}, u32[]{:S(2)}) collective-permute-start(f32[3,64,128]{2,1,0:T(8,128)S(1)} %get-tuple-element.59), channel_id=1, source_target_pairs={{0,1},{1,0},{2,3},{3,2},{4,5},{5,4},{6,7},{7,6},{8,9},{9,8},{10,11... | collective-permute-start | bytes 294920 | tf_op jit(solution)/shard_map/ppermute | solution.py:585
  62.3 4.5 %collective-permute-start.16 = (f32[72,128]{1,0:T(8,128)S(1)}, f32[72,128]{1,0:T(8,128)S(1)}, u32[]{:S(2)}, u32[]{:S(2)}) collective-permute-start(f32[72,128]{1,0:T(8,128)S(1)} %get-tuple-element.63), channel_id=1, source_target_pairs={{0,6},{1,3},{2,0},{3,5},{4,2},{5,7},{6,4},{7,1},{8,14},{9,11},{10,... | collective-permute-start | bytes 110600 | tf_op jit(solution)/shard_map/ppermute | solution.py:585
  65.2 1.7 %collective-permute-start.17 = (f32[72,128]{1,0:T(8,128)S(1)}, f32[72,128]{1,0:T(8,128)S(1)}, u32[]{:S(2)}, u32[]{:S(2)}) collective-permute-start(f32[72,128]{1,0:T(8,128)S(1)} %get-tuple-element.62), channel_id=1, source_target_pairs={{0,1},{1,0},{2,3},{3,2},{4,5},{5,4},{6,7},{7,6},{8,9},{9,8},{10,11... | collective-permute-start | bytes 110600 | tf_op jit(solution)/shard_map/ppermute | solution.py:585
  65.2 5.2 %collective-permute-start.15 = (f32[72,128]{1,0:T(8,128)S(1)}, f32[72,128]{1,0:T(8,128)S(1)}, u32[]{:S(2)}, u32[]{:S(2)}) collective-permute-start(f32[72,128]{1,0:T(8,128)S(1)} %get-tuple-element.62), channel_id=1, source_target_pairs={{1,2},{0,7},{3,4},{2,1},{5,6},{4,3},{7,0},{6,5},{9,10},{8,15},{11,... | collective-permute-start | bytes 110600 | tf_op jit(solution)/shard_map/ppermute | solution.py:585

commit v7 on v5

--- a/solution.py
+++ b/solution.py
@@ -615,9 +615,10 @@
     )(v1, outer, inner, fields, free, mod_inner, mod_outer, moments)
     v2_high = move(v2, "down")
     (moments,) = call(third_kernel, [(8, width)], name="third")(v2, v2_high, mod_own, moments)
-    devices = 2 * mods * slabs
+    moments = moments + move(moments, "swap")
+    chips = mods * slabs
     gathered = lax.all_to_all(
-        jnp.broadcast_to(moments, (devices, 8, width)), AXES, 0, 0, tiled=True
+        jnp.broadcast_to(moments, (chips, 8, width)), ("mod", "slab"), 0, 0, tiled=True
     )
     slope, keep, send = call(
         combine_kernel, [plane, (3, half, width), (3, half, width)], [layer, layer], name="combine"

time: 65.5 us -> 66.6 us (1.017)
  starting transfers between devices: 18.9 us -> 22.9 us
  blocking collectives: 18.3 us -> 14.9 us
    ppermute x12 -> x13, starting transfers between devices: 15.5 us -> 19.4 us  [move(): return lax.ppermute(value, AXES, path[name])]
    all_to_all x1, blocking collectives: 18.3 us -> 14.9 us  [local(): lax.all_to_all(jnp.broadcast_to(moments, (chips, 8, width)), ('mod', 'sla...]
    ppermute x12 -> x13, waiting for transfers between devices: 16.3 us -> 17.1 us  [move(): return lax.ppermute(value, AXES, path[name])]
  transfers between devices with their start and end apart: 15 -> 16, of which waited for: 9 -> 10; matrix products, arithmetic and copies ran while one was open for 1% -> 1% of each run, Pallas kernels for 2% -> 2%
where the time goes in v7:
time: 66.6 us; the launch traced here: 66.4 us
  starting transfers between devices  22.9 us (34%)
  waiting for transfers between devices  20.2 us (30%)
  blocking collectives  14.9 us (22%)
  Pallas kernels  5.9 us (9%)
  other arithmetic  1.02 us (2%)
  between operations  0.76 us (1%)
  local copies, waits for them, and re-layouts  0.75 us (1%)
    ppermute x13, starting transfers between devices, move(): return lax.ppermute(value, AXES, path[name])  19.4 us
    ppermute x13, waiting for transfers between devices, move(): return lax.ppermute(value, AXES, path[name])  17.1 us
    all_to_all x1, blocking collectives, local(): lax.all_to_all(jnp.broadcast_to(moments, (chips, 8, width)), ('mod', 'sla...  14.9 us
    ppermute x3, starting transfers between devices, local(): lax.ppermute(slope, 'mod', pairs)  3.55 us
    ppermute x3, waiting for transfers between devices, local(): lax.ppermute(slope, 'mod', pairs)  3.07 us
    pallas_call x1, Pallas kernels, local(): call(start_body, [layer, layer, plane, plane, plane, plane, plane, (8, wi...  1.54 us
  transfers between devices with their start and end apart: 16, of which 10 were waited for; matrix products, arithmetic and copies ran while one was open for 1% of the time, Pallas kernels for 2%

profile of v7, /device:TPU:0, one launch (start us, length us, event | category | flops | bytes accessed | tf_op | source)
XLA Modules:
  0.0 66.4 jit_solution(8916632391101496382)
XLA Ops:
  0.6 0.0 copy-start.1
  0.6 0.0 copy-start
  0.6 1.0 %subtract_convert_fusion.free = f32[3,2,64,128]{3,2,1,0:T(8,128)S(1)} fusion(s32[3,2,64,128]{3,2,1,0:T(8,128)} %param.4), kind=kLoop, calls=%fused_computation.1 | loop fusion | flops 98304 | bytes 393216 | tf_op jit(solution)/shard_map/convert_element_type | solution.py:582
  1.6 0.0 copy-done.1
  1.6 0.0 copy-done
  1.7 0.1 prepare.1
  1.8 0.5 collective-permute-start.4
  2.3 2.6 %collective-permute-start = (f32[4,64,128]{2,1,0:T(8,128)S(1)}, f32[4,64,128]{2,1,0:T(8,128)S(1)}, u32[]{:S(2)}, u32[]{:S(2)}) collective-permute-start(f32[4,64,128]{2,1,0:T(8,128)S(1)} %get-tuple-element.30), channel_id=1, source_target_pairs={{0,2},{1,31},{2,4},{3,1},{4,6},{5,3},{6,8},{7,5},{8,10},{9,7},{10,... | collective-permute-start | bytes 393224 | tf_op jit(solution)/shard_map/ppermute | solution.py:577
  4.9 4.1 %collective-permute-start.1 = (f32[4,64,128]{2,1,0:T(8,128)S(1)}, f32[4,64,128]{2,1,0:T(8,128)S(1)}, u32[]{:S(2)}, u32[]{:S(2)}) collective-permute-start(f32[4,64,128]{2,1,0:T(8,128)S(1)} %get-tuple-element.31), channel_id=1, source_target_pairs={{1,2},{0,31},{3,4},{2,1},{5,6},{4,3},{7,8},{6,5},{9,10},{8,7},{11,... | collective-permute-start | bytes 393224 | tf_op jit(solution)/shard_map/ppermute | solution.py:577
  9.0 0.0 collective-permute-start.2
  9.1 1.6 %collective-permute-start.3 = (f32[64,128]{1,0:T(8,128)S(1)}, f32[64,128]{1,0:T(8,128)S(1)}, u32[]{:S(2)}, u32[]{:S(2)}) collective-permute-start(f32[64,128]{1,0:T(8,128)S(1)} %get-tuple-element.33), channel_id=1, source_target_pairs={{0,2},{1,3},{2,4},{3,5},{4,6},{5,7},{6,8},{7,9},{8,10},{9,11},{10,... | collective-permute-start | bytes 98312 | tf_op jit(solution)/shard_map/ppermute | solution.py:577
  10.7 0.0 collective-permute-done.4.swap
  10.7 0.7 %start_inner.1 = (f32[3,128,128]{2,1,0:T(8,128)S(1)}, f32[3,128,128]{2,1,0:T(8,128)S(1)}, f32[3,128,128]{2,1,0:T(8,128)S(1)}, f32[12,128,128]{2,1,0:T(8,128)S(1)}, f32[3,128,128]{2,1,0:T(8,128)S(1)}) custom-call(f32[11,64,128]{2,1,0:T(8,128)S(1)} %get-tuple-element.34.own, f32[11,64,128]{2,1,0:T(8,128)S(1)} %collective-permute-done.4.swap), custom_call_target="tpu_custom_call" | custom-call | flops 10000000 | bytes 4000000 | tf_op jit(solution)/shard_map/start_inner/pallas_call | solution.py:597
  11.4 5.1 %collective-permute-done.2.refs_2_ = f32[64,128]{1,0:T(8,128)S(1)} collective-permute-done((f32[64,128]{1,0:T(8,128)S(1)}, f32[64,128]{1,0:T(8,128)S(1)}, u32[]{:S(2)}, u32[]{:S(2)}) %collective-permute-start.2) | collective-permute-done | bytes 32800 | tf_op jit(solution)/shard_map/ppermute | solution.py:577
  16.5 0.4 collective-permute-done.3.refs_3_
  17.0 0.0 collective-permute-done.refs_0_
  17.0 0.0 collective-permute-done.1.refs_1_
  17.0 1.5 %start_outer.1 = (f32[3,128,128]{2,1,0:T(8,128)S(1)}, f32[3,128,128]{2,1,0:T(8,128)S(1)}, f32[128,128]{1,0:T(8,128)S(1)}, f32[128,128]{1,0:T(8,128)S(1)}, f32[12...) custom-call(f32[4,64,128]{2,1,0:T(8,128)S(1)} %collective-permute-done.refs_0_, ...), custom_call_target="tpu_custom_call" | custom-call | tf_op jit(solution)/shard_map/start_outer/pallas_call | solution.py:604
  18.5 0.2 collective-permute-start.6
  18.7 0.7 collective-permute-start.5
  19.4 0.6 collective-permute-done.6.inner
  20.0 0.4 second_inner.1.fields
  20.4 0.0 collective-permute-done.5.outer
  20.4 1.1 %second_outer.1 = (f32[3,128,128]{2,1,0:T(8,128)S(1)}, f32[3,128,128]{2,1,0:T(8,128)S(1)}, f32[8,128]{1,0:T(8,128)S(1)}) custom-call(f32[3,128,128]{2,1,0:T(8,128)S(1)} %get-tuple-element.41.v1, f32[3,128,128]{2,1,0:T(8,128)S(1)} %collective-permute-done.5.outer, f32[3,128,128]{2,1,0:T(8,128)S(1)} %collective-permute-done.6.inner, ...), custom_call_target="tpu_custom_call" | custom-call | tf_op jit(solution)/shard_map/second_outer/pallas_call | solution.py:613
  21.6 1.3 %collective-permute-start.7 = (f32[3,128,128]{2,1,0:T(8,128)S(1)}, f32[3,128,128]{2,1,0:T(8,128)S(1)}, u32[]{:S(2)}, u32[]{:S(2)}) collective-permute-start(f32[3,128,128]{2,1,0:T(8,128)S(1)} %get-tuple-element.45.v2), channel_id=1, source_target_pairs={{1,0},{3,2},{2,1},{5,4},{4,3},{7,6},{6,5},{9,8},{8,7},{11,10},{10,... | collective-permute-start | bytes 589832 | tf_op jit(solution)/shard_map/ppermute | solution.py:577
  22.9 9.3 %collective-permute-done.7.v2_high = f32[3,128,128]{2,1,0:T(8,128)S(1)} collective-permute-done((f32[3,128,128]{2,1,0:T(8,128)S(1)}, f32[3,128,128]{2,1,0:T(8,128)S(1)}, u32[]{:S(2)}, u32[]{:S(2)}) %collective-permute-start.7) | collective-permute-done | bytes 196640 | tf_op jit(solution)/shard_map/ppermute | solution.py:577
  32.1 0.4 third.1
  32.6 4.2 %collective-permute-start.8 = (f32[8,128]{1,0:T(8,128)S(1)}, f32[8,128]{1,0:T(8,128)S(1)}, u32[]{:S(2)}, u32[]{:S(2)}) collective-permute-start(f32[8,128]{1,0:T(8,128)S(1)} %third.1), channel_id=1, source_target_pairs={{0,1},{1,0},{2,3},{3,2},{4,5},{5,4},{6,7},{7,6},{8,9},{9,8},{10,11... | collective-permute-start | bytes 12296 | tf_op jit(solution)/shard_map/ppermute | solution.py:577
  36.8 0.8 %collective-permute-done.8 = f32[8,128]{1,0:T(8,128)S(1)} collective-permute-done((f32[8,128]{1,0:T(8,128)S(1)}, f32[8,128]{1,0:T(8,128)S(1)}, u32[]{:S(2)}, u32[]{:S(2)}) %collective-permute-start.8) | collective-permute-done | bytes 4128 | tf_op jit(solution)/shard_map/ppermute | solution.py:577
  37.6 14.9 %all_to_all.5.gathered = f32[16,8,128]{2,1,0:T(8,128)S(1)} all-to-all(f32[16,8,128]{2,1,0:T(8,128)S(1)} %broadcast_in_dim.3), channel_id=1, replica_groups=mesh['mod'=4,'slab'=4,'sub'=2] {'mod','slab'}, dimensions={0} | all-to-all | bytes 131072 | tf_op jit(solution)/shard_map/all_to_all | solution.py:620
  52.5 0.7 %combine.1 = (f32[128,128]{1,0:T(8,128)S(1)}, f32[3,64,128]{2,1,0:T(8,128)S(1)}, f32[3,64,128]{2,1,0:T(8,128)S(1)}) custom-call(f32[16,8,128]{2,1,0:T(8,128)S(1)} %all_to_all.5.gathered, f32[3,128,128]{2,1,0:T(8,128)S(1)} %get-tuple-element.36.refs_4_.v0, f32[3,128,128]{2,1,0:T(8,128)S(1)} %get-tuple-element.48.v0_high, ...), custom_call_target="tpu_custom_call" | custom-call | tf_op jit(solution)/shard_map/combine/pallas_call | solution.py:623
  53.2 0.1 collective-permute-start.9
  53.3 0.8 %collective-permute-start.10 = (f32[128,128]{1,0:T(8,128)S(1)}, f32[128,128]{1,0:T(8,128)S(1)}, u32[]{:S(2)}, u32[]{:S(2)}) collective-permute-start(f32[128,128]{1,0:T(8,128)S(1)} %get-tuple-element.53.refs_0_), channel_id=1, source_target_pairs={{0,8},{8,0},{16,24},{24,16},{1,9},{9,1},{17,25},{25,17},{2,10},{10... | collective-permute-start | bytes 196616 | tf_op jit(solution)/shard_map/ppermute | solution.py:626
  54.1 0.7 collective-permute-start.11
  54.7 2.1 %collective-permute-start.12 = (f32[128,128]{1,0:T(8,128)S(1)}, f32[128,128]{1,0:T(8,128)S(1)}, u32[]{:S(2)}, u32[]{:S(2)}) collective-permute-start(f32[128,128]{1,0:T(8,128)S(1)} %get-tuple-element.53.refs_0_), channel_id=1, source_target_pairs={{0,24},{8,16},{16,8},{24,0},{1,25},{9,17},{17,9},{25,1},{2,26},{10... | collective-permute-start | bytes 196616 | tf_op jit(solution)/shard_map/ppermute | solution.py:626
  56.8 1.0 %collective-permute-done.10.refs_1_ = f32[128,128]{1,0:T(8,128)S(1)} collective-permute-done((f32[128,128]{1,0:T(8,128)S(1)}, f32[128,128]{1,0:T(8,128)S(1)}, u32[]{:S(2)}, u32[]{:S(2)}) %collective-permute-start.10) | collective-permute-done | bytes 65568 | tf_op jit(solution)/shard_map/ppermute | solution.py:626
  57.8 1.3 %collective-permute-done.11.refs_2_ = f32[128,128]{1,0:T(8,128)S(1)} collective-permute-done((f32[128,128]{1,0:T(8,128)S(1)}, f32[128,128]{1,0:T(8,128)S(1)}, u32[]{:S(2)}, u32[]{:S(2)}) %collective-permute-start.11) | collective-permute-done | bytes 65568 | tf_op jit(solution)/shard_map/ppermute | solution.py:626
  59.0 0.8 %collective-permute-done.12.refs_3_ = f32[128,128]{1,0:T(8,128)S(1)} collective-permute-done((f32[128,128]{1,0:T(8,128)S(1)}, f32[128,128]{1,0:T(8,128)S(1)}, u32[]{:S(2)}, u32[]{:S(2)}) %collective-permute-start.12) | collective-permute-done | bytes 65568 | tf_op jit(solution)/shard_map/ppermute | solution.py:626
  59.9 0.1 collective-permute-start.13
  60.0 0.8 %collective-permute-start.15 = (f32[72,128]{1,0:T(8,128)S(1)}, f32[72,128]{1,0:T(8,128)S(1)}, u32[]{:S(2)}, u32[]{:S(2)}) collective-permute-start(f32[72,128]{1,0:T(8,128)S(1)} %get-tuple-element.56), channel_id=1, source_target_pairs={{0,1},{1,0},{2,3},{3,2},{4,5},{5,4},{6,7},{7,6},{8,9},{9,8},{10,11... | collective-permute-start | bytes 110600 | tf_op jit(solution)/shard_map/ppermute | solution.py:577
  60.7 3.2 %collective-permute-start.14 = (f32[72,128]{1,0:T(8,128)S(1)}, f32[72,128]{1,0:T(8,128)S(1)}, u32[]{:S(2)}, u32[]{:S(2)}) collective-permute-start(f32[72,128]{1,0:T(8,128)S(1)} %get-tuple-element.57), channel_id=1, source_target_pairs={{0,6},{1,3},{2,0},{3,5},{4,2},{5,7},{6,4},{7,1},{8,14},{9,11},{10,... | collective-permute-start | bytes 110600 | tf_op jit(solution)/shard_map/ppermute | solution.py:577
  63.9 0.0 collective-permute-done.9
  64.0 0.7 %copy.5 = f32[3,2,64,128]{3,2,1,0:T(8,128)} copy(f32[3,2,64,128]{3,2,0,1:T(8,128)S(1)} %pad_maximum_fusion) | data formatting | bytes 393216
  64.6 0.5 collective-permute-done.13.outer
  65.2 0.4 collective-permute-done.14.far
  65.5 0.0 collective-permute-done.15.partner
  65.6 0.9 %gradient.1 = f32[2,64,128]{2,1,0:T(8,128)} custom-call(f32[128,128]{1,0:T(8,128)S(1)} %get-tuple-element.55.scaled, f32[72,128]{1,0:T(8,128)S(1)} %collective-permute-done.13.outer, f32[72,128]{1,0:T(8,128)S(1)} %collective-permute-done.14.far, f32[72,128]{1,0:T(8,128)S(1)} %collective-permute-done.15.partner), custom_call_target="tpu_custom_call" | custom-call | tf_op jit(solution)/shard_map/gradient/pallas_call | solution.py:639
  (5 shorter events, 0.1 us)
Async XLA Ops:
  0.6 1.0 %copy-start.1 = (f32[2,64,128]{2,1,0:T(8,128)S(1)}, f32[2,64,128]{2,1,0:T(8,128)}, u32[]{:S(2)}) copy-start(f32[2,64,128]{2,1,0:T(8,128)} %design.1) | copy-start | bytes 196612
  0.6 1.1 %copy-start = (s32[3,2,64,128]{3,2,1,0:T(8,128)S(1)}, s32[3,2,64,128]{3,2,1,0:T(8,128)}, u32[]{:S(2)}) copy-start(s32[3,2,64,128]{3,2,1,0:T(8,128)} %load.1) | copy-start | bytes 589828
  1.8 8.9 %collective-permute-start.4 = (f32[11,64,128]{2,1,0:T(8,128)S(1)}, f32[11,64,128]{2,1,0:T(8,128)S(1)}, u32[]{:S(2)}, u32[]{:S(2)}) collective-permute-start(f32[11,64,128]{2,1,0:T(8,128)S(1)} %get-tuple-element.35), channel_id=1, source_target_pairs={{0,1},{1,0},{2,3},{3,2},{4,5},{5,4},{6,7},{7,6},{8,9},{9,8},{10,11... | collective-permute-start | bytes 1081352 | tf_op jit(solution)/shard_map/ppermute | solution.py:577
  2.3 14.7 %collective-permute-start = (f32[4,64,128]{2,1,0:T(8,128)S(1)}, f32[4,64,128]{2,1,0:T(8,128)S(1)}, u32[]{:S(2)}, u32[]{:S(2)}) collective-permute-start(f32[4,64,128]{2,1,0:T(8,128)S(1)} %get-tuple-element.30), channel_id=1, source_target_pairs={{0,2},{1,31},{2,4},{3,1},{4,6},{5,3},{6,8},{7,5},{8,10},{9,7},{10,... | collective-permute-start | bytes 393224 | tf_op jit(solution)/shard_map/ppermute | solution.py:577
  4.9 12.0 %collective-permute-start.1 = (f32[4,64,128]{2,1,0:T(8,128)S(1)}, f32[4,64,128]{2,1,0:T(8,128)S(1)}, u32[]{:S(2)}, u32[]{:S(2)}) collective-permute-start(f32[4,64,128]{2,1,0:T(8,128)S(1)} %get-tuple-element.31), channel_id=1, source_target_pairs={{1,2},{0,31},{3,4},{2,1},{5,6},{4,3},{7,8},{6,5},{9,10},{8,7},{11,... | collective-permute-start | bytes 393224 | tf_op jit(solution)/shard_map/ppermute | solution.py:577
  9.0 7.5 %collective-permute-start.2 = (f32[64,128]{1,0:T(8,128)S(1)}, f32[64,128]{1,0:T(8,128)S(1)}, u32[]{:S(2)}, u32[]{:S(2)}) collective-permute-start(f32[64,128]{1,0:T(8,128)S(1)} %get-tuple-element.32), channel_id=1, source_target_pairs={{0,3},{1,2},{2,5},{3,4},{4,7},{5,6},{6,9},{7,8},{8,11},{9,10},{10,... | collective-permute-start | bytes 98312 | tf_op jit(solution)/shard_map/ppermute | solution.py:577
  9.1 7.9 %collective-permute-start.3 = (f32[64,128]{1,0:T(8,128)S(1)}, f32[64,128]{1,0:T(8,128)S(1)}, u32[]{:S(2)}, u32[]{:S(2)}) collective-permute-start(f32[64,128]{1,0:T(8,128)S(1)} %get-tuple-element.33), channel_id=1, source_target_pairs={{0,2},{1,3},{2,4},{3,5},{4,6},{5,7},{6,8},{7,9},{8,10},{9,11},{10,... | collective-permute-start | bytes 98312 | tf_op jit(solution)/shard_map/ppermute | solution.py:577
  18.5 1.5 %collective-permute-start.6 = (f32[3,128,128]{2,1,0:T(8,128)S(1)}, f32[3,128,128]{2,1,0:T(8,128)S(1)}, u32[]{:S(2)}, u32[]{:S(2)}) collective-permute-start(f32[3,128,128]{2,1,0:T(8,128)S(1)} %get-tuple-element.41.v1), channel_id=1, source_target_pairs={{0,1},{1,0},{2,3},{3,2},{4,5},{5,4},{6,7},{7,6},{8,9},{9,8},{10,11... | collective-permute-start | bytes 589832 | tf_op jit(solution)/shard_map/ppermute | solution.py:577
  18.7 1.7 %collective-permute-start.5 = (f32[3,128,128]{2,1,0:T(8,128)S(1)}, f32[3,128,128]{2,1,0:T(8,128)S(1)}, u32[]{:S(2)}, u32[]{:S(2)}) collective-permute-start(f32[3,128,128]{2,1,0:T(8,128)S(1)} %get-tuple-element.41.v1), channel_id=1, source_target_pairs={{1,2},{3,4},{2,1},{5,6},{4,3},{7,8},{6,5},{9,10},{8,7},{11,12},{10... | collective-permute-start | bytes 589832 | tf_op jit(solution)/shard_map/ppermute | solution.py:577
  21.6 10.6 %collective-permute-start.7 = (f32[3,128,128]{2,1,0:T(8,128)S(1)}, f32[3,128,128]{2,1,0:T(8,128)S(1)}, u32[]{:S(2)}, u32[]{:S(2)}) collective-permute-start(f32[3,128,128]{2,1,0:T(8,128)S(1)} %get-tuple-element.45.v2), channel_id=1, source_target_pairs={{1,0},{3,2},{2,1},{5,4},{4,3},{7,6},{6,5},{9,8},{8,7},{11,10},{10,... | collective-permute-start | bytes 589832 | tf_op jit(solution)/shard_map/ppermute | solution.py:577
  32.6 5.0 %collective-permute-start.8 = (f32[8,128]{1,0:T(8,128)S(1)}, f32[8,128]{1,0:T(8,128)S(1)}, u32[]{:S(2)}, u32[]{:S(2)}) collective-permute-start(f32[8,128]{1,0:T(8,128)S(1)} %third.1), channel_id=1, source_target_pairs={{0,1},{1,0},{2,3},{3,2},{4,5},{5,4},{6,7},{7,6},{8,9},{9,8},{10,11... | collective-permute-start | bytes 12296 | tf_op jit(solution)/shard_map/ppermute | solution.py:577
  53.2 10.7 %collective-permute-start.9 = (f32[3,64,128]{2,1,0:T(8,128)S(1)}, f32[3,64,128]{2,1,0:T(8,128)S(1)}, u32[]{:S(2)}, u32[]{:S(2)}) collective-permute-start(f32[3,64,128]{2,1,0:T(8,128)S(1)} %get-tuple-element.52), channel_id=1, source_target_pairs={{0,1},{1,0},{2,3},{3,2},{4,5},{5,4},{6,7},{7,6},{8,9},{9,8},{10,11... | collective-permute-start | bytes 294920 | tf_op jit(solution)/shard_map/ppermute | solution.py:577
  53.3 4.5 %collective-permute-start.10 = (f32[128,128]{1,0:T(8,128)S(1)}, f32[128,128]{1,0:T(8,128)S(1)}, u32[]{:S(2)}, u32[]{:S(2)}) collective-permute-start(f32[128,128]{1,0:T(8,128)S(1)} %get-tuple-element.53.refs_0_), channel_id=1, source_target_pairs={{0,8},{8,0},{16,24},{24,16},{1,9},{9,1},{17,25},{25,17},{2,10},{10... | collective-permute-start | bytes 196616 | tf_op jit(solution)/shard_map/ppermute | solution.py:626
  54.1 5.0 %collective-permute-start.11 = (f32[128,128]{1,0:T(8,128)S(1)}, f32[128,128]{1,0:T(8,128)S(1)}, u32[]{:S(2)}, u32[]{:S(2)}) collective-permute-start(f32[128,128]{1,0:T(8,128)S(1)} %get-tuple-element.53.refs_0_), channel_id=1, source_target_pairs={{0,16},{8,24},{16,0},{24,8},{1,17},{9,25},{17,1},{25,9},{2,18},{10... | collective-permute-start | bytes 196616 | tf_op jit(solution)/shard_map/ppermute | solution.py:626
  54.7 5.2 %collective-permute-start.12 = (f32[128,128]{1,0:T(8,128)S(1)}, f32[128,128]{1,0:T(8,128)S(1)}, u32[]{:S(2)}, u32[]{:S(2)}) collective-permute-start(f32[128,128]{1,0:T(8,128)S(1)} %get-tuple-element.53.refs_0_), channel_id=1, source_target_pairs={{0,24},{8,16},{16,8},{24,0},{1,25},{9,17},{17,9},{25,1},{2,26},{10... | collective-permute-start | bytes 196616 | tf_op jit(solution)/shard_map/ppermute | solution.py:626
  59.9 5.2 %collective-permute-start.13 = (f32[72,128]{1,0:T(8,128)S(1)}, f32[72,128]{1,0:T(8,128)S(1)}, u32[]{:S(2)}, u32[]{:S(2)}) collective-permute-start(f32[72,128]{1,0:T(8,128)S(1)} %get-tuple-element.56), channel_id=1, source_target_pairs={{1,2},{0,7},{3,4},{2,1},{5,6},{4,3},{7,0},{6,5},{9,10},{8,15},{11,... | collective-permute-start | bytes 110600 | tf_op jit(solution)/shard_map/ppermute | solution.py:577
  60.0 5.6 %collective-permute-start.15 = (f32[72,128]{1,0:T(8,128)S(1)}, f32[72,128]{1,0:T(8,128)S(1)}, u32[]{:S(2)}, u32[]{:S(2)}) collective-permute-start(f32[72,128]{1,0:T(8,128)S(1)} %get-tuple-element.56), channel_id=1, source_target_pairs={{0,1},{1,0},{2,3},{3,2},{4,5},{5,4},{6,7},{7,6},{8,9},{9,8},{10,11... | collective-permute-start | bytes 110600 | tf_op jit(solution)/shard_map/ppermute | solution.py:577
  60.7 4.8 %collective-permute-start.14 = (f32[72,128]{1,0:T(8,128)S(1)}, f32[72,128]{1,0:T(8,128)S(1)}, u32[]{:S(2)}, u32[]{:S(2)}) collective-permute-start(f32[72,128]{1,0:T(8,128)S(1)} %get-tuple-element.57), channel_id=1, source_target_pairs={{0,6},{1,3},{2,0},{3,5},{4,2},{5,7},{6,4},{7,1},{8,14},{9,11},{10,... | collective-permute-start | bytes 110600 | tf_op jit(solution)/shard_map/ppermute | solution.py:577

commit v8 on v5

--- a/solution.py
+++ b/solution.py
@@ -384,7 +384,10 @@
     )
 
 
-def third_kernel(v2, v2_high, mod_own, before, moments):
+def third_kernel(v2_outer, v2_inner, v2, mod_own, before, moments, v2_high):
+    even = lax.axis_index("sub") == 0
+    for k in range(3):
+        v2_high[k] = jnp.where(even, v2_inner[k], v2_outer[k])
     count = v2.shape[1]
     total = [jnp.zeros((ROWS, v2.shape[2]), jnp.float32)]
 
@@ -556,7 +559,8 @@
         third=built([(0, 1, 1), (1, 1, 0)], True),
         fourth=built([(0, 1, 0), (1, 1, 1)], True),
         outer=built([(1, 1, 0), (0, -1, 1)], False),
-        down=built([(1, 0, 0), (0, -1, 1)], False),
+        down=built([(0, -1, 1)], False),
+        across=built([(1, 0, 0)], False),
         halo_cross=in_module([(1, 1, 0), (0, -1, 1)]),
         halo_same=in_module([(0, -1, 0), (1, 1, 1)]),
     )
@@ -613,8 +617,11 @@
     v2, v1_high, moments = call(
         second_outer_kernel, [layer, layer, (8, width)], name="second_outer"
     )(v1, outer, inner, fields, free, mod_inner, mod_outer, moments)
-    v2_high = move(v2, "down")
-    (moments,) = call(third_kernel, [(8, width)], name="third")(v2, v2_high, mod_own, moments)
+    v2_outer = move(v2, "down")
+    v2_inner = move(v2, "across")
+    moments, v2_high = call(third_kernel, [(8, width), layer], name="third")(
+        v2_outer, v2_inner, v2, mod_own, moments
+    )
     devices = 2 * mods * slabs
     gathered = lax.all_to_all(
         jnp.broadcast_to(moments, (devices, 8, width)), AXES, 0, 0, tiled=True

time: 65.5 us -> 65.3 us (level)
  starting transfers between devices: 18.9 us -> 19.6 us
    ppermute x12 -> x13, starting transfers between devices: 15.5 us -> 16.1 us  [move(): return lax.ppermute(value, AXES, path[name])]
    all_to_all x1, blocking collectives: 18.3 us -> 17.7 us  [local(): lax.all_to_all(jnp.broadcast_to(moments, (devices, 8, width)), AXES, 0, 0...]
    ppermute x12 -> x13, waiting for transfers between devices: 16.3 us -> 16.3 us  [move(): return lax.ppermute(value, AXES, path[name])]
  transfers between devices with their start and end apart: 15 -> 16, of which waited for: 9 -> 9; matrix products, arithmetic and copies ran while one was open for 1% -> 1% of each run, Pallas kernels for 2% -> 2%
where the time goes in v8:
time: 65.3 us; the launch traced here: 65.1 us
  starting transfers between devices  19.6 us (30%)
  waiting for transfers between devices  19.3 us (30%)
  blocking collectives  17.7 us (27%)
  Pallas kernels  5.95 us (9%)
  other arithmetic  1.02 us (2%)
  between operations  0.77 us (1%)
  local copies, waits for them, and re-layouts  0.75 us (1%)
    all_to_all x1, blocking collectives, local(): lax.all_to_all(jnp.broadcast_to(moments, (devices, 8, width)), AXES, 0, 0...  17.7 us
    ppermute x13, waiting for transfers between devices, move(): return lax.ppermute(value, AXES, path[name])  16.3 us
    ppermute x13, starting transfers between devices, move(): return lax.ppermute(value, AXES, path[name])  16.1 us
    ppermute x3, starting transfers between devices, local(): lax.ppermute(slope, 'mod', pairs)  3.49 us
    ppermute x3, waiting for transfers between devices, local(): lax.ppermute(slope, 'mod', pairs)  2.97 us
    pallas_call x1, Pallas kernels, local(): call(start_body, [layer, layer, plane, plane, plane, plane, plane, (8, wi...  1.54 us
  transfers between devices with their start and end apart: 16, of which 9 were waited for; matrix products, arithmetic and copies ran while one was open for 1% of the time, Pallas kernels for 2%

profile of v8, /device:TPU:0, one launch (start us, length us, event | category | flops | bytes accessed | tf_op | source)
XLA Modules:
  0.0 65.1 jit_solution(4623627584627306775)
XLA Ops:
  0.6 0.0 copy-start.1
  0.6 0.0 copy-start
  0.6 1.0 %subtract_convert_fusion.free = f32[3,2,64,128]{3,2,1,0:T(8,128)S(1)} fusion(s32[3,2,64,128]{3,2,1,0:T(8,128)} %param.4), kind=kLoop, calls=%fused_computation.1 | loop fusion | flops 98304 | bytes 393216 | tf_op jit(solution)/shard_map/convert_element_type | solution.py:586
  1.6 0.0 copy-done.1
  1.6 0.0 copy-done
  1.7 0.1 prepare.1
  1.8 0.5 collective-permute-start.4
  2.3 2.6 %collective-permute-start = (f32[4,64,128]{2,1,0:T(8,128)S(1)}, f32[4,64,128]{2,1,0:T(8,128)S(1)}, u32[]{:S(2)}, u32[]{:S(2)}) collective-permute-start(f32[4,64,128]{2,1,0:T(8,128)S(1)} %get-tuple-element.32), channel_id=1, source_target_pairs={{0,2},{1,31},{2,4},{3,1},{4,6},{5,3},{6,8},{7,5},{8,10},{9,7},{10,... | collective-permute-start | bytes 393224 | tf_op jit(solution)/shard_map/ppermute | solution.py:581
  4.9 4.1 %collective-permute-start.1 = (f32[4,64,128]{2,1,0:T(8,128)S(1)}, f32[4,64,128]{2,1,0:T(8,128)S(1)}, u32[]{:S(2)}, u32[]{:S(2)}) collective-permute-start(f32[4,64,128]{2,1,0:T(8,128)S(1)} %get-tuple-element.33), channel_id=1, source_target_pairs={{1,2},{0,31},{3,4},{2,1},{5,6},{4,3},{7,8},{6,5},{9,10},{8,7},{11,... | collective-permute-start | bytes 393224 | tf_op jit(solution)/shard_map/ppermute | solution.py:581
  9.0 0.0 collective-permute-start.2
  9.1 1.6 %collective-permute-start.3 = (f32[64,128]{1,0:T(8,128)S(1)}, f32[64,128]{1,0:T(8,128)S(1)}, u32[]{:S(2)}, u32[]{:S(2)}) collective-permute-start(f32[64,128]{1,0:T(8,128)S(1)} %get-tuple-element.35), channel_id=1, source_target_pairs={{0,2},{1,3},{2,4},{3,5},{4,6},{5,7},{6,8},{7,9},{8,10},{9,11},{10,... | collective-permute-start | bytes 98312 | tf_op jit(solution)/shard_map/ppermute | solution.py:581
  10.7 0.0 collective-permute-done.4.swap
  10.7 0.7 %start_inner.1 = (f32[3,128,128]{2,1,0:T(8,128)S(1)}, f32[3,128,128]{2,1,0:T(8,128)S(1)}, f32[3,128,128]{2,1,0:T(8,128)S(1)}, f32[12,128,128]{2,1,0:T(8,128)S(1)}, f32[3,128,128]{2,1,0:T(8,128)S(1)}) custom-call(f32[11,64,128]{2,1,0:T(8,128)S(1)} %get-tuple-element.36.own, f32[11,64,128]{2,1,0:T(8,128)S(1)} %collective-permute-done.4.swap), custom_call_target="tpu_custom_call" | custom-call | flops 10000000 | bytes 4000000 | tf_op jit(solution)/shard_map/start_inner/pallas_call | solution.py:601
  11.4 5.1 %collective-permute-done.2.refs_2_ = f32[64,128]{1,0:T(8,128)S(1)} collective-permute-done((f32[64,128]{1,0:T(8,128)S(1)}, f32[64,128]{1,0:T(8,128)S(1)}, u32[]{:S(2)}, u32[]{:S(2)}) %collective-permute-start.2) | collective-permute-done | bytes 32800 | tf_op jit(solution)/shard_map/ppermute | solution.py:581
  16.5 0.4 collective-permute-done.3.refs_3_
  17.0 0.0 collective-permute-done.refs_0_
  17.0 0.0 collective-permute-done.1.refs_1_
  17.0 1.5 %start_outer.1 = (f32[3,128,128]{2,1,0:T(8,128)S(1)}, f32[3,128,128]{2,1,0:T(8,128)S(1)}, f32[128,128]{1,0:T(8,128)S(1)}, f32[128,128]{1,0:T(8,128)S(1)}, f32[12...) custom-call(f32[4,64,128]{2,1,0:T(8,128)S(1)} %collective-permute-done.refs_0_, ...), custom_call_target="tpu_custom_call" | custom-call | tf_op jit(solution)/shard_map/start_outer/pallas_call | solution.py:608
  18.5 0.2 collective-permute-start.6
  18.7 0.7 %collective-permute-start.5 = (f32[3,128,128]{2,1,0:T(8,128)S(1)}, f32[3,128,128]{2,1,0:T(8,128)S(1)}, u32[]{:S(2)}, u32[]{:S(2)}) collective-permute-start(f32[3,128,128]{2,1,0:T(8,128)S(1)} %get-tuple-element.43.v1), channel_id=1, source_target_pairs={{1,2},{3,4},{2,1},{5,6},{4,3},{7,8},{6,5},{9,10},{8,7},{11,12},{10... | collective-permute-start | bytes 589832 | tf_op jit(solution)/shard_map/ppermute | solution.py:581
  19.4 0.6 collective-permute-done.6.inner
  20.0 0.4 second_inner.1.fields
  20.4 0.0 collective-permute-done.5.outer
  20.4 1.1 %second_outer.1 = (f32[3,128,128]{2,1,0:T(8,128)S(1)}, f32[3,128,128]{2,1,0:T(8,128)S(1)}, f32[8,128]{1,0:T(8,128)S(1)}) custom-call(f32[3,128,128]{2,1,0:T(8,128)S(1)} %get-tuple-element.43.v1, f32[3,128,128]{2,1,0:T(8,128)S(1)} %collective-permute-done.5.outer, f32[3,128,128]{2,1,0:T(8,128)S(1)} %collective-permute-done.6.inner, ...), custom_call_target="tpu_custom_call" | custom-call | tf_op jit(solution)/shard_map/second_outer/pallas_call | solution.py:617
  21.6 0.7 %collective-permute-start.7 = (f32[3,128,128]{2,1,0:T(8,128)S(1)}, f32[3,128,128]{2,1,0:T(8,128)S(1)}, u32[]{:S(2)}, u32[]{:S(2)}) collective-permute-start(f32[3,128,128]{2,1,0:T(8,128)S(1)} %get-tuple-element.47.v2), channel_id=1, source_target_pairs={{2,1},{4,3},{6,5},{8,7},{10,9},{12,11},{14,13},{16,15},{18,17},{20... | collective-permute-start | bytes 589832 | tf_op jit(solution)/shard_map/ppermute | solution.py:581
  22.2 1.3 %collective-permute-start.8 = (f32[3,128,128]{2,1,0:T(8,128)S(1)}, f32[3,128,128]{2,1,0:T(8,128)S(1)}, u32[]{:S(2)}, u32[]{:S(2)}) collective-permute-start(f32[3,128,128]{2,1,0:T(8,128)S(1)} %get-tuple-element.47.v2), channel_id=1, source_target_pairs={{1,0},{3,2},{5,4},{7,6},{9,8},{11,10},{13,12},{15,14},{17,16},{19,... | collective-permute-start | bytes 589832 | tf_op jit(solution)/shard_map/ppermute | solution.py:581
  23.5 0.0 collective-permute-done.7.v2_outer
  23.6 9.2 %collective-permute-done.8.v2_inner = f32[3,128,128]{2,1,0:T(8,128)S(1)} collective-permute-done((f32[3,128,128]{2,1,0:T(8,128)S(1)}, f32[3,128,128]{2,1,0:T(8,128)S(1)}, u32[]{:S(2)}, u32[]{:S(2)}) %collective-permute-start.8) | collective-permute-done | bytes 196640 | tf_op jit(solution)/shard_map/ppermute | solution.py:581
  32.8 0.5 third.1
  33.3 17.7 %all_to_all.5.gathered = f32[32,8,128]{2,1,0:T(8,128)S(1)} all-to-all(f32[32,8,128]{2,1,0:T(8,128)S(1)} %broadcast_in_dim.3), channel_id=1, replica_groups=mesh['mod'=4,'slab'=4,'sub'=2] {'mod','slab','sub'}, dimensions={0} | all-to-all | bytes 262144 | tf_op jit(solution)/shard_map/all_to_all | solution.py:626
  51.0 0.7 %combine.1 = (f32[128,128]{1,0:T(8,128)S(1)}, f32[3,64,128]{2,1,0:T(8,128)S(1)}, f32[3,64,128]{2,1,0:T(8,128)S(1)}) custom-call(f32[32,8,128]{2,1,0:T(8,128)S(1)} %all_to_all.5.gathered, f32[3,128,128]{2,1,0:T(8,128)S(1)} %get-tuple-element.38.refs_4_.v0, f32[3,128,128]{2,1,0:T(8,128)S(1)} %get-tuple-element.51.v0_high, ...), custom_call_target="tpu_custom_call" | custom-call | tf_op jit(solution)/shard_map/combine/pallas_call | solution.py:629
  51.7 0.4 collective-permute-start.9
  52.1 0.6 collective-permute-start.10
  52.6 0.7 %collective-permute-start.11 = (f32[128,128]{1,0:T(8,128)S(1)}, f32[128,128]{1,0:T(8,128)S(1)}, u32[]{:S(2)}, u32[]{:S(2)}) collective-permute-start(f32[128,128]{1,0:T(8,128)S(1)} %get-tuple-element.57.refs_0_), channel_id=1, source_target_pairs={{0,16},{8,24},{16,0},{24,8},{1,17},{9,25},{17,1},{25,9},{2,18},{10... | collective-permute-start | bytes 196616 | tf_op jit(solution)/shard_map/ppermute | solution.py:632
  53.3 2.2 %collective-permute-start.12 = (f32[128,128]{1,0:T(8,128)S(1)}, f32[128,128]{1,0:T(8,128)S(1)}, u32[]{:S(2)}, u32[]{:S(2)}) collective-permute-start(f32[128,128]{1,0:T(8,128)S(1)} %get-tuple-element.57.refs_0_), channel_id=1, source_target_pairs={{0,24},{8,16},{16,8},{24,0},{1,25},{9,17},{17,9},{25,1},{2,26},{10... | collective-permute-start | bytes 196616 | tf_op jit(solution)/shard_map/ppermute | solution.py:632
  55.5 0.8 %collective-permute-done.10.refs_1_ = f32[128,128]{1,0:T(8,128)S(1)} collective-permute-done((f32[128,128]{1,0:T(8,128)S(1)}, f32[128,128]{1,0:T(8,128)S(1)}, u32[]{:S(2)}, u32[]{:S(2)}) %collective-permute-start.10) | collective-permute-done | bytes 65568 | tf_op jit(solution)/shard_map/ppermute | solution.py:632
  56.3 1.3 %collective-permute-done.11.refs_2_ = f32[128,128]{1,0:T(8,128)S(1)} collective-permute-done((f32[128,128]{1,0:T(8,128)S(1)}, f32[128,128]{1,0:T(8,128)S(1)}, u32[]{:S(2)}, u32[]{:S(2)}) %collective-permute-start.11) | collective-permute-done | bytes 65568 | tf_op jit(solution)/shard_map/ppermute | solution.py:632
  57.6 0.9 %collective-permute-done.12.refs_3_ = f32[128,128]{1,0:T(8,128)S(1)} collective-permute-done((f32[128,128]{1,0:T(8,128)S(1)}, f32[128,128]{1,0:T(8,128)S(1)}, u32[]{:S(2)}, u32[]{:S(2)}) %collective-permute-start.12) | collective-permute-done | bytes 65568 | tf_op jit(solution)/shard_map/ppermute | solution.py:632
  58.5 0.1 collective-permute-start.13
  58.6 0.4 collective-permute-start.15
  59.0 3.5 %collective-permute-start.14 = (f32[72,128]{1,0:T(8,128)S(1)}, f32[72,128]{1,0:T(8,128)S(1)}, u32[]{:S(2)}, u32[]{:S(2)}) collective-permute-start(f32[72,128]{1,0:T(8,128)S(1)} %get-tuple-element.61), channel_id=1, source_target_pairs={{0,6},{1,3},{2,0},{3,5},{4,2},{5,7},{6,4},{7,1},{8,14},{9,11},{10,... | collective-permute-start | bytes 110600 | tf_op jit(solution)/shard_map/ppermute | solution.py:581
  62.5 0.0 collective-permute-done.9
  62.6 0.7 %copy.5 = f32[3,2,64,128]{3,2,1,0:T(8,128)} copy(f32[3,2,64,128]{3,2,0,1:T(8,128)S(1)} %pad_maximum_fusion) | data formatting | bytes 393216
  63.3 0.5 collective-permute-done.13.outer
  63.8 0.4 collective-permute-done.14.far
  64.2 0.0 collective-permute-done.15.partner
  64.2 0.9 %gradient.1 = f32[2,64,128]{2,1,0:T(8,128)} custom-call(f32[128,128]{1,0:T(8,128)S(1)} %get-tuple-element.59.scaled, f32[72,128]{1,0:T(8,128)S(1)} %collective-permute-done.13.outer, f32[72,128]{1,0:T(8,128)S(1)} %collective-permute-done.14.far, f32[72,128]{1,0:T(8,128)S(1)} %collective-permute-done.15.partner), custom_call_target="tpu_custom_call" | custom-call | tf_op jit(solution)/shard_map/gradient/pallas_call | solution.py:645
  (4 shorter events, 0.1 us)
Async XLA Ops:
  0.6 1.0 %copy-start.1 = (f32[2,64,128]{2,1,0:T(8,128)S(1)}, f32[2,64,128]{2,1,0:T(8,128)}, u32[]{:S(2)}) copy-start(f32[2,64,128]{2,1,0:T(8,128)} %design.1) | copy-start | bytes 196612
  0.6 1.1 %copy-start = (s32[3,2,64,128]{3,2,1,0:T(8,128)S(1)}, s32[3,2,64,128]{3,2,1,0:T(8,128)}, u32[]{:S(2)}) copy-start(s32[3,2,64,128]{3,2,1,0:T(8,128)} %load.1) | copy-start | bytes 589828
  1.8 8.9 %collective-permute-start.4 = (f32[11,64,128]{2,1,0:T(8,128)S(1)}, f32[11,64,128]{2,1,0:T(8,128)S(1)}, u32[]{:S(2)}, u32[]{:S(2)}) collective-permute-start(f32[11,64,128]{2,1,0:T(8,128)S(1)} %get-tuple-element.37), channel_id=1, source_target_pairs={{0,1},{1,0},{2,3},{3,2},{4,5},{5,4},{6,7},{7,6},{8,9},{9,8},{10,11... | collective-permute-start | bytes 1081352 | tf_op jit(solution)/shard_map/ppermute | solution.py:581
  2.3 14.7 %collective-permute-start = (f32[4,64,128]{2,1,0:T(8,128)S(1)}, f32[4,64,128]{2,1,0:T(8,128)S(1)}, u32[]{:S(2)}, u32[]{:S(2)}) collective-permute-start(f32[4,64,128]{2,1,0:T(8,128)S(1)} %get-tuple-element.32), channel_id=1, source_target_pairs={{0,2},{1,31},{2,4},{3,1},{4,6},{5,3},{6,8},{7,5},{8,10},{9,7},{10,... | collective-permute-start | bytes 393224 | tf_op jit(solution)/shard_map/ppermute | solution.py:581
  4.9 12.0 %collective-permute-start.1 = (f32[4,64,128]{2,1,0:T(8,128)S(1)}, f32[4,64,128]{2,1,0:T(8,128)S(1)}, u32[]{:S(2)}, u32[]{:S(2)}) collective-permute-start(f32[4,64,128]{2,1,0:T(8,128)S(1)} %get-tuple-element.33), channel_id=1, source_target_pairs={{1,2},{0,31},{3,4},{2,1},{5,6},{4,3},{7,8},{6,5},{9,10},{8,7},{11,... | collective-permute-start | bytes 393224 | tf_op jit(solution)/shard_map/ppermute | solution.py:581
  9.0 7.5 %collective-permute-start.2 = (f32[64,128]{1,0:T(8,128)S(1)}, f32[64,128]{1,0:T(8,128)S(1)}, u32[]{:S(2)}, u32[]{:S(2)}) collective-permute-start(f32[64,128]{1,0:T(8,128)S(1)} %get-tuple-element.34), channel_id=1, source_target_pairs={{0,3},{1,2},{2,5},{3,4},{4,7},{5,6},{6,9},{7,8},{8,11},{9,10},{10,... | collective-permute-start | bytes 98312 | tf_op jit(solution)/shard_map/ppermute | solution.py:581
  9.1 7.9 %collective-permute-start.3 = (f32[64,128]{1,0:T(8,128)S(1)}, f32[64,128]{1,0:T(8,128)S(1)}, u32[]{:S(2)}, u32[]{:S(2)}) collective-permute-start(f32[64,128]{1,0:T(8,128)S(1)} %get-tuple-element.35), channel_id=1, source_target_pairs={{0,2},{1,3},{2,4},{3,5},{4,6},{5,7},{6,8},{7,9},{8,10},{9,11},{10,... | collective-permute-start | bytes 98312 | tf_op jit(solution)/shard_map/ppermute | solution.py:581
  18.5 1.5 %collective-permute-start.6 = (f32[3,128,128]{2,1,0:T(8,128)S(1)}, f32[3,128,128]{2,1,0:T(8,128)S(1)}, u32[]{:S(2)}, u32[]{:S(2)}) collective-permute-start(f32[3,128,128]{2,1,0:T(8,128)S(1)} %get-tuple-element.43.v1), channel_id=1, source_target_pairs={{0,1},{1,0},{2,3},{3,2},{4,5},{5,4},{6,7},{7,6},{8,9},{9,8},{10,11... | collective-permute-start | bytes 589832 | tf_op jit(solution)/shard_map/ppermute | solution.py:581
  18.7 1.7 %collective-permute-start.5 = (f32[3,128,128]{2,1,0:T(8,128)S(1)}, f32[3,128,128]{2,1,0:T(8,128)S(1)}, u32[]{:S(2)}, u32[]{:S(2)}) collective-permute-start(f32[3,128,128]{2,1,0:T(8,128)S(1)} %get-tuple-element.43.v1), channel_id=1, source_target_pairs={{1,2},{3,4},{2,1},{5,6},{4,3},{7,8},{6,5},{9,10},{8,7},{11,12},{10... | collective-permute-start | bytes 589832 | tf_op jit(solution)/shard_map/ppermute | solution.py:581
  21.6 2.0 %collective-permute-start.7 = (f32[3,128,128]{2,1,0:T(8,128)S(1)}, f32[3,128,128]{2,1,0:T(8,128)S(1)}, u32[]{:S(2)}, u32[]{:S(2)}) collective-permute-start(f32[3,128,128]{2,1,0:T(8,128)S(1)} %get-tuple-element.47.v2), channel_id=1, source_target_pairs={{2,1},{4,3},{6,5},{8,7},{10,9},{12,11},{14,13},{16,15},{18,17},{20... | collective-permute-start | bytes 589832 | tf_op jit(solution)/shard_map/ppermute | solution.py:581
  22.2 10.6 %collective-permute-start.8 = (f32[3,128,128]{2,1,0:T(8,128)S(1)}, f32[3,128,128]{2,1,0:T(8,128)S(1)}, u32[]{:S(2)}, u32[]{:S(2)}) collective-permute-start(f32[3,128,128]{2,1,0:T(8,128)S(1)} %get-tuple-element.47.v2), channel_id=1, source_target_pairs={{1,0},{3,2},{5,4},{7,6},{9,8},{11,10},{13,12},{15,14},{17,16},{19,... | collective-permute-start | bytes 589832 | tf_op jit(solution)/shard_map/ppermute | solution.py:581
  51.7 10.9 %collective-permute-start.9 = (f32[3,64,128]{2,1,0:T(8,128)S(1)}, f32[3,64,128]{2,1,0:T(8,128)S(1)}, u32[]{:S(2)}, u32[]{:S(2)}) collective-permute-start(f32[3,64,128]{2,1,0:T(8,128)S(1)} %get-tuple-element.56), channel_id=1, source_target_pairs={{0,1},{1,0},{2,3},{3,2},{4,5},{5,4},{6,7},{7,6},{8,9},{9,8},{10,11... | collective-permute-start | bytes 294920 | tf_op jit(solution)/shard_map/ppermute | solution.py:581
  52.1 4.3 %collective-permute-start.10 = (f32[128,128]{1,0:T(8,128)S(1)}, f32[128,128]{1,0:T(8,128)S(1)}, u32[]{:S(2)}, u32[]{:S(2)}) collective-permute-start(f32[128,128]{1,0:T(8,128)S(1)} %get-tuple-element.57.refs_0_), channel_id=1, source_target_pairs={{0,8},{8,0},{16,24},{24,16},{1,9},{9,1},{17,25},{25,17},{2,10},{10... | collective-permute-start | bytes 196616 | tf_op jit(solution)/shard_map/ppermute | solution.py:632
  52.6 5.0 %collective-permute-start.11 = (f32[128,128]{1,0:T(8,128)S(1)}, f32[128,128]{1,0:T(8,128)S(1)}, u32[]{:S(2)}, u32[]{:S(2)}) collective-permute-start(f32[128,128]{1,0:T(8,128)S(1)} %get-tuple-element.57.refs_0_), channel_id=1, source_target_pairs={{0,16},{8,24},{16,0},{24,8},{1,17},{9,25},{17,1},{25,9},{2,18},{10... | collective-permute-start | bytes 196616 | tf_op jit(solution)/shard_map/ppermute | solution.py:632
  53.3 5.2 %collective-permute-start.12 = (f32[128,128]{1,0:T(8,128)S(1)}, f32[128,128]{1,0:T(8,128)S(1)}, u32[]{:S(2)}, u32[]{:S(2)}) collective-permute-start(f32[128,128]{1,0:T(8,128)S(1)} %get-tuple-element.57.refs_0_), channel_id=1, source_target_pairs={{0,24},{8,16},{16,8},{24,0},{1,25},{9,17},{17,9},{25,1},{2,26},{10... | collective-permute-start | bytes 196616 | tf_op jit(solution)/shard_map/ppermute | solution.py:632
  58.5 5.2 %collective-permute-start.13 = (f32[72,128]{1,0:T(8,128)S(1)}, f32[72,128]{1,0:T(8,128)S(1)}, u32[]{:S(2)}, u32[]{:S(2)}) collective-permute-start(f32[72,128]{1,0:T(8,128)S(1)} %get-tuple-element.60), channel_id=1, source_target_pairs={{1,2},{0,7},{3,4},{2,1},{5,6},{4,3},{7,0},{6,5},{9,10},{8,15},{11,... | collective-permute-start | bytes 110600 | tf_op jit(solution)/shard_map/ppermute | solution.py:581
  58.6 5.6 %collective-permute-start.15 = (f32[72,128]{1,0:T(8,128)S(1)}, f32[72,128]{1,0:T(8,128)S(1)}, u32[]{:S(2)}, u32[]{:S(2)}) collective-permute-start(f32[72,128]{1,0:T(8,128)S(1)} %get-tuple-element.60), channel_id=1, source_target_pairs={{0,1},{1,0},{2,3},{3,2},{4,5},{5,4},{6,7},{7,6},{8,9},{9,8},{10,11... | collective-permute-start | bytes 110600 | tf_op jit(solution)/shard_map/ppermute | solution.py:581
  59.0 5.1 %collective-permute-start.14 = (f32[72,128]{1,0:T(8,128)S(1)}, f32[72,128]{1,0:T(8,128)S(1)}, u32[]{:S(2)}, u32[]{:S(2)}) collective-permute-start(f32[72,128]{1,0:T(8,128)S(1)} %get-tuple-element.61), channel_id=1, source_target_pairs={{0,6},{1,3},{2,0},{3,5},{4,2},{5,7},{6,4},{7,1},{8,14},{9,11},{10,... | collective-permute-start | bytes 110600 | tf_op jit(solution)/shard_map/ppermute | solution.py:581

commit v9 on v8

--- a/solution.py
+++ b/solution.py
@@ -441,38 +441,37 @@
 
 
 def combine_kernel(
-    gathered, v0, v0_high, v1, v1_high, v2, v2_high, slope_factor,
-    slope, keep, send,
-    own, high,
+    gathered, v0, v0_high, v1, v1_high, v2, v2_high, slope_factor, slope, factors, own, high
 ):
-    sub = lax.axis_index("sub")
     count = v0.shape[1]
-    half = count // 2
     sums = jnp.sum(jnp.sum(gathered[...], axis=0), axis=1, keepdims=True)
     c0, c1, c2 = coefficients([sums[k : k + 1] for k in range(6)])
+    for n, c in enumerate((c0, c1, c2)):
+        factors[n] = jnp.broadcast_to(c, factors.shape[1:])
     for k in range(3):
         own[k] = c0 * v0[k] + c1 * v1[k] + c2 * v2[k]
         high[k] = c0 * v0_high[k] + c1 * v1_high[k] + c2 * v2_high[k]
 
-    mine = pl.ds(pl.multiple_of(sub * half, half), half)
-    other = pl.ds(pl.multiple_of((1 - sub) * half, half), half)
-    for k in range(3):
-        keep[k] = own[k, mine, :]
-        send[k] = own[k, other, :]
-
     def use(y0, energy):
         slope[pl.ds(y0, ROWS), :] = slope_factor[pl.ds(y0, ROWS), :] * energy
 
-    energy_loop(
-        count,
-        lambda k, y: own[k, pl.ds(y, ROWS), :],
-        lambda k, y: high[k, pl.ds(y, ROWS), :],
-        use,
-    )
+    energy_loop(count, rows_of(own), rows_of(high), use)
+
+
+def displace_kernel(factors, v0, v0_inner, v1, v1_inner, v2, v2_inner, displacement):
+    sub = lax.axis_index("sub")
+    half = displacement.shape[2]
+    mine = pl.ds(pl.multiple_of(sub * half, half), half)
+    c0, c1, c2 = (factors[n][:1, :1] for n in range(3))
+    for k in range(3):
+        displacement[k, sub] = c0 * v0[k, mine, :] + c1 * v1[k, mine, :] + c2 * v2[k, mine, :]
+        displacement[k, 1 - sub] = (
+            c0 * v0_inner[k, mine, :] + c1 * v1_inner[k, mine, :] + c2 * v2_inner[k, mine, :]
+        )
 
 
 def scale_kernel(*refs):
-    slopes, (chain_factor, scaled, same, cross) = refs[:-4], refs[-4:]
+    slopes, (chain_factor, scaled, same, cross, across) = refs[:-5], refs[-5:]
     sub = lax.axis_index("sub")
     total = slopes[0][...]
     for other in slopes[1:]:
@@ -482,6 +481,7 @@
     shift = scaled.shape[0] - window
     same[...] = scaled[pl.ds(pl.multiple_of(sub * shift, 8), window), :]
     cross[...] = scaled[pl.ds(pl.multiple_of((1 - sub) * shift, 8), window), :]
+    across[...] = cross[...]
 
 
 def gradient_kernel(scaled, outer, far, partner, gradient, planes, sums):
@@ -560,7 +560,6 @@
         fourth=built([(0, 1, 0), (1, 1, 1)], True),
         outer=built([(1, 1, 0), (0, -1, 1)], False),
         down=built([(0, -1, 1)], False),
-        across=built([(1, 0, 0)], False),
         halo_cross=in_module([(1, 1, 0), (0, -1, 1)]),
         halo_same=in_module([(0, -1, 0), (1, 1, 1)]),
     )
@@ -618,7 +617,7 @@
         second_outer_kernel, [layer, layer, (8, width)], name="second_outer"
     )(v1, outer, inner, fields, free, mod_inner, mod_outer, moments)
     v2_outer = move(v2, "down")
-    v2_inner = move(v2, "across")
+    v2_inner = move(v2, "swap")
     moments, v2_high = call(third_kernel, [(8, width), layer], name="third")(
         v2_outer, v2_inner, v2, mod_own, moments
     )
@@ -626,22 +625,21 @@
     gathered = lax.all_to_all(
         jnp.broadcast_to(moments, (devices, 8, width)), AXES, 0, 0, tiled=True
     )
-    slope, keep, send = call(
-        combine_kernel, [plane, (3, half, width), (3, half, width)], [layer, layer], name="combine"
+    slope, factors = call(
+        combine_kernel, [plane, (3, 8, width)], [layer, layer], name="combine"
     )(gathered, v0, v0_high, v1, v1_high, v2, v2_high, slope_factor)
     slopes = [slope] + [lax.ppermute(slope, "mod", pairs) for pairs in module_routes(mods)]
-    received = move(send, "swap")
+    (displacement,) = call(displace_kernel, [(3, 2, half, width)], name="displace", work=True)(
+        factors, v0, v0_inner, v1, inner, v2, v2_inner
+    )
     window = half + 8
-    scaled, same, cross = call(
-        scale_kernel, [plane, (window, width), (window, width)], name="scale"
+    scaled, same, cross, across = call(
+        scale_kernel, [plane, (window, width), (window, width), (window, width)], name="scale"
     )(*slopes, chain_factor)
+    scaled, displacement = lax.optimization_barrier((scaled, displacement))
     outer = move(cross, "halo_cross")
     far = move(same, "halo_same")
-    partner = move(cross, "swap")
-    even = lax.axis_index("sub") == 0
-    displacement = jnp.stack(
-        [jnp.where(even, keep, received), jnp.where(even, received, keep)], axis=1
-    )
+    partner = move(across, "swap")
     (gradient,) = call(
         gradient_kernel, [(2, half, width)], [(4, window, width), (window, width)], name="gradient"
     )(scaled, outer, far, partner)

time: 65.3 us -> 64.7 us (level)
  waiting for transfers between devices: 19.3 us -> 13.1 us
  starting transfers between devices: 19.6 us -> 22.8 us
  blocking collectives: 17.7 us -> 20.1 us
  Pallas kernels: 5.95 us -> 6.71 us
  local copies, waits for them, and re-layouts: 0.75 us -> 0.03 us
    ppermute x13 -> x12, waiting for transfers between devices: 16.3 us -> 10 us  [move(): return lax.ppermute(value, AXES, path[name])]
    ppermute x13 -> x12, starting transfers between devices: 16.1 us -> 19.3 us  [move(): return lax.ppermute(value, AXES, path[name])]
    all_to_all x1, blocking collectives: 17.7 us -> 20.1 us  [local(): lax.all_to_all(jnp.broadcast_to(moments, (devices, 8, width)), AXES, 0, 0...]
    pallas_call x2 -> x3, Pallas kernels: 0.72 us -> 1.47 us  [the longest x1 0.75 us: local(): call(displace_kernel, [(3, 2, half, width)], name='displace', work=True)]
    unnamed x5 -> x4, local copies, waits for them, and re-layouts: 0.74 us -> 0.02 us
  transfers between devices with their start and end apart: 16 -> 15, of which waited for: 9 -> 8; matrix products, arithmetic and copies ran while one was open for 1% -> 0% of each run, Pallas kernels for 2% -> 3%
where the time goes in v9:
time: 64.7 us; the launch traced here: 64.5 us
  starting transfers between devices  22.8 us (35%)
  blocking collectives  20.1 us (31%)
  waiting for transfers between devices  13.1 us (20%)
  Pallas kernels  6.71 us (10%)
  other arithmetic  0.99 us (2%)
  between operations  0.74 us (1%)
    all_to_all x1, blocking collectives, local(): lax.all_to_all(jnp.broadcast_to(moments, (devices, 8, width)), AXES, 0, 0...  20.1 us
    ppermute x12, starting transfers between devices, move(): return lax.ppermute(value, AXES, path[name])  19.3 us
    ppermute x12, waiting for transfers between devices, move(): return lax.ppermute(value, AXES, path[name])  10 us
    ppermute x3, starting transfers between devices, local(): lax.ppermute(slope, 'mod', pairs)  3.55 us
    ppermute x3, waiting for transfers between devices, local(): lax.ppermute(slope, 'mod', pairs)  3.06 us
    pallas_call x1, Pallas kernels, local(): call(start_body, [layer, layer, plane, plane, plane, plane, plane, (8, wi...  1.54 us
  transfers between devices with their start and end apart: 15, of which 8 were waited for; matrix products, arithmetic and copies ran while one was open for 0% of the time, Pallas kernels for 3%

profile of v9, /device:TPU:0, one launch (start us, length us, event | category | flops | bytes accessed | tf_op | source)
XLA Modules:
  0.0 64.5 jit_solution(8436527594804562048)
XLA Ops:
  0.6 0.0 copy-start
  0.6 0.0 copy-start.1
  0.6 1.0 %subtract_convert_fusion.free = f32[3,2,64,128]{3,2,1,0:T(8,128)S(1)} fusion(s32[3,2,64,128]{3,2,1,0:T(8,128)} %param.4), kind=kLoop, calls=%fused_computation | loop fusion | flops 98304 | bytes 393216 | tf_op jit(solution)/shard_map/convert_element_type | solution.py:585
  1.6 0.0 copy-done
  1.7 0.0 copy-done.1
  1.7 0.1 prepare.1
  1.7 0.5 collective-permute-start.4
  2.3 2.6 %collective-permute-start = (f32[4,64,128]{2,1,0:T(8,128)S(1)}, f32[4,64,128]{2,1,0:T(8,128)S(1)}, u32[]{:S(2)}, u32[]{:S(2)}) collective-permute-start(f32[4,64,128]{2,1,0:T(8,128)S(1)} %get-tuple-element.34), channel_id=1, source_target_pairs={{0,2},{1,31},{2,4},{3,1},{4,6},{5,3},{6,8},{7,5},{8,10},{9,7},{10,... | collective-permute-start | bytes 393224 | tf_op jit(solution)/shard_map/ppermute | solution.py:580
  4.9 4.1 %collective-permute-start.1 = (f32[4,64,128]{2,1,0:T(8,128)S(1)}, f32[4,64,128]{2,1,0:T(8,128)S(1)}, u32[]{:S(2)}, u32[]{:S(2)}) collective-permute-start(f32[4,64,128]{2,1,0:T(8,128)S(1)} %get-tuple-element.35), channel_id=1, source_target_pairs={{1,2},{0,31},{3,4},{2,1},{5,6},{4,3},{7,8},{6,5},{9,10},{8,7},{11,... | collective-permute-start | bytes 393224 | tf_op jit(solution)/shard_map/ppermute | solution.py:580
  9.0 0.0 collective-permute-start.2
  9.0 1.6 %collective-permute-start.3 = (f32[64,128]{1,0:T(8,128)S(1)}, f32[64,128]{1,0:T(8,128)S(1)}, u32[]{:S(2)}, u32[]{:S(2)}) collective-permute-start(f32[64,128]{1,0:T(8,128)S(1)} %get-tuple-element.37), channel_id=1, source_target_pairs={{0,2},{1,3},{2,4},{3,5},{4,6},{5,7},{6,8},{7,9},{8,10},{9,11},{10,... | collective-permute-start | bytes 98312 | tf_op jit(solution)/shard_map/ppermute | solution.py:580
  10.6 0.0 collective-permute-done.4.swap
  10.6 0.7 %start_inner.1 = (f32[3,128,128]{2,1,0:T(8,128)S(1)}, f32[3,128,128]{2,1,0:T(8,128)S(1)}, f32[3,128,128]{2,1,0:T(8,128)S(1)}, f32[12,128,128]{2,1,0:T(8,128)S(1)}, f32[3,128,128]{2,1,0:T(8,128)S(1)}) custom-call(f32[11,64,128]{2,1,0:T(8,128)S(1)} %get-tuple-element.38.own, f32[11,64,128]{2,1,0:T(8,128)S(1)} %collective-permute-done.4.swap), custom_call_target="tpu_custom_call" | custom-call | flops 10000000 | bytes 4000000 | tf_op jit(solution)/shard_map/start_inner/pallas_call | solution.py:600
  11.4 5.1 %collective-permute-done.2.refs_2_ = f32[64,128]{1,0:T(8,128)S(1)} collective-permute-done((f32[64,128]{1,0:T(8,128)S(1)}, f32[64,128]{1,0:T(8,128)S(1)}, u32[]{:S(2)}, u32[]{:S(2)}) %collective-permute-start.2) | collective-permute-done | bytes 32800 | tf_op jit(solution)/shard_map/ppermute | solution.py:580
  16.5 0.4 collective-permute-done.3.refs_3_
  16.9 0.0 collective-permute-done.refs_0_
  16.9 0.0 collective-permute-done.1.refs_1_
  16.9 1.5 %start_outer.1 = (f32[3,128,128]{2,1,0:T(8,128)S(1)}, f32[3,128,128]{2,1,0:T(8,128)S(1)}, f32[128,128]{1,0:T(8,128)S(1)}, f32[128,128]{1,0:T(8,128)S(1)}, f32[12...) custom-call(f32[4,64,128]{2,1,0:T(8,128)S(1)} %collective-permute-done.refs_0_, ...), custom_call_target="tpu_custom_call" | custom-call | tf_op jit(solution)/shard_map/start_outer/pallas_call | solution.py:607
  18.5 0.2 collective-permute-start.6
  18.7 0.7 %collective-permute-start.5 = (f32[3,128,128]{2,1,0:T(8,128)S(1)}, f32[3,128,128]{2,1,0:T(8,128)S(1)}, u32[]{:S(2)}, u32[]{:S(2)}) collective-permute-start(f32[3,128,128]{2,1,0:T(8,128)S(1)} %get-tuple-element.45.v1), channel_id=1, source_target_pairs={{1,2},{3,4},{2,1},{5,6},{4,3},{7,8},{6,5},{9,10},{8,7},{11,12},{10... | collective-permute-start | bytes 589832 | tf_op jit(solution)/shard_map/ppermute | solution.py:580
  19.4 0.6 collective-permute-done.6.inner.v1_inner
  20.0 0.4 second_inner.1.fields
  20.4 0.0 collective-permute-done.5.outer
  20.4 1.1 %second_outer.1 = (f32[3,128,128]{2,1,0:T(8,128)S(1)}, f32[3,128,128]{2,1,0:T(8,128)S(1)}, f32[8,128]{1,0:T(8,128)S(1)}) custom-call(f32[3,128,128]{2,1,0:T(8,128)S(1)} %get-tuple-element.45.v1, f32[3,128,128]{2,1,0:T(8,128)S(1)} %collective-permute-done.5.outer, f32[3,128,128]{2,1,0:T(8,128)S(1)} %collective-permute-done.6.inner.v1_inner, ...), custom_call_target="tpu_custom_call" | custom-call | tf_op jit(solution)/shard_map/second_outer/pallas_call | solution.py:616
  21.5 7.8 %collective-permute-start.8 = (f32[3,128,128]{2,1,0:T(8,128)S(1)}, f32[3,128,128]{2,1,0:T(8,128)S(1)}, u32[]{:S(2)}, u32[]{:S(2)}) collective-permute-start(f32[3,128,128]{2,1,0:T(8,128)S(1)} %get-tuple-element.49.v2), channel_id=1, source_target_pairs={{0,1},{1,0},{2,3},{3,2},{4,5},{5,4},{6,7},{7,6},{8,9},{9,8},{10,11... | collective-permute-start | bytes 589832 | tf_op jit(solution)/shard_map/ppermute | solution.py:580
  29.3 0.7 %collective-permute-start.7 = (f32[3,128,128]{2,1,0:T(8,128)S(1)}, f32[3,128,128]{2,1,0:T(8,128)S(1)}, u32[]{:S(2)}, u32[]{:S(2)}) collective-permute-start(f32[3,128,128]{2,1,0:T(8,128)S(1)} %get-tuple-element.49.v2), channel_id=1, source_target_pairs={{2,1},{4,3},{6,5},{8,7},{10,9},{12,11},{14,13},{16,15},{18,17},{20... | collective-permute-start | bytes 589832 | tf_op jit(solution)/shard_map/ppermute | solution.py:580
  30.0 0.4 collective-permute-done.8.v2_inner
  30.4 0.0 collective-permute-done.7.v2_outer
  30.4 0.5 third.1
  30.9 20.1 %all_to_all.5.gathered = f32[32,8,128]{2,1,0:T(8,128)S(1)} all-to-all(f32[32,8,128]{2,1,0:T(8,128)S(1)} %broadcast_in_dim.3), channel_id=1, replica_groups=mesh['mod'=4,'slab'=4,'sub'=2] {'mod','slab','sub'}, dimensions={0} | all-to-all | bytes 262144 | tf_op jit(solution)/shard_map/all_to_all | solution.py:625
  51.0 0.7 %combine.1 = (f32[128,128]{1,0:T(8,128)S(1)}, f32[3,8,128]{2,1,0:T(8,128)S(1)}) custom-call(f32[32,8,128]{2,1,0:T(8,128)S(1)} %all_to_all.5.gathered, f32[3,128,128]{2,1,0:T(8,128)S(1)} %get-tuple-element.40.refs_4_.v0, f32[3,128,128]{2,1,0:T(8,128)S(1)} %get-tuple-element.53.v0_high, f32[3,128,128]{2,1,0:T(8,128)S(1)} %get-tuple-element.45.v1, ...), custom_call_target="tpu_custom_call" | custom-call | tf_op jit(solution)/shard_map/combine/pallas_call | solution.py:628
  51.7 1.0 %collective-permute-start.11 = (f32[128,128]{1,0:T(8,128)S(1)}, f32[128,128]{1,0:T(8,128)S(1)}, u32[]{:S(2)}, u32[]{:S(2)}) collective-permute-start(f32[128,128]{1,0:T(8,128)S(1)} %get-tuple-element.57.refs_0_), channel_id=1, source_target_pairs={{0,24},{8,16},{16,8},{24,0},{1,25},{9,17},{17,9},{25,1},{2,26},{10... | collective-permute-start | bytes 196616 | tf_op jit(solution)/shard_map/ppermute | solution.py:631
  52.8 1.3 %collective-permute-start.10 = (f32[128,128]{1,0:T(8,128)S(1)}, f32[128,128]{1,0:T(8,128)S(1)}, u32[]{:S(2)}, u32[]{:S(2)}) collective-permute-start(f32[128,128]{1,0:T(8,128)S(1)} %get-tuple-element.57.refs_0_), channel_id=1, source_target_pairs={{0,16},{8,24},{16,0},{24,8},{1,17},{9,25},{17,1},{25,9},{2,18},{10... | collective-permute-start | bytes 196616 | tf_op jit(solution)/shard_map/ppermute | solution.py:631
  54.1 1.2 %collective-permute-start.9 = (f32[128,128]{1,0:T(8,128)S(1)}, f32[128,128]{1,0:T(8,128)S(1)}, u32[]{:S(2)}, u32[]{:S(2)}) collective-permute-start(f32[128,128]{1,0:T(8,128)S(1)} %get-tuple-element.57.refs_0_), channel_id=1, source_target_pairs={{0,8},{8,0},{16,24},{24,16},{1,9},{9,1},{17,25},{25,17},{2,10},{10... | collective-permute-start | bytes 196616 | tf_op jit(solution)/shard_map/ppermute | solution.py:631
  55.3 2.3 %collective-permute-done.11.refs_3_ = f32[128,128]{1,0:T(8,128)S(1)} collective-permute-done((f32[128,128]{1,0:T(8,128)S(1)}, f32[128,128]{1,0:T(8,128)S(1)}, u32[]{:S(2)}, u32[]{:S(2)}) %collective-permute-start.11) | collective-permute-done | bytes 65568 | tf_op jit(solution)/shard_map/ppermute | solution.py:631
  57.6 0.2 collective-permute-done.10.refs_2_
  57.8 0.5 collective-permute-done.9.refs_1_
  58.4 0.1 collective-permute-start.12
  58.4 1.0 %collective-permute-start.13 = (f32[72,128]{1,0:T(8,128)S(1)}, f32[72,128]{1,0:T(8,128)S(1)}, u32[]{:S(2)}, u32[]{:S(2)}) collective-permute-start(f32[72,128]{1,0:T(8,128)S(1)} %get-tuple-element.64), channel_id=1, source_target_pairs={{0,6},{1,3},{2,0},{3,5},{4,2},{5,7},{6,4},{7,1},{8,14},{9,11},{10,... | collective-permute-start | bytes 110600 | tf_op jit(solution)/shard_map/ppermute | solution.py:580
  59.4 0.0 collective-permute-start.14
  59.4 0.7 %displace.1 = f32[3,2,64,128]{3,2,1,0:T(8,128)} custom-call(f32[3,8,128]{2,1,0:T(8,128)S(1)} %get-tuple-element.60.factors, f32[3,128,128]{2,1,0:T(8,128)S(1)} %get-tuple-element.40.refs_4_.v0, f32[3,128,128]{2,1,0:T(8,128)S(1)} %get-tuple-element.41.refs_5_.v0_inner, f32[3,128,128]{2,1,0:T(8,128)S(1)} %get-tuple-element.45.v1, ...), custom_call_target="tpu_custom_call" | custom-call | flops 10000000 | bytes 4000000 | tf_op jit(solution)/shard_map/displace/pallas_call | solution.py:632
  60.2 3.5 %collective-permute-done.12.outer = f32[72,128]{1,0:T(8,128)S(1)} collective-permute-done((f32[72,128]{1,0:T(8,128)S(1)}, f32[72,128]{1,0:T(8,128)S(1)}, u32[]{:S(2)}, u32[]{:S(2)}) %collective-permute-start.12) | collective-permute-done | bytes 36896 | tf_op jit(solution)/shard_map/ppermute | solution.py:580
  63.6 0.0 collective-permute-done.13.far
  63.6 0.0 collective-permute-done.14.partner
  63.6 0.9 %gradient.1 = f32[2,64,128]{2,1,0:T(8,128)} custom-call(f32[128,128]{1,0:T(8,128)S(1)} %get-tuple-element.62.scaled, f32[72,128]{1,0:T(8,128)S(1)} %collective-permute-done.12.outer, f32[72,128]{1,0:T(8,128)S(1)} %collective-permute-done.13.far, f32[72,128]{1,0:T(8,128)S(1)} %collective-permute-done.14.partner), custom_call_target="tpu_custom_call" | custom-call | tf_op jit(solution)/shard_map/gradient/pallas_call | solution.py:643
  (2 shorter events, 0.0 us)
Async XLA Ops:
  0.6 1.0 %copy-start = (s32[3,2,64,128]{3,2,1,0:T(8,128)S(1)}, s32[3,2,64,128]{3,2,1,0:T(8,128)}, u32[]{:S(2)}) copy-start(s32[3,2,64,128]{3,2,1,0:T(8,128)} %load.1) | copy-start | bytes 589828
  0.6 1.0 %copy-start.1 = (f32[2,64,128]{2,1,0:T(8,128)S(1)}, f32[2,64,128]{2,1,0:T(8,128)}, u32[]{:S(2)}) copy-start(f32[2,64,128]{2,1,0:T(8,128)} %design.1) | copy-start | bytes 196612
  1.7 8.9 %collective-permute-start.4 = (f32[11,64,128]{2,1,0:T(8,128)S(1)}, f32[11,64,128]{2,1,0:T(8,128)S(1)}, u32[]{:S(2)}, u32[]{:S(2)}) collective-permute-start(f32[11,64,128]{2,1,0:T(8,128)S(1)} %get-tuple-element.39), channel_id=1, source_target_pairs={{0,1},{1,0},{2,3},{3,2},{4,5},{5,4},{6,7},{7,6},{8,9},{9,8},{10,11... | collective-permute-start | bytes 1081352 | tf_op jit(solution)/shard_map/ppermute | solution.py:580
  2.3 14.7 %collective-permute-start = (f32[4,64,128]{2,1,0:T(8,128)S(1)}, f32[4,64,128]{2,1,0:T(8,128)S(1)}, u32[]{:S(2)}, u32[]{:S(2)}) collective-permute-start(f32[4,64,128]{2,1,0:T(8,128)S(1)} %get-tuple-element.34), channel_id=1, source_target_pairs={{0,2},{1,31},{2,4},{3,1},{4,6},{5,3},{6,8},{7,5},{8,10},{9,7},{10,... | collective-permute-start | bytes 393224 | tf_op jit(solution)/shard_map/ppermute | solution.py:580
  4.9 12.0 %collective-permute-start.1 = (f32[4,64,128]{2,1,0:T(8,128)S(1)}, f32[4,64,128]{2,1,0:T(8,128)S(1)}, u32[]{:S(2)}, u32[]{:S(2)}) collective-permute-start(f32[4,64,128]{2,1,0:T(8,128)S(1)} %get-tuple-element.35), channel_id=1, source_target_pairs={{1,2},{0,31},{3,4},{2,1},{5,6},{4,3},{7,8},{6,5},{9,10},{8,7},{11,... | collective-permute-start | bytes 393224 | tf_op jit(solution)/shard_map/ppermute | solution.py:580
  9.0 7.5 %collective-permute-start.2 = (f32[64,128]{1,0:T(8,128)S(1)}, f32[64,128]{1,0:T(8,128)S(1)}, u32[]{:S(2)}, u32[]{:S(2)}) collective-permute-start(f32[64,128]{1,0:T(8,128)S(1)} %get-tuple-element.36), channel_id=1, source_target_pairs={{0,3},{1,2},{2,5},{3,4},{4,7},{5,6},{6,9},{7,8},{8,11},{9,10},{10,... | collective-permute-start | bytes 98312 | tf_op jit(solution)/shard_map/ppermute | solution.py:580
  9.0 7.9 %collective-permute-start.3 = (f32[64,128]{1,0:T(8,128)S(1)}, f32[64,128]{1,0:T(8,128)S(1)}, u32[]{:S(2)}, u32[]{:S(2)}) collective-permute-start(f32[64,128]{1,0:T(8,128)S(1)} %get-tuple-element.37), channel_id=1, source_target_pairs={{0,2},{1,3},{2,4},{3,5},{4,6},{5,7},{6,8},{7,9},{8,10},{9,11},{10,... | collective-permute-start | bytes 98312 | tf_op jit(solution)/shard_map/ppermute | solution.py:580
  18.5 1.5 %collective-permute-start.6 = (f32[3,128,128]{2,1,0:T(8,128)S(1)}, f32[3,128,128]{2,1,0:T(8,128)S(1)}, u32[]{:S(2)}, u32[]{:S(2)}) collective-permute-start(f32[3,128,128]{2,1,0:T(8,128)S(1)} %get-tuple-element.45.v1), channel_id=1, source_target_pairs={{0,1},{1,0},{2,3},{3,2},{4,5},{5,4},{6,7},{7,6},{8,9},{9,8},{10,11... | collective-permute-start | bytes 589832 | tf_op jit(solution)/shard_map/ppermute | solution.py:580
  18.7 1.7 %collective-permute-start.5 = (f32[3,128,128]{2,1,0:T(8,128)S(1)}, f32[3,128,128]{2,1,0:T(8,128)S(1)}, u32[]{:S(2)}, u32[]{:S(2)}) collective-permute-start(f32[3,128,128]{2,1,0:T(8,128)S(1)} %get-tuple-element.45.v1), channel_id=1, source_target_pairs={{1,2},{3,4},{2,1},{5,6},{4,3},{7,8},{6,5},{9,10},{8,7},{11,12},{10... | collective-permute-start | bytes 589832 | tf_op jit(solution)/shard_map/ppermute | solution.py:580
  21.5 8.8 %collective-permute-start.8 = (f32[3,128,128]{2,1,0:T(8,128)S(1)}, f32[3,128,128]{2,1,0:T(8,128)S(1)}, u32[]{:S(2)}, u32[]{:S(2)}) collective-permute-start(f32[3,128,128]{2,1,0:T(8,128)S(1)} %get-tuple-element.49.v2), channel_id=1, source_target_pairs={{0,1},{1,0},{2,3},{3,2},{4,5},{5,4},{6,7},{7,6},{8,9},{9,8},{10,11... | collective-permute-start | bytes 589832 | tf_op jit(solution)/shard_map/ppermute | solution.py:580
  29.3 1.1 %collective-permute-start.7 = (f32[3,128,128]{2,1,0:T(8,128)S(1)}, f32[3,128,128]{2,1,0:T(8,128)S(1)}, u32[]{:S(2)}, u32[]{:S(2)}) collective-permute-start(f32[3,128,128]{2,1,0:T(8,128)S(1)} %get-tuple-element.49.v2), channel_id=1, source_target_pairs={{2,1},{4,3},{6,5},{8,7},{10,9},{12,11},{14,13},{16,15},{18,17},{20... | collective-permute-start | bytes 589832 | tf_op jit(solution)/shard_map/ppermute | solution.py:580
  51.7 5.9 %collective-permute-start.11 = (f32[128,128]{1,0:T(8,128)S(1)}, f32[128,128]{1,0:T(8,128)S(1)}, u32[]{:S(2)}, u32[]{:S(2)}) collective-permute-start(f32[128,128]{1,0:T(8,128)S(1)} %get-tuple-element.57.refs_0_), channel_id=1, source_target_pairs={{0,24},{8,16},{16,8},{24,0},{1,25},{9,17},{17,9},{25,1},{2,26},{10... | collective-permute-start | bytes 196616 | tf_op jit(solution)/shard_map/ppermute | solution.py:631
  52.8 5.1 %collective-permute-start.10 = (f32[128,128]{1,0:T(8,128)S(1)}, f32[128,128]{1,0:T(8,128)S(1)}, u32[]{:S(2)}, u32[]{:S(2)}) collective-permute-start(f32[128,128]{1,0:T(8,128)S(1)} %get-tuple-element.57.refs_0_), channel_id=1, source_target_pairs={{0,16},{8,24},{16,0},{24,8},{1,17},{9,25},{17,1},{25,9},{2,18},{10... | collective-permute-start | bytes 196616 | tf_op jit(solution)/shard_map/ppermute | solution.py:631
  54.1 4.3 %collective-permute-start.9 = (f32[128,128]{1,0:T(8,128)S(1)}, f32[128,128]{1,0:T(8,128)S(1)}, u32[]{:S(2)}, u32[]{:S(2)}) collective-permute-start(f32[128,128]{1,0:T(8,128)S(1)} %get-tuple-element.57.refs_0_), channel_id=1, source_target_pairs={{0,8},{8,0},{16,24},{24,16},{1,9},{9,1},{17,25},{25,17},{2,10},{10... | collective-permute-start | bytes 196616 | tf_op jit(solution)/shard_map/ppermute | solution.py:631
  58.4 5.2 %collective-permute-start.12 = (f32[72,128]{1,0:T(8,128)S(1)}, f32[72,128]{1,0:T(8,128)S(1)}, u32[]{:S(2)}, u32[]{:S(2)}) collective-permute-start(f32[72,128]{1,0:T(8,128)S(1)} %get-tuple-element.63), channel_id=1, source_target_pairs={{1,2},{0,7},{3,4},{2,1},{5,6},{4,3},{7,0},{6,5},{9,10},{8,15},{11,... | collective-permute-start | bytes 110600 | tf_op jit(solution)/shard_map/ppermute | solution.py:580
  58.4 5.2 %collective-permute-start.13 = (f32[72,128]{1,0:T(8,128)S(1)}, f32[72,128]{1,0:T(8,128)S(1)}, u32[]{:S(2)}, u32[]{:S(2)}) collective-permute-start(f32[72,128]{1,0:T(8,128)S(1)} %get-tuple-element.64), channel_id=1, source_target_pairs={{0,6},{1,3},{2,0},{3,5},{4,2},{5,7},{6,4},{7,1},{8,14},{9,11},{10,... | collective-permute-start | bytes 110600 | tf_op jit(solution)/shard_map/ppermute | solution.py:580
  59.4 4.2 %collective-permute-start.14 = (f32[72,128]{1,0:T(8,128)S(1)}, f32[72,128]{1,0:T(8,128)S(1)}, u32[]{:S(2)}, u32[]{:S(2)}) collective-permute-start(f32[72,128]{1,0:T(8,128)S(1)} %get-tuple-element.65), channel_id=1, source_target_pairs={{0,1},{1,0},{2,3},{3,2},{4,5},{5,4},{6,7},{7,6},{8,9},{9,8},{10,11... | collective-permute-start | bytes 110600 | tf_op jit(solution)/shard_map/ppermute | solution.py:580

commit v10 on v9

--- a/solution.py
+++ b/solution.py
@@ -314,8 +314,7 @@
 
 
 def start_outer_kernel(
-    mods, slabs,
-    first, second, third, fourth, v0, v0_inner, free, fields, parts,
+    first, second, third, fourth, ends_first, ends_second, v0, v0_inner, free, fields, parts,
     v1, v0_high, mod_inner, mod_outer, mod_own, slope_factor, chain_factor, moments,
     v0_outer, near, deep,
 ):
@@ -325,16 +324,14 @@
     even = sub == 0
     mine = pl.ds(pl.multiple_of(sub * half, half), half)
     other = pl.ds(pl.multiple_of((1 - sub) * half, half), half)
-    near[mine, :] = first[3]
-    near[other, :] = second[3]
+    near[mine, :] = first[3] + ends_first[...]
+    near[other, :] = second[3] + ends_second[...]
     deep[mine, :] = fourth[...]
     deep[other, :] = third[...]
     starts = (mod == 0) & (slab == 0) & even
-    ends = (mod == mods - 1) & (slab == slabs - 1) & (sub == 1)
-    inside = jnp.where(ends, 0.0, 1.0)
-    for k in range(3):
-        v0_outer[k, mine, :] = first[k] * inside
-        v0_outer[k, other, :] = second[k] * inside
+    for k in range(3):
+        v0_outer[k, mine, :] = first[k]
+        v0_outer[k, other, :] = second[k]
         v0_high[k] = jnp.where(even, v0_inner[k], v0_outer[k])
 
     side = filter_side(near[...])
@@ -529,6 +526,8 @@
     def at(chip, sub):
         return 2 * chip + sub
 
+    last = (mods - 1) * slabs
+
     def beside(chip, steps, cyclic):
         target = chip + steps
         if cyclic:
@@ -554,10 +553,12 @@
 
     return dict(
         swap=built([(0, 0, 1), (1, 0, 0)], True),
-        first=built([(0, 1, 0), (1, -1, 1)], True),
-        second=built([(1, 1, 0), (0, -1, 1)], True),
-        third=built([(0, 1, 1), (1, 1, 0)], True),
-        fourth=built([(0, 1, 0), (1, 1, 1)], True),
+        first=built([(0, 1, 0), (1, -1, 1)], False),
+        second=built([(1, 1, 0), (0, -1, 1)], False),
+        third=in_module([(0, 1, 1), (1, 1, 0)]),
+        fourth=in_module([(0, 1, 0), (1, 1, 1)]),
+        ends_first=[(at(slabs - 1, 0), at(0, 0)), (at(last, 1), at(chips - 1, 1))],
+        ends_second=[(at(slabs - 1, 1), at(0, 0)), (at(last, 0), at(chips - 1, 1))],
         outer=built([(1, 1, 0), (0, -1, 1)], False),
         down=built([(0, -1, 1)], False),
         halo_cross=in_module([(1, 1, 0), (0, -1, 1)]),
@@ -590,12 +591,11 @@
     )(free, load, design)
     first = move(first, "first")
     second = move(second, "second")
+    ends_first = move(third, "ends_first")
+    ends_second = move(fourth, "ends_second")
     third = move(third, "third")
     fourth = move(fourth, "fourth")
     swap = move(swap, "swap")
-
-    def start_body(*refs):
-        start_outer_kernel(mods, slabs, *refs)
 
     v0, v0_inner, free, fields, parts = call(
         start_inner_kernel,
@@ -605,11 +605,11 @@
         work=True,
     )(own, swap)
     v1, v0_high, mod_inner, mod_outer, mod_own, slope_factor, chain_factor, moments = call(
-        start_body,
+        start_outer_kernel,
         [layer, layer, plane, plane, plane, plane, plane, (8, width)],
         [layer, plane, plane],
         name="start_outer",
-    )(first, second, third, fourth, v0, v0_inner, free, fields, parts)
+    )(first, second, third, fourth, ends_first, ends_second, v0, v0_inner, free, fields, parts)
     outer = move(v1, "outer")
     inner = move(v1, "swap")
     (fields,) = call(second_inner_kernel, [(12,) + plane], name="second_inner", work=True)(v1, inner)

time: 64.7 us -> 73.2 us (1.13)
  waiting for transfers between devices: 13.1 us -> 16.5 us
  blocking collectives: 20.1 us -> 23.3 us
  starting transfers between devices: 22.8 us -> 24.7 us
    ppermute x12 -> x14, waiting for transfers between devices: 10 us -> 13.4 us  [move(): return lax.ppermute(value, AXES, path[name])]
    all_to_all x1, blocking collectives: 20.1 us -> 23.3 us  [local(): lax.all_to_all(jnp.broadcast_to(moments, (devices, 8, width)), AXES, 0, 0...]
    ppermute x12 -> x14, starting transfers between devices: 19.3 us -> 21.1 us  [move(): return lax.ppermute(value, AXES, path[name])]
  transfers between devices with their start and end apart: 15 -> 17, of which waited for: 8 -> 9; matrix products, arithmetic and copies ran while one was open for 0% -> 0% of each run, Pallas kernels for 3% -> 3%
where the time goes in v10:
time: 73.2 us; the launch traced here: 73 us
  starting transfers between devices  24.7 us (34%)
  blocking collectives  23.3 us (32%)
  waiting for transfers between devices  16.5 us (23%)
  Pallas kernels  6.73 us (9%)
  other arithmetic  0.99 us (1%)
  between operations  0.79 us (1%)
    all_to_all x1, blocking collectives, local(): lax.all_to_all(jnp.broadcast_to(moments, (devices, 8, width)), AXES, 0, 0...  23.3 us
    ppermute x14, starting transfers between devices, move(): return lax.ppermute(value, AXES, path[name])  21.1 us
    ppermute x14, waiting for transfers between devices, move(): return lax.ppermute(value, AXES, path[name])  13.4 us
    ppermute x3, starting transfers between devices, local(): lax.ppermute(slope, 'mod', pairs)  3.55 us
    ppermute x3, waiting for transfers between devices, local(): lax.ppermute(slope, 'mod', pairs)  3.06 us
    pallas_call x1, Pallas kernels, local(): call(start_outer_kernel, [layer, layer, plane, plane, plane, plane, plane...  1.55 us
  transfers between devices with their start and end apart: 17, of which 9 were waited for; matrix products, arithmetic and copies ran while one was open for 0% of the time, Pallas kernels for 3%

profile of v10, /device:TPU:0, one launch (start us, length us, event | category | flops | bytes accessed | tf_op | source)
XLA Modules:
  0.0 73.0 jit_solution(14579504055158939462)
XLA Ops:
  0.6 0.0 copy-start
  0.6 1.0 %subtract_convert_fusion.free = f32[3,2,64,128]{3,2,1,0:T(8,128)S(1)} fusion(s32[3,2,64,128]{3,2,1,0:T(8,128)} %param.4), kind=kLoop, calls=%fused_computation | loop fusion | flops 98304 | bytes 393216 | tf_op jit(solution)/shard_map/convert_element_type | solution.py:586
  1.6 0.0 copy-done
  1.7 0.0 copy-done.1
  1.7 0.1 prepare.1
  1.7 0.5 collective-permute-start.6
  2.3 4.5 %collective-permute-start = (f32[4,64,128]{2,1,0:T(8,128)S(1)}, f32[4,64,128]{2,1,0:T(8,128)S(1)}, u32[]{:S(2)}, u32[]{:S(2)}) collective-permute-start(f32[4,64,128]{2,1,0:T(8,128)S(1)} %get-tuple-element.34), channel_id=1, source_target_pairs={{0,2},{2,4},{3,1},{4,6},{5,3},{6,8},{7,5},{8,10},{9,7},{10,12},{11... | collective-permute-start | bytes 393224 | tf_op jit(solution)/shard_map/ppermute | solution.py:581
  6.8 0.7 collective-permute-start.1
  7.4 1.3 %collective-permute-start.4 = (f32[64,128]{1,0:T(8,128)S(1)}, f32[64,128]{1,0:T(8,128)S(1)}, u32[]{:S(2)}, u32[]{:S(2)}) collective-permute-start(f32[64,128]{1,0:T(8,128)S(1)} %get-tuple-element.36), channel_id=1, source_target_pairs={{6,0},{25,31}} | collective-permute-start | bytes 98312 | tf_op jit(solution)/shard_map/ppermute | solution.py:581
  8.7 3.5 %collective-permute-start.2 = (f32[64,128]{1,0:T(8,128)S(1)}, f32[64,128]{1,0:T(8,128)S(1)}, u32[]{:S(2)}, u32[]{:S(2)}) collective-permute-start(f32[64,128]{1,0:T(8,128)S(1)} %get-tuple-element.36), channel_id=1, source_target_pairs={{0,3},{1,2},{2,5},{3,4},{4,7},{5,6},{6,1},{7,0},{8,11},{9,10},{10,... | collective-permute-start | bytes 98312 | tf_op jit(solution)/shard_map/ppermute | solution.py:581
  12.3 3.6 %collective-permute-done.4.ends_first = f32[64,128]{1,0:T(8,128)S(1)} collective-permute-done((f32[64,128]{1,0:T(8,128)S(1)}, f32[64,128]{1,0:T(8,128)S(1)}, u32[]{:S(2)}, u32[]{:S(2)}) %collective-permute-start.4) | collective-permute-done | bytes 32800 | tf_op jit(solution)/shard_map/ppermute | solution.py:581
  15.9 1.3 %collective-permute-start.5 = (f32[64,128]{1,0:T(8,128)S(1)}, f32[64,128]{1,0:T(8,128)S(1)}, u32[]{:S(2)}, u32[]{:S(2)}) collective-permute-start(f32[64,128]{1,0:T(8,128)S(1)} %get-tuple-element.37), channel_id=1, source_target_pairs={{7,0},{24,31}} | collective-permute-start | bytes 98312 | tf_op jit(solution)/shard_map/ppermute | solution.py:581
  17.2 0.0 collective-permute-done.6.swap
  17.2 0.1 collective-permute-start.3
  17.3 0.7 %start_inner.1 = (f32[3,128,128]{2,1,0:T(8,128)S(1)}, f32[3,128,128]{2,1,0:T(8,128)S(1)}, f32[3,128,128]{2,1,0:T(8,128)S(1)}, f32[12,128,128]{2,1,0:T(8,128)S(1)}, f32[3,128,128]{2,1,0:T(8,128)S(1)}) custom-call(f32[11,64,128]{2,1,0:T(8,128)S(1)} %get-tuple-element.38.own, f32[11,64,128]{2,1,0:T(8,128)S(1)} %collective-permute-done.6.swap), custom_call_target="tpu_custom_call" | custom-call | flops 10000000 | bytes 4000000 | tf_op jit(solution)/shard_map/start_inner/pallas_call | solution.py:600
  18.0 0.0 collective-permute-done.2.third
  18.0 5.2 %collective-permute-done.5.ends_second = f32[64,128]{1,0:T(8,128)S(1)} collective-permute-done((f32[64,128]{1,0:T(8,128)S(1)}, f32[64,128]{1,0:T(8,128)S(1)}, u32[]{:S(2)}, u32[]{:S(2)}) %collective-permute-start.5) | collective-permute-done | bytes 32800 | tf_op jit(solution)/shard_map/ppermute | solution.py:581
  23.2 0.1 collective-permute-done.3.fourth
  23.3 0.0 collective-permute-done.first
  23.3 0.0 collective-permute-done.1.second
  23.3 1.5 %start_outer.1 = (f32[3,128,128]{2,1,0:T(8,128)S(1)}, f32[3,128,128]{2,1,0:T(8,128)S(1)}, f32[128,128]{1,0:T(8,128)S(1)}, f32[128,128]{1,0:T(8,128)S(1)}, f32[12...) custom-call(f32[4,64,128]{2,1,0:T(8,128)S(1)} %collective-permute-done.first, ...), custom_call_target="tpu_custom_call" | custom-call | tf_op jit(solution)/shard_map/start_outer/pallas_call | solution.py:607
  24.9 0.2 collective-permute-start.8
  25.1 0.7 collective-permute-start.7
  25.7 0.6 collective-permute-done.8.inner.v1_inner
  26.4 0.4 second_inner.1.fields
  26.8 0.0 collective-permute-done.7.outer
  26.8 1.1 %second_outer.1 = (f32[3,128,128]{2,1,0:T(8,128)S(1)}, f32[3,128,128]{2,1,0:T(8,128)S(1)}, f32[8,128]{1,0:T(8,128)S(1)}) custom-call(f32[3,128,128]{2,1,0:T(8,128)S(1)} %get-tuple-element.45.v1, f32[3,128,128]{2,1,0:T(8,128)S(1)} %collective-permute-done.7.outer, f32[3,128,128]{2,1,0:T(8,128)S(1)} %collective-permute-done.8.inner.v1_inner, ...), custom_call_target="tpu_custom_call" | custom-call | tf_op jit(solution)/shard_map/second_outer/pallas_call | solution.py:616
  27.9 6.7 %collective-permute-start.10 = (f32[3,128,128]{2,1,0:T(8,128)S(1)}, f32[3,128,128]{2,1,0:T(8,128)S(1)}, u32[]{:S(2)}, u32[]{:S(2)}) collective-permute-start(f32[3,128,128]{2,1,0:T(8,128)S(1)} %get-tuple-element.49.v2), channel_id=1, source_target_pairs={{0,1},{1,0},{2,3},{3,2},{4,5},{5,4},{6,7},{7,6},{8,9},{9,8},{10,11... | collective-permute-start | bytes 589832 | tf_op jit(solution)/shard_map/ppermute | solution.py:581
  34.6 0.7 collective-permute-start.9
  35.3 0.4 collective-permute-done.10.v2_inner
  35.7 0.0 collective-permute-done.9.v2_outer
  35.7 0.5 third.1
  36.2 23.3 %all_to_all.5.gathered = f32[32,8,128]{2,1,0:T(8,128)S(1)} all-to-all(f32[32,8,128]{2,1,0:T(8,128)S(1)} %broadcast_in_dim.3), channel_id=1, replica_groups=mesh['mod'=4,'slab'=4,'sub'=2] {'mod','slab','sub'}, dimensions={0} | all-to-all | bytes 262144 | tf_op jit(solution)/shard_map/all_to_all | solution.py:625
  59.5 0.7 combine.1
  60.2 1.0 %collective-permute-start.13 = (f32[128,128]{1,0:T(8,128)S(1)}, f32[128,128]{1,0:T(8,128)S(1)}, u32[]{:S(2)}, u32[]{:S(2)}) collective-permute-start(f32[128,128]{1,0:T(8,128)S(1)} %get-tuple-element.57.refs_0_), channel_id=1, source_target_pairs={{0,24},{8,16},{16,8},{24,0},{1,25},{9,17},{17,9},{25,1},{2,26},{10... | collective-permute-start | bytes 196616 | tf_op jit(solution)/shard_map/ppermute | solution.py:631
  61.2 1.3 %collective-permute-start.12 = (f32[128,128]{1,0:T(8,128)S(1)}, f32[128,128]{1,0:T(8,128)S(1)}, u32[]{:S(2)}, u32[]{:S(2)}) collective-permute-start(f32[128,128]{1,0:T(8,128)S(1)} %get-tuple-element.57.refs_0_), channel_id=1, source_target_pairs={{0,16},{8,24},{16,0},{24,8},{1,17},{9,25},{17,1},{25,9},{2,18},{10... | collective-permute-start | bytes 196616 | tf_op jit(solution)/shard_map/ppermute | solution.py:631
  62.5 1.2 %collective-permute-start.11 = (f32[128,128]{1,0:T(8,128)S(1)}, f32[128,128]{1,0:T(8,128)S(1)}, u32[]{:S(2)}, u32[]{:S(2)}) collective-permute-start(f32[128,128]{1,0:T(8,128)S(1)} %get-tuple-element.57.refs_0_), channel_id=1, source_target_pairs={{0,8},{8,0},{16,24},{24,16},{1,9},{9,1},{17,25},{25,17},{2,10},{10... | collective-permute-start | bytes 196616 | tf_op jit(solution)/shard_map/ppermute | solution.py:631
  63.7 2.3 %collective-permute-done.13.refs_3_ = f32[128,128]{1,0:T(8,128)S(1)} collective-permute-done((f32[128,128]{1,0:T(8,128)S(1)}, f32[128,128]{1,0:T(8,128)S(1)}, u32[]{:S(2)}, u32[]{:S(2)}) %collective-permute-start.13) | collective-permute-done | bytes 65568 | tf_op jit(solution)/shard_map/ppermute | solution.py:631
  66.1 0.2 collective-permute-done.12.refs_2_
  66.3 0.5 collective-permute-done.11.refs_1_
  66.8 0.1 collective-permute-start.14
  66.9 1.0 %collective-permute-start.15 = (f32[72,128]{1,0:T(8,128)S(1)}, f32[72,128]{1,0:T(8,128)S(1)}, u32[]{:S(2)}, u32[]{:S(2)}) collective-permute-start(f32[72,128]{1,0:T(8,128)S(1)} %get-tuple-element.64), channel_id=1, source_target_pairs={{0,6},{1,3},{2,0},{3,5},{4,2},{5,7},{6,4},{7,1},{8,14},{9,11},{10,... | collective-permute-start | bytes 110600 | tf_op jit(solution)/shard_map/ppermute | solution.py:581
  67.9 0.0 collective-permute-start.16
  67.9 0.7 %displace.1 = f32[3,2,64,128]{3,2,1,0:T(8,128)} custom-call(f32[3,8,128]{2,1,0:T(8,128)S(1)} %get-tuple-element.60.factors, f32[3,128,128]{2,1,0:T(8,128)S(1)} %get-tuple-element.40.v0, f32[3,128,128]{2,1,0:T(8,128)S(1)} %get-tuple-element.41.v0_inner, f32[3,128,128]{2,1,0:T(8,128)S(1)} %get-tuple-element.45.v1, ...), custom_call_target="tpu_custom_call" | custom-call | flops 10000000 | bytes 4000000 | tf_op jit(solution)/shard_map/displace/pallas_call | solution.py:632
  68.6 3.5 %collective-permute-done.14.outer = f32[72,128]{1,0:T(8,128)S(1)} collective-permute-done((f32[72,128]{1,0:T(8,128)S(1)}, f32[72,128]{1,0:T(8,128)S(1)}, u32[]{:S(2)}, u32[]{:S(2)}) %collective-permute-start.14) | collective-permute-done | bytes 36896 | tf_op jit(solution)/shard_map/ppermute | solution.py:581
  72.1 0.0 collective-permute-done.15.far
  72.1 0.0 collective-permute-done.16.partner
  72.1 0.9 %gradient.1 = f32[2,64,128]{2,1,0:T(8,128)} custom-call(f32[128,128]{1,0:T(8,128)S(1)} %get-tuple-element.62.scaled, f32[72,128]{1,0:T(8,128)S(1)} %collective-permute-done.14.outer, f32[72,128]{1,0:T(8,128)S(1)} %collective-permute-done.15.far, f32[72,128]{1,0:T(8,128)S(1)} %collective-permute-done.16.partner), custom_call_target="tpu_custom_call" | custom-call | tf_op jit(solution)/shard_map/gradient/pallas_call | solution.py:643
  (3 shorter events, 0.0 us)
Async XLA Ops:
  0.6 1.0 %copy-start = (s32[3,2,64,128]{3,2,1,0:T(8,128)S(1)}, s32[3,2,64,128]{3,2,1,0:T(8,128)}, u32[]{:S(2)}) copy-start(s32[3,2,64,128]{3,2,1,0:T(8,128)} %load.1) | copy-start | bytes 589828
  0.6 1.0 %copy-start.1 = (f32[2,64,128]{2,1,0:T(8,128)S(1)}, f32[2,64,128]{2,1,0:T(8,128)}, u32[]{:S(2)}) copy-start(f32[2,64,128]{2,1,0:T(8,128)} %design.1) | copy-start | bytes 196612
  1.7 15.5 %collective-permute-start.6 = (f32[11,64,128]{2,1,0:T(8,128)S(1)}, f32[11,64,128]{2,1,0:T(8,128)S(1)}, u32[]{:S(2)}, u32[]{:S(2)}) collective-permute-start(f32[11,64,128]{2,1,0:T(8,128)S(1)} %get-tuple-element.39), channel_id=1, source_target_pairs={{0,1},{1,0},{2,3},{3,2},{4,5},{5,4},{6,7},{7,6},{8,9},{9,8},{10,11... | collective-permute-start | bytes 1081352 | tf_op jit(solution)/shard_map/ppermute | solution.py:581
  2.3 21.1 %collective-permute-start = (f32[4,64,128]{2,1,0:T(8,128)S(1)}, f32[4,64,128]{2,1,0:T(8,128)S(1)}, u32[]{:S(2)}, u32[]{:S(2)}) collective-permute-start(f32[4,64,128]{2,1,0:T(8,128)S(1)} %get-tuple-element.34), channel_id=1, source_target_pairs={{0,2},{2,4},{3,1},{4,6},{5,3},{6,8},{7,5},{8,10},{9,7},{10,12},{11... | collective-permute-start | bytes 393224 | tf_op jit(solution)/shard_map/ppermute | solution.py:581
  6.8 16.6 %collective-permute-start.1 = (f32[4,64,128]{2,1,0:T(8,128)S(1)}, f32[4,64,128]{2,1,0:T(8,128)S(1)}, u32[]{:S(2)}, u32[]{:S(2)}) collective-permute-start(f32[4,64,128]{2,1,0:T(8,128)S(1)} %get-tuple-element.35), channel_id=1, source_target_pairs={{1,2},{3,4},{2,1},{5,6},{4,3},{7,8},{6,5},{9,10},{8,7},{11,12},{10... | collective-permute-start | bytes 393224 | tf_op jit(solution)/shard_map/ppermute | solution.py:581
  7.4 8.5 %collective-permute-start.4 = (f32[64,128]{1,0:T(8,128)S(1)}, f32[64,128]{1,0:T(8,128)S(1)}, u32[]{:S(2)}, u32[]{:S(2)}) collective-permute-start(f32[64,128]{1,0:T(8,128)S(1)} %get-tuple-element.36), channel_id=1, source_target_pairs={{6,0},{25,31}} | collective-permute-start | bytes 98312 | tf_op jit(solution)/shard_map/ppermute | solution.py:581
  8.7 9.3 %collective-permute-start.2 = (f32[64,128]{1,0:T(8,128)S(1)}, f32[64,128]{1,0:T(8,128)S(1)}, u32[]{:S(2)}, u32[]{:S(2)}) collective-permute-start(f32[64,128]{1,0:T(8,128)S(1)} %get-tuple-element.36), channel_id=1, source_target_pairs={{0,3},{1,2},{2,5},{3,4},{4,7},{5,6},{6,1},{7,0},{8,11},{9,10},{10,... | collective-permute-start | bytes 98312 | tf_op jit(solution)/shard_map/ppermute | solution.py:581
  15.9 7.3 %collective-permute-start.5 = (f32[64,128]{1,0:T(8,128)S(1)}, f32[64,128]{1,0:T(8,128)S(1)}, u32[]{:S(2)}, u32[]{:S(2)}) collective-permute-start(f32[64,128]{1,0:T(8,128)S(1)} %get-tuple-element.37), channel_id=1, source_target_pairs={{7,0},{24,31}} | collective-permute-start | bytes 98312 | tf_op jit(solution)/shard_map/ppermute | solution.py:581
  17.2 6.1 %collective-permute-start.3 = (f32[64,128]{1,0:T(8,128)S(1)}, f32[64,128]{1,0:T(8,128)S(1)}, u32[]{:S(2)}, u32[]{:S(2)}) collective-permute-start(f32[64,128]{1,0:T(8,128)S(1)} %get-tuple-element.37), channel_id=1, source_target_pairs={{0,2},{1,3},{2,4},{3,5},{4,6},{5,7},{6,0},{7,1},{8,10},{9,11},{10,... | collective-permute-start | bytes 98312 | tf_op jit(solution)/shard_map/ppermute | solution.py:581
  24.9 1.5 %collective-permute-start.8 = (f32[3,128,128]{2,1,0:T(8,128)S(1)}, f32[3,128,128]{2,1,0:T(8,128)S(1)}, u32[]{:S(2)}, u32[]{:S(2)}) collective-permute-start(f32[3,128,128]{2,1,0:T(8,128)S(1)} %get-tuple-element.45.v1), channel_id=1, source_target_pairs={{0,1},{1,0},{2,3},{3,2},{4,5},{5,4},{6,7},{7,6},{8,9},{9,8},{10,11... | collective-permute-start | bytes 589832 | tf_op jit(solution)/shard_map/ppermute | solution.py:581
  25.1 1.7 %collective-permute-start.7 = (f32[3,128,128]{2,1,0:T(8,128)S(1)}, f32[3,128,128]{2,1,0:T(8,128)S(1)}, u32[]{:S(2)}, u32[]{:S(2)}) collective-permute-start(f32[3,128,128]{2,1,0:T(8,128)S(1)} %get-tuple-element.45.v1), channel_id=1, source_target_pairs={{1,2},{3,4},{2,1},{5,6},{4,3},{7,8},{6,5},{9,10},{8,7},{11,12},{10... | collective-permute-start | bytes 589832 | tf_op jit(solution)/shard_map/ppermute | solution.py:581
  27.9 7.8 %collective-permute-start.10 = (f32[3,128,128]{2,1,0:T(8,128)S(1)}, f32[3,128,128]{2,1,0:T(8,128)S(1)}, u32[]{:S(2)}, u32[]{:S(2)}) collective-permute-start(f32[3,128,128]{2,1,0:T(8,128)S(1)} %get-tuple-element.49.v2), channel_id=1, source_target_pairs={{0,1},{1,0},{2,3},{3,2},{4,5},{5,4},{6,7},{7,6},{8,9},{9,8},{10,11... | collective-permute-start | bytes 589832 | tf_op jit(solution)/shard_map/ppermute | solution.py:581
  34.6 1.1 %collective-permute-start.9 = (f32[3,128,128]{2,1,0:T(8,128)S(1)}, f32[3,128,128]{2,1,0:T(8,128)S(1)}, u32[]{:S(2)}, u32[]{:S(2)}) collective-permute-start(f32[3,128,128]{2,1,0:T(8,128)S(1)} %get-tuple-element.49.v2), channel_id=1, source_target_pairs={{2,1},{4,3},{6,5},{8,7},{10,9},{12,11},{14,13},{16,15},{18,17},{20... | collective-permute-start | bytes 589832 | tf_op jit(solution)/shard_map/ppermute | solution.py:581
  60.2 5.9 %collective-permute-start.13 = (f32[128,128]{1,0:T(8,128)S(1)}, f32[128,128]{1,0:T(8,128)S(1)}, u32[]{:S(2)}, u32[]{:S(2)}) collective-permute-start(f32[128,128]{1,0:T(8,128)S(1)} %get-tuple-element.57.refs_0_), channel_id=1, source_target_pairs={{0,24},{8,16},{16,8},{24,0},{1,25},{9,17},{17,9},{25,1},{2,26},{10... | collective-permute-start | bytes 196616 | tf_op jit(solution)/shard_map/ppermute | solution.py:631
  61.2 5.1 %collective-permute-start.12 = (f32[128,128]{1,0:T(8,128)S(1)}, f32[128,128]{1,0:T(8,128)S(1)}, u32[]{:S(2)}, u32[]{:S(2)}) collective-permute-start(f32[128,128]{1,0:T(8,128)S(1)} %get-tuple-element.57.refs_0_), channel_id=1, source_target_pairs={{0,16},{8,24},{16,0},{24,8},{1,17},{9,25},{17,1},{25,9},{2,18},{10... | collective-permute-start | bytes 196616 | tf_op jit(solution)/shard_map/ppermute | solution.py:631
  62.5 4.3 %collective-permute-start.11 = (f32[128,128]{1,0:T(8,128)S(1)}, f32[128,128]{1,0:T(8,128)S(1)}, u32[]{:S(2)}, u32[]{:S(2)}) collective-permute-start(f32[128,128]{1,0:T(8,128)S(1)} %get-tuple-element.57.refs_0_), channel_id=1, source_target_pairs={{0,8},{8,0},{16,24},{24,16},{1,9},{9,1},{17,25},{25,17},{2,10},{10... | collective-permute-start | bytes 196616 | tf_op jit(solution)/shard_map/ppermute | solution.py:631
  66.8 5.2 %collective-permute-start.14 = (f32[72,128]{1,0:T(8,128)S(1)}, f32[72,128]{1,0:T(8,128)S(1)}, u32[]{:S(2)}, u32[]{:S(2)}) collective-permute-start(f32[72,128]{1,0:T(8,128)S(1)} %get-tuple-element.63), channel_id=1, source_target_pairs={{1,2},{0,7},{3,4},{2,1},{5,6},{4,3},{7,0},{6,5},{9,10},{8,15},{11,... | collective-permute-start | bytes 110600 | tf_op jit(solution)/shard_map/ppermute | solution.py:581
  66.9 5.2 %collective-permute-start.15 = (f32[72,128]{1,0:T(8,128)S(1)}, f32[72,128]{1,0:T(8,128)S(1)}, u32[]{:S(2)}, u32[]{:S(2)}) collective-permute-start(f32[72,128]{1,0:T(8,128)S(1)} %get-tuple-element.64), channel_id=1, source_target_pairs={{0,6},{1,3},{2,0},{3,5},{4,2},{5,7},{6,4},{7,1},{8,14},{9,11},{10,... | collective-permute-start | bytes 110600 | tf_op jit(solution)/shard_map/ppermute | solution.py:581
  67.9 4.2 %collective-permute-start.16 = (f32[72,128]{1,0:T(8,128)S(1)}, f32[72,128]{1,0:T(8,128)S(1)}, u32[]{:S(2)}, u32[]{:S(2)}) collective-permute-start(f32[72,128]{1,0:T(8,128)S(1)} %get-tuple-element.65), channel_id=1, source_target_pairs={{0,1},{1,0},{2,3},{3,2},{4,5},{5,4},{6,7},{7,6},{8,9},{9,8},{10,11... | collective-permute-start | bytes 110600 | tf_op jit(solution)/shard_map/ppermute | solution.py:581

commit v11 on v9

--- a/solution.py
+++ b/solution.py
@@ -556,8 +556,8 @@
         swap=built([(0, 0, 1), (1, 0, 0)], True),
         first=built([(0, 1, 0), (1, -1, 1)], True),
         second=built([(1, 1, 0), (0, -1, 1)], True),
-        third=built([(0, 1, 1), (1, 1, 0)], True),
-        fourth=built([(0, 1, 0), (1, 1, 1)], True),
+        third=in_module([(0, 1, 1), (1, 1, 0)]),
+        fourth=in_module([(0, 1, 0), (1, 1, 1)]),
         outer=built([(1, 1, 0), (0, -1, 1)], False),
         down=built([(0, -1, 1)], False),
         halo_cross=in_module([(1, 1, 0), (0, -1, 1)]),

time: 64.7 us -> 64.7 us (level)
  blocking collectives: 20.1 us -> 23.1 us
  starting transfers between devices: 22.8 us -> 20.8 us
  waiting for transfers between devices: 13.1 us -> 12.1 us
    all_to_all x1, blocking collectives: 20.1 us -> 23.1 us  [local(): lax.all_to_all(jnp.broadcast_to(moments, (devices, 8, width)), AXES, 0, 0...]
    ppermute x12, starting transfers between devices: 19.3 us -> 17.2 us  [move(): return lax.ppermute(value, AXES, path[name])]
    ppermute x12, waiting for transfers between devices: 10 us -> 9.03 us  [move(): return lax.ppermute(value, AXES, path[name])]
  transfers between devices with their start and end apart: 15 -> 15, of which waited for: 8 -> 9; matrix products, arithmetic and copies ran while one was open for 0% -> 0% of each run, Pallas kernels for 3% -> 3%
where the time goes in v11:
time: 64.7 us; the launch traced here: 64.5 us
  blocking collectives  23.1 us (36%)
  starting transfers between devices  20.8 us (32%)
  waiting for transfers between devices  12.1 us (19%)
  Pallas kernels  6.71 us (10%)
  other arithmetic  0.99 us (2%)
  between operations  0.75 us (1%)
    all_to_all x1, blocking collectives, local(): lax.all_to_all(jnp.broadcast_to(moments, (devices, 8, width)), AXES, 0, 0...  23.1 us
    ppermute x12, starting transfers between devices, move(): return lax.ppermute(value, AXES, path[name])  17.2 us
    ppermute x12, waiting for transfers between devices, move(): return lax.ppermute(value, AXES, path[name])  9.03 us
    ppermute x3, starting transfers between devices, local(): lax.ppermute(slope, 'mod', pairs)  3.55 us
    ppermute x3, waiting for transfers between devices, local(): lax.ppermute(slope, 'mod', pairs)  3.06 us
    pallas_call x1, Pallas kernels, local(): call(start_body, [layer, layer, plane, plane, plane, plane, plane, (8, wi...  1.53 us
  transfers between devices with their start and end apart: 15, of which 9 were waited for; matrix products, arithmetic and copies ran while one was open for 0% of the time, Pallas kernels for 3%

profile of v11, /device:TPU:0, one launch (start us, length us, event | category | flops | bytes accessed | tf_op | source)
XLA Modules:
  0.0 64.5 jit_solution(13122288556734821205)
XLA Ops:
  0.6 0.0 copy-start
  0.6 0.0 copy-start.1
  0.6 1.0 %subtract_convert_fusion.free = f32[3,2,64,128]{3,2,1,0:T(8,128)S(1)} fusion(s32[3,2,64,128]{3,2,1,0:T(8,128)} %param.4), kind=kLoop, calls=%fused_computation | loop fusion | flops 98304 | bytes 393216 | tf_op jit(solution)/shard_map/convert_element_type | solution.py:585
  1.6 0.0 copy-done
  1.7 0.0 copy-done.1
  1.7 0.1 prepare.1
  1.7 0.5 collective-permute-start.4
  2.3 2.6 %collective-permute-start = (f32[4,64,128]{2,1,0:T(8,128)S(1)}, f32[4,64,128]{2,1,0:T(8,128)S(1)}, u32[]{:S(2)}, u32[]{:S(2)}) collective-permute-start(f32[4,64,128]{2,1,0:T(8,128)S(1)} %get-tuple-element.34), channel_id=1, source_target_pairs={{0,2},{1,31},{2,4},{3,1},{4,6},{5,3},{6,8},{7,5},{8,10},{9,7},{10,... | collective-permute-start | bytes 393224 | tf_op jit(solution)/shard_map/ppermute | solution.py:580
  4.9 4.1 %collective-permute-start.1 = (f32[4,64,128]{2,1,0:T(8,128)S(1)}, f32[4,64,128]{2,1,0:T(8,128)S(1)}, u32[]{:S(2)}, u32[]{:S(2)}) collective-permute-start(f32[4,64,128]{2,1,0:T(8,128)S(1)} %get-tuple-element.35), channel_id=1, source_target_pairs={{1,2},{0,31},{3,4},{2,1},{5,6},{4,3},{7,8},{6,5},{9,10},{8,7},{11,... | collective-permute-start | bytes 393224 | tf_op jit(solution)/shard_map/ppermute | solution.py:580
  9.0 0.0 collective-permute-start.2
  9.0 1.6 %collective-permute-start.3 = (f32[64,128]{1,0:T(8,128)S(1)}, f32[64,128]{1,0:T(8,128)S(1)}, u32[]{:S(2)}, u32[]{:S(2)}) collective-permute-start(f32[64,128]{1,0:T(8,128)S(1)} %get-tuple-element.37), channel_id=1, source_target_pairs={{0,2},{1,3},{2,4},{3,5},{4,6},{5,7},{6,0},{7,1},{8,10},{9,11},{10,... | collective-permute-start | bytes 98312 | tf_op jit(solution)/shard_map/ppermute | solution.py:580
  10.6 0.0 collective-permute-done.4.swap
  10.6 0.7 %start_inner.1 = (f32[3,128,128]{2,1,0:T(8,128)S(1)}, f32[3,128,128]{2,1,0:T(8,128)S(1)}, f32[3,128,128]{2,1,0:T(8,128)S(1)}, f32[12,128,128]{2,1,0:T(8,128)S(1)}, f32[3,128,128]{2,1,0:T(8,128)S(1)}) custom-call(f32[11,64,128]{2,1,0:T(8,128)S(1)} %get-tuple-element.38.own, f32[11,64,128]{2,1,0:T(8,128)S(1)} %collective-permute-done.4.swap), custom_call_target="tpu_custom_call" | custom-call | flops 10000000 | bytes 4000000 | tf_op jit(solution)/shard_map/start_inner/pallas_call | solution.py:600
  11.4 3.3 %collective-permute-done.2.refs_2_ = f32[64,128]{1,0:T(8,128)S(1)} collective-permute-done((f32[64,128]{1,0:T(8,128)S(1)}, f32[64,128]{1,0:T(8,128)S(1)}, u32[]{:S(2)}, u32[]{:S(2)}) %collective-permute-start.2) | collective-permute-done | bytes 32800 | tf_op jit(solution)/shard_map/ppermute | solution.py:580
  14.7 0.5 collective-permute-done.3.refs_3_
  15.2 0.0 collective-permute-done.refs_0_
  15.2 0.6 collective-permute-done.1.refs_1_
  15.8 1.5 %start_outer.1 = (f32[3,128,128]{2,1,0:T(8,128)S(1)}, f32[3,128,128]{2,1,0:T(8,128)S(1)}, f32[128,128]{1,0:T(8,128)S(1)}, f32[128,128]{1,0:T(8,128)S(1)}, f32[12...) custom-call(f32[4,64,128]{2,1,0:T(8,128)S(1)} %collective-permute-done.refs_0_, ...), custom_call_target="tpu_custom_call" | custom-call | tf_op jit(solution)/shard_map/start_outer/pallas_call | solution.py:607
  17.3 0.1 collective-permute-start.6
  17.4 0.7 %collective-permute-start.5 = (f32[3,128,128]{2,1,0:T(8,128)S(1)}, f32[3,128,128]{2,1,0:T(8,128)S(1)}, u32[]{:S(2)}, u32[]{:S(2)}) collective-permute-start(f32[3,128,128]{2,1,0:T(8,128)S(1)} %get-tuple-element.45.v1), channel_id=1, source_target_pairs={{1,2},{3,4},{2,1},{5,6},{4,3},{7,8},{6,5},{9,10},{8,7},{11,12},{10... | collective-permute-start | bytes 589832 | tf_op jit(solution)/shard_map/ppermute | solution.py:580
  18.1 0.7 %collective-permute-done.6.inner.v1_inner = f32[3,128,128]{2,1,0:T(8,128)S(1)} collective-permute-done((f32[3,128,128]{2,1,0:T(8,128)S(1)}, f32[3,128,128]{2,1,0:T(8,128)S(1)}, u32[]{:S(2)}, u32[]{:S(2)}) %collective-permute-start.6) | collective-permute-done | bytes 196640 | tf_op jit(solution)/shard_map/ppermute | solution.py:580
  18.8 0.4 second_inner.1.fields
  19.3 0.0 collective-permute-done.5.outer
  19.3 1.1 %second_outer.1 = (f32[3,128,128]{2,1,0:T(8,128)S(1)}, f32[3,128,128]{2,1,0:T(8,128)S(1)}, f32[8,128]{1,0:T(8,128)S(1)}) custom-call(f32[3,128,128]{2,1,0:T(8,128)S(1)} %get-tuple-element.45.v1, f32[3,128,128]{2,1,0:T(8,128)S(1)} %collective-permute-done.5.outer, f32[3,128,128]{2,1,0:T(8,128)S(1)} %collective-permute-done.6.inner.v1_inner, ...), custom_call_target="tpu_custom_call" | custom-call | tf_op jit(solution)/shard_map/second_outer/pallas_call | solution.py:616
  20.4 5.9 %collective-permute-start.8 = (f32[3,128,128]{2,1,0:T(8,128)S(1)}, f32[3,128,128]{2,1,0:T(8,128)S(1)}, u32[]{:S(2)}, u32[]{:S(2)}) collective-permute-start(f32[3,128,128]{2,1,0:T(8,128)S(1)} %get-tuple-element.49.v2), channel_id=1, source_target_pairs={{0,1},{1,0},{2,3},{3,2},{4,5},{5,4},{6,7},{7,6},{8,9},{9,8},{10,11... | collective-permute-start | bytes 589832 | tf_op jit(solution)/shard_map/ppermute | solution.py:580
  26.3 0.7 %collective-permute-start.7 = (f32[3,128,128]{2,1,0:T(8,128)S(1)}, f32[3,128,128]{2,1,0:T(8,128)S(1)}, u32[]{:S(2)}, u32[]{:S(2)}) collective-permute-start(f32[3,128,128]{2,1,0:T(8,128)S(1)} %get-tuple-element.49.v2), channel_id=1, source_target_pairs={{2,1},{4,3},{6,5},{8,7},{10,9},{12,11},{14,13},{16,15},{18,17},{20... | collective-permute-start | bytes 589832 | tf_op jit(solution)/shard_map/ppermute | solution.py:580
  27.0 0.4 collective-permute-done.8.v2_inner
  27.4 0.0 collective-permute-done.7.v2_outer
  27.4 0.5 third.1
  27.9 23.1 %all_to_all.5.gathered = f32[32,8,128]{2,1,0:T(8,128)S(1)} all-to-all(f32[32,8,128]{2,1,0:T(8,128)S(1)} %broadcast_in_dim.3), channel_id=1, replica_groups=mesh['mod'=4,'slab'=4,'sub'=2] {'mod','slab','sub'}, dimensions={0} | all-to-all | bytes 262144 | tf_op jit(solution)/shard_map/all_to_all | solution.py:625
  51.0 0.7 %combine.1 = (f32[128,128]{1,0:T(8,128)S(1)}, f32[3,8,128]{2,1,0:T(8,128)S(1)}) custom-call(f32[32,8,128]{2,1,0:T(8,128)S(1)} %all_to_all.5.gathered, f32[3,128,128]{2,1,0:T(8,128)S(1)} %get-tuple-element.40.refs_4_.v0, f32[3,128,128]{2,1,0:T(8,128)S(1)} %get-tuple-element.53.v0_high, f32[3,128,128]{2,1,0:T(8,128)S(1)} %get-tuple-element.45.v1, ...), custom_call_target="tpu_custom_call" | custom-call | tf_op jit(solution)/shard_map/combine/pallas_call | solution.py:628
  51.7 1.0 %collective-permute-start.11 = (f32[128,128]{1,0:T(8,128)S(1)}, f32[128,128]{1,0:T(8,128)S(1)}, u32[]{:S(2)}, u32[]{:S(2)}) collective-permute-start(f32[128,128]{1,0:T(8,128)S(1)} %get-tuple-element.57.refs_0_), channel_id=1, source_target_pairs={{0,24},{8,16},{16,8},{24,0},{1,25},{9,17},{17,9},{25,1},{2,26},{10... | collective-permute-start | bytes 196616 | tf_op jit(solution)/shard_map/ppermute | solution.py:631
  52.8 1.3 %collective-permute-start.10 = (f32[128,128]{1,0:T(8,128)S(1)}, f32[128,128]{1,0:T(8,128)S(1)}, u32[]{:S(2)}, u32[]{:S(2)}) collective-permute-start(f32[128,128]{1,0:T(8,128)S(1)} %get-tuple-element.57.refs_0_), channel_id=1, source_target_pairs={{0,16},{8,24},{16,0},{24,8},{1,17},{9,25},{17,1},{25,9},{2,18},{10... | collective-permute-start | bytes 196616 | tf_op jit(solution)/shard_map/ppermute | solution.py:631
  54.1 1.2 %collective-permute-start.9 = (f32[128,128]{1,0:T(8,128)S(1)}, f32[128,128]{1,0:T(8,128)S(1)}, u32[]{:S(2)}, u32[]{:S(2)}) collective-permute-start(f32[128,128]{1,0:T(8,128)S(1)} %get-tuple-element.57.refs_0_), channel_id=1, source_target_pairs={{0,8},{8,0},{16,24},{24,16},{1,9},{9,1},{17,25},{25,17},{2,10},{10... | collective-permute-start | bytes 196616 | tf_op jit(solution)/shard_map/ppermute | solution.py:631
  55.3 2.3 %collective-permute-done.11.refs_3_ = f32[128,128]{1,0:T(8,128)S(1)} collective-permute-done((f32[128,128]{1,0:T(8,128)S(1)}, f32[128,128]{1,0:T(8,128)S(1)}, u32[]{:S(2)}, u32[]{:S(2)}) %collective-permute-start.11) | collective-permute-done | bytes 65568 | tf_op jit(solution)/shard_map/ppermute | solution.py:631
  57.6 0.2 collective-permute-done.10.refs_2_
  57.8 0.5 collective-permute-done.9.refs_1_
  58.4 0.1 collective-permute-start.12
  58.4 1.0 %collective-permute-start.13 = (f32[72,128]{1,0:T(8,128)S(1)}, f32[72,128]{1,0:T(8,128)S(1)}, u32[]{:S(2)}, u32[]{:S(2)}) collective-permute-start(f32[72,128]{1,0:T(8,128)S(1)} %get-tuple-element.64), channel_id=1, source_target_pairs={{0,6},{1,3},{2,0},{3,5},{4,2},{5,7},{6,4},{7,1},{8,14},{9,11},{10,... | collective-permute-start | bytes 110600 | tf_op jit(solution)/shard_map/ppermute | solution.py:580
  59.4 0.0 collective-permute-start.14
  59.4 0.7 %displace.1 = f32[3,2,64,128]{3,2,1,0:T(8,128)} custom-call(f32[3,8,128]{2,1,0:T(8,128)S(1)} %get-tuple-element.60.factors, f32[3,128,128]{2,1,0:T(8,128)S(1)} %get-tuple-element.40.refs_4_.v0, f32[3,128,128]{2,1,0:T(8,128)S(1)} %get-tuple-element.41.refs_5_.v0_inner, f32[3,128,128]{2,1,0:T(8,128)S(1)} %get-tuple-element.45.v1, ...), custom_call_target="tpu_custom_call" | custom-call | flops 10000000 | bytes 4000000 | tf_op jit(solution)/shard_map/displace/pallas_call | solution.py:632
  60.2 3.5 %collective-permute-done.12.outer = f32[72,128]{1,0:T(8,128)S(1)} collective-permute-done((f32[72,128]{1,0:T(8,128)S(1)}, f32[72,128]{1,0:T(8,128)S(1)}, u32[]{:S(2)}, u32[]{:S(2)}) %collective-permute-start.12) | collective-permute-done | bytes 36896 | tf_op jit(solution)/shard_map/ppermute | solution.py:580
  63.6 0.0 collective-permute-done.13.far
  63.6 0.0 collective-permute-done.14.partner
  63.6 0.9 %gradient.1 = f32[2,64,128]{2,1,0:T(8,128)} custom-call(f32[128,128]{1,0:T(8,128)S(1)} %get-tuple-element.62.scaled, f32[72,128]{1,0:T(8,128)S(1)} %collective-permute-done.12.outer, f32[72,128]{1,0:T(8,128)S(1)} %collective-permute-done.13.far, f32[72,128]{1,0:T(8,128)S(1)} %collective-permute-done.14.partner), custom_call_target="tpu_custom_call" | custom-call | tf_op jit(solution)/shard_map/gradient/pallas_call | solution.py:643
  (2 shorter events, 0.0 us)
Async XLA Ops:
  0.6 1.0 %copy-start = (s32[3,2,64,128]{3,2,1,0:T(8,128)S(1)}, s32[3,2,64,128]{3,2,1,0:T(8,128)}, u32[]{:S(2)}) copy-start(s32[3,2,64,128]{3,2,1,0:T(8,128)} %load.1) | copy-start | bytes 589828
  0.6 1.0 %copy-start.1 = (f32[2,64,128]{2,1,0:T(8,128)S(1)}, f32[2,64,128]{2,1,0:T(8,128)}, u32[]{:S(2)}) copy-start(f32[2,64,128]{2,1,0:T(8,128)} %design.1) | copy-start | bytes 196612
  1.7 8.9 %collective-permute-start.4 = (f32[11,64,128]{2,1,0:T(8,128)S(1)}, f32[11,64,128]{2,1,0:T(8,128)S(1)}, u32[]{:S(2)}, u32[]{:S(2)}) collective-permute-start(f32[11,64,128]{2,1,0:T(8,128)S(1)} %get-tuple-element.39), channel_id=1, source_target_pairs={{0,1},{1,0},{2,3},{3,2},{4,5},{5,4},{6,7},{7,6},{8,9},{9,8},{10,11... | collective-permute-start | bytes 1081352 | tf_op jit(solution)/shard_map/ppermute | solution.py:580
  2.3 12.9 %collective-permute-start = (f32[4,64,128]{2,1,0:T(8,128)S(1)}, f32[4,64,128]{2,1,0:T(8,128)S(1)}, u32[]{:S(2)}, u32[]{:S(2)}) collective-permute-start(f32[4,64,128]{2,1,0:T(8,128)S(1)} %get-tuple-element.34), channel_id=1, source_target_pairs={{0,2},{1,31},{2,4},{3,1},{4,6},{5,3},{6,8},{7,5},{8,10},{9,7},{10,... | collective-permute-start | bytes 393224 | tf_op jit(solution)/shard_map/ppermute | solution.py:580
  4.9 10.9 %collective-permute-start.1 = (f32[4,64,128]{2,1,0:T(8,128)S(1)}, f32[4,64,128]{2,1,0:T(8,128)S(1)}, u32[]{:S(2)}, u32[]{:S(2)}) collective-permute-start(f32[4,64,128]{2,1,0:T(8,128)S(1)} %get-tuple-element.35), channel_id=1, source_target_pairs={{1,2},{0,31},{3,4},{2,1},{5,6},{4,3},{7,8},{6,5},{9,10},{8,7},{11,... | collective-permute-start | bytes 393224 | tf_op jit(solution)/shard_map/ppermute | solution.py:580
  9.0 5.7 %collective-permute-start.2 = (f32[64,128]{1,0:T(8,128)S(1)}, f32[64,128]{1,0:T(8,128)S(1)}, u32[]{:S(2)}, u32[]{:S(2)}) collective-permute-start(f32[64,128]{1,0:T(8,128)S(1)} %get-tuple-element.36), channel_id=1, source_target_pairs={{0,3},{1,2},{2,5},{3,4},{4,7},{5,6},{6,1},{7,0},{8,11},{9,10},{10,... | collective-permute-start | bytes 98312 | tf_op jit(solution)/shard_map/ppermute | solution.py:580
  9.0 6.2 %collective-permute-start.3 = (f32[64,128]{1,0:T(8,128)S(1)}, f32[64,128]{1,0:T(8,128)S(1)}, u32[]{:S(2)}, u32[]{:S(2)}) collective-permute-start(f32[64,128]{1,0:T(8,128)S(1)} %get-tuple-element.37), channel_id=1, source_target_pairs={{0,2},{1,3},{2,4},{3,5},{4,6},{5,7},{6,0},{7,1},{8,10},{9,11},{10,... | collective-permute-start | bytes 98312 | tf_op jit(solution)/shard_map/ppermute | solution.py:580
  17.3 1.5 %collective-permute-start.6 = (f32[3,128,128]{2,1,0:T(8,128)S(1)}, f32[3,128,128]{2,1,0:T(8,128)S(1)}, u32[]{:S(2)}, u32[]{:S(2)}) collective-permute-start(f32[3,128,128]{2,1,0:T(8,128)S(1)} %get-tuple-element.45.v1), channel_id=1, source_target_pairs={{0,1},{1,0},{2,3},{3,2},{4,5},{5,4},{6,7},{7,6},{8,9},{9,8},{10,11... | collective-permute-start | bytes 589832 | tf_op jit(solution)/shard_map/ppermute | solution.py:580
  17.4 1.9 %collective-permute-start.5 = (f32[3,128,128]{2,1,0:T(8,128)S(1)}, f32[3,128,128]{2,1,0:T(8,128)S(1)}, u32[]{:S(2)}, u32[]{:S(2)}) collective-permute-start(f32[3,128,128]{2,1,0:T(8,128)S(1)} %get-tuple-element.45.v1), channel_id=1, source_target_pairs={{1,2},{3,4},{2,1},{5,6},{4,3},{7,8},{6,5},{9,10},{8,7},{11,12},{10... | collective-permute-start | bytes 589832 | tf_op jit(solution)/shard_map/ppermute | solution.py:580
  20.4 7.0 %collective-permute-start.8 = (f32[3,128,128]{2,1,0:T(8,128)S(1)}, f32[3,128,128]{2,1,0:T(8,128)S(1)}, u32[]{:S(2)}, u32[]{:S(2)}) collective-permute-start(f32[3,128,128]{2,1,0:T(8,128)S(1)} %get-tuple-element.49.v2), channel_id=1, source_target_pairs={{0,1},{1,0},{2,3},{3,2},{4,5},{5,4},{6,7},{7,6},{8,9},{9,8},{10,11... | collective-permute-start | bytes 589832 | tf_op jit(solution)/shard_map/ppermute | solution.py:580
  26.3 1.1 %collective-permute-start.7 = (f32[3,128,128]{2,1,0:T(8,128)S(1)}, f32[3,128,128]{2,1,0:T(8,128)S(1)}, u32[]{:S(2)}, u32[]{:S(2)}) collective-permute-start(f32[3,128,128]{2,1,0:T(8,128)S(1)} %get-tuple-element.49.v2), channel_id=1, source_target_pairs={{2,1},{4,3},{6,5},{8,7},{10,9},{12,11},{14,13},{16,15},{18,17},{20... | collective-permute-start | bytes 589832 | tf_op jit(solution)/shard_map/ppermute | solution.py:580
  51.7 5.9 %collective-permute-start.11 = (f32[128,128]{1,0:T(8,128)S(1)}, f32[128,128]{1,0:T(8,128)S(1)}, u32[]{:S(2)}, u32[]{:S(2)}) collective-permute-start(f32[128,128]{1,0:T(8,128)S(1)} %get-tuple-element.57.refs_0_), channel_id=1, source_target_pairs={{0,24},{8,16},{16,8},{24,0},{1,25},{9,17},{17,9},{25,1},{2,26},{10... | collective-permute-start | bytes 196616 | tf_op jit(solution)/shard_map/ppermute | solution.py:631
  52.8 5.1 %collective-permute-start.10 = (f32[128,128]{1,0:T(8,128)S(1)}, f32[128,128]{1,0:T(8,128)S(1)}, u32[]{:S(2)}, u32[]{:S(2)}) collective-permute-start(f32[128,128]{1,0:T(8,128)S(1)} %get-tuple-element.57.refs_0_), channel_id=1, source_target_pairs={{0,16},{8,24},{16,0},{24,8},{1,17},{9,25},{17,1},{25,9},{2,18},{10... | collective-permute-start | bytes 196616 | tf_op jit(solution)/shard_map/ppermute | solution.py:631
  54.1 4.3 %collective-permute-start.9 = (f32[128,128]{1,0:T(8,128)S(1)}, f32[128,128]{1,0:T(8,128)S(1)}, u32[]{:S(2)}, u32[]{:S(2)}) collective-permute-start(f32[128,128]{1,0:T(8,128)S(1)} %get-tuple-element.57.refs_0_), channel_id=1, source_target_pairs={{0,8},{8,0},{16,24},{24,16},{1,9},{9,1},{17,25},{25,17},{2,10},{10... | collective-permute-start | bytes 196616 | tf_op jit(solution)/shard_map/ppermute | solution.py:631
  58.4 5.2 %collective-permute-start.12 = (f32[72,128]{1,0:T(8,128)S(1)}, f32[72,128]{1,0:T(8,128)S(1)}, u32[]{:S(2)}, u32[]{:S(2)}) collective-permute-start(f32[72,128]{1,0:T(8,128)S(1)} %get-tuple-element.63), channel_id=1, source_target_pairs={{1,2},{0,7},{3,4},{2,1},{5,6},{4,3},{7,0},{6,5},{9,10},{8,15},{11,... | collective-permute-start | bytes 110600 | tf_op jit(solution)/shard_map/ppermute | solution.py:580
  58.4 5.2 %collective-permute-start.13 = (f32[72,128]{1,0:T(8,128)S(1)}, f32[72,128]{1,0:T(8,128)S(1)}, u32[]{:S(2)}, u32[]{:S(2)}) collective-permute-start(f32[72,128]{1,0:T(8,128)S(1)} %get-tuple-element.64), channel_id=1, source_target_pairs={{0,6},{1,3},{2,0},{3,5},{4,2},{5,7},{6,4},{7,1},{8,14},{9,11},{10,... | collective-permute-start | bytes 110600 | tf_op jit(solution)/shard_map/ppermute | solution.py:580
  59.4 4.2 %collective-permute-start.14 = (f32[72,128]{1,0:T(8,128)S(1)}, f32[72,128]{1,0:T(8,128)S(1)}, u32[]{:S(2)}, u32[]{:S(2)}) collective-permute-start(f32[72,128]{1,0:T(8,128)S(1)} %get-tuple-element.65), channel_id=1, source_target_pairs={{0,1},{1,0},{2,3},{3,2},{4,5},{5,4},{6,7},{7,6},{8,9},{9,8},{10,11... | collective-permute-start | bytes 110600 | tf_op jit(solution)/shard_map/ppermute | solution.py:580

commit v12 on v11

--- a/solution.py
+++ b/solution.py
@@ -369,7 +369,8 @@
 
 
 def second_outer_kernel(
-    v1, outer, inner, fields, free, mod_inner, mod_outer, before, v2, v1_high, moments
+    v1, outer, inner, fields, free, mod_inner, mod_outer, before,
+    v2, v1_high, moments, window, upper,
 ):
     sub = lax.axis_index("sub")
     count = v1.shape[1]
@@ -382,29 +383,48 @@
     moments[...] = before[...] + jnp.concatenate(
         [zero, line(cross), line(square), zero], axis=0
     )
-
-
-def third_kernel(v2_outer, v2_inner, v2, mod_own, before, moments, v2_high):
-    even = lax.axis_index("sub") == 0
-    for k in range(3):
-        v2_high[k] = jnp.where(even, v2_inner[k], v2_outer[k])
-    count = v2.shape[1]
-    total = [jnp.zeros((ROWS, v2.shape[2]), jnp.float32)]
-
-    def use(y0, energy):
-        total[0] += energy * mod_own[pl.ds(y0, ROWS), :]
-
-    energy_loop(
-        count,
-        lambda k, y: v2[k, pl.ds(y, ROWS), :],
-        lambda k, y: v2_high[k, pl.ds(y, ROWS), :],
-        use,
-    )
-    width = v2.shape[2]
+    size, half = window.shape[1], upper.shape[1]
+    for k in range(3):
+        window[k] = v2[k, pl.ds(pl.multiple_of(sub * (count - size), 8), size), :]
+        upper[k] = v2[k, pl.ds(count - half, half), :]
+
+
+def third_kernel(mods, slabs, outer, inner, v2, mod_own, mod_outer, before, moments):
+    mod, slab, sub = (lax.axis_index(a) for a in AXES)
+    even = sub == 0
+    ends = (mod == mods - 1) & (slab == slabs - 1) & (sub == 1)
+    count, width = v2.shape[1:]
+    half = count // 2
+    shift = count - outer.shape[1]
+    upper_part = jnp.where(even | ends, 1.0, 0.0)
+    outer_part = jnp.where(even, 1.0, 0.0)
+
+    def above(k, y):
+        beyond = outer[k, pl.ds(y, ROWS), :] if y < half + ROWS - 1 else jnp.zeros((ROWS, width))
+        return jnp.where(even, inner[k, pl.ds(y, ROWS), :], beyond)
+
+    def above_upper(k, y):
+        return jnp.where(even, inner[k, pl.ds(y, ROWS), :], 0.0)
+
+    def below(k, y):
+        return outer[k, pl.ds(y - shift, ROWS), :]
+
+    total = jnp.zeros((ROWS, width), jnp.float32)
+    for y0 in range(0, count, ROWS):
+        part = pl.ds(y0, ROWS)
+        lower_half = y0 < half
+        _, own = layer_modes(rows_of(v2), y0, count)
+        _, high = layer_modes(above if lower_half else above_upper, y0, count)
+        energy = element_energy(element_modes(own, high, 1.0)) * mod_own[part, :]
+        total += energy if lower_half else energy * upper_part
+        if not lower_half:
+            _, low = layer_modes(below, y0, count)
+            energy = element_energy(element_modes(low, own, 1.0)) * mod_outer[part, :]
+            total += energy * outer_part
     moments[...] = before[...] + jnp.concatenate(
         [
             jnp.zeros((5, width), jnp.float32),
-            line(total[0]),
+            line(total),
             jnp.zeros((2, width), jnp.float32),
         ],
         axis=0,
@@ -441,16 +461,25 @@
 
 
 def combine_kernel(
-    gathered, v0, v0_high, v1, v1_high, v2, v2_high, slope_factor, slope, factors, own, high
+    gathered, v0, v0_high, v1, v1_high, v2, v2_outer, v2_inner, v2_upper, slope_factor,
+    slope, factors,
+    own, high,
 ):
+    even = lax.axis_index("sub") == 0
     count = v0.shape[1]
+    half = count // 2
     sums = jnp.sum(jnp.sum(gathered[...], axis=0), axis=1, keepdims=True)
     c0, c1, c2 = coefficients([sums[k : k + 1] for k in range(6)])
     for n, c in enumerate((c0, c1, c2)):
         factors[n] = jnp.broadcast_to(c, factors.shape[1:])
     for k in range(3):
         own[k] = c0 * v0[k] + c1 * v1[k] + c2 * v2[k]
-        high[k] = c0 * v0_high[k] + c1 * v1_high[k] + c2 * v2_high[k]
+        for part, beyond in (
+            (pl.ds(0, half), v2_outer[k, pl.ds(0, half), :]),
+            (pl.ds(half, half), v2_upper[k]),
+        ):
+            third = jnp.where(even, v2_inner[k, part, :], beyond)
+            high[k, part, :] = c0 * v0_high[k, part, :] + c1 * v1_high[k, part, :] + c2 * third
 
     def use(y0, energy):
         slope[pl.ds(y0, ROWS), :] = slope_factor[pl.ds(y0, ROWS), :] * energy
@@ -613,13 +642,21 @@
     outer = move(v1, "outer")
     inner = move(v1, "swap")
     (fields,) = call(second_inner_kernel, [(12,) + plane], name="second_inner", work=True)(v1, inner)
-    v2, v1_high, moments = call(
-        second_outer_kernel, [layer, layer, (8, width)], name="second_outer"
+    window = half + 8
+    v2, v1_high, moments, v2_window, v2_upper = call(
+        second_outer_kernel,
+        [layer, layer, (8, width), (3, window, width), (3, half, width)],
+        name="second_outer",
     )(v1, outer, inner, fields, free, mod_inner, mod_outer, moments)
-    v2_outer = move(v2, "down")
+    v2_outer = move(v2_window, "outer")
     v2_inner = move(v2, "swap")
-    moments, v2_high = call(third_kernel, [(8, width), layer], name="third")(
-        v2_outer, v2_inner, v2, mod_own, moments
+    v2_upper = move(v2_upper, "down")
+
+    def third_body(*refs):
+        third_kernel(mods, slabs, *refs)
+
+    (moments,) = call(third_body, [(8, width)], name="third")(
+        v2_outer, v2_inner, v2, mod_own, mod_outer, moments
     )
     devices = 2 * mods * slabs
     gathered = lax.all_to_all(
@@ -627,7 +664,7 @@
     )
     slope, factors = call(
         combine_kernel, [plane, (3, 8, width)], [layer, layer], name="combine"
-    )(gathered, v0, v0_high, v1, v1_high, v2, v2_high, slope_factor)
+    )(gathered, v0, v0_high, v1, v1_high, v2, v2_outer, v2_inner, v2_upper, slope_factor)
     slopes = [slope] + [lax.ppermute(slope, "mod", pairs) for pairs in module_routes(mods)]
     (displacement,) = call(displace_kernel, [(3, 2, half, width)], name="displace", work=True)(
         factors, v0, v0_inner, v1, inner, v2, v2_inner

time: 64.7 us -> 67.5 us (1.043)
  blocking collectives: 23.1 us -> 0 us
  starting transfers between devices: 20.8 us -> 38.7 us
  waiting for transfers between devices: 12.1 us -> 19.3 us
    all_to_all x1 -> x0, blocking collectives: 23.1 us -> none  [local(): lax.all_to_all(jnp.broadcast_to(moments, (devices, 8, width)), AXES, 0, 0...]
    all_to_all x0 -> x1, starting transfers between devices: none -> 14.2 us  [local(): lax.all_to_all(jnp.broadcast_to(moments, (devices, 8, width)), AXES, 0, 0...]
    all_to_all x0 -> x1, waiting for transfers between devices: none -> 7.49 us  [local(): lax.all_to_all(jnp.broadcast_to(moments, (devices, 8, width)), AXES, 0, 0...]
    ppermute x12 -> x13, starting transfers between devices: 17.2 us -> 20.9 us  [move(): return lax.ppermute(value, AXES, path[name])]
    ppermute x12 -> x13, waiting for transfers between devices: 9.03 us -> 8.78 us  [move(): return lax.ppermute(value, AXES, path[name])]
  transfers between devices with their start and end apart: 15 -> 17, of which waited for: 9 -> 11; matrix products, arithmetic and copies ran while one was open for 0% -> 0% of each run, Pallas kernels for 3% -> 3%
where the time goes in v12:
time: 67.5 us; the launch traced here: 67.3 us
  starting transfers between devices  38.7 us (57%)
  waiting for transfers between devices  19.3 us (29%)
  Pallas kernels  6.83 us (10%)
  other arithmetic  0.99 us (1%)
  between operations  0.77 us (1%)
  local copies, waits for them, and re-layouts  0.69 us (1%)
    ppermute x13, starting transfers between devices, move(): return lax.ppermute(value, AXES, path[name])  20.9 us
    all_to_all x1, starting transfers between devices, local(): lax.all_to_all(jnp.broadcast_to(moments, (devices, 8, width)), AXES, 0, 0...  14.2 us
    ppermute x13, waiting for transfers between devices, move(): return lax.ppermute(value, AXES, path[name])  8.78 us
    all_to_all x1, waiting for transfers between devices, local(): lax.all_to_all(jnp.broadcast_to(moments, (devices, 8, width)), AXES, 0, 0...  7.49 us
    ppermute x3, starting transfers between devices, local(): lax.ppermute(slope, 'mod', pairs)  3.55 us
    ppermute x3, waiting for transfers between devices, local(): lax.ppermute(slope, 'mod', pairs)  3.06 us
    pallas_call x1, Pallas kernels, local(): call(start_body, [layer, layer, plane, plane, plane, plane, plane, (8, wi...  1.54 us
  transfers between devices with their start and end apart: 17, of which 11 were waited for; matrix products, arithmetic and copies ran while one was open for 0% of the time, Pallas kernels for 3%

profile of v12, /device:TPU:0, one launch (start us, length us, event | category | flops | bytes accessed | tf_op | source)
XLA Modules:
  0.0 67.3 jit_solution(4213019587760137402)
XLA Ops:
  0.6 0.0 copy-start
  0.6 1.0 %subtract_convert_fusion.free = f32[3,2,64,128]{3,2,1,0:T(8,128)S(1)} fusion(s32[3,2,64,128]{3,2,1,0:T(8,128)} %param.4), kind=kLoop, calls=%fused_computation | loop fusion | flops 98304 | bytes 393216 | tf_op jit(solution)/shard_map/convert_element_type | solution.py:614
  1.6 0.0 copy-done
  1.7 0.0 copy-done.1
  1.7 0.1 prepare.1
  1.7 0.5 collective-permute-start.4
  2.3 2.6 %collective-permute-start = (f32[4,64,128]{2,1,0:T(8,128)S(1)}, f32[4,64,128]{2,1,0:T(8,128)S(1)}, u32[]{:S(2)}, u32[]{:S(2)}) collective-permute-start(f32[4,64,128]{2,1,0:T(8,128)S(1)} %get-tuple-element.34), channel_id=1, source_target_pairs={{0,2},{1,31},{2,4},{3,1},{4,6},{5,3},{6,8},{7,5},{8,10},{9,7},{10,... | collective-permute-start | bytes 393224 | tf_op jit(solution)/shard_map/ppermute | solution.py:609
  4.9 4.1 %collective-permute-start.1 = (f32[4,64,128]{2,1,0:T(8,128)S(1)}, f32[4,64,128]{2,1,0:T(8,128)S(1)}, u32[]{:S(2)}, u32[]{:S(2)}) collective-permute-start(f32[4,64,128]{2,1,0:T(8,128)S(1)} %get-tuple-element.35), channel_id=1, source_target_pairs={{1,2},{0,31},{3,4},{2,1},{5,6},{4,3},{7,8},{6,5},{9,10},{8,7},{11,... | collective-permute-start | bytes 393224 | tf_op jit(solution)/shard_map/ppermute | solution.py:609
  9.0 0.0 collective-permute-start.2
  9.0 1.6 %collective-permute-start.3 = (f32[64,128]{1,0:T(8,128)S(1)}, f32[64,128]{1,0:T(8,128)S(1)}, u32[]{:S(2)}, u32[]{:S(2)}) collective-permute-start(f32[64,128]{1,0:T(8,128)S(1)} %get-tuple-element.37), channel_id=1, source_target_pairs={{0,2},{1,3},{2,4},{3,5},{4,6},{5,7},{6,0},{7,1},{8,10},{9,11},{10,... | collective-permute-start | bytes 98312 | tf_op jit(solution)/shard_map/ppermute | solution.py:609
  10.6 0.0 collective-permute-done.4.swap
  10.6 0.7 %start_inner.1 = (f32[3,128,128]{2,1,0:T(8,128)S(1)}, f32[3,128,128]{2,1,0:T(8,128)S(1)}, f32[3,128,128]{2,1,0:T(8,128)S(1)}, f32[12,128,128]{2,1,0:T(8,128)S(1)}, f32[3,128,128]{2,1,0:T(8,128)S(1)}) custom-call(f32[11,64,128]{2,1,0:T(8,128)S(1)} %get-tuple-element.38.own, f32[11,64,128]{2,1,0:T(8,128)S(1)} %collective-permute-done.4.swap), custom_call_target="tpu_custom_call" | custom-call | flops 10000000 | bytes 4000000 | tf_op jit(solution)/shard_map/start_inner/pallas_call | solution.py:629
  11.4 3.3 %collective-permute-done.2.refs_2_ = f32[64,128]{1,0:T(8,128)S(1)} collective-permute-done((f32[64,128]{1,0:T(8,128)S(1)}, f32[64,128]{1,0:T(8,128)S(1)}, u32[]{:S(2)}, u32[]{:S(2)}) %collective-permute-start.2) | collective-permute-done | bytes 32800 | tf_op jit(solution)/shard_map/ppermute | solution.py:609
  14.7 0.5 collective-permute-done.3.refs_3_
  15.2 0.0 collective-permute-done.refs_0_
  15.2 0.6 collective-permute-done.1.refs_1_
  15.8 1.5 %start_outer.1 = (f32[3,128,128]{2,1,0:T(8,128)S(1)}, f32[3,128,128]{2,1,0:T(8,128)S(1)}, f32[128,128]{1,0:T(8,128)S(1)}, f32[128,128]{1,0:T(8,128)S(1)}, f32[12...) custom-call(f32[4,64,128]{2,1,0:T(8,128)S(1)} %collective-permute-done.refs_0_, ...), custom_call_target="tpu_custom_call" | custom-call | tf_op jit(solution)/shard_map/start_outer/pallas_call | solution.py:636
  17.3 0.1 collective-permute-start.6
  17.4 0.7 collective-permute-start.5
  18.1 0.7 %collective-permute-done.6.inner.v1_inner = f32[3,128,128]{2,1,0:T(8,128)S(1)} collective-permute-done((f32[3,128,128]{2,1,0:T(8,128)S(1)}, f32[3,128,128]{2,1,0:T(8,128)S(1)}, u32[]{:S(2)}, u32[]{:S(2)}) %collective-permute-start.6) | collective-permute-done | bytes 196640 | tf_op jit(solution)/shard_map/ppermute | solution.py:609
  18.8 0.4 second_inner.1.fields
  19.3 0.0 collective-permute-done.5.outer
  19.3 1.1 %second_outer.1 = (f32[3,128,128]{2,1,0:T(8,128)S(1)}, f32[3,128,128]{2,1,0:T(8,128)S(1)}, f32[8,128]{1,0:T(8,128)S(1)}, f32[3,72,128]{2,1,0:T(8,128)S(1)}, f32[3,64,128]{2,1,0:T(8,128)S(1)}) custom-call(f32[3,128,128]{2,1,0:T(8,128)S(1)} %get-tuple-element.45.v1, f32[3,128,128]{2,1,0:T(8,128)S(1)} %collective-permute-done.5.outer, ...), custom_call_target="tpu_custom_call" | custom-call | tf_op jit(solution)/shard_map/second_outer/pallas_call | solution.py:646
  20.4 5.9 %collective-permute-start.8 = (f32[3,128,128]{2,1,0:T(8,128)S(1)}, f32[3,128,128]{2,1,0:T(8,128)S(1)}, u32[]{:S(2)}, u32[]{:S(2)}) collective-permute-start(f32[3,128,128]{2,1,0:T(8,128)S(1)} %get-tuple-element.50.refs_2_.v2), channel_id=1, source_target_pairs={{0,1},{1,0},{2,3},{3,2},{4,5},{5,4},{6,7},{7,6},{8,9},{9,8},{10,11... | collective-permute-start | bytes 589832 | tf_op jit(solution)/shard_map/ppermute | solution.py:609
  26.3 0.7 collective-permute-start.7
  27.0 0.0 collective-permute-done.7.refs_0_.v2_outer
  27.0 0.4 collective-permute-done.8.refs_1_.v2_inner
  27.4 0.6 third.1
  28.0 0.7 broadcast_in_dim.3
  28.7 14.2 %all-to-all-start = ((f32[32,8,128]{2,1,0:T(8,128)}), f32[32,8,128]{2,1,0:T(8,128)S(1)}, u32[]{:S(2)}, u32[]{:S(2)}) async-start(f32[32,8,128]{2,1,0:T(8,128)} %broadcast_in_dim.3), calls=%async_computation | async-start | bytes 262144 | tf_op jit(solution)/shard_map/all_to_all | solution.py:662
  42.9 0.7 collective-permute-start.9
  43.6 0.0 collective-permute-done.9.v2_upper
  43.6 7.5 %all-to-all-done.gathered = f32[32,8,128]{2,1,0:T(8,128)S(1)} async-done(((f32[32,8,128]{2,1,0:T(8,128)}), f32[32,8,128]{2,1,0:T(8,128)S(1)}, u32[]{:S(2)}, u32[]{:S(2)}) %all-to-all-start) | async-done | bytes 131104 | tf_op jit(solution)/shard_map/all_to_all | solution.py:662
  51.1 0.7 %combine.1 = (f32[128,128]{1,0:T(8,128)S(1)}, f32[3,8,128]{2,1,0:T(8,128)S(1)}) custom-call(f32[32,8,128]{2,1,0:T(8,128)S(1)} %all-to-all-done.gathered, f32[3,128,128]{2,1,0:T(8,128)S(1)} %get-tuple-element.40.refs_4_.v0, f32[3,128,128]{2,1,0:T(8,128)S(1)} %get-tuple-element.53.v0_high, f32[3,128,128]{2,1,0:T(8,128)S(1)} %get-tuple-element.45.v1, ...), custom_call_target="tpu_custom_call" | custom-call | tf_op jit(solution)/shard_map/combine/pallas_call | solution.py:665
  51.8 1.8 %collective-permute-start.12 = (f32[128,128]{1,0:T(8,128)S(1)}, f32[128,128]{1,0:T(8,128)S(1)}, u32[]{:S(2)}, u32[]{:S(2)}) collective-permute-start(f32[128,128]{1,0:T(8,128)S(1)} %get-tuple-element.57.refs_0_), channel_id=1, source_target_pairs={{0,24},{8,16},{16,8},{24,0},{1,25},{9,17},{17,9},{25,1},{2,26},{10... | collective-permute-start | bytes 196616 | tf_op jit(solution)/shard_map/ppermute | solution.py:668
  53.6 0.6 collective-permute-start.11
  54.2 1.2 %collective-permute-start.10 = (f32[128,128]{1,0:T(8,128)S(1)}, f32[128,128]{1,0:T(8,128)S(1)}, u32[]{:S(2)}, u32[]{:S(2)}) collective-permute-start(f32[128,128]{1,0:T(8,128)S(1)} %get-tuple-element.57.refs_0_), channel_id=1, source_target_pairs={{0,8},{8,0},{16,24},{24,16},{1,9},{9,1},{17,25},{25,17},{2,10},{10... | collective-permute-start | bytes 196616 | tf_op jit(solution)/shard_map/ppermute | solution.py:668
  55.4 2.3 %collective-permute-done.12.refs_3_ = f32[128,128]{1,0:T(8,128)S(1)} collective-permute-done((f32[128,128]{1,0:T(8,128)S(1)}, f32[128,128]{1,0:T(8,128)S(1)}, u32[]{:S(2)}, u32[]{:S(2)}) %collective-permute-start.12) | collective-permute-done | bytes 65568 | tf_op jit(solution)/shard_map/ppermute | solution.py:668
  57.6 0.5 collective-permute-done.11.refs_2_
  58.2 0.2 collective-permute-done.10.refs_1_
  58.5 4.0 %collective-permute-start.13 = (f32[72,128]{1,0:T(8,128)S(1)}, f32[72,128]{1,0:T(8,128)S(1)}, u32[]{:S(2)}, u32[]{:S(2)}) collective-permute-start(f32[72,128]{1,0:T(8,128)S(1)} %get-tuple-element.63), channel_id=1, source_target_pairs={{1,2},{0,7},{3,4},{2,1},{5,6},{4,3},{7,0},{6,5},{9,10},{8,15},{11,... | collective-permute-start | bytes 110600 | tf_op jit(solution)/shard_map/ppermute | solution.py:609
  62.5 0.0 collective-permute-start.14
  62.5 0.0 collective-permute-start.15
  62.5 0.7 %displace.1 = f32[3,2,64,128]{3,2,1,0:T(8,128)} custom-call(f32[3,8,128]{2,1,0:T(8,128)S(1)} %get-tuple-element.60.factors, f32[3,128,128]{2,1,0:T(8,128)S(1)} %get-tuple-element.40.refs_4_.v0, f32[3,128,128]{2,1,0:T(8,128)S(1)} %get-tuple-element.41.refs_5_.v0_inner, f32[3,128,128]{2,1,0:T(8,128)S(1)} %get-tuple-element.45.v1, ...), custom_call_target="tpu_custom_call" | custom-call | flops 10000000 | bytes 4000000 | tf_op jit(solution)/shard_map/displace/pallas_call | solution.py:669
  63.2 0.9 %collective-permute-done.13.outer = f32[72,128]{1,0:T(8,128)S(1)} collective-permute-done((f32[72,128]{1,0:T(8,128)S(1)}, f32[72,128]{1,0:T(8,128)S(1)}, u32[]{:S(2)}, u32[]{:S(2)}) %collective-permute-start.13) | collective-permute-done | bytes 36896 | tf_op jit(solution)/shard_map/ppermute | solution.py:609
  64.1 2.3 %collective-permute-done.14.far = f32[72,128]{1,0:T(8,128)S(1)} collective-permute-done((f32[72,128]{1,0:T(8,128)S(1)}, f32[72,128]{1,0:T(8,128)S(1)}, u32[]{:S(2)}, u32[]{:S(2)}) %collective-permute-start.14) | collective-permute-done | bytes 36896 | tf_op jit(solution)/shard_map/ppermute | solution.py:609
  66.4 0.0 collective-permute-done.15.partner
  66.4 0.9 %gradient.1 = f32[2,64,128]{2,1,0:T(8,128)} custom-call(f32[128,128]{1,0:T(8,128)S(1)} %get-tuple-element.62.scaled, f32[72,128]{1,0:T(8,128)S(1)} %collective-permute-done.13.outer, f32[72,128]{1,0:T(8,128)S(1)} %collective-permute-done.14.far, f32[72,128]{1,0:T(8,128)S(1)} %collective-permute-done.15.partner), custom_call_target="tpu_custom_call" | custom-call | tf_op jit(solution)/shard_map/gradient/pallas_call | solution.py:680
  (2 shorter events, 0.0 us)
Async XLA Ops:
  0.6 1.0 %copy-start = (s32[3,2,64,128]{3,2,1,0:T(8,128)S(1)}, s32[3,2,64,128]{3,2,1,0:T(8,128)}, u32[]{:S(2)}) copy-start(s32[3,2,64,128]{3,2,1,0:T(8,128)} %load.1) | copy-start | bytes 589828
  0.6 1.0 %copy-start.1 = (f32[2,64,128]{2,1,0:T(8,128)S(1)}, f32[2,64,128]{2,1,0:T(8,128)}, u32[]{:S(2)}) copy-start(f32[2,64,128]{2,1,0:T(8,128)} %design.1) | copy-start | bytes 196612
  1.7 8.9 %collective-permute-start.4 = (f32[11,64,128]{2,1,0:T(8,128)S(1)}, f32[11,64,128]{2,1,0:T(8,128)S(1)}, u32[]{:S(2)}, u32[]{:S(2)}) collective-permute-start(f32[11,64,128]{2,1,0:T(8,128)S(1)} %get-tuple-element.39), channel_id=1, source_target_pairs={{0,1},{1,0},{2,3},{3,2},{4,5},{5,4},{6,7},{7,6},{8,9},{9,8},{10,11... | collective-permute-start | bytes 1081352 | tf_op jit(solution)/shard_map/ppermute | solution.py:609
  2.3 12.9 %collective-permute-start = (f32[4,64,128]{2,1,0:T(8,128)S(1)}, f32[4,64,128]{2,1,0:T(8,128)S(1)}, u32[]{:S(2)}, u32[]{:S(2)}) collective-permute-start(f32[4,64,128]{2,1,0:T(8,128)S(1)} %get-tuple-element.34), channel_id=1, source_target_pairs={{0,2},{1,31},{2,4},{3,1},{4,6},{5,3},{6,8},{7,5},{8,10},{9,7},{10,... | collective-permute-start | bytes 393224 | tf_op jit(solution)/shard_map/ppermute | solution.py:609
  4.9 10.9 %collective-permute-start.1 = (f32[4,64,128]{2,1,0:T(8,128)S(1)}, f32[4,64,128]{2,1,0:T(8,128)S(1)}, u32[]{:S(2)}, u32[]{:S(2)}) collective-permute-start(f32[4,64,128]{2,1,0:T(8,128)S(1)} %get-tuple-element.35), channel_id=1, source_target_pairs={{1,2},{0,31},{3,4},{2,1},{5,6},{4,3},{7,8},{6,5},{9,10},{8,7},{11,... | collective-permute-start | bytes 393224 | tf_op jit(solution)/shard_map/ppermute | solution.py:609
  9.0 5.7 %collective-permute-start.2 = (f32[64,128]{1,0:T(8,128)S(1)}, f32[64,128]{1,0:T(8,128)S(1)}, u32[]{:S(2)}, u32[]{:S(2)}) collective-permute-start(f32[64,128]{1,0:T(8,128)S(1)} %get-tuple-element.36), channel_id=1, source_target_pairs={{0,3},{1,2},{2,5},{3,4},{4,7},{5,6},{6,1},{7,0},{8,11},{9,10},{10,... | collective-permute-start | bytes 98312 | tf_op jit(solution)/shard_map/ppermute | solution.py:609
  9.0 6.2 %collective-permute-start.3 = (f32[64,128]{1,0:T(8,128)S(1)}, f32[64,128]{1,0:T(8,128)S(1)}, u32[]{:S(2)}, u32[]{:S(2)}) collective-permute-start(f32[64,128]{1,0:T(8,128)S(1)} %get-tuple-element.37), channel_id=1, source_target_pairs={{0,2},{1,3},{2,4},{3,5},{4,6},{5,7},{6,0},{7,1},{8,10},{9,11},{10,... | collective-permute-start | bytes 98312 | tf_op jit(solution)/shard_map/ppermute | solution.py:609
  17.3 1.5 %collective-permute-start.6 = (f32[3,128,128]{2,1,0:T(8,128)S(1)}, f32[3,128,128]{2,1,0:T(8,128)S(1)}, u32[]{:S(2)}, u32[]{:S(2)}) collective-permute-start(f32[3,128,128]{2,1,0:T(8,128)S(1)} %get-tuple-element.45.v1), channel_id=1, source_target_pairs={{0,1},{1,0},{2,3},{3,2},{4,5},{5,4},{6,7},{7,6},{8,9},{9,8},{10,11... | collective-permute-start | bytes 589832 | tf_op jit(solution)/shard_map/ppermute | solution.py:609
  17.4 1.8 %collective-permute-start.5 = (f32[3,128,128]{2,1,0:T(8,128)S(1)}, f32[3,128,128]{2,1,0:T(8,128)S(1)}, u32[]{:S(2)}, u32[]{:S(2)}) collective-permute-start(f32[3,128,128]{2,1,0:T(8,128)S(1)} %get-tuple-element.45.v1), channel_id=1, source_target_pairs={{1,2},{3,4},{2,1},{5,6},{4,3},{7,8},{6,5},{9,10},{8,7},{11,12},{10... | collective-permute-start | bytes 589832 | tf_op jit(solution)/shard_map/ppermute | solution.py:609
  20.4 7.0 %collective-permute-start.8 = (f32[3,128,128]{2,1,0:T(8,128)S(1)}, f32[3,128,128]{2,1,0:T(8,128)S(1)}, u32[]{:S(2)}, u32[]{:S(2)}) collective-permute-start(f32[3,128,128]{2,1,0:T(8,128)S(1)} %get-tuple-element.50.refs_2_.v2), channel_id=1, source_target_pairs={{0,1},{1,0},{2,3},{3,2},{4,5},{5,4},{6,7},{7,6},{8,9},{9,8},{10,11... | collective-permute-start | bytes 589832 | tf_op jit(solution)/shard_map/ppermute | solution.py:609
  26.3 0.7 collective-permute-start.7
  28.7 22.4 %all-to-all-start = ((f32[32,8,128]{2,1,0:T(8,128)}), f32[32,8,128]{2,1,0:T(8,128)S(1)}, u32[]{:S(2)}, u32[]{:S(2)}) async-start(f32[32,8,128]{2,1,0:T(8,128)} %broadcast_in_dim.3), calls=%async_computation | async-start | bytes 262144 | tf_op jit(solution)/shard_map/all_to_all | solution.py:662
  42.9 0.7 %collective-permute-start.9 = (f32[3,64,128]{2,1,0:T(8,128)S(1)}, f32[3,64,128]{2,1,0:T(8,128)S(1)}, u32[]{:S(2)}, u32[]{:S(2)}) collective-permute-start(f32[3,64,128]{2,1,0:T(8,128)S(1)} %get-tuple-element.55), channel_id=1, source_target_pairs={{2,1},{4,3},{6,5},{8,7},{10,9},{12,11},{14,13},{16,15},{18,17},{20... | collective-permute-start | bytes 294920 | tf_op jit(solution)/shard_map/ppermute | solution.py:609
  51.8 5.8 %collective-permute-start.12 = (f32[128,128]{1,0:T(8,128)S(1)}, f32[128,128]{1,0:T(8,128)S(1)}, u32[]{:S(2)}, u32[]{:S(2)}) collective-permute-start(f32[128,128]{1,0:T(8,128)S(1)} %get-tuple-element.57.refs_0_), channel_id=1, source_target_pairs={{0,24},{8,16},{16,8},{24,0},{1,25},{9,17},{17,9},{25,1},{2,26},{10... | collective-permute-start | bytes 196616 | tf_op jit(solution)/shard_map/ppermute | solution.py:668
  53.6 4.6 %collective-permute-start.11 = (f32[128,128]{1,0:T(8,128)S(1)}, f32[128,128]{1,0:T(8,128)S(1)}, u32[]{:S(2)}, u32[]{:S(2)}) collective-permute-start(f32[128,128]{1,0:T(8,128)S(1)} %get-tuple-element.57.refs_0_), channel_id=1, source_target_pairs={{0,16},{8,24},{16,0},{24,8},{1,17},{9,25},{17,1},{25,9},{2,18},{10... | collective-permute-start | bytes 196616 | tf_op jit(solution)/shard_map/ppermute | solution.py:668
  54.2 4.3 %collective-permute-start.10 = (f32[128,128]{1,0:T(8,128)S(1)}, f32[128,128]{1,0:T(8,128)S(1)}, u32[]{:S(2)}, u32[]{:S(2)}) collective-permute-start(f32[128,128]{1,0:T(8,128)S(1)} %get-tuple-element.57.refs_0_), channel_id=1, source_target_pairs={{0,8},{8,0},{16,24},{24,16},{1,9},{9,1},{17,25},{25,17},{2,10},{10... | collective-permute-start | bytes 196616 | tf_op jit(solution)/shard_map/ppermute | solution.py:668
  58.5 5.7 %collective-permute-start.13 = (f32[72,128]{1,0:T(8,128)S(1)}, f32[72,128]{1,0:T(8,128)S(1)}, u32[]{:S(2)}, u32[]{:S(2)}) collective-permute-start(f32[72,128]{1,0:T(8,128)S(1)} %get-tuple-element.63), channel_id=1, source_target_pairs={{1,2},{0,7},{3,4},{2,1},{5,6},{4,3},{7,0},{6,5},{9,10},{8,15},{11,... | collective-permute-start | bytes 110600 | tf_op jit(solution)/shard_map/ppermute | solution.py:609
  62.5 4.0 %collective-permute-start.14 = (f32[72,128]{1,0:T(8,128)S(1)}, f32[72,128]{1,0:T(8,128)S(1)}, u32[]{:S(2)}, u32[]{:S(2)}) collective-permute-start(f32[72,128]{1,0:T(8,128)S(1)} %get-tuple-element.64), channel_id=1, source_target_pairs={{0,6},{1,3},{2,0},{3,5},{4,2},{5,7},{6,4},{7,1},{8,14},{9,11},{10,... | collective-permute-start | bytes 110600 | tf_op jit(solution)/shard_map/ppermute | solution.py:609
  62.5 4.0 %collective-permute-start.15 = (f32[72,128]{1,0:T(8,128)S(1)}, f32[72,128]{1,0:T(8,128)S(1)}, u32[]{:S(2)}, u32[]{:S(2)}) collective-permute-start(f32[72,128]{1,0:T(8,128)S(1)} %get-tuple-element.65), channel_id=1, source_target_pairs={{0,1},{1,0},{2,3},{3,2},{4,5},{5,4},{6,7},{7,6},{8,9},{9,8},{10,11... | collective-permute-start | bytes 110600 | tf_op jit(solution)/shard_map/ppermute | solution.py:609

commit v13 on v11

--- a/solution.py
+++ b/solution.py
@@ -15,7 +15,7 @@
 filter_reach = 1.8
 
 AXES = ("mod", "slab", "sub")
-ROWS = 8
+ROWS = 16
 FACE = filter_reach - 1.0
 EDGE = filter_reach - math.sqrt(2.0)
 CORNER = filter_reach - math.sqrt(3.0)

time: 64.7 us -> 64.1 us (level)
  no operation moved by 1% of the time
where the time goes in v13:
time: 64.1 us; the launch traced here: 63.9 us
  blocking collectives  23.1 us (36%)
  starting transfers between devices  20.8 us (32%)
  waiting for transfers between devices  12.1 us (19%)
  Pallas kernels  6.13 us (10%)
  other arithmetic  0.99 us (2%)
  between operations  0.74 us (1%)
    all_to_all x1, blocking collectives, local(): lax.all_to_all(jnp.broadcast_to(moments, (devices, 8, width)), AXES, 0, 0...  23.1 us
    ppermute x12, starting transfers between devices, move(): return lax.ppermute(value, AXES, path[name])  17.2 us
    ppermute x12, waiting for transfers between devices, move(): return lax.ppermute(value, AXES, path[name])  9.02 us
    ppermute x3, starting transfers between devices, local(): lax.ppermute(slope, 'mod', pairs)  3.55 us
    ppermute x3, waiting for transfers between devices, local(): lax.ppermute(slope, 'mod', pairs)  3.06 us
  transfers between devices with their start and end apart: 15, of which 9 were waited for; matrix products, arithmetic and copies ran while one was open for 0% of the time, Pallas kernels for 3%

profile of v13, /device:TPU:0, one launch (start us, length us, event | category | flops | bytes accessed | tf_op | source)
XLA Modules:
  0.0 63.9 jit_solution(12441892382580333403)
XLA Ops:
  0.6 0.0 copy-start
  0.6 0.0 copy-start.1
  0.6 1.0 %subtract_convert_fusion.free = f32[3,2,64,128]{3,2,1,0:T(8,128)S(1)} fusion(s32[3,2,64,128]{3,2,1,0:T(8,128)} %param.4), kind=kLoop, calls=%fused_computation | loop fusion | flops 98304 | bytes 393216 | tf_op jit(solution)/shard_map/convert_element_type | solution.py:585
  1.6 0.0 copy-done
  1.7 0.0 copy-done.1
  1.7 0.1 prepare.1
  1.7 0.5 collective-permute-start.4
  2.3 2.6 %collective-permute-start = (f32[4,64,128]{2,1,0:T(8,128)S(1)}, f32[4,64,128]{2,1,0:T(8,128)S(1)}, u32[]{:S(2)}, u32[]{:S(2)}) collective-permute-start(f32[4,64,128]{2,1,0:T(8,128)S(1)} %get-tuple-element.34), channel_id=1, source_target_pairs={{0,2},{1,31},{2,4},{3,1},{4,6},{5,3},{6,8},{7,5},{8,10},{9,7},{10,... | collective-permute-start | bytes 393224 | tf_op jit(solution)/shard_map/ppermute | solution.py:580
  4.9 4.1 %collective-permute-start.1 = (f32[4,64,128]{2,1,0:T(8,128)S(1)}, f32[4,64,128]{2,1,0:T(8,128)S(1)}, u32[]{:S(2)}, u32[]{:S(2)}) collective-permute-start(f32[4,64,128]{2,1,0:T(8,128)S(1)} %get-tuple-element.35), channel_id=1, source_target_pairs={{1,2},{0,31},{3,4},{2,1},{5,6},{4,3},{7,8},{6,5},{9,10},{8,7},{11,... | collective-permute-start | bytes 393224 | tf_op jit(solution)/shard_map/ppermute | solution.py:580
  9.0 0.0 collective-permute-start.2
  9.0 1.6 %collective-permute-start.3 = (f32[64,128]{1,0:T(8,128)S(1)}, f32[64,128]{1,0:T(8,128)S(1)}, u32[]{:S(2)}, u32[]{:S(2)}) collective-permute-start(f32[64,128]{1,0:T(8,128)S(1)} %get-tuple-element.37), channel_id=1, source_target_pairs={{0,2},{1,3},{2,4},{3,5},{4,6},{5,7},{6,0},{7,1},{8,10},{9,11},{10,... | collective-permute-start | bytes 98312 | tf_op jit(solution)/shard_map/ppermute | solution.py:580
  10.6 0.0 collective-permute-done.4.swap
  10.6 0.7 %start_inner.1 = (f32[3,128,128]{2,1,0:T(8,128)S(1)}, f32[3,128,128]{2,1,0:T(8,128)S(1)}, f32[3,128,128]{2,1,0:T(8,128)S(1)}, f32[12,128,128]{2,1,0:T(8,128)S(1)}, f32[3,128,128]{2,1,0:T(8,128)S(1)}) custom-call(f32[11,64,128]{2,1,0:T(8,128)S(1)} %get-tuple-element.38.own, f32[11,64,128]{2,1,0:T(8,128)S(1)} %collective-permute-done.4.swap), custom_call_target="tpu_custom_call" | custom-call | flops 10000000 | bytes 4000000 | tf_op jit(solution)/shard_map/start_inner/pallas_call | solution.py:600
  11.4 3.3 %collective-permute-done.2.refs_2_ = f32[64,128]{1,0:T(8,128)S(1)} collective-permute-done((f32[64,128]{1,0:T(8,128)S(1)}, f32[64,128]{1,0:T(8,128)S(1)}, u32[]{:S(2)}, u32[]{:S(2)}) %collective-permute-start.2) | collective-permute-done | bytes 32800 | tf_op jit(solution)/shard_map/ppermute | solution.py:580
  14.7 0.5 collective-permute-done.3.refs_3_
  15.2 0.0 collective-permute-done.refs_0_
  15.2 0.6 collective-permute-done.1.refs_1_
  15.8 1.2 %start_outer.1 = (f32[3,128,128]{2,1,0:T(8,128)S(1)}, f32[3,128,128]{2,1,0:T(8,128)S(1)}, f32[128,128]{1,0:T(8,128)S(1)}, f32[128,128]{1,0:T(8,128)S(1)}, f32[12...) custom-call(f32[4,64,128]{2,1,0:T(8,128)S(1)} %collective-permute-done.refs_0_, ...), custom_call_target="tpu_custom_call" | custom-call | tf_op jit(solution)/shard_map/start_outer/pallas_call | solution.py:607
  17.0 0.1 collective-permute-start.6
  17.1 0.7 %collective-permute-start.5 = (f32[3,128,128]{2,1,0:T(8,128)S(1)}, f32[3,128,128]{2,1,0:T(8,128)S(1)}, u32[]{:S(2)}, u32[]{:S(2)}) collective-permute-start(f32[3,128,128]{2,1,0:T(8,128)S(1)} %get-tuple-element.45.v1), channel_id=1, source_target_pairs={{1,2},{3,4},{2,1},{5,6},{4,3},{7,8},{6,5},{9,10},{8,7},{11,12},{10... | collective-permute-start | bytes 589832 | tf_op jit(solution)/shard_map/ppermute | solution.py:580
  17.7 0.7 %collective-permute-done.6.inner.v1_inner = f32[3,128,128]{2,1,0:T(8,128)S(1)} collective-permute-done((f32[3,128,128]{2,1,0:T(8,128)S(1)}, f32[3,128,128]{2,1,0:T(8,128)S(1)}, u32[]{:S(2)}, u32[]{:S(2)}) %collective-permute-start.6) | collective-permute-done | bytes 196640 | tf_op jit(solution)/shard_map/ppermute | solution.py:580
  18.5 0.4 second_inner.1.fields
  18.9 0.0 collective-permute-done.5.outer
  18.9 0.9 %second_outer.1 = (f32[3,128,128]{2,1,0:T(8,128)S(1)}, f32[3,128,128]{2,1,0:T(8,128)S(1)}, f32[8,128]{1,0:T(8,128)S(1)}) custom-call(f32[3,128,128]{2,1,0:T(8,128)S(1)} %get-tuple-element.45.v1, f32[3,128,128]{2,1,0:T(8,128)S(1)} %collective-permute-done.5.outer, f32[3,128,128]{2,1,0:T(8,128)S(1)} %collective-permute-done.6.inner.v1_inner, ...), custom_call_target="tpu_custom_call" | custom-call | tf_op jit(solution)/shard_map/second_outer/pallas_call | solution.py:616
  19.8 5.9 %collective-permute-start.8 = (f32[3,128,128]{2,1,0:T(8,128)S(1)}, f32[3,128,128]{2,1,0:T(8,128)S(1)}, u32[]{:S(2)}, u32[]{:S(2)}) collective-permute-start(f32[3,128,128]{2,1,0:T(8,128)S(1)} %get-tuple-element.49.v2), channel_id=1, source_target_pairs={{0,1},{1,0},{2,3},{3,2},{4,5},{5,4},{6,7},{7,6},{8,9},{9,8},{10,11... | collective-permute-start | bytes 589832 | tf_op jit(solution)/shard_map/ppermute | solution.py:580
  25.7 0.7 %collective-permute-start.7 = (f32[3,128,128]{2,1,0:T(8,128)S(1)}, f32[3,128,128]{2,1,0:T(8,128)S(1)}, u32[]{:S(2)}, u32[]{:S(2)}) collective-permute-start(f32[3,128,128]{2,1,0:T(8,128)S(1)} %get-tuple-element.49.v2), channel_id=1, source_target_pairs={{2,1},{4,3},{6,5},{8,7},{10,9},{12,11},{14,13},{16,15},{18,17},{20... | collective-permute-start | bytes 589832 | tf_op jit(solution)/shard_map/ppermute | solution.py:580
  26.4 0.4 collective-permute-done.8.v2_inner
  26.8 0.0 collective-permute-done.7.v2_outer
  26.8 0.5 third.1
  27.3 23.1 %all_to_all.5.gathered = f32[32,8,128]{2,1,0:T(8,128)S(1)} all-to-all(f32[32,8,128]{2,1,0:T(8,128)S(1)} %broadcast_in_dim.3), channel_id=1, replica_groups=mesh['mod'=4,'slab'=4,'sub'=2] {'mod','slab','sub'}, dimensions={0} | all-to-all | bytes 262144 | tf_op jit(solution)/shard_map/all_to_all | solution.py:625
  50.4 0.7 %combine.1 = (f32[128,128]{1,0:T(8,128)S(1)}, f32[3,8,128]{2,1,0:T(8,128)S(1)}) custom-call(f32[32,8,128]{2,1,0:T(8,128)S(1)} %all_to_all.5.gathered, f32[3,128,128]{2,1,0:T(8,128)S(1)} %get-tuple-element.40.refs_4_.v0, f32[3,128,128]{2,1,0:T(8,128)S(1)} %get-tuple-element.53.v0_high, f32[3,128,128]{2,1,0:T(8,128)S(1)} %get-tuple-element.45.v1, ...), custom_call_target="tpu_custom_call" | custom-call | tf_op jit(solution)/shard_map/combine/pallas_call | solution.py:628
  51.1 1.0 %collective-permute-start.11 = (f32[128,128]{1,0:T(8,128)S(1)}, f32[128,128]{1,0:T(8,128)S(1)}, u32[]{:S(2)}, u32[]{:S(2)}) collective-permute-start(f32[128,128]{1,0:T(8,128)S(1)} %get-tuple-element.57.refs_0_), channel_id=1, source_target_pairs={{0,24},{8,16},{16,8},{24,0},{1,25},{9,17},{17,9},{25,1},{2,26},{10... | collective-permute-start | bytes 196616 | tf_op jit(solution)/shard_map/ppermute | solution.py:631
  52.2 1.3 %collective-permute-start.10 = (f32[128,128]{1,0:T(8,128)S(1)}, f32[128,128]{1,0:T(8,128)S(1)}, u32[]{:S(2)}, u32[]{:S(2)}) collective-permute-start(f32[128,128]{1,0:T(8,128)S(1)} %get-tuple-element.57.refs_0_), channel_id=1, source_target_pairs={{0,16},{8,24},{16,0},{24,8},{1,17},{9,25},{17,1},{25,9},{2,18},{10... | collective-permute-start | bytes 196616 | tf_op jit(solution)/shard_map/ppermute | solution.py:631
  53.5 1.2 %collective-permute-start.9 = (f32[128,128]{1,0:T(8,128)S(1)}, f32[128,128]{1,0:T(8,128)S(1)}, u32[]{:S(2)}, u32[]{:S(2)}) collective-permute-start(f32[128,128]{1,0:T(8,128)S(1)} %get-tuple-element.57.refs_0_), channel_id=1, source_target_pairs={{0,8},{8,0},{16,24},{24,16},{1,9},{9,1},{17,25},{25,17},{2,10},{10... | collective-permute-start | bytes 196616 | tf_op jit(solution)/shard_map/ppermute | solution.py:631
  54.7 2.3 %collective-permute-done.11.refs_3_ = f32[128,128]{1,0:T(8,128)S(1)} collective-permute-done((f32[128,128]{1,0:T(8,128)S(1)}, f32[128,128]{1,0:T(8,128)S(1)}, u32[]{:S(2)}, u32[]{:S(2)}) %collective-permute-start.11) | collective-permute-done | bytes 65568 | tf_op jit(solution)/shard_map/ppermute | solution.py:631
  57.0 0.2 collective-permute-done.10.refs_2_
  57.2 0.5 collective-permute-done.9.refs_1_
  57.8 0.1 collective-permute-start.12
  57.8 1.0 %collective-permute-start.13 = (f32[72,128]{1,0:T(8,128)S(1)}, f32[72,128]{1,0:T(8,128)S(1)}, u32[]{:S(2)}, u32[]{:S(2)}) collective-permute-start(f32[72,128]{1,0:T(8,128)S(1)} %get-tuple-element.64), channel_id=1, source_target_pairs={{0,6},{1,3},{2,0},{3,5},{4,2},{5,7},{6,4},{7,1},{8,14},{9,11},{10,... | collective-permute-start | bytes 110600 | tf_op jit(solution)/shard_map/ppermute | solution.py:580
  58.8 0.0 collective-permute-start.14
  58.8 0.7 %displace.1 = f32[3,2,64,128]{3,2,1,0:T(8,128)} custom-call(f32[3,8,128]{2,1,0:T(8,128)S(1)} %get-tuple-element.60.factors, f32[3,128,128]{2,1,0:T(8,128)S(1)} %get-tuple-element.40.refs_4_.v0, f32[3,128,128]{2,1,0:T(8,128)S(1)} %get-tuple-element.41.refs_5_.v0_inner, f32[3,128,128]{2,1,0:T(8,128)S(1)} %get-tuple-element.45.v1, ...), custom_call_target="tpu_custom_call" | custom-call | flops 10000000 | bytes 4000000 | tf_op jit(solution)/shard_map/displace/pallas_call | solution.py:632
  59.6 3.5 %collective-permute-done.12.outer = f32[72,128]{1,0:T(8,128)S(1)} collective-permute-done((f32[72,128]{1,0:T(8,128)S(1)}, f32[72,128]{1,0:T(8,128)S(1)}, u32[]{:S(2)}, u32[]{:S(2)}) %collective-permute-start.12) | collective-permute-done | bytes 36896 | tf_op jit(solution)/shard_map/ppermute | solution.py:580
  63.0 0.0 collective-permute-done.13.far
  63.0 0.0 collective-permute-done.14.partner
  63.0 0.9 %gradient.1 = f32[2,64,128]{2,1,0:T(8,128)} custom-call(f32[128,128]{1,0:T(8,128)S(1)} %get-tuple-element.62.scaled, f32[72,128]{1,0:T(8,128)S(1)} %collective-permute-done.12.outer, f32[72,128]{1,0:T(8,128)S(1)} %collective-permute-done.13.far, f32[72,128]{1,0:T(8,128)S(1)} %collective-permute-done.14.partner), custom_call_target="tpu_custom_call" | custom-call | tf_op jit(solution)/shard_map/gradient/pallas_call | solution.py:643
  (2 shorter events, 0.0 us)
Async XLA Ops:
  0.6 1.0 %copy-start = (s32[3,2,64,128]{3,2,1,0:T(8,128)S(1)}, s32[3,2,64,128]{3,2,1,0:T(8,128)}, u32[]{:S(2)}) copy-start(s32[3,2,64,128]{3,2,1,0:T(8,128)} %load.1) | copy-start | bytes 589828
  0.6 1.0 %copy-start.1 = (f32[2,64,128]{2,1,0:T(8,128)S(1)}, f32[2,64,128]{2,1,0:T(8,128)}, u32[]{:S(2)}) copy-start(f32[2,64,128]{2,1,0:T(8,128)} %design.1) | copy-start | bytes 196612
  1.7 8.9 %collective-permute-start.4 = (f32[11,64,128]{2,1,0:T(8,128)S(1)}, f32[11,64,128]{2,1,0:T(8,128)S(1)}, u32[]{:S(2)}, u32[]{:S(2)}) collective-permute-start(f32[11,64,128]{2,1,0:T(8,128)S(1)} %get-tuple-element.39), channel_id=1, source_target_pairs={{0,1},{1,0},{2,3},{3,2},{4,5},{5,4},{6,7},{7,6},{8,9},{9,8},{10,11... | collective-permute-start | bytes 1081352 | tf_op jit(solution)/shard_map/ppermute | solution.py:580
  2.3 12.9 %collective-permute-start = (f32[4,64,128]{2,1,0:T(8,128)S(1)}, f32[4,64,128]{2,1,0:T(8,128)S(1)}, u32[]{:S(2)}, u32[]{:S(2)}) collective-permute-start(f32[4,64,128]{2,1,0:T(8,128)S(1)} %get-tuple-element.34), channel_id=1, source_target_pairs={{0,2},{1,31},{2,4},{3,1},{4,6},{5,3},{6,8},{7,5},{8,10},{9,7},{10,... | collective-permute-start | bytes 393224 | tf_op jit(solution)/shard_map/ppermute | solution.py:580
  4.9 10.9 %collective-permute-start.1 = (f32[4,64,128]{2,1,0:T(8,128)S(1)}, f32[4,64,128]{2,1,0:T(8,128)S(1)}, u32[]{:S(2)}, u32[]{:S(2)}) collective-permute-start(f32[4,64,128]{2,1,0:T(8,128)S(1)} %get-tuple-element.35), channel_id=1, source_target_pairs={{1,2},{0,31},{3,4},{2,1},{5,6},{4,3},{7,8},{6,5},{9,10},{8,7},{11,... | collective-permute-start | bytes 393224 | tf_op jit(solution)/shard_map/ppermute | solution.py:580
  9.0 5.7 %collective-permute-start.2 = (f32[64,128]{1,0:T(8,128)S(1)}, f32[64,128]{1,0:T(8,128)S(1)}, u32[]{:S(2)}, u32[]{:S(2)}) collective-permute-start(f32[64,128]{1,0:T(8,128)S(1)} %get-tuple-element.36), channel_id=1, source_target_pairs={{0,3},{1,2},{2,5},{3,4},{4,7},{5,6},{6,1},{7,0},{8,11},{9,10},{10,... | collective-permute-start | bytes 98312 | tf_op jit(solution)/shard_map/ppermute | solution.py:580
  9.0 6.2 %collective-permute-start.3 = (f32[64,128]{1,0:T(8,128)S(1)}, f32[64,128]{1,0:T(8,128)S(1)}, u32[]{:S(2)}, u32[]{:S(2)}) collective-permute-start(f32[64,128]{1,0:T(8,128)S(1)} %get-tuple-element.37), channel_id=1, source_target_pairs={{0,2},{1,3},{2,4},{3,5},{4,6},{5,7},{6,0},{7,1},{8,10},{9,11},{10,... | collective-permute-start | bytes 98312 | tf_op jit(solution)/shard_map/ppermute | solution.py:580
  17.0 1.5 %collective-permute-start.6 = (f32[3,128,128]{2,1,0:T(8,128)S(1)}, f32[3,128,128]{2,1,0:T(8,128)S(1)}, u32[]{:S(2)}, u32[]{:S(2)}) collective-permute-start(f32[3,128,128]{2,1,0:T(8,128)S(1)} %get-tuple-element.45.v1), channel_id=1, source_target_pairs={{0,1},{1,0},{2,3},{3,2},{4,5},{5,4},{6,7},{7,6},{8,9},{9,8},{10,11... | collective-permute-start | bytes 589832 | tf_op jit(solution)/shard_map/ppermute | solution.py:580
  17.1 1.9 %collective-permute-start.5 = (f32[3,128,128]{2,1,0:T(8,128)S(1)}, f32[3,128,128]{2,1,0:T(8,128)S(1)}, u32[]{:S(2)}, u32[]{:S(2)}) collective-permute-start(f32[3,128,128]{2,1,0:T(8,128)S(1)} %get-tuple-element.45.v1), channel_id=1, source_target_pairs={{1,2},{3,4},{2,1},{5,6},{4,3},{7,8},{6,5},{9,10},{8,7},{11,12},{10... | collective-permute-start | bytes 589832 | tf_op jit(solution)/shard_map/ppermute | solution.py:580
  19.8 7.0 %collective-permute-start.8 = (f32[3,128,128]{2,1,0:T(8,128)S(1)}, f32[3,128,128]{2,1,0:T(8,128)S(1)}, u32[]{:S(2)}, u32[]{:S(2)}) collective-permute-start(f32[3,128,128]{2,1,0:T(8,128)S(1)} %get-tuple-element.49.v2), channel_id=1, source_target_pairs={{0,1},{1,0},{2,3},{3,2},{4,5},{5,4},{6,7},{7,6},{8,9},{9,8},{10,11... | collective-permute-start | bytes 589832 | tf_op jit(solution)/shard_map/ppermute | solution.py:580
  25.7 1.1 %collective-permute-start.7 = (f32[3,128,128]{2,1,0:T(8,128)S(1)}, f32[3,128,128]{2,1,0:T(8,128)S(1)}, u32[]{:S(2)}, u32[]{:S(2)}) collective-permute-start(f32[3,128,128]{2,1,0:T(8,128)S(1)} %get-tuple-element.49.v2), channel_id=1, source_target_pairs={{2,1},{4,3},{6,5},{8,7},{10,9},{12,11},{14,13},{16,15},{18,17},{20... | collective-permute-start | bytes 589832 | tf_op jit(solution)/shard_map/ppermute | solution.py:580
  51.1 5.9 %collective-permute-start.11 = (f32[128,128]{1,0:T(8,128)S(1)}, f32[128,128]{1,0:T(8,128)S(1)}, u32[]{:S(2)}, u32[]{:S(2)}) collective-permute-start(f32[128,128]{1,0:T(8,128)S(1)} %get-tuple-element.57.refs_0_), channel_id=1, source_target_pairs={{0,24},{8,16},{16,8},{24,0},{1,25},{9,17},{17,9},{25,1},{2,26},{10... | collective-permute-start | bytes 196616 | tf_op jit(solution)/shard_map/ppermute | solution.py:631
  52.2 5.1 %collective-permute-start.10 = (f32[128,128]{1,0:T(8,128)S(1)}, f32[128,128]{1,0:T(8,128)S(1)}, u32[]{:S(2)}, u32[]{:S(2)}) collective-permute-start(f32[128,128]{1,0:T(8,128)S(1)} %get-tuple-element.57.refs_0_), channel_id=1, source_target_pairs={{0,16},{8,24},{16,0},{24,8},{1,17},{9,25},{17,1},{25,9},{2,18},{10... | collective-permute-start | bytes 196616 | tf_op jit(solution)/shard_map/ppermute | solution.py:631
  53.5 4.3 %collective-permute-start.9 = (f32[128,128]{1,0:T(8,128)S(1)}, f32[128,128]{1,0:T(8,128)S(1)}, u32[]{:S(2)}, u32[]{:S(2)}) collective-permute-start(f32[128,128]{1,0:T(8,128)S(1)} %get-tuple-element.57.refs_0_), channel_id=1, source_target_pairs={{0,8},{8,0},{16,24},{24,16},{1,9},{9,1},{17,25},{25,17},{2,10},{10... | collective-permute-start | bytes 196616 | tf_op jit(solution)/shard_map/ppermute | solution.py:631
  57.8 5.2 %collective-permute-start.12 = (f32[72,128]{1,0:T(8,128)S(1)}, f32[72,128]{1,0:T(8,128)S(1)}, u32[]{:S(2)}, u32[]{:S(2)}) collective-permute-start(f32[72,128]{1,0:T(8,128)S(1)} %get-tuple-element.63), channel_id=1, source_target_pairs={{1,2},{0,7},{3,4},{2,1},{5,6},{4,3},{7,0},{6,5},{9,10},{8,15},{11,... | collective-permute-start | bytes 110600 | tf_op jit(solution)/shard_map/ppermute | solution.py:580
  57.8 5.2 %collective-permute-start.13 = (f32[72,128]{1,0:T(8,128)S(1)}, f32[72,128]{1,0:T(8,128)S(1)}, u32[]{:S(2)}, u32[]{:S(2)}) collective-permute-start(f32[72,128]{1,0:T(8,128)S(1)} %get-tuple-element.64), channel_id=1, source_target_pairs={{0,6},{1,3},{2,0},{3,5},{4,2},{5,7},{6,4},{7,1},{8,14},{9,11},{10,... | collective-permute-start | bytes 110600 | tf_op jit(solution)/shard_map/ppermute | solution.py:580
  58.8 4.2 %collective-permute-start.14 = (f32[72,128]{1,0:T(8,128)S(1)}, f32[72,128]{1,0:T(8,128)S(1)}, u32[]{:S(2)}, u32[]{:S(2)}) collective-permute-start(f32[72,128]{1,0:T(8,128)S(1)} %get-tuple-element.65), channel_id=1, source_target_pairs={{0,1},{1,0},{2,3},{3,2},{4,5},{5,4},{6,7},{7,6},{8,9},{9,8},{10,11... | collective-permute-start | bytes 110600 | tf_op jit(solution)/shard_map/ppermute | solution.py:580

commit v14 on v13

--- a/solution.py
+++ b/solution.py
@@ -15,7 +15,7 @@
 filter_reach = 1.8
 
 AXES = ("mod", "slab", "sub")
-ROWS = 16
+ROWS = 32
 FACE = filter_reach - 1.0
 EDGE = filter_reach - math.sqrt(2.0)
 CORNER = filter_reach - math.sqrt(3.0)

time: 64.1 us -> 63.8 us (level)
  no operation moved by 1% of the time
where the time goes in v14:
time: 63.8 us; the launch traced here: 63.6 us
  blocking collectives  23.1 us (36%)
  starting transfers between devices  20.8 us (33%)
  waiting for transfers between devices  12.1 us (19%)
  Pallas kernels  5.92 us (9%)
  other arithmetic  0.99 us (2%)
  between operations  0.74 us (1%)
    all_to_all x1, blocking collectives, local(): lax.all_to_all(jnp.broadcast_to(moments, (devices, 8, width)), AXES, 0, 0...  23.1 us
    ppermute x12, starting transfers between devices, move(): return lax.ppermute(value, AXES, path[name])  17.2 us
    ppermute x12, waiting for transfers between devices, move(): return lax.ppermute(value, AXES, path[name])  9 us
    ppermute x3, starting transfers between devices, local(): lax.ppermute(slope, 'mod', pairs)  3.55 us
    ppermute x3, waiting for transfers between devices, local(): lax.ppermute(slope, 'mod', pairs)  3.06 us
  transfers between devices with their start and end apart: 15, of which 9 were waited for; matrix products, arithmetic and copies ran while one was open for 0% of the time, Pallas kernels for 3%

profile of v14, /device:TPU:0, one launch (start us, length us, event | category | flops | bytes accessed | tf_op | source)
XLA Modules:
  0.0 63.6 jit_solution(16876983024563783658)
XLA Ops:
  0.6 0.0 copy-start
  0.6 0.0 copy-start.1
  0.6 1.0 %subtract_convert_fusion.free = f32[3,2,64,128]{3,2,1,0:T(8,128)S(1)} fusion(s32[3,2,64,128]{3,2,1,0:T(8,128)} %param.4), kind=kLoop, calls=%fused_computation | loop fusion | flops 98304 | bytes 393216 | tf_op jit(solution)/shard_map/convert_element_type | solution.py:585
  1.6 0.0 copy-done
  1.7 0.0 copy-done.1
  1.7 0.1 prepare.1
  1.7 0.5 collective-permute-start.4
  2.3 2.6 %collective-permute-start = (f32[4,64,128]{2,1,0:T(8,128)S(1)}, f32[4,64,128]{2,1,0:T(8,128)S(1)}, u32[]{:S(2)}, u32[]{:S(2)}) collective-permute-start(f32[4,64,128]{2,1,0:T(8,128)S(1)} %get-tuple-element.34), channel_id=1, source_target_pairs={{0,2},{1,31},{2,4},{3,1},{4,6},{5,3},{6,8},{7,5},{8,10},{9,7},{10,... | collective-permute-start | bytes 393224 | tf_op jit(solution)/shard_map/ppermute | solution.py:580
  4.9 4.1 %collective-permute-start.1 = (f32[4,64,128]{2,1,0:T(8,128)S(1)}, f32[4,64,128]{2,1,0:T(8,128)S(1)}, u32[]{:S(2)}, u32[]{:S(2)}) collective-permute-start(f32[4,64,128]{2,1,0:T(8,128)S(1)} %get-tuple-element.35), channel_id=1, source_target_pairs={{1,2},{0,31},{3,4},{2,1},{5,6},{4,3},{7,8},{6,5},{9,10},{8,7},{11,... | collective-permute-start | bytes 393224 | tf_op jit(solution)/shard_map/ppermute | solution.py:580
  9.0 0.0 collective-permute-start.2
  9.0 1.6 %collective-permute-start.3 = (f32[64,128]{1,0:T(8,128)S(1)}, f32[64,128]{1,0:T(8,128)S(1)}, u32[]{:S(2)}, u32[]{:S(2)}) collective-permute-start(f32[64,128]{1,0:T(8,128)S(1)} %get-tuple-element.37), channel_id=1, source_target_pairs={{0,2},{1,3},{2,4},{3,5},{4,6},{5,7},{6,0},{7,1},{8,10},{9,11},{10,... | collective-permute-start | bytes 98312 | tf_op jit(solution)/shard_map/ppermute | solution.py:580
  10.6 0.0 collective-permute-done.4.swap
  10.6 0.8 %start_inner.1 = (f32[3,128,128]{2,1,0:T(8,128)S(1)}, f32[3,128,128]{2,1,0:T(8,128)S(1)}, f32[3,128,128]{2,1,0:T(8,128)S(1)}, f32[12,128,128]{2,1,0:T(8,128)S(1)}, f32[3,128,128]{2,1,0:T(8,128)S(1)}) custom-call(f32[11,64,128]{2,1,0:T(8,128)S(1)} %get-tuple-element.38.own, f32[11,64,128]{2,1,0:T(8,128)S(1)} %collective-permute-done.4.swap), custom_call_target="tpu_custom_call" | custom-call | flops 10000000 | bytes 4000000 | tf_op jit(solution)/shard_map/start_inner/pallas_call | solution.py:600
  11.4 3.3 %collective-permute-done.2.refs_2_ = f32[64,128]{1,0:T(8,128)S(1)} collective-permute-done((f32[64,128]{1,0:T(8,128)S(1)}, f32[64,128]{1,0:T(8,128)S(1)}, u32[]{:S(2)}, u32[]{:S(2)}) %collective-permute-start.2) | collective-permute-done | bytes 32800 | tf_op jit(solution)/shard_map/ppermute | solution.py:580
  14.7 0.5 collective-permute-done.3.refs_3_
  15.2 0.0 collective-permute-done.refs_0_
  15.2 0.6 collective-permute-done.1.refs_1_
  15.8 1.0 %start_outer.1 = (f32[3,128,128]{2,1,0:T(8,128)S(1)}, f32[3,128,128]{2,1,0:T(8,128)S(1)}, f32[128,128]{1,0:T(8,128)S(1)}, f32[128,128]{1,0:T(8,128)S(1)}, f32[12...) custom-call(f32[4,64,128]{2,1,0:T(8,128)S(1)} %collective-permute-done.refs_0_, ...), custom_call_target="tpu_custom_call" | custom-call | tf_op jit(solution)/shard_map/start_outer/pallas_call | solution.py:607
  16.8 0.1 collective-permute-start.6
  16.9 0.7 %collective-permute-start.5 = (f32[3,128,128]{2,1,0:T(8,128)S(1)}, f32[3,128,128]{2,1,0:T(8,128)S(1)}, u32[]{:S(2)}, u32[]{:S(2)}) collective-permute-start(f32[3,128,128]{2,1,0:T(8,128)S(1)} %get-tuple-element.45.v1), channel_id=1, source_target_pairs={{1,2},{3,4},{2,1},{5,6},{4,3},{7,8},{6,5},{9,10},{8,7},{11,12},{10... | collective-permute-start | bytes 589832 | tf_op jit(solution)/shard_map/ppermute | solution.py:580
  17.6 0.7 %collective-permute-done.6.inner.v1_inner = f32[3,128,128]{2,1,0:T(8,128)S(1)} collective-permute-done((f32[3,128,128]{2,1,0:T(8,128)S(1)}, f32[3,128,128]{2,1,0:T(8,128)S(1)}, u32[]{:S(2)}, u32[]{:S(2)}) %collective-permute-start.6) | collective-permute-done | bytes 196640 | tf_op jit(solution)/shard_map/ppermute | solution.py:580
  18.3 0.4 second_inner.1.fields
  18.8 0.0 collective-permute-done.5.outer
  18.8 0.8 %second_outer.1 = (f32[3,128,128]{2,1,0:T(8,128)S(1)}, f32[3,128,128]{2,1,0:T(8,128)S(1)}, f32[8,128]{1,0:T(8,128)S(1)}) custom-call(f32[3,128,128]{2,1,0:T(8,128)S(1)} %get-tuple-element.45.v1, f32[3,128,128]{2,1,0:T(8,128)S(1)} %collective-permute-done.5.outer, f32[3,128,128]{2,1,0:T(8,128)S(1)} %collective-permute-done.6.inner.v1_inner, ...), custom_call_target="tpu_custom_call" | custom-call | tf_op jit(solution)/shard_map/second_outer/pallas_call | solution.py:616
  19.6 5.9 %collective-permute-start.8 = (f32[3,128,128]{2,1,0:T(8,128)S(1)}, f32[3,128,128]{2,1,0:T(8,128)S(1)}, u32[]{:S(2)}, u32[]{:S(2)}) collective-permute-start(f32[3,128,128]{2,1,0:T(8,128)S(1)} %get-tuple-element.49.v2), channel_id=1, source_target_pairs={{0,1},{1,0},{2,3},{3,2},{4,5},{5,4},{6,7},{7,6},{8,9},{9,8},{10,11... | collective-permute-start | bytes 589832 | tf_op jit(solution)/shard_map/ppermute | solution.py:580
  25.5 0.7 %collective-permute-start.7 = (f32[3,128,128]{2,1,0:T(8,128)S(1)}, f32[3,128,128]{2,1,0:T(8,128)S(1)}, u32[]{:S(2)}, u32[]{:S(2)}) collective-permute-start(f32[3,128,128]{2,1,0:T(8,128)S(1)} %get-tuple-element.49.v2), channel_id=1, source_target_pairs={{2,1},{4,3},{6,5},{8,7},{10,9},{12,11},{14,13},{16,15},{18,17},{20... | collective-permute-start | bytes 589832 | tf_op jit(solution)/shard_map/ppermute | solution.py:580
  26.1 0.4 collective-permute-done.8.v2_inner
  26.5 0.0 collective-permute-done.7.v2_outer
  26.5 0.5 third.1
  27.0 23.1 %all_to_all.5.gathered = f32[32,8,128]{2,1,0:T(8,128)S(1)} all-to-all(f32[32,8,128]{2,1,0:T(8,128)S(1)} %broadcast_in_dim.3), channel_id=1, replica_groups=mesh['mod'=4,'slab'=4,'sub'=2] {'mod','slab','sub'}, dimensions={0} | all-to-all | bytes 262144 | tf_op jit(solution)/shard_map/all_to_all | solution.py:625
  50.2 0.7 %combine.1 = (f32[128,128]{1,0:T(8,128)S(1)}, f32[3,8,128]{2,1,0:T(8,128)S(1)}) custom-call(f32[32,8,128]{2,1,0:T(8,128)S(1)} %all_to_all.5.gathered, f32[3,128,128]{2,1,0:T(8,128)S(1)} %get-tuple-element.40.refs_4_.v0, f32[3,128,128]{2,1,0:T(8,128)S(1)} %get-tuple-element.53.v0_high, f32[3,128,128]{2,1,0:T(8,128)S(1)} %get-tuple-element.45.v1, ...), custom_call_target="tpu_custom_call" | custom-call | tf_op jit(solution)/shard_map/combine/pallas_call | solution.py:628
  50.9 1.0 %collective-permute-start.11 = (f32[128,128]{1,0:T(8,128)S(1)}, f32[128,128]{1,0:T(8,128)S(1)}, u32[]{:S(2)}, u32[]{:S(2)}) collective-permute-start(f32[128,128]{1,0:T(8,128)S(1)} %get-tuple-element.57.refs_0_), channel_id=1, source_target_pairs={{0,24},{8,16},{16,8},{24,0},{1,25},{9,17},{17,9},{25,1},{2,26},{10... | collective-permute-start | bytes 196616 | tf_op jit(solution)/shard_map/ppermute | solution.py:631
  51.9 1.3 %collective-permute-start.10 = (f32[128,128]{1,0:T(8,128)S(1)}, f32[128,128]{1,0:T(8,128)S(1)}, u32[]{:S(2)}, u32[]{:S(2)}) collective-permute-start(f32[128,128]{1,0:T(8,128)S(1)} %get-tuple-element.57.refs_0_), channel_id=1, source_target_pairs={{0,16},{8,24},{16,0},{24,8},{1,17},{9,25},{17,1},{25,9},{2,18},{10... | collective-permute-start | bytes 196616 | tf_op jit(solution)/shard_map/ppermute | solution.py:631
  53.2 1.2 %collective-permute-start.9 = (f32[128,128]{1,0:T(8,128)S(1)}, f32[128,128]{1,0:T(8,128)S(1)}, u32[]{:S(2)}, u32[]{:S(2)}) collective-permute-start(f32[128,128]{1,0:T(8,128)S(1)} %get-tuple-element.57.refs_0_), channel_id=1, source_target_pairs={{0,8},{8,0},{16,24},{24,16},{1,9},{9,1},{17,25},{25,17},{2,10},{10... | collective-permute-start | bytes 196616 | tf_op jit(solution)/shard_map/ppermute | solution.py:631
  54.4 2.3 %collective-permute-done.11.refs_3_ = f32[128,128]{1,0:T(8,128)S(1)} collective-permute-done((f32[128,128]{1,0:T(8,128)S(1)}, f32[128,128]{1,0:T(8,128)S(1)}, u32[]{:S(2)}, u32[]{:S(2)}) %collective-permute-start.11) | collective-permute-done | bytes 65568 | tf_op jit(solution)/shard_map/ppermute | solution.py:631
  56.7 0.2 collective-permute-done.10.refs_2_
  57.0 0.5 collective-permute-done.9.refs_1_
  57.5 0.1 collective-permute-start.12
  57.6 1.0 %collective-permute-start.13 = (f32[72,128]{1,0:T(8,128)S(1)}, f32[72,128]{1,0:T(8,128)S(1)}, u32[]{:S(2)}, u32[]{:S(2)}) collective-permute-start(f32[72,128]{1,0:T(8,128)S(1)} %get-tuple-element.64), channel_id=1, source_target_pairs={{0,6},{1,3},{2,0},{3,5},{4,2},{5,7},{6,4},{7,1},{8,14},{9,11},{10,... | collective-permute-start | bytes 110600 | tf_op jit(solution)/shard_map/ppermute | solution.py:580
  58.6 0.0 collective-permute-start.14
  58.6 0.7 %displace.1 = f32[3,2,64,128]{3,2,1,0:T(8,128)} custom-call(f32[3,8,128]{2,1,0:T(8,128)S(1)} %get-tuple-element.60.factors, f32[3,128,128]{2,1,0:T(8,128)S(1)} %get-tuple-element.40.refs_4_.v0, f32[3,128,128]{2,1,0:T(8,128)S(1)} %get-tuple-element.41.refs_5_.v0_inner, f32[3,128,128]{2,1,0:T(8,128)S(1)} %get-tuple-element.45.v1, ...), custom_call_target="tpu_custom_call" | custom-call | flops 10000000 | bytes 4000000 | tf_op jit(solution)/shard_map/displace/pallas_call | solution.py:632
  59.3 3.5 %collective-permute-done.12.outer = f32[72,128]{1,0:T(8,128)S(1)} collective-permute-done((f32[72,128]{1,0:T(8,128)S(1)}, f32[72,128]{1,0:T(8,128)S(1)}, u32[]{:S(2)}, u32[]{:S(2)}) %collective-permute-start.12) | collective-permute-done | bytes 36896 | tf_op jit(solution)/shard_map/ppermute | solution.py:580
  62.8 0.0 collective-permute-done.13.far
  62.8 0.0 collective-permute-done.14.partner
  62.8 0.9 %gradient.1 = f32[2,64,128]{2,1,0:T(8,128)} custom-call(f32[128,128]{1,0:T(8,128)S(1)} %get-tuple-element.62.scaled, f32[72,128]{1,0:T(8,128)S(1)} %collective-permute-done.12.outer, f32[72,128]{1,0:T(8,128)S(1)} %collective-permute-done.13.far, f32[72,128]{1,0:T(8,128)S(1)} %collective-permute-done.14.partner), custom_call_target="tpu_custom_call" | custom-call | tf_op jit(solution)/shard_map/gradient/pallas_call | solution.py:643
  (2 shorter events, 0.0 us)
Async XLA Ops:
  0.6 1.0 %copy-start = (s32[3,2,64,128]{3,2,1,0:T(8,128)S(1)}, s32[3,2,64,128]{3,2,1,0:T(8,128)}, u32[]{:S(2)}) copy-start(s32[3,2,64,128]{3,2,1,0:T(8,128)} %load.1) | copy-start | bytes 589828
  0.6 1.0 %copy-start.1 = (f32[2,64,128]{2,1,0:T(8,128)S(1)}, f32[2,64,128]{2,1,0:T(8,128)}, u32[]{:S(2)}) copy-start(f32[2,64,128]{2,1,0:T(8,128)} %design.1) | copy-start | bytes 196612
  1.7 8.9 %collective-permute-start.4 = (f32[11,64,128]{2,1,0:T(8,128)S(1)}, f32[11,64,128]{2,1,0:T(8,128)S(1)}, u32[]{:S(2)}, u32[]{:S(2)}) collective-permute-start(f32[11,64,128]{2,1,0:T(8,128)S(1)} %get-tuple-element.39), channel_id=1, source_target_pairs={{0,1},{1,0},{2,3},{3,2},{4,5},{5,4},{6,7},{7,6},{8,9},{9,8},{10,11... | collective-permute-start | bytes 1081352 | tf_op jit(solution)/shard_map/ppermute | solution.py:580
  2.3 12.9 %collective-permute-start = (f32[4,64,128]{2,1,0:T(8,128)S(1)}, f32[4,64,128]{2,1,0:T(8,128)S(1)}, u32[]{:S(2)}, u32[]{:S(2)}) collective-permute-start(f32[4,64,128]{2,1,0:T(8,128)S(1)} %get-tuple-element.34), channel_id=1, source_target_pairs={{0,2},{1,31},{2,4},{3,1},{4,6},{5,3},{6,8},{7,5},{8,10},{9,7},{10,... | collective-permute-start | bytes 393224 | tf_op jit(solution)/shard_map/ppermute | solution.py:580
  4.9 10.9 %collective-permute-start.1 = (f32[4,64,128]{2,1,0:T(8,128)S(1)}, f32[4,64,128]{2,1,0:T(8,128)S(1)}, u32[]{:S(2)}, u32[]{:S(2)}) collective-permute-start(f32[4,64,128]{2,1,0:T(8,128)S(1)} %get-tuple-element.35), channel_id=1, source_target_pairs={{1,2},{0,31},{3,4},{2,1},{5,6},{4,3},{7,8},{6,5},{9,10},{8,7},{11,... | collective-permute-start | bytes 393224 | tf_op jit(solution)/shard_map/ppermute | solution.py:580
  9.0 5.7 %collective-permute-start.2 = (f32[64,128]{1,0:T(8,128)S(1)}, f32[64,128]{1,0:T(8,128)S(1)}, u32[]{:S(2)}, u32[]{:S(2)}) collective-permute-start(f32[64,128]{1,0:T(8,128)S(1)} %get-tuple-element.36), channel_id=1, source_target_pairs={{0,3},{1,2},{2,5},{3,4},{4,7},{5,6},{6,1},{7,0},{8,11},{9,10},{10,... | collective-permute-start | bytes 98312 | tf_op jit(solution)/shard_map/ppermute | solution.py:580
  9.0 6.2 %collective-permute-start.3 = (f32[64,128]{1,0:T(8,128)S(1)}, f32[64,128]{1,0:T(8,128)S(1)}, u32[]{:S(2)}, u32[]{:S(2)}) collective-permute-start(f32[64,128]{1,0:T(8,128)S(1)} %get-tuple-element.37), channel_id=1, source_target_pairs={{0,2},{1,3},{2,4},{3,5},{4,6},{5,7},{6,0},{7,1},{8,10},{9,11},{10,... | collective-permute-start | bytes 98312 | tf_op jit(solution)/shard_map/ppermute | solution.py:580
  16.8 1.5 %collective-permute-start.6 = (f32[3,128,128]{2,1,0:T(8,128)S(1)}, f32[3,128,128]{2,1,0:T(8,128)S(1)}, u32[]{:S(2)}, u32[]{:S(2)}) collective-permute-start(f32[3,128,128]{2,1,0:T(8,128)S(1)} %get-tuple-element.45.v1), channel_id=1, source_target_pairs={{0,1},{1,0},{2,3},{3,2},{4,5},{5,4},{6,7},{7,6},{8,9},{9,8},{10,11... | collective-permute-start | bytes 589832 | tf_op jit(solution)/shard_map/ppermute | solution.py:580
  16.9 1.9 %collective-permute-start.5 = (f32[3,128,128]{2,1,0:T(8,128)S(1)}, f32[3,128,128]{2,1,0:T(8,128)S(1)}, u32[]{:S(2)}, u32[]{:S(2)}) collective-permute-start(f32[3,128,128]{2,1,0:T(8,128)S(1)} %get-tuple-element.45.v1), channel_id=1, source_target_pairs={{1,2},{3,4},{2,1},{5,6},{4,3},{7,8},{6,5},{9,10},{8,7},{11,12},{10... | collective-permute-start | bytes 589832 | tf_op jit(solution)/shard_map/ppermute | solution.py:580
  19.6 6.9 %collective-permute-start.8 = (f32[3,128,128]{2,1,0:T(8,128)S(1)}, f32[3,128,128]{2,1,0:T(8,128)S(1)}, u32[]{:S(2)}, u32[]{:S(2)}) collective-permute-start(f32[3,128,128]{2,1,0:T(8,128)S(1)} %get-tuple-element.49.v2), channel_id=1, source_target_pairs={{0,1},{1,0},{2,3},{3,2},{4,5},{5,4},{6,7},{7,6},{8,9},{9,8},{10,11... | collective-permute-start | bytes 589832 | tf_op jit(solution)/shard_map/ppermute | solution.py:580
  25.5 1.1 %collective-permute-start.7 = (f32[3,128,128]{2,1,0:T(8,128)S(1)}, f32[3,128,128]{2,1,0:T(8,128)S(1)}, u32[]{:S(2)}, u32[]{:S(2)}) collective-permute-start(f32[3,128,128]{2,1,0:T(8,128)S(1)} %get-tuple-element.49.v2), channel_id=1, source_target_pairs={{2,1},{4,3},{6,5},{8,7},{10,9},{12,11},{14,13},{16,15},{18,17},{20... | collective-permute-start | bytes 589832 | tf_op jit(solution)/shard_map/ppermute | solution.py:580
  50.9 5.9 %collective-permute-start.11 = (f32[128,128]{1,0:T(8,128)S(1)}, f32[128,128]{1,0:T(8,128)S(1)}, u32[]{:S(2)}, u32[]{:S(2)}) collective-permute-start(f32[128,128]{1,0:T(8,128)S(1)} %get-tuple-element.57.refs_0_), channel_id=1, source_target_pairs={{0,24},{8,16},{16,8},{24,0},{1,25},{9,17},{17,9},{25,1},{2,26},{10... | collective-permute-start | bytes 196616 | tf_op jit(solution)/shard_map/ppermute | solution.py:631
  51.9 5.1 %collective-permute-start.10 = (f32[128,128]{1,0:T(8,128)S(1)}, f32[128,128]{1,0:T(8,128)S(1)}, u32[]{:S(2)}, u32[]{:S(2)}) collective-permute-start(f32[128,128]{1,0:T(8,128)S(1)} %get-tuple-element.57.refs_0_), channel_id=1, source_target_pairs={{0,16},{8,24},{16,0},{24,8},{1,17},{9,25},{17,1},{25,9},{2,18},{10... | collective-permute-start | bytes 196616 | tf_op jit(solution)/shard_map/ppermute | solution.py:631
  53.2 4.3 %collective-permute-start.9 = (f32[128,128]{1,0:T(8,128)S(1)}, f32[128,128]{1,0:T(8,128)S(1)}, u32[]{:S(2)}, u32[]{:S(2)}) collective-permute-start(f32[128,128]{1,0:T(8,128)S(1)} %get-tuple-element.57.refs_0_), channel_id=1, source_target_pairs={{0,8},{8,0},{16,24},{24,16},{1,9},{9,1},{17,25},{25,17},{2,10},{10... | collective-permute-start | bytes 196616 | tf_op jit(solution)/shard_map/ppermute | solution.py:631
  57.5 5.2 %collective-permute-start.12 = (f32[72,128]{1,0:T(8,128)S(1)}, f32[72,128]{1,0:T(8,128)S(1)}, u32[]{:S(2)}, u32[]{:S(2)}) collective-permute-start(f32[72,128]{1,0:T(8,128)S(1)} %get-tuple-element.63), channel_id=1, source_target_pairs={{1,2},{0,7},{3,4},{2,1},{5,6},{4,3},{7,0},{6,5},{9,10},{8,15},{11,... | collective-permute-start | bytes 110600 | tf_op jit(solution)/shard_map/ppermute | solution.py:580
  57.6 5.2 %collective-permute-start.13 = (f32[72,128]{1,0:T(8,128)S(1)}, f32[72,128]{1,0:T(8,128)S(1)}, u32[]{:S(2)}, u32[]{:S(2)}) collective-permute-start(f32[72,128]{1,0:T(8,128)S(1)} %get-tuple-element.64), channel_id=1, source_target_pairs={{0,6},{1,3},{2,0},{3,5},{4,2},{5,7},{6,4},{7,1},{8,14},{9,11},{10,... | collective-permute-start | bytes 110600 | tf_op jit(solution)/shard_map/ppermute | solution.py:580
  58.6 4.2 %collective-permute-start.14 = (f32[72,128]{1,0:T(8,128)S(1)}, f32[72,128]{1,0:T(8,128)S(1)}, u32[]{:S(2)}, u32[]{:S(2)}) collective-permute-start(f32[72,128]{1,0:T(8,128)S(1)} %get-tuple-element.65), channel_id=1, source_target_pairs={{0,1},{1,0},{2,3},{3,2},{4,5},{5,4},{6,7},{7,6},{8,9},{9,8},{10,11... | collective-permute-start | bytes 110600 | tf_op jit(solution)/shard_map/ppermute | solution.py:580

commit v15 on v14

--- a/solution.py
+++ b/solution.py
@@ -15,7 +15,7 @@
 filter_reach = 1.8
 
 AXES = ("mod", "slab", "sub")
-ROWS = 32
+ROWS = 64
 FACE = filter_reach - 1.0
 EDGE = filter_reach - math.sqrt(2.0)
 CORNER = filter_reach - math.sqrt(3.0)

time: 63.8 us -> 63.8 us (level)
  no operation moved by 1% of the time
where the time goes in v15:
time: 63.8 us; the launch traced here: 63.6 us
  blocking collectives  23.1 us (36%)
  starting transfers between devices  20.7 us (32%)
  waiting for transfers between devices  12 us (19%)
  Pallas kernels  5.97 us (9%)
  other arithmetic  0.99 us (2%)
  between operations  0.74 us (1%)
    all_to_all x1, blocking collectives, local(): lax.all_to_all(jnp.broadcast_to(moments, (devices, 8, width)), AXES, 0, 0...  23.1 us
    ppermute x12, starting transfers between devices, move(): return lax.ppermute(value, AXES, path[name])  17.2 us
    ppermute x12, waiting for transfers between devices, move(): return lax.ppermute(value, AXES, path[name])  8.98 us
    ppermute x3, starting transfers between devices, local(): lax.ppermute(slope, 'mod', pairs)  3.55 us
    ppermute x3, waiting for transfers between devices, local(): lax.ppermute(slope, 'mod', pairs)  3.06 us
  transfers between devices with their start and end apart: 15, of which 9 were waited for; matrix products, arithmetic and copies ran while one was open for 0% of the time, Pallas kernels for 3%

profile of v15, /device:TPU:0, one launch (start us, length us, event | category | flops | bytes accessed | tf_op | source)
XLA Modules:
  0.0 63.6 jit_solution(6451393414553092833)
XLA Ops:
  0.6 0.0 copy-start
  0.6 0.0 copy-start.1
  0.6 1.0 %subtract_convert_fusion.free = f32[3,2,64,128]{3,2,1,0:T(8,128)S(1)} fusion(s32[3,2,64,128]{3,2,1,0:T(8,128)} %param.4), kind=kLoop, calls=%fused_computation | loop fusion | flops 98304 | bytes 393216 | tf_op jit(solution)/shard_map/convert_element_type | solution.py:585
  1.6 0.0 copy-done
  1.7 0.0 copy-done.1
  1.7 0.1 prepare.1
  1.7 0.5 collective-permute-start.4
  2.3 2.6 %collective-permute-start = (f32[4,64,128]{2,1,0:T(8,128)S(1)}, f32[4,64,128]{2,1,0:T(8,128)S(1)}, u32[]{:S(2)}, u32[]{:S(2)}) collective-permute-start(f32[4,64,128]{2,1,0:T(8,128)S(1)} %get-tuple-element.34), channel_id=1, source_target_pairs={{0,2},{1,31},{2,4},{3,1},{4,6},{5,3},{6,8},{7,5},{8,10},{9,7},{10,... | collective-permute-start | bytes 393224 | tf_op jit(solution)/shard_map/ppermute | solution.py:580
  4.9 4.1 %collective-permute-start.1 = (f32[4,64,128]{2,1,0:T(8,128)S(1)}, f32[4,64,128]{2,1,0:T(8,128)S(1)}, u32[]{:S(2)}, u32[]{:S(2)}) collective-permute-start(f32[4,64,128]{2,1,0:T(8,128)S(1)} %get-tuple-element.35), channel_id=1, source_target_pairs={{1,2},{0,31},{3,4},{2,1},{5,6},{4,3},{7,8},{6,5},{9,10},{8,7},{11,... | collective-permute-start | bytes 393224 | tf_op jit(solution)/shard_map/ppermute | solution.py:580
  9.0 0.0 collective-permute-start.2
  9.0 1.6 %collective-permute-start.3 = (f32[64,128]{1,0:T(8,128)S(1)}, f32[64,128]{1,0:T(8,128)S(1)}, u32[]{:S(2)}, u32[]{:S(2)}) collective-permute-start(f32[64,128]{1,0:T(8,128)S(1)} %get-tuple-element.37), channel_id=1, source_target_pairs={{0,2},{1,3},{2,4},{3,5},{4,6},{5,7},{6,0},{7,1},{8,10},{9,11},{10,... | collective-permute-start | bytes 98312 | tf_op jit(solution)/shard_map/ppermute | solution.py:580
  10.6 0.0 collective-permute-done.4.swap
  10.6 0.8 %start_inner.1 = (f32[3,128,128]{2,1,0:T(8,128)S(1)}, f32[3,128,128]{2,1,0:T(8,128)S(1)}, f32[3,128,128]{2,1,0:T(8,128)S(1)}, f32[12,128,128]{2,1,0:T(8,128)S(1)}, f32[3,128,128]{2,1,0:T(8,128)S(1)}) custom-call(f32[11,64,128]{2,1,0:T(8,128)S(1)} %get-tuple-element.38.own, f32[11,64,128]{2,1,0:T(8,128)S(1)} %collective-permute-done.4.swap), custom_call_target="tpu_custom_call" | custom-call | flops 10000000 | bytes 4000000 | tf_op jit(solution)/shard_map/start_inner/pallas_call | solution.py:600
  11.4 3.2 %collective-permute-done.2.refs_2_ = f32[64,128]{1,0:T(8,128)S(1)} collective-permute-done((f32[64,128]{1,0:T(8,128)S(1)}, f32[64,128]{1,0:T(8,128)S(1)}, u32[]{:S(2)}, u32[]{:S(2)}) %collective-permute-start.2) | collective-permute-done | bytes 32800 | tf_op jit(solution)/shard_map/ppermute | solution.py:580
  14.7 0.5 collective-permute-done.3.refs_3_
  15.2 0.0 collective-permute-done.refs_0_
  15.2 0.6 collective-permute-done.1.refs_1_
  15.8 1.0 %start_outer.1 = (f32[3,128,128]{2,1,0:T(8,128)S(1)}, f32[3,128,128]{2,1,0:T(8,128)S(1)}, f32[128,128]{1,0:T(8,128)S(1)}, f32[128,128]{1,0:T(8,128)S(1)}, f32[12...) custom-call(f32[4,64,128]{2,1,0:T(8,128)S(1)} %collective-permute-done.refs_0_, ...), custom_call_target="tpu_custom_call" | custom-call | tf_op jit(solution)/shard_map/start_outer/pallas_call | solution.py:607
  16.8 0.1 collective-permute-start.6
  16.9 0.7 %collective-permute-start.5 = (f32[3,128,128]{2,1,0:T(8,128)S(1)}, f32[3,128,128]{2,1,0:T(8,128)S(1)}, u32[]{:S(2)}, u32[]{:S(2)}) collective-permute-start(f32[3,128,128]{2,1,0:T(8,128)S(1)} %get-tuple-element.45.v1), channel_id=1, source_target_pairs={{1,2},{3,4},{2,1},{5,6},{4,3},{7,8},{6,5},{9,10},{8,7},{11,12},{10... | collective-permute-start | bytes 589832 | tf_op jit(solution)/shard_map/ppermute | solution.py:580
  17.6 0.7 %collective-permute-done.6.inner.v1_inner = f32[3,128,128]{2,1,0:T(8,128)S(1)} collective-permute-done((f32[3,128,128]{2,1,0:T(8,128)S(1)}, f32[3,128,128]{2,1,0:T(8,128)S(1)}, u32[]{:S(2)}, u32[]{:S(2)}) %collective-permute-start.6) | collective-permute-done | bytes 196640 | tf_op jit(solution)/shard_map/ppermute | solution.py:580
  18.3 0.5 second_inner.1.fields
  18.8 0.0 collective-permute-done.5.outer
  18.8 0.8 %second_outer.1 = (f32[3,128,128]{2,1,0:T(8,128)S(1)}, f32[3,128,128]{2,1,0:T(8,128)S(1)}, f32[8,128]{1,0:T(8,128)S(1)}) custom-call(f32[3,128,128]{2,1,0:T(8,128)S(1)} %get-tuple-element.45.v1, f32[3,128,128]{2,1,0:T(8,128)S(1)} %collective-permute-done.5.outer, f32[3,128,128]{2,1,0:T(8,128)S(1)} %collective-permute-done.6.inner.v1_inner, ...), custom_call_target="tpu_custom_call" | custom-call | tf_op jit(solution)/shard_map/second_outer/pallas_call | solution.py:616
  19.6 5.8 %collective-permute-start.8 = (f32[3,128,128]{2,1,0:T(8,128)S(1)}, f32[3,128,128]{2,1,0:T(8,128)S(1)}, u32[]{:S(2)}, u32[]{:S(2)}) collective-permute-start(f32[3,128,128]{2,1,0:T(8,128)S(1)} %get-tuple-element.49.v2), channel_id=1, source_target_pairs={{0,1},{1,0},{2,3},{3,2},{4,5},{5,4},{6,7},{7,6},{8,9},{9,8},{10,11... | collective-permute-start | bytes 589832 | tf_op jit(solution)/shard_map/ppermute | solution.py:580
  25.4 0.7 %collective-permute-start.7 = (f32[3,128,128]{2,1,0:T(8,128)S(1)}, f32[3,128,128]{2,1,0:T(8,128)S(1)}, u32[]{:S(2)}, u32[]{:S(2)}) collective-permute-start(f32[3,128,128]{2,1,0:T(8,128)S(1)} %get-tuple-element.49.v2), channel_id=1, source_target_pairs={{2,1},{4,3},{6,5},{8,7},{10,9},{12,11},{14,13},{16,15},{18,17},{20... | collective-permute-start | bytes 589832 | tf_op jit(solution)/shard_map/ppermute | solution.py:580
  26.1 0.4 collective-permute-done.8.v2_inner
  26.5 0.0 collective-permute-done.7.v2_outer
  26.5 0.5 third.1
  27.0 23.1 %all_to_all.5.gathered = f32[32,8,128]{2,1,0:T(8,128)S(1)} all-to-all(f32[32,8,128]{2,1,0:T(8,128)S(1)} %broadcast_in_dim.3), channel_id=1, replica_groups=mesh['mod'=4,'slab'=4,'sub'=2] {'mod','slab','sub'}, dimensions={0} | all-to-all | bytes 262144 | tf_op jit(solution)/shard_map/all_to_all | solution.py:625
  50.2 0.7 %combine.1 = (f32[128,128]{1,0:T(8,128)S(1)}, f32[3,8,128]{2,1,0:T(8,128)S(1)}) custom-call(f32[32,8,128]{2,1,0:T(8,128)S(1)} %all_to_all.5.gathered, f32[3,128,128]{2,1,0:T(8,128)S(1)} %get-tuple-element.40.refs_4_.v0, f32[3,128,128]{2,1,0:T(8,128)S(1)} %get-tuple-element.53.v0_high, f32[3,128,128]{2,1,0:T(8,128)S(1)} %get-tuple-element.45.v1, ...), custom_call_target="tpu_custom_call" | custom-call | tf_op jit(solution)/shard_map/combine/pallas_call | solution.py:628
  50.9 1.0 %collective-permute-start.11 = (f32[128,128]{1,0:T(8,128)S(1)}, f32[128,128]{1,0:T(8,128)S(1)}, u32[]{:S(2)}, u32[]{:S(2)}) collective-permute-start(f32[128,128]{1,0:T(8,128)S(1)} %get-tuple-element.57.refs_0_), channel_id=1, source_target_pairs={{0,24},{8,16},{16,8},{24,0},{1,25},{9,17},{17,9},{25,1},{2,26},{10... | collective-permute-start | bytes 196616 | tf_op jit(solution)/shard_map/ppermute | solution.py:631
  51.9 1.3 %collective-permute-start.10 = (f32[128,128]{1,0:T(8,128)S(1)}, f32[128,128]{1,0:T(8,128)S(1)}, u32[]{:S(2)}, u32[]{:S(2)}) collective-permute-start(f32[128,128]{1,0:T(8,128)S(1)} %get-tuple-element.57.refs_0_), channel_id=1, source_target_pairs={{0,16},{8,24},{16,0},{24,8},{1,17},{9,25},{17,1},{25,9},{2,18},{10... | collective-permute-start | bytes 196616 | tf_op jit(solution)/shard_map/ppermute | solution.py:631
  53.2 1.2 %collective-permute-start.9 = (f32[128,128]{1,0:T(8,128)S(1)}, f32[128,128]{1,0:T(8,128)S(1)}, u32[]{:S(2)}, u32[]{:S(2)}) collective-permute-start(f32[128,128]{1,0:T(8,128)S(1)} %get-tuple-element.57.refs_0_), channel_id=1, source_target_pairs={{0,8},{8,0},{16,24},{24,16},{1,9},{9,1},{17,25},{25,17},{2,10},{10... | collective-permute-start | bytes 196616 | tf_op jit(solution)/shard_map/ppermute | solution.py:631
  54.4 2.3 %collective-permute-done.11.refs_3_ = f32[128,128]{1,0:T(8,128)S(1)} collective-permute-done((f32[128,128]{1,0:T(8,128)S(1)}, f32[128,128]{1,0:T(8,128)S(1)}, u32[]{:S(2)}, u32[]{:S(2)}) %collective-permute-start.11) | collective-permute-done | bytes 65568 | tf_op jit(solution)/shard_map/ppermute | solution.py:631
  56.7 0.2 collective-permute-done.10.refs_2_
  57.0 0.5 collective-permute-done.9.refs_1_
  57.5 0.1 collective-permute-start.12
  57.6 1.0 %collective-permute-start.13 = (f32[72,128]{1,0:T(8,128)S(1)}, f32[72,128]{1,0:T(8,128)S(1)}, u32[]{:S(2)}, u32[]{:S(2)}) collective-permute-start(f32[72,128]{1,0:T(8,128)S(1)} %get-tuple-element.64), channel_id=1, source_target_pairs={{0,6},{1,3},{2,0},{3,5},{4,2},{5,7},{6,4},{7,1},{8,14},{9,11},{10,... | collective-permute-start | bytes 110600 | tf_op jit(solution)/shard_map/ppermute | solution.py:580
  58.5 0.0 collective-permute-start.14
  58.6 0.7 %displace.1 = f32[3,2,64,128]{3,2,1,0:T(8,128)} custom-call(f32[3,8,128]{2,1,0:T(8,128)S(1)} %get-tuple-element.60.factors, f32[3,128,128]{2,1,0:T(8,128)S(1)} %get-tuple-element.40.refs_4_.v0, f32[3,128,128]{2,1,0:T(8,128)S(1)} %get-tuple-element.41.refs_5_.v0_inner, f32[3,128,128]{2,1,0:T(8,128)S(1)} %get-tuple-element.45.v1, ...), custom_call_target="tpu_custom_call" | custom-call | flops 10000000 | bytes 4000000 | tf_op jit(solution)/shard_map/displace/pallas_call | solution.py:632
  59.3 3.5 %collective-permute-done.12.outer = f32[72,128]{1,0:T(8,128)S(1)} collective-permute-done((f32[72,128]{1,0:T(8,128)S(1)}, f32[72,128]{1,0:T(8,128)S(1)}, u32[]{:S(2)}, u32[]{:S(2)}) %collective-permute-start.12) | collective-permute-done | bytes 36896 | tf_op jit(solution)/shard_map/ppermute | solution.py:580
  62.8 0.0 collective-permute-done.13.far
  62.8 0.0 collective-permute-done.14.partner
  62.8 0.9 %gradient.1 = f32[2,64,128]{2,1,0:T(8,128)} custom-call(f32[128,128]{1,0:T(8,128)S(1)} %get-tuple-element.62.scaled, f32[72,128]{1,0:T(8,128)S(1)} %collective-permute-done.12.outer, f32[72,128]{1,0:T(8,128)S(1)} %collective-permute-done.13.far, f32[72,128]{1,0:T(8,128)S(1)} %collective-permute-done.14.partner), custom_call_target="tpu_custom_call" | custom-call | tf_op jit(solution)/shard_map/gradient/pallas_call | solution.py:643
  (2 shorter events, 0.0 us)
Async XLA Ops:
  0.6 1.0 %copy-start = (s32[3,2,64,128]{3,2,1,0:T(8,128)S(1)}, s32[3,2,64,128]{3,2,1,0:T(8,128)}, u32[]{:S(2)}) copy-start(s32[3,2,64,128]{3,2,1,0:T(8,128)} %load.1) | copy-start | bytes 589828
  0.6 1.0 %copy-start.1 = (f32[2,64,128]{2,1,0:T(8,128)S(1)}, f32[2,64,128]{2,1,0:T(8,128)}, u32[]{:S(2)}) copy-start(f32[2,64,128]{2,1,0:T(8,128)} %design.1) | copy-start | bytes 196612
  1.7 8.9 %collective-permute-start.4 = (f32[11,64,128]{2,1,0:T(8,128)S(1)}, f32[11,64,128]{2,1,0:T(8,128)S(1)}, u32[]{:S(2)}, u32[]{:S(2)}) collective-permute-start(f32[11,64,128]{2,1,0:T(8,128)S(1)} %get-tuple-element.39), channel_id=1, source_target_pairs={{0,1},{1,0},{2,3},{3,2},{4,5},{5,4},{6,7},{7,6},{8,9},{9,8},{10,11... | collective-permute-start | bytes 1081352 | tf_op jit(solution)/shard_map/ppermute | solution.py:580
  2.3 12.9 %collective-permute-start = (f32[4,64,128]{2,1,0:T(8,128)S(1)}, f32[4,64,128]{2,1,0:T(8,128)S(1)}, u32[]{:S(2)}, u32[]{:S(2)}) collective-permute-start(f32[4,64,128]{2,1,0:T(8,128)S(1)} %get-tuple-element.34), channel_id=1, source_target_pairs={{0,2},{1,31},{2,4},{3,1},{4,6},{5,3},{6,8},{7,5},{8,10},{9,7},{10,... | collective-permute-start | bytes 393224 | tf_op jit(solution)/shard_map/ppermute | solution.py:580
  4.9 10.9 %collective-permute-start.1 = (f32[4,64,128]{2,1,0:T(8,128)S(1)}, f32[4,64,128]{2,1,0:T(8,128)S(1)}, u32[]{:S(2)}, u32[]{:S(2)}) collective-permute-start(f32[4,64,128]{2,1,0:T(8,128)S(1)} %get-tuple-element.35), channel_id=1, source_target_pairs={{1,2},{0,31},{3,4},{2,1},{5,6},{4,3},{7,8},{6,5},{9,10},{8,7},{11,... | collective-permute-start | bytes 393224 | tf_op jit(solution)/shard_map/ppermute | solution.py:580
  9.0 5.7 %collective-permute-start.2 = (f32[64,128]{1,0:T(8,128)S(1)}, f32[64,128]{1,0:T(8,128)S(1)}, u32[]{:S(2)}, u32[]{:S(2)}) collective-permute-start(f32[64,128]{1,0:T(8,128)S(1)} %get-tuple-element.36), channel_id=1, source_target_pairs={{0,3},{1,2},{2,5},{3,4},{4,7},{5,6},{6,1},{7,0},{8,11},{9,10},{10,... | collective-permute-start | bytes 98312 | tf_op jit(solution)/shard_map/ppermute | solution.py:580
  9.0 6.2 %collective-permute-start.3 = (f32[64,128]{1,0:T(8,128)S(1)}, f32[64,128]{1,0:T(8,128)S(1)}, u32[]{:S(2)}, u32[]{:S(2)}) collective-permute-start(f32[64,128]{1,0:T(8,128)S(1)} %get-tuple-element.37), channel_id=1, source_target_pairs={{0,2},{1,3},{2,4},{3,5},{4,6},{5,7},{6,0},{7,1},{8,10},{9,11},{10,... | collective-permute-start | bytes 98312 | tf_op jit(solution)/shard_map/ppermute | solution.py:580
  16.8 1.5 %collective-permute-start.6 = (f32[3,128,128]{2,1,0:T(8,128)S(1)}, f32[3,128,128]{2,1,0:T(8,128)S(1)}, u32[]{:S(2)}, u32[]{:S(2)}) collective-permute-start(f32[3,128,128]{2,1,0:T(8,128)S(1)} %get-tuple-element.45.v1), channel_id=1, source_target_pairs={{0,1},{1,0},{2,3},{3,2},{4,5},{5,4},{6,7},{7,6},{8,9},{9,8},{10,11... | collective-permute-start | bytes 589832 | tf_op jit(solution)/shard_map/ppermute | solution.py:580
  16.9 1.9 %collective-permute-start.5 = (f32[3,128,128]{2,1,0:T(8,128)S(1)}, f32[3,128,128]{2,1,0:T(8,128)S(1)}, u32[]{:S(2)}, u32[]{:S(2)}) collective-permute-start(f32[3,128,128]{2,1,0:T(8,128)S(1)} %get-tuple-element.45.v1), channel_id=1, source_target_pairs={{1,2},{3,4},{2,1},{5,6},{4,3},{7,8},{6,5},{9,10},{8,7},{11,12},{10... | collective-permute-start | bytes 589832 | tf_op jit(solution)/shard_map/ppermute | solution.py:580
  19.6 6.9 %collective-permute-start.8 = (f32[3,128,128]{2,1,0:T(8,128)S(1)}, f32[3,128,128]{2,1,0:T(8,128)S(1)}, u32[]{:S(2)}, u32[]{:S(2)}) collective-permute-start(f32[3,128,128]{2,1,0:T(8,128)S(1)} %get-tuple-element.49.v2), channel_id=1, source_target_pairs={{0,1},{1,0},{2,3},{3,2},{4,5},{5,4},{6,7},{7,6},{8,9},{9,8},{10,11... | collective-permute-start | bytes 589832 | tf_op jit(solution)/shard_map/ppermute | solution.py:580
  25.4 1.1 %collective-permute-start.7 = (f32[3,128,128]{2,1,0:T(8,128)S(1)}, f32[3,128,128]{2,1,0:T(8,128)S(1)}, u32[]{:S(2)}, u32[]{:S(2)}) collective-permute-start(f32[3,128,128]{2,1,0:T(8,128)S(1)} %get-tuple-element.49.v2), channel_id=1, source_target_pairs={{2,1},{4,3},{6,5},{8,7},{10,9},{12,11},{14,13},{16,15},{18,17},{20... | collective-permute-start | bytes 589832 | tf_op jit(solution)/shard_map/ppermute | solution.py:580
  50.9 5.9 %collective-permute-start.11 = (f32[128,128]{1,0:T(8,128)S(1)}, f32[128,128]{1,0:T(8,128)S(1)}, u32[]{:S(2)}, u32[]{:S(2)}) collective-permute-start(f32[128,128]{1,0:T(8,128)S(1)} %get-tuple-element.57.refs_0_), channel_id=1, source_target_pairs={{0,24},{8,16},{16,8},{24,0},{1,25},{9,17},{17,9},{25,1},{2,26},{10... | collective-permute-start | bytes 196616 | tf_op jit(solution)/shard_map/ppermute | solution.py:631
  51.9 5.1 %collective-permute-start.10 = (f32[128,128]{1,0:T(8,128)S(1)}, f32[128,128]{1,0:T(8,128)S(1)}, u32[]{:S(2)}, u32[]{:S(2)}) collective-permute-start(f32[128,128]{1,0:T(8,128)S(1)} %get-tuple-element.57.refs_0_), channel_id=1, source_target_pairs={{0,16},{8,24},{16,0},{24,8},{1,17},{9,25},{17,1},{25,9},{2,18},{10... | collective-permute-start | bytes 196616 | tf_op jit(solution)/shard_map/ppermute | solution.py:631
  53.2 4.3 %collective-permute-start.9 = (f32[128,128]{1,0:T(8,128)S(1)}, f32[128,128]{1,0:T(8,128)S(1)}, u32[]{:S(2)}, u32[]{:S(2)}) collective-permute-start(f32[128,128]{1,0:T(8,128)S(1)} %get-tuple-element.57.refs_0_), channel_id=1, source_target_pairs={{0,8},{8,0},{16,24},{24,16},{1,9},{9,1},{17,25},{25,17},{2,10},{10... | collective-permute-start | bytes 196616 | tf_op jit(solution)/shard_map/ppermute | solution.py:631
  57.5 5.2 %collective-permute-start.12 = (f32[72,128]{1,0:T(8,128)S(1)}, f32[72,128]{1,0:T(8,128)S(1)}, u32[]{:S(2)}, u32[]{:S(2)}) collective-permute-start(f32[72,128]{1,0:T(8,128)S(1)} %get-tuple-element.63), channel_id=1, source_target_pairs={{1,2},{0,7},{3,4},{2,1},{5,6},{4,3},{7,0},{6,5},{9,10},{8,15},{11,... | collective-permute-start | bytes 110600 | tf_op jit(solution)/shard_map/ppermute | solution.py:580
  57.6 5.2 %collective-permute-start.13 = (f32[72,128]{1,0:T(8,128)S(1)}, f32[72,128]{1,0:T(8,128)S(1)}, u32[]{:S(2)}, u32[]{:S(2)}) collective-permute-start(f32[72,128]{1,0:T(8,128)S(1)} %get-tuple-element.64), channel_id=1, source_target_pairs={{0,6},{1,3},{2,0},{3,5},{4,2},{5,7},{6,4},{7,1},{8,14},{9,11},{10,... | collective-permute-start | bytes 110600 | tf_op jit(solution)/shard_map/ppermute | solution.py:580
  58.5 4.2 %collective-permute-start.14 = (f32[72,128]{1,0:T(8,128)S(1)}, f32[72,128]{1,0:T(8,128)S(1)}, u32[]{:S(2)}, u32[]{:S(2)}) collective-permute-start(f32[72,128]{1,0:T(8,128)S(1)} %get-tuple-element.65), channel_id=1, source_target_pairs={{0,1},{1,0},{2,3},{3,2},{4,5},{5,4},{6,7},{7,6},{8,9},{9,8},{10,11... | collective-permute-start | bytes 110600 | tf_op jit(solution)/shard_map/ppermute | solution.py:580

commit v16 on v15

--- a/solution.py
+++ b/solution.py
@@ -15,7 +15,7 @@
 filter_reach = 1.8
 
 AXES = ("mod", "slab", "sub")
-ROWS = 64
+ROWS = 128
 FACE = filter_reach - 1.0
 EDGE = filter_reach - math.sqrt(2.0)
 CORNER = filter_reach - math.sqrt(3.0)

time: 63.8 us -> 63.8 us (level)
  no operation moved by 1% of the time
where the time goes in v16:
time: 63.8 us; the launch traced here: 63.7 us
  blocking collectives  23.1 us (36%)
  starting transfers between devices  20.7 us (32%)
  waiting for transfers between devices  12 us (19%)
  Pallas kernels  6.04 us (9%)
  other arithmetic  0.99 us (2%)
  between operations  0.74 us (1%)
    all_to_all x1, blocking collectives, local(): lax.all_to_all(jnp.broadcast_to(moments, (devices, 8, width)), AXES, 0, 0...  23.1 us
    ppermute x12, starting transfers between devices, move(): return lax.ppermute(value, AXES, path[name])  17.2 us
    ppermute x12, waiting for transfers between devices, move(): return lax.ppermute(value, AXES, path[name])  8.95 us
    ppermute x3, starting transfers between devices, local(): lax.ppermute(slope, 'mod', pairs)  3.55 us
    ppermute x3, waiting for transfers between devices, local(): lax.ppermute(slope, 'mod', pairs)  3.06 us
  transfers between devices with their start and end apart: 15, of which 9 were waited for; matrix products, arithmetic and copies ran while one was open for 0% of the time, Pallas kernels for 3%

profile of v16, /device:TPU:0, one launch (start us, length us, event | category | flops | bytes accessed | tf_op | source)
XLA Modules:
  0.0 63.7 jit_solution(9034864598755654627)
XLA Ops:
  0.6 0.0 copy-start
  0.6 0.0 copy-start.1
  0.6 1.0 %subtract_convert_fusion.free = f32[3,2,64,128]{3,2,1,0:T(8,128)S(1)} fusion(s32[3,2,64,128]{3,2,1,0:T(8,128)} %param.4), kind=kLoop, calls=%fused_computation | loop fusion | flops 98304 | bytes 393216 | tf_op jit(solution)/shard_map/convert_element_type | solution.py:585
  1.6 0.0 copy-done
  1.7 0.0 copy-done.1
  1.7 0.1 prepare.1
  1.7 0.5 collective-permute-start.4
  2.3 2.6 %collective-permute-start = (f32[4,64,128]{2,1,0:T(8,128)S(1)}, f32[4,64,128]{2,1,0:T(8,128)S(1)}, u32[]{:S(2)}, u32[]{:S(2)}) collective-permute-start(f32[4,64,128]{2,1,0:T(8,128)S(1)} %get-tuple-element.34), channel_id=1, source_target_pairs={{0,2},{1,31},{2,4},{3,1},{4,6},{5,3},{6,8},{7,5},{8,10},{9,7},{10,... | collective-permute-start | bytes 393224 | tf_op jit(solution)/shard_map/ppermute | solution.py:580
  4.9 4.1 %collective-permute-start.1 = (f32[4,64,128]{2,1,0:T(8,128)S(1)}, f32[4,64,128]{2,1,0:T(8,128)S(1)}, u32[]{:S(2)}, u32[]{:S(2)}) collective-permute-start(f32[4,64,128]{2,1,0:T(8,128)S(1)} %get-tuple-element.35), channel_id=1, source_target_pairs={{1,2},{0,31},{3,4},{2,1},{5,6},{4,3},{7,8},{6,5},{9,10},{8,7},{11,... | collective-permute-start | bytes 393224 | tf_op jit(solution)/shard_map/ppermute | solution.py:580
  9.0 0.0 collective-permute-start.2
  9.0 1.6 %collective-permute-start.3 = (f32[64,128]{1,0:T(8,128)S(1)}, f32[64,128]{1,0:T(8,128)S(1)}, u32[]{:S(2)}, u32[]{:S(2)}) collective-permute-start(f32[64,128]{1,0:T(8,128)S(1)} %get-tuple-element.37), channel_id=1, source_target_pairs={{0,2},{1,3},{2,4},{3,5},{4,6},{5,7},{6,0},{7,1},{8,10},{9,11},{10,... | collective-permute-start | bytes 98312 | tf_op jit(solution)/shard_map/ppermute | solution.py:580
  10.6 0.0 collective-permute-done.4.swap
  10.6 0.8 %start_inner.1 = (f32[3,128,128]{2,1,0:T(8,128)S(1)}, f32[3,128,128]{2,1,0:T(8,128)S(1)}, f32[3,128,128]{2,1,0:T(8,128)S(1)}, f32[12,128,128]{2,1,0:T(8,128)S(1)}, f32[3,128,128]{2,1,0:T(8,128)S(1)}) custom-call(f32[11,64,128]{2,1,0:T(8,128)S(1)} %get-tuple-element.38.own, f32[11,64,128]{2,1,0:T(8,128)S(1)} %collective-permute-done.4.swap), custom_call_target="tpu_custom_call" | custom-call | flops 10000000 | bytes 4000000 | tf_op jit(solution)/shard_map/start_inner/pallas_call | solution.py:600
  11.5 3.2 %collective-permute-done.2.refs_2_ = f32[64,128]{1,0:T(8,128)S(1)} collective-permute-done((f32[64,128]{1,0:T(8,128)S(1)}, f32[64,128]{1,0:T(8,128)S(1)}, u32[]{:S(2)}, u32[]{:S(2)}) %collective-permute-start.2) | collective-permute-done | bytes 32800 | tf_op jit(solution)/shard_map/ppermute | solution.py:580
  14.7 0.5 collective-permute-done.3.refs_3_
  15.2 0.0 collective-permute-done.refs_0_
  15.2 0.6 collective-permute-done.1.refs_1_
  15.8 1.0 %start_outer.1 = (f32[3,128,128]{2,1,0:T(8,128)S(1)}, f32[3,128,128]{2,1,0:T(8,128)S(1)}, f32[128,128]{1,0:T(8,128)S(1)}, f32[128,128]{1,0:T(8,128)S(1)}, f32[12...) custom-call(f32[4,64,128]{2,1,0:T(8,128)S(1)} %collective-permute-done.refs_0_, ...), custom_call_target="tpu_custom_call" | custom-call | tf_op jit(solution)/shard_map/start_outer/pallas_call | solution.py:607
  16.8 0.1 collective-permute-start.6
  16.9 0.7 %collective-permute-start.5 = (f32[3,128,128]{2,1,0:T(8,128)S(1)}, f32[3,128,128]{2,1,0:T(8,128)S(1)}, u32[]{:S(2)}, u32[]{:S(2)}) collective-permute-start(f32[3,128,128]{2,1,0:T(8,128)S(1)} %get-tuple-element.45.v1), channel_id=1, source_target_pairs={{1,2},{3,4},{2,1},{5,6},{4,3},{7,8},{6,5},{9,10},{8,7},{11,12},{10... | collective-permute-start | bytes 589832 | tf_op jit(solution)/shard_map/ppermute | solution.py:580
  17.6 0.7 %collective-permute-done.6.inner.v1_inner = f32[3,128,128]{2,1,0:T(8,128)S(1)} collective-permute-done((f32[3,128,128]{2,1,0:T(8,128)S(1)}, f32[3,128,128]{2,1,0:T(8,128)S(1)}, u32[]{:S(2)}, u32[]{:S(2)}) %collective-permute-start.6) | collective-permute-done | bytes 196640 | tf_op jit(solution)/shard_map/ppermute | solution.py:580
  18.3 0.5 second_inner.1.fields
  18.8 0.0 collective-permute-done.5.outer
  18.8 0.8 %second_outer.1 = (f32[3,128,128]{2,1,0:T(8,128)S(1)}, f32[3,128,128]{2,1,0:T(8,128)S(1)}, f32[8,128]{1,0:T(8,128)S(1)}) custom-call(f32[3,128,128]{2,1,0:T(8,128)S(1)} %get-tuple-element.45.v1, f32[3,128,128]{2,1,0:T(8,128)S(1)} %collective-permute-done.5.outer, f32[3,128,128]{2,1,0:T(8,128)S(1)} %collective-permute-done.6.inner.v1_inner, ...), custom_call_target="tpu_custom_call" | custom-call | tf_op jit(solution)/shard_map/second_outer/pallas_call | solution.py:616
  19.6 5.8 %collective-permute-start.8 = (f32[3,128,128]{2,1,0:T(8,128)S(1)}, f32[3,128,128]{2,1,0:T(8,128)S(1)}, u32[]{:S(2)}, u32[]{:S(2)}) collective-permute-start(f32[3,128,128]{2,1,0:T(8,128)S(1)} %get-tuple-element.49.v2), channel_id=1, source_target_pairs={{0,1},{1,0},{2,3},{3,2},{4,5},{5,4},{6,7},{7,6},{8,9},{9,8},{10,11... | collective-permute-start | bytes 589832 | tf_op jit(solution)/shard_map/ppermute | solution.py:580
  25.4 0.7 %collective-permute-start.7 = (f32[3,128,128]{2,1,0:T(8,128)S(1)}, f32[3,128,128]{2,1,0:T(8,128)S(1)}, u32[]{:S(2)}, u32[]{:S(2)}) collective-permute-start(f32[3,128,128]{2,1,0:T(8,128)S(1)} %get-tuple-element.49.v2), channel_id=1, source_target_pairs={{2,1},{4,3},{6,5},{8,7},{10,9},{12,11},{14,13},{16,15},{18,17},{20... | collective-permute-start | bytes 589832 | tf_op jit(solution)/shard_map/ppermute | solution.py:580
  26.1 0.4 collective-permute-done.8.v2_inner
  26.5 0.0 collective-permute-done.7.v2_outer
  26.5 0.5 third.1
  27.0 23.1 %all_to_all.5.gathered = f32[32,8,128]{2,1,0:T(8,128)S(1)} all-to-all(f32[32,8,128]{2,1,0:T(8,128)S(1)} %broadcast_in_dim.3), channel_id=1, replica_groups=mesh['mod'=4,'slab'=4,'sub'=2] {'mod','slab','sub'}, dimensions={0} | all-to-all | bytes 262144 | tf_op jit(solution)/shard_map/all_to_all | solution.py:625
  50.2 0.7 %combine.1 = (f32[128,128]{1,0:T(8,128)S(1)}, f32[3,8,128]{2,1,0:T(8,128)S(1)}) custom-call(f32[32,8,128]{2,1,0:T(8,128)S(1)} %all_to_all.5.gathered, f32[3,128,128]{2,1,0:T(8,128)S(1)} %get-tuple-element.40.refs_4_.v0, f32[3,128,128]{2,1,0:T(8,128)S(1)} %get-tuple-element.53.v0_high, f32[3,128,128]{2,1,0:T(8,128)S(1)} %get-tuple-element.45.v1, ...), custom_call_target="tpu_custom_call" | custom-call | tf_op jit(solution)/shard_map/combine/pallas_call | solution.py:628
  50.9 1.0 %collective-permute-start.11 = (f32[128,128]{1,0:T(8,128)S(1)}, f32[128,128]{1,0:T(8,128)S(1)}, u32[]{:S(2)}, u32[]{:S(2)}) collective-permute-start(f32[128,128]{1,0:T(8,128)S(1)} %get-tuple-element.57.refs_0_), channel_id=1, source_target_pairs={{0,24},{8,16},{16,8},{24,0},{1,25},{9,17},{17,9},{25,1},{2,26},{10... | collective-permute-start | bytes 196616 | tf_op jit(solution)/shard_map/ppermute | solution.py:631
  51.9 1.3 %collective-permute-start.10 = (f32[128,128]{1,0:T(8,128)S(1)}, f32[128,128]{1,0:T(8,128)S(1)}, u32[]{:S(2)}, u32[]{:S(2)}) collective-permute-start(f32[128,128]{1,0:T(8,128)S(1)} %get-tuple-element.57.refs_0_), channel_id=1, source_target_pairs={{0,16},{8,24},{16,0},{24,8},{1,17},{9,25},{17,1},{25,9},{2,18},{10... | collective-permute-start | bytes 196616 | tf_op jit(solution)/shard_map/ppermute | solution.py:631
  53.2 1.2 %collective-permute-start.9 = (f32[128,128]{1,0:T(8,128)S(1)}, f32[128,128]{1,0:T(8,128)S(1)}, u32[]{:S(2)}, u32[]{:S(2)}) collective-permute-start(f32[128,128]{1,0:T(8,128)S(1)} %get-tuple-element.57.refs_0_), channel_id=1, source_target_pairs={{0,8},{8,0},{16,24},{24,16},{1,9},{9,1},{17,25},{25,17},{2,10},{10... | collective-permute-start | bytes 196616 | tf_op jit(solution)/shard_map/ppermute | solution.py:631
  54.5 2.3 %collective-permute-done.11.refs_3_ = f32[128,128]{1,0:T(8,128)S(1)} collective-permute-done((f32[128,128]{1,0:T(8,128)S(1)}, f32[128,128]{1,0:T(8,128)S(1)}, u32[]{:S(2)}, u32[]{:S(2)}) %collective-permute-start.11) | collective-permute-done | bytes 65568 | tf_op jit(solution)/shard_map/ppermute | solution.py:631
  56.8 0.2 collective-permute-done.10.refs_2_
  57.0 0.5 collective-permute-done.9.refs_1_
  57.5 0.1 collective-permute-start.12
  57.6 1.0 %collective-permute-start.13 = (f32[72,128]{1,0:T(8,128)S(1)}, f32[72,128]{1,0:T(8,128)S(1)}, u32[]{:S(2)}, u32[]{:S(2)}) collective-permute-start(f32[72,128]{1,0:T(8,128)S(1)} %get-tuple-element.64), channel_id=1, source_target_pairs={{0,6},{1,3},{2,0},{3,5},{4,2},{5,7},{6,4},{7,1},{8,14},{9,11},{10,... | collective-permute-start | bytes 110600 | tf_op jit(solution)/shard_map/ppermute | solution.py:580
  58.6 0.0 collective-permute-start.14
  58.6 0.7 %displace.1 = f32[3,2,64,128]{3,2,1,0:T(8,128)} custom-call(f32[3,8,128]{2,1,0:T(8,128)S(1)} %get-tuple-element.60.factors, f32[3,128,128]{2,1,0:T(8,128)S(1)} %get-tuple-element.40.refs_4_.v0, f32[3,128,128]{2,1,0:T(8,128)S(1)} %get-tuple-element.41.refs_5_.v0_inner, f32[3,128,128]{2,1,0:T(8,128)S(1)} %get-tuple-element.45.v1, ...), custom_call_target="tpu_custom_call" | custom-call | flops 10000000 | bytes 4000000 | tf_op jit(solution)/shard_map/displace/pallas_call | solution.py:632
  59.3 3.5 %collective-permute-done.12.outer = f32[72,128]{1,0:T(8,128)S(1)} collective-permute-done((f32[72,128]{1,0:T(8,128)S(1)}, f32[72,128]{1,0:T(8,128)S(1)}, u32[]{:S(2)}, u32[]{:S(2)}) %collective-permute-start.12) | collective-permute-done | bytes 36896 | tf_op jit(solution)/shard_map/ppermute | solution.py:580
  62.8 0.0 collective-permute-done.13.far
  62.8 0.0 collective-permute-done.14.partner
  62.8 0.9 %gradient.1 = f32[2,64,128]{2,1,0:T(8,128)} custom-call(f32[128,128]{1,0:T(8,128)S(1)} %get-tuple-element.62.scaled, f32[72,128]{1,0:T(8,128)S(1)} %collective-permute-done.12.outer, f32[72,128]{1,0:T(8,128)S(1)} %collective-permute-done.13.far, f32[72,128]{1,0:T(8,128)S(1)} %collective-permute-done.14.partner), custom_call_target="tpu_custom_call" | custom-call | tf_op jit(solution)/shard_map/gradient/pallas_call | solution.py:643
  (2 shorter events, 0.0 us)
Async XLA Ops:
  0.6 1.0 %copy-start = (s32[3,2,64,128]{3,2,1,0:T(8,128)S(1)}, s32[3,2,64,128]{3,2,1,0:T(8,128)}, u32[]{:S(2)}) copy-start(s32[3,2,64,128]{3,2,1,0:T(8,128)} %load.1) | copy-start | bytes 589828
  0.6 1.0 %copy-start.1 = (f32[2,64,128]{2,1,0:T(8,128)S(1)}, f32[2,64,128]{2,1,0:T(8,128)}, u32[]{:S(2)}) copy-start(f32[2,64,128]{2,1,0:T(8,128)} %design.1) | copy-start | bytes 196612
  1.7 8.9 %collective-permute-start.4 = (f32[11,64,128]{2,1,0:T(8,128)S(1)}, f32[11,64,128]{2,1,0:T(8,128)S(1)}, u32[]{:S(2)}, u32[]{:S(2)}) collective-permute-start(f32[11,64,128]{2,1,0:T(8,128)S(1)} %get-tuple-element.39), channel_id=1, source_target_pairs={{0,1},{1,0},{2,3},{3,2},{4,5},{5,4},{6,7},{7,6},{8,9},{9,8},{10,11... | collective-permute-start | bytes 1081352 | tf_op jit(solution)/shard_map/ppermute | solution.py:580
  2.3 12.9 %collective-permute-start = (f32[4,64,128]{2,1,0:T(8,128)S(1)}, f32[4,64,128]{2,1,0:T(8,128)S(1)}, u32[]{:S(2)}, u32[]{:S(2)}) collective-permute-start(f32[4,64,128]{2,1,0:T(8,128)S(1)} %get-tuple-element.34), channel_id=1, source_target_pairs={{0,2},{1,31},{2,4},{3,1},{4,6},{5,3},{6,8},{7,5},{8,10},{9,7},{10,... | collective-permute-start | bytes 393224 | tf_op jit(solution)/shard_map/ppermute | solution.py:580
  4.9 10.9 %collective-permute-start.1 = (f32[4,64,128]{2,1,0:T(8,128)S(1)}, f32[4,64,128]{2,1,0:T(8,128)S(1)}, u32[]{:S(2)}, u32[]{:S(2)}) collective-permute-start(f32[4,64,128]{2,1,0:T(8,128)S(1)} %get-tuple-element.35), channel_id=1, source_target_pairs={{1,2},{0,31},{3,4},{2,1},{5,6},{4,3},{7,8},{6,5},{9,10},{8,7},{11,... | collective-permute-start | bytes 393224 | tf_op jit(solution)/shard_map/ppermute | solution.py:580
  9.0 5.7 %collective-permute-start.2 = (f32[64,128]{1,0:T(8,128)S(1)}, f32[64,128]{1,0:T(8,128)S(1)}, u32[]{:S(2)}, u32[]{:S(2)}) collective-permute-start(f32[64,128]{1,0:T(8,128)S(1)} %get-tuple-element.36), channel_id=1, source_target_pairs={{0,3},{1,2},{2,5},{3,4},{4,7},{5,6},{6,1},{7,0},{8,11},{9,10},{10,... | collective-permute-start | bytes 98312 | tf_op jit(solution)/shard_map/ppermute | solution.py:580
  9.0 6.2 %collective-permute-start.3 = (f32[64,128]{1,0:T(8,128)S(1)}, f32[64,128]{1,0:T(8,128)S(1)}, u32[]{:S(2)}, u32[]{:S(2)}) collective-permute-start(f32[64,128]{1,0:T(8,128)S(1)} %get-tuple-element.37), channel_id=1, source_target_pairs={{0,2},{1,3},{2,4},{3,5},{4,6},{5,7},{6,0},{7,1},{8,10},{9,11},{10,... | collective-permute-start | bytes 98312 | tf_op jit(solution)/shard_map/ppermute | solution.py:580
  16.8 1.5 %collective-permute-start.6 = (f32[3,128,128]{2,1,0:T(8,128)S(1)}, f32[3,128,128]{2,1,0:T(8,128)S(1)}, u32[]{:S(2)}, u32[]{:S(2)}) collective-permute-start(f32[3,128,128]{2,1,0:T(8,128)S(1)} %get-tuple-element.45.v1), channel_id=1, source_target_pairs={{0,1},{1,0},{2,3},{3,2},{4,5},{5,4},{6,7},{7,6},{8,9},{9,8},{10,11... | collective-permute-start | bytes 589832 | tf_op jit(solution)/shard_map/ppermute | solution.py:580
  16.9 1.9 %collective-permute-start.5 = (f32[3,128,128]{2,1,0:T(8,128)S(1)}, f32[3,128,128]{2,1,0:T(8,128)S(1)}, u32[]{:S(2)}, u32[]{:S(2)}) collective-permute-start(f32[3,128,128]{2,1,0:T(8,128)S(1)} %get-tuple-element.45.v1), channel_id=1, source_target_pairs={{1,2},{3,4},{2,1},{5,6},{4,3},{7,8},{6,5},{9,10},{8,7},{11,12},{10... | collective-permute-start | bytes 589832 | tf_op jit(solution)/shard_map/ppermute | solution.py:580
  19.6 6.9 %collective-permute-start.8 = (f32[3,128,128]{2,1,0:T(8,128)S(1)}, f32[3,128,128]{2,1,0:T(8,128)S(1)}, u32[]{:S(2)}, u32[]{:S(2)}) collective-permute-start(f32[3,128,128]{2,1,0:T(8,128)S(1)} %get-tuple-element.49.v2), channel_id=1, source_target_pairs={{0,1},{1,0},{2,3},{3,2},{4,5},{5,4},{6,7},{7,6},{8,9},{9,8},{10,11... | collective-permute-start | bytes 589832 | tf_op jit(solution)/shard_map/ppermute | solution.py:580
  25.4 1.1 %collective-permute-start.7 = (f32[3,128,128]{2,1,0:T(8,128)S(1)}, f32[3,128,128]{2,1,0:T(8,128)S(1)}, u32[]{:S(2)}, u32[]{:S(2)}) collective-permute-start(f32[3,128,128]{2,1,0:T(8,128)S(1)} %get-tuple-element.49.v2), channel_id=1, source_target_pairs={{2,1},{4,3},{6,5},{8,7},{10,9},{12,11},{14,13},{16,15},{18,17},{20... | collective-permute-start | bytes 589832 | tf_op jit(solution)/shard_map/ppermute | solution.py:580
  50.9 5.9 %collective-permute-start.11 = (f32[128,128]{1,0:T(8,128)S(1)}, f32[128,128]{1,0:T(8,128)S(1)}, u32[]{:S(2)}, u32[]{:S(2)}) collective-permute-start(f32[128,128]{1,0:T(8,128)S(1)} %get-tuple-element.57.refs_0_), channel_id=1, source_target_pairs={{0,24},{8,16},{16,8},{24,0},{1,25},{9,17},{17,9},{25,1},{2,26},{10... | collective-permute-start | bytes 196616 | tf_op jit(solution)/shard_map/ppermute | solution.py:631
  51.9 5.1 %collective-permute-start.10 = (f32[128,128]{1,0:T(8,128)S(1)}, f32[128,128]{1,0:T(8,128)S(1)}, u32[]{:S(2)}, u32[]{:S(2)}) collective-permute-start(f32[128,128]{1,0:T(8,128)S(1)} %get-tuple-element.57.refs_0_), channel_id=1, source_target_pairs={{0,16},{8,24},{16,0},{24,8},{1,17},{9,25},{17,1},{25,9},{2,18},{10... | collective-permute-start | bytes 196616 | tf_op jit(solution)/shard_map/ppermute | solution.py:631
  53.2 4.3 %collective-permute-start.9 = (f32[128,128]{1,0:T(8,128)S(1)}, f32[128,128]{1,0:T(8,128)S(1)}, u32[]{:S(2)}, u32[]{:S(2)}) collective-permute-start(f32[128,128]{1,0:T(8,128)S(1)} %get-tuple-element.57.refs_0_), channel_id=1, source_target_pairs={{0,8},{8,0},{16,24},{24,16},{1,9},{9,1},{17,25},{25,17},{2,10},{10... | collective-permute-start | bytes 196616 | tf_op jit(solution)/shard_map/ppermute | solution.py:631
  57.5 5.2 %collective-permute-start.12 = (f32[72,128]{1,0:T(8,128)S(1)}, f32[72,128]{1,0:T(8,128)S(1)}, u32[]{:S(2)}, u32[]{:S(2)}) collective-permute-start(f32[72,128]{1,0:T(8,128)S(1)} %get-tuple-element.63), channel_id=1, source_target_pairs={{1,2},{0,7},{3,4},{2,1},{5,6},{4,3},{7,0},{6,5},{9,10},{8,15},{11,... | collective-permute-start | bytes 110600 | tf_op jit(solution)/shard_map/ppermute | solution.py:580
  57.6 5.2 %collective-permute-start.13 = (f32[72,128]{1,0:T(8,128)S(1)}, f32[72,128]{1,0:T(8,128)S(1)}, u32[]{:S(2)}, u32[]{:S(2)}) collective-permute-start(f32[72,128]{1,0:T(8,128)S(1)} %get-tuple-element.64), channel_id=1, source_target_pairs={{0,6},{1,3},{2,0},{3,5},{4,2},{5,7},{6,4},{7,1},{8,14},{9,11},{10,... | collective-permute-start | bytes 110600 | tf_op jit(solution)/shard_map/ppermute | solution.py:580
  58.6 4.2 %collective-permute-start.14 = (f32[72,128]{1,0:T(8,128)S(1)}, f32[72,128]{1,0:T(8,128)S(1)}, u32[]{:S(2)}, u32[]{:S(2)}) collective-permute-start(f32[72,128]{1,0:T(8,128)S(1)} %get-tuple-element.65), channel_id=1, source_target_pairs={{0,1},{1,0},{2,3},{3,2},{4,5},{5,4},{6,7},{7,6},{8,9},{9,8},{10,11... | collective-permute-start | bytes 110600 | tf_op jit(solution)/shard_map/ppermute | solution.py:580

commit v17 on v15

--- a/solution.py
+++ b/solution.py
@@ -16,6 +16,7 @@
 
 AXES = ("mod", "slab", "sub")
 ROWS = 64
+FEW = 16
 FACE = filter_reach - 1.0
 EDGE = filter_reach - math.sqrt(2.0)
 CORNER = filter_reach - math.sqrt(3.0)
@@ -93,9 +94,9 @@
     return jnp.where(rows(x.shape) > 0, pltpu.roll(x, 1, 0), 0.0)
 
 
-def two_rows(read, y0, count):
+def two_rows(read, y0, count, size):
     here = read(y0)
-    above = y_up(here) if y0 + ROWS == count else read(y0 + 1)
+    above = y_up(here) if y0 + size == count else read(y0 + 1)
     return here, above
 
 
@@ -152,10 +153,10 @@
     return fields
 
 
-def layer_modes(read, y0, count):
+def layer_modes(read, y0, count, size=ROWS):
     heres, modes = [], []
     for k in range(3):
-        here, above = two_rows(lambda y, k=k: read(k, y), y0, count)
+        here, above = two_rows(lambda y, k=k: read(k, y), y0, count, size)
         heres.append(here)
         modes.append(face_modes(here, above))
     return heres, modes
@@ -202,14 +203,14 @@
 
 
 def energy_loop(count, read_own, read_high, use):
-    for y0 in range(0, count, ROWS):
-        _, own = layer_modes(read_own, y0, count)
-        _, high = layer_modes(read_high, y0, count)
+    for y0 in range(0, count, FEW):
+        _, own = layer_modes(read_own, y0, count, FEW)
+        _, high = layer_modes(read_high, y0, count, FEW)
         use(y0, element_energy(element_modes(own, high, 1.0)))
 
 
-def rows_of(ref):
-    return lambda k, y: ref[k, pl.ds(y, ROWS), :]
+def rows_of(ref, size=ROWS):
+    return lambda k, y: ref[k, pl.ds(y, size), :]
 
 
 def inner_side(sub):
@@ -389,15 +390,15 @@
     for k in range(3):
         v2_high[k] = jnp.where(even, v2_inner[k], v2_outer[k])
     count = v2.shape[1]
-    total = [jnp.zeros((ROWS, v2.shape[2]), jnp.float32)]
+    total = [jnp.zeros((FEW, v2.shape[2]), jnp.float32)]
 
     def use(y0, energy):
-        total[0] += energy * mod_own[pl.ds(y0, ROWS), :]
+        total[0] += energy * mod_own[pl.ds(y0, FEW), :]
 
     energy_loop(
         count,
-        lambda k, y: v2[k, pl.ds(y, ROWS), :],
-        lambda k, y: v2_high[k, pl.ds(y, ROWS), :],
+        lambda k, y: v2[k, pl.ds(y, FEW), :],
+        lambda k, y: v2_high[k, pl.ds(y, FEW), :],
         use,
     )
     width = v2.shape[2]
@@ -453,9 +454,9 @@
         high[k] = c0 * v0_high[k] + c1 * v1_high[k] + c2 * v2_high[k]
 
     def use(y0, energy):
-        slope[pl.ds(y0, ROWS), :] = slope_factor[pl.ds(y0, ROWS), :] * energy
-
-    energy_loop(count, rows_of(own), rows_of(high), use)
+        slope[pl.ds(y0, FEW), :] = slope_factor[pl.ds(y0, FEW), :] * energy
+
+    energy_loop(count, rows_of(own, FEW), rows_of(high, FEW), use)
 
 
 def displace_kernel(factors, v0, v0_inner, v1, v1_inner, v2, v2_inner, displacement):

time: 63.8 us -> 63.8 us (level)
  no operation moved by 1% of the time
where the time goes in v17:
time: 63.8 us; the launch traced here: 63.6 us
  blocking collectives  23.1 us (36%)
  starting transfers between devices  20.7 us (32%)
  waiting for transfers between devices  12 us (19%)
  Pallas kernels  5.93 us (9%)
  other arithmetic  0.99 us (2%)
  between operations  0.74 us (1%)
    all_to_all x1, blocking collectives, local(): lax.all_to_all(jnp.broadcast_to(moments, (devices, 8, width)), AXES, 0, 0...  23.1 us
    ppermute x12, starting transfers between devices, move(): return lax.ppermute(value, AXES, path[name])  17.2 us
    ppermute x12, waiting for transfers between devices, move(): return lax.ppermute(value, AXES, path[name])  8.98 us
    ppermute x3, starting transfers between devices, local(): lax.ppermute(slope, 'mod', pairs)  3.55 us
    ppermute x3, waiting for transfers between devices, local(): lax.ppermute(slope, 'mod', pairs)  3.06 us
  transfers between devices with their start and end apart: 15, of which 9 were waited for; matrix products, arithmetic and copies ran while one was open for 0% of the time, Pallas kernels for 3%

profile of v17, /device:TPU:0, one launch (start us, length us, event | category | flops | bytes accessed | tf_op | source)
XLA Modules:
  0.0 63.6 jit_solution(6170372910395625748)
XLA Ops:
  0.6 0.0 copy-start
  0.6 0.0 copy-start.1
  0.6 1.0 %subtract_convert_fusion.free = f32[3,2,64,128]{3,2,1,0:T(8,128)S(1)} fusion(s32[3,2,64,128]{3,2,1,0:T(8,128)} %param.4), kind=kLoop, calls=%fused_computation | loop fusion | flops 98304 | bytes 393216 | tf_op jit(solution)/shard_map/convert_element_type | solution.py:586
  1.6 0.0 copy-done
  1.7 0.0 copy-done.1
  1.7 0.1 prepare.1
  1.7 0.5 collective-permute-start.4
  2.3 2.6 %collective-permute-start = (f32[4,64,128]{2,1,0:T(8,128)S(1)}, f32[4,64,128]{2,1,0:T(8,128)S(1)}, u32[]{:S(2)}, u32[]{:S(2)}) collective-permute-start(f32[4,64,128]{2,1,0:T(8,128)S(1)} %get-tuple-element.34), channel_id=1, source_target_pairs={{0,2},{1,31},{2,4},{3,1},{4,6},{5,3},{6,8},{7,5},{8,10},{9,7},{10,... | collective-permute-start | bytes 393224 | tf_op jit(solution)/shard_map/ppermute | solution.py:581
  4.9 4.1 %collective-permute-start.1 = (f32[4,64,128]{2,1,0:T(8,128)S(1)}, f32[4,64,128]{2,1,0:T(8,128)S(1)}, u32[]{:S(2)}, u32[]{:S(2)}) collective-permute-start(f32[4,64,128]{2,1,0:T(8,128)S(1)} %get-tuple-element.35), channel_id=1, source_target_pairs={{1,2},{0,31},{3,4},{2,1},{5,6},{4,3},{7,8},{6,5},{9,10},{8,7},{11,... | collective-permute-start | bytes 393224 | tf_op jit(solution)/shard_map/ppermute | solution.py:581
  9.0 0.0 collective-permute-start.2
  9.0 1.6 %collective-permute-start.3 = (f32[64,128]{1,0:T(8,128)S(1)}, f32[64,128]{1,0:T(8,128)S(1)}, u32[]{:S(2)}, u32[]{:S(2)}) collective-permute-start(f32[64,128]{1,0:T(8,128)S(1)} %get-tuple-element.37), channel_id=1, source_target_pairs={{0,2},{1,3},{2,4},{3,5},{4,6},{5,7},{6,0},{7,1},{8,10},{9,11},{10,... | collective-permute-start | bytes 98312 | tf_op jit(solution)/shard_map/ppermute | solution.py:581
  10.6 0.0 collective-permute-done.4.swap
  10.6 0.8 %start_inner.1 = (f32[3,128,128]{2,1,0:T(8,128)S(1)}, f32[3,128,128]{2,1,0:T(8,128)S(1)}, f32[3,128,128]{2,1,0:T(8,128)S(1)}, f32[12,128,128]{2,1,0:T(8,128)S(1)}, f32[3,128,128]{2,1,0:T(8,128)S(1)}) custom-call(f32[11,64,128]{2,1,0:T(8,128)S(1)} %get-tuple-element.38.own, f32[11,64,128]{2,1,0:T(8,128)S(1)} %collective-permute-done.4.swap), custom_call_target="tpu_custom_call" | custom-call | flops 10000000 | bytes 4000000 | tf_op jit(solution)/shard_map/start_inner/pallas_call | solution.py:601
  11.4 3.2 %collective-permute-done.2.refs_2_ = f32[64,128]{1,0:T(8,128)S(1)} collective-permute-done((f32[64,128]{1,0:T(8,128)S(1)}, f32[64,128]{1,0:T(8,128)S(1)}, u32[]{:S(2)}, u32[]{:S(2)}) %collective-permute-start.2) | collective-permute-done | bytes 32800 | tf_op jit(solution)/shard_map/ppermute | solution.py:581
  14.7 0.5 collective-permute-done.3.refs_3_
  15.2 0.0 collective-permute-done.refs_0_
  15.2 0.6 collective-permute-done.1.refs_1_
  15.8 1.0 %start_outer.1 = (f32[3,128,128]{2,1,0:T(8,128)S(1)}, f32[3,128,128]{2,1,0:T(8,128)S(1)}, f32[128,128]{1,0:T(8,128)S(1)}, f32[128,128]{1,0:T(8,128)S(1)}, f32[12...) custom-call(f32[4,64,128]{2,1,0:T(8,128)S(1)} %collective-permute-done.refs_0_, ...), custom_call_target="tpu_custom_call" | custom-call | tf_op jit(solution)/shard_map/start_outer/pallas_call | solution.py:608
  16.8 0.1 collective-permute-start.6
  16.9 0.7 %collective-permute-start.5 = (f32[3,128,128]{2,1,0:T(8,128)S(1)}, f32[3,128,128]{2,1,0:T(8,128)S(1)}, u32[]{:S(2)}, u32[]{:S(2)}) collective-permute-start(f32[3,128,128]{2,1,0:T(8,128)S(1)} %get-tuple-element.45.v1), channel_id=1, source_target_pairs={{1,2},{3,4},{2,1},{5,6},{4,3},{7,8},{6,5},{9,10},{8,7},{11,12},{10... | collective-permute-start | bytes 589832 | tf_op jit(solution)/shard_map/ppermute | solution.py:581
  17.6 0.7 %collective-permute-done.6.inner.v1_inner = f32[3,128,128]{2,1,0:T(8,128)S(1)} collective-permute-done((f32[3,128,128]{2,1,0:T(8,128)S(1)}, f32[3,128,128]{2,1,0:T(8,128)S(1)}, u32[]{:S(2)}, u32[]{:S(2)}) %collective-permute-start.6) | collective-permute-done | bytes 196640 | tf_op jit(solution)/shard_map/ppermute | solution.py:581
  18.3 0.5 second_inner.1.fields
  18.8 0.0 collective-permute-done.5.outer
  18.8 0.8 %second_outer.1 = (f32[3,128,128]{2,1,0:T(8,128)S(1)}, f32[3,128,128]{2,1,0:T(8,128)S(1)}, f32[8,128]{1,0:T(8,128)S(1)}) custom-call(f32[3,128,128]{2,1,0:T(8,128)S(1)} %get-tuple-element.45.v1, f32[3,128,128]{2,1,0:T(8,128)S(1)} %collective-permute-done.5.outer, f32[3,128,128]{2,1,0:T(8,128)S(1)} %collective-permute-done.6.inner.v1_inner, ...), custom_call_target="tpu_custom_call" | custom-call | tf_op jit(solution)/shard_map/second_outer/pallas_call | solution.py:617
  19.6 5.8 %collective-permute-start.8 = (f32[3,128,128]{2,1,0:T(8,128)S(1)}, f32[3,128,128]{2,1,0:T(8,128)S(1)}, u32[]{:S(2)}, u32[]{:S(2)}) collective-permute-start(f32[3,128,128]{2,1,0:T(8,128)S(1)} %get-tuple-element.49.v2), channel_id=1, source_target_pairs={{0,1},{1,0},{2,3},{3,2},{4,5},{5,4},{6,7},{7,6},{8,9},{9,8},{10,11... | collective-permute-start | bytes 589832 | tf_op jit(solution)/shard_map/ppermute | solution.py:581
  25.4 0.7 %collective-permute-start.7 = (f32[3,128,128]{2,1,0:T(8,128)S(1)}, f32[3,128,128]{2,1,0:T(8,128)S(1)}, u32[]{:S(2)}, u32[]{:S(2)}) collective-permute-start(f32[3,128,128]{2,1,0:T(8,128)S(1)} %get-tuple-element.49.v2), channel_id=1, source_target_pairs={{2,1},{4,3},{6,5},{8,7},{10,9},{12,11},{14,13},{16,15},{18,17},{20... | collective-permute-start | bytes 589832 | tf_op jit(solution)/shard_map/ppermute | solution.py:581
  26.1 0.4 collective-permute-done.8.v2_inner
  26.5 0.0 collective-permute-done.7.v2_outer
  26.5 0.5 third.1
  27.0 23.1 %all_to_all.5.gathered = f32[32,8,128]{2,1,0:T(8,128)S(1)} all-to-all(f32[32,8,128]{2,1,0:T(8,128)S(1)} %broadcast_in_dim.3), channel_id=1, replica_groups=mesh['mod'=4,'slab'=4,'sub'=2] {'mod','slab','sub'}, dimensions={0} | all-to-all | bytes 262144 | tf_op jit(solution)/shard_map/all_to_all | solution.py:626
  50.1 0.7 %combine.1 = (f32[128,128]{1,0:T(8,128)S(1)}, f32[3,8,128]{2,1,0:T(8,128)S(1)}) custom-call(f32[32,8,128]{2,1,0:T(8,128)S(1)} %all_to_all.5.gathered, f32[3,128,128]{2,1,0:T(8,128)S(1)} %get-tuple-element.40.refs_4_.v0, f32[3,128,128]{2,1,0:T(8,128)S(1)} %get-tuple-element.53.v0_high, f32[3,128,128]{2,1,0:T(8,128)S(1)} %get-tuple-element.45.v1, ...), custom_call_target="tpu_custom_call" | custom-call | tf_op jit(solution)/shard_map/combine/pallas_call | solution.py:629
  50.8 1.0 %collective-permute-start.11 = (f32[128,128]{1,0:T(8,128)S(1)}, f32[128,128]{1,0:T(8,128)S(1)}, u32[]{:S(2)}, u32[]{:S(2)}) collective-permute-start(f32[128,128]{1,0:T(8,128)S(1)} %get-tuple-element.57.refs_0_), channel_id=1, source_target_pairs={{0,24},{8,16},{16,8},{24,0},{1,25},{9,17},{17,9},{25,1},{2,26},{10... | collective-permute-start | bytes 196616 | tf_op jit(solution)/shard_map/ppermute | solution.py:632
  51.9 1.3 %collective-permute-start.10 = (f32[128,128]{1,0:T(8,128)S(1)}, f32[128,128]{1,0:T(8,128)S(1)}, u32[]{:S(2)}, u32[]{:S(2)}) collective-permute-start(f32[128,128]{1,0:T(8,128)S(1)} %get-tuple-element.57.refs_0_), channel_id=1, source_target_pairs={{0,16},{8,24},{16,0},{24,8},{1,17},{9,25},{17,1},{25,9},{2,18},{10... | collective-permute-start | bytes 196616 | tf_op jit(solution)/shard_map/ppermute | solution.py:632
  53.2 1.2 %collective-permute-start.9 = (f32[128,128]{1,0:T(8,128)S(1)}, f32[128,128]{1,0:T(8,128)S(1)}, u32[]{:S(2)}, u32[]{:S(2)}) collective-permute-start(f32[128,128]{1,0:T(8,128)S(1)} %get-tuple-element.57.refs_0_), channel_id=1, source_target_pairs={{0,8},{8,0},{16,24},{24,16},{1,9},{9,1},{17,25},{25,17},{2,10},{10... | collective-permute-start | bytes 196616 | tf_op jit(solution)/shard_map/ppermute | solution.py:632
  54.4 2.3 %collective-permute-done.11.refs_3_ = f32[128,128]{1,0:T(8,128)S(1)} collective-permute-done((f32[128,128]{1,0:T(8,128)S(1)}, f32[128,128]{1,0:T(8,128)S(1)}, u32[]{:S(2)}, u32[]{:S(2)}) %collective-permute-start.11) | collective-permute-done | bytes 65568 | tf_op jit(solution)/shard_map/ppermute | solution.py:632
  56.7 0.2 collective-permute-done.10.refs_2_
  56.9 0.5 collective-permute-done.9.refs_1_
  57.5 0.1 collective-permute-start.12
  57.5 1.0 %collective-permute-start.13 = (f32[72,128]{1,0:T(8,128)S(1)}, f32[72,128]{1,0:T(8,128)S(1)}, u32[]{:S(2)}, u32[]{:S(2)}) collective-permute-start(f32[72,128]{1,0:T(8,128)S(1)} %get-tuple-element.64), channel_id=1, source_target_pairs={{0,6},{1,3},{2,0},{3,5},{4,2},{5,7},{6,4},{7,1},{8,14},{9,11},{10,... | collective-permute-start | bytes 110600 | tf_op jit(solution)/shard_map/ppermute | solution.py:581
  58.5 0.0 collective-permute-start.14
  58.5 0.7 %displace.1 = f32[3,2,64,128]{3,2,1,0:T(8,128)} custom-call(f32[3,8,128]{2,1,0:T(8,128)S(1)} %get-tuple-element.60.factors, f32[3,128,128]{2,1,0:T(8,128)S(1)} %get-tuple-element.40.refs_4_.v0, f32[3,128,128]{2,1,0:T(8,128)S(1)} %get-tuple-element.41.refs_5_.v0_inner, f32[3,128,128]{2,1,0:T(8,128)S(1)} %get-tuple-element.45.v1, ...), custom_call_target="tpu_custom_call" | custom-call | flops 10000000 | bytes 4000000 | tf_op jit(solution)/shard_map/displace/pallas_call | solution.py:633
  59.3 3.5 %collective-permute-done.12.outer = f32[72,128]{1,0:T(8,128)S(1)} collective-permute-done((f32[72,128]{1,0:T(8,128)S(1)}, f32[72,128]{1,0:T(8,128)S(1)}, u32[]{:S(2)}, u32[]{:S(2)}) %collective-permute-start.12) | collective-permute-done | bytes 36896 | tf_op jit(solution)/shard_map/ppermute | solution.py:581
  62.7 0.0 collective-permute-done.13.far
  62.7 0.0 collective-permute-done.14.partner
  62.7 0.9 %gradient.1 = f32[2,64,128]{2,1,0:T(8,128)} custom-call(f32[128,128]{1,0:T(8,128)S(1)} %get-tuple-element.62.scaled, f32[72,128]{1,0:T(8,128)S(1)} %collective-permute-done.12.outer, f32[72,128]{1,0:T(8,128)S(1)} %collective-permute-done.13.far, f32[72,128]{1,0:T(8,128)S(1)} %collective-permute-done.14.partner), custom_call_target="tpu_custom_call" | custom-call | tf_op jit(solution)/shard_map/gradient/pallas_call | solution.py:644
  (2 shorter events, 0.0 us)
Async XLA Ops:
  0.6 1.0 %copy-start = (s32[3,2,64,128]{3,2,1,0:T(8,128)S(1)}, s32[3,2,64,128]{3,2,1,0:T(8,128)}, u32[]{:S(2)}) copy-start(s32[3,2,64,128]{3,2,1,0:T(8,128)} %load.1) | copy-start | bytes 589828
  0.6 1.0 %copy-start.1 = (f32[2,64,128]{2,1,0:T(8,128)S(1)}, f32[2,64,128]{2,1,0:T(8,128)}, u32[]{:S(2)}) copy-start(f32[2,64,128]{2,1,0:T(8,128)} %design.1) | copy-start | bytes 196612
  1.7 8.9 %collective-permute-start.4 = (f32[11,64,128]{2,1,0:T(8,128)S(1)}, f32[11,64,128]{2,1,0:T(8,128)S(1)}, u32[]{:S(2)}, u32[]{:S(2)}) collective-permute-start(f32[11,64,128]{2,1,0:T(8,128)S(1)} %get-tuple-element.39), channel_id=1, source_target_pairs={{0,1},{1,0},{2,3},{3,2},{4,5},{5,4},{6,7},{7,6},{8,9},{9,8},{10,11... | collective-permute-start | bytes 1081352 | tf_op jit(solution)/shard_map/ppermute | solution.py:581
  2.3 12.9 %collective-permute-start = (f32[4,64,128]{2,1,0:T(8,128)S(1)}, f32[4,64,128]{2,1,0:T(8,128)S(1)}, u32[]{:S(2)}, u32[]{:S(2)}) collective-permute-start(f32[4,64,128]{2,1,0:T(8,128)S(1)} %get-tuple-element.34), channel_id=1, source_target_pairs={{0,2},{1,31},{2,4},{3,1},{4,6},{5,3},{6,8},{7,5},{8,10},{9,7},{10,... | collective-permute-start | bytes 393224 | tf_op jit(solution)/shard_map/ppermute | solution.py:581
  4.9 10.9 %collective-permute-start.1 = (f32[4,64,128]{2,1,0:T(8,128)S(1)}, f32[4,64,128]{2,1,0:T(8,128)S(1)}, u32[]{:S(2)}, u32[]{:S(2)}) collective-permute-start(f32[4,64,128]{2,1,0:T(8,128)S(1)} %get-tuple-element.35), channel_id=1, source_target_pairs={{1,2},{0,31},{3,4},{2,1},{5,6},{4,3},{7,8},{6,5},{9,10},{8,7},{11,... | collective-permute-start | bytes 393224 | tf_op jit(solution)/shard_map/ppermute | solution.py:581
  9.0 5.7 %collective-permute-start.2 = (f32[64,128]{1,0:T(8,128)S(1)}, f32[64,128]{1,0:T(8,128)S(1)}, u32[]{:S(2)}, u32[]{:S(2)}) collective-permute-start(f32[64,128]{1,0:T(8,128)S(1)} %get-tuple-element.36), channel_id=1, source_target_pairs={{0,3},{1,2},{2,5},{3,4},{4,7},{5,6},{6,1},{7,0},{8,11},{9,10},{10,... | collective-permute-start | bytes 98312 | tf_op jit(solution)/shard_map/ppermute | solution.py:581
  9.0 6.2 %collective-permute-start.3 = (f32[64,128]{1,0:T(8,128)S(1)}, f32[64,128]{1,0:T(8,128)S(1)}, u32[]{:S(2)}, u32[]{:S(2)}) collective-permute-start(f32[64,128]{1,0:T(8,128)S(1)} %get-tuple-element.37), channel_id=1, source_target_pairs={{0,2},{1,3},{2,4},{3,5},{4,6},{5,7},{6,0},{7,1},{8,10},{9,11},{10,... | collective-permute-start | bytes 98312 | tf_op jit(solution)/shard_map/ppermute | solution.py:581
  16.8 1.5 %collective-permute-start.6 = (f32[3,128,128]{2,1,0:T(8,128)S(1)}, f32[3,128,128]{2,1,0:T(8,128)S(1)}, u32[]{:S(2)}, u32[]{:S(2)}) collective-permute-start(f32[3,128,128]{2,1,0:T(8,128)S(1)} %get-tuple-element.45.v1), channel_id=1, source_target_pairs={{0,1},{1,0},{2,3},{3,2},{4,5},{5,4},{6,7},{7,6},{8,9},{9,8},{10,11... | collective-permute-start | bytes 589832 | tf_op jit(solution)/shard_map/ppermute | solution.py:581
  16.9 1.9 %collective-permute-start.5 = (f32[3,128,128]{2,1,0:T(8,128)S(1)}, f32[3,128,128]{2,1,0:T(8,128)S(1)}, u32[]{:S(2)}, u32[]{:S(2)}) collective-permute-start(f32[3,128,128]{2,1,0:T(8,128)S(1)} %get-tuple-element.45.v1), channel_id=1, source_target_pairs={{1,2},{3,4},{2,1},{5,6},{4,3},{7,8},{6,5},{9,10},{8,7},{11,12},{10... | collective-permute-start | bytes 589832 | tf_op jit(solution)/shard_map/ppermute | solution.py:581
  19.6 6.9 %collective-permute-start.8 = (f32[3,128,128]{2,1,0:T(8,128)S(1)}, f32[3,128,128]{2,1,0:T(8,128)S(1)}, u32[]{:S(2)}, u32[]{:S(2)}) collective-permute-start(f32[3,128,128]{2,1,0:T(8,128)S(1)} %get-tuple-element.49.v2), channel_id=1, source_target_pairs={{0,1},{1,0},{2,3},{3,2},{4,5},{5,4},{6,7},{7,6},{8,9},{9,8},{10,11... | collective-permute-start | bytes 589832 | tf_op jit(solution)/shard_map/ppermute | solution.py:581
  25.4 1.1 %collective-permute-start.7 = (f32[3,128,128]{2,1,0:T(8,128)S(1)}, f32[3,128,128]{2,1,0:T(8,128)S(1)}, u32[]{:S(2)}, u32[]{:S(2)}) collective-permute-start(f32[3,128,128]{2,1,0:T(8,128)S(1)} %get-tuple-element.49.v2), channel_id=1, source_target_pairs={{2,1},{4,3},{6,5},{8,7},{10,9},{12,11},{14,13},{16,15},{18,17},{20... | collective-permute-start | bytes 589832 | tf_op jit(solution)/shard_map/ppermute | solution.py:581
  50.8 5.9 %collective-permute-start.11 = (f32[128,128]{1,0:T(8,128)S(1)}, f32[128,128]{1,0:T(8,128)S(1)}, u32[]{:S(2)}, u32[]{:S(2)}) collective-permute-start(f32[128,128]{1,0:T(8,128)S(1)} %get-tuple-element.57.refs_0_), channel_id=1, source_target_pairs={{0,24},{8,16},{16,8},{24,0},{1,25},{9,17},{17,9},{25,1},{2,26},{10... | collective-permute-start | bytes 196616 | tf_op jit(solution)/shard_map/ppermute | solution.py:632
  51.9 5.1 %collective-permute-start.10 = (f32[128,128]{1,0:T(8,128)S(1)}, f32[128,128]{1,0:T(8,128)S(1)}, u32[]{:S(2)}, u32[]{:S(2)}) collective-permute-start(f32[128,128]{1,0:T(8,128)S(1)} %get-tuple-element.57.refs_0_), channel_id=1, source_target_pairs={{0,16},{8,24},{16,0},{24,8},{1,17},{9,25},{17,1},{25,9},{2,18},{10... | collective-permute-start | bytes 196616 | tf_op jit(solution)/shard_map/ppermute | solution.py:632
  53.2 4.3 %collective-permute-start.9 = (f32[128,128]{1,0:T(8,128)S(1)}, f32[128,128]{1,0:T(8,128)S(1)}, u32[]{:S(2)}, u32[]{:S(2)}) collective-permute-start(f32[128,128]{1,0:T(8,128)S(1)} %get-tuple-element.57.refs_0_), channel_id=1, source_target_pairs={{0,8},{8,0},{16,24},{24,16},{1,9},{9,1},{17,25},{25,17},{2,10},{10... | collective-permute-start | bytes 196616 | tf_op jit(solution)/shard_map/ppermute | solution.py:632
  57.5 5.2 %collective-permute-start.12 = (f32[72,128]{1,0:T(8,128)S(1)}, f32[72,128]{1,0:T(8,128)S(1)}, u32[]{:S(2)}, u32[]{:S(2)}) collective-permute-start(f32[72,128]{1,0:T(8,128)S(1)} %get-tuple-element.63), channel_id=1, source_target_pairs={{1,2},{0,7},{3,4},{2,1},{5,6},{4,3},{7,0},{6,5},{9,10},{8,15},{11,... | collective-permute-start | bytes 110600 | tf_op jit(solution)/shard_map/ppermute | solution.py:581
  57.5 5.2 %collective-permute-start.13 = (f32[72,128]{1,0:T(8,128)S(1)}, f32[72,128]{1,0:T(8,128)S(1)}, u32[]{:S(2)}, u32[]{:S(2)}) collective-permute-start(f32[72,128]{1,0:T(8,128)S(1)} %get-tuple-element.64), channel_id=1, source_target_pairs={{0,6},{1,3},{2,0},{3,5},{4,2},{5,7},{6,4},{7,1},{8,14},{9,11},{10,... | collective-permute-start | bytes 110600 | tf_op jit(solution)/shard_map/ppermute | solution.py:581
  58.5 4.2 %collective-permute-start.14 = (f32[72,128]{1,0:T(8,128)S(1)}, f32[72,128]{1,0:T(8,128)S(1)}, u32[]{:S(2)}, u32[]{:S(2)}) collective-permute-start(f32[72,128]{1,0:T(8,128)S(1)} %get-tuple-element.65), channel_id=1, source_target_pairs={{0,1},{1,0},{2,3},{3,2},{4,5},{5,4},{6,7},{7,6},{8,9},{9,8},{10,11... | collective-permute-start | bytes 110600 | tf_op jit(solution)/shard_map/ppermute | solution.py:581

commit v18 on v15

--- a/solution.py
+++ b/solution.py
@@ -364,15 +364,12 @@
     )
 
 
-def second_inner_kernel(v1, inner, fields):
-    fields_loop(v1.shape[1], rows_of(v1), rows_of(inner), inner_side(lax.axis_index("sub")), fields)
-
-
 def second_outer_kernel(
-    v1, outer, inner, fields, free, mod_inner, mod_outer, before, v2, v1_high, moments
+    v1, outer, inner, free, mod_inner, mod_outer, before, v2, v1_high, moments, fields
 ):
     sub = lax.axis_index("sub")
     count = v1.shape[1]
+    fields_loop(count, rows_of(v1), rows_of(inner), inner_side(sub), fields)
     for k in range(3):
         v1_high[k] = jnp.where(sub == 0, inner[k], outer[k])
     _, cross, square = operator_loop(
@@ -612,10 +609,9 @@
     )(first, second, third, fourth, v0, v0_inner, free, fields, parts)
     outer = move(v1, "outer")
     inner = move(v1, "swap")
-    (fields,) = call(second_inner_kernel, [(12,) + plane], name="second_inner", work=True)(v1, inner)
     v2, v1_high, moments = call(
-        second_outer_kernel, [layer, layer, (8, width)], name="second_outer"
-    )(v1, outer, inner, fields, free, mod_inner, mod_outer, moments)
+        second_outer_kernel, [layer, layer, (8, width)], [(12,) + plane], name="second"
+    )(v1, outer, inner, free, mod_inner, mod_outer, moments)
     v2_outer = move(v2, "down")
     v2_inner = move(v2, "swap")
     moments, v2_high = call(third_kernel, [(8, width), layer], name="third")(

time: 63.8 us -> 64.2 us (level)
  transfers between devices with their start and end apart: 15 -> 15, of which waited for: 9 -> 9; matrix products, arithmetic and copies ran while one was open for 0% -> 0% of each run, Pallas kernels for 3% -> 2%
where the time goes in v18:
time: 64.2 us; the launch traced here: 64.1 us
  blocking collectives  23.1 us (36%)
  starting transfers between devices  21.2 us (33%)
  waiting for transfers between devices  12 us (19%)
  Pallas kernels  5.91 us (9%)
  other arithmetic  0.99 us (2%)
  between operations  0.73 us (1%)
    all_to_all x1, blocking collectives, local(): lax.all_to_all(jnp.broadcast_to(moments, (devices, 8, width)), AXES, 0, 0...  23.1 us
    ppermute x12, starting transfers between devices, move(): return lax.ppermute(value, AXES, path[name])  17.7 us
    ppermute x12, waiting for transfers between devices, move(): return lax.ppermute(value, AXES, path[name])  8.97 us
    ppermute x3, starting transfers between devices, local(): lax.ppermute(slope, 'mod', pairs)  3.55 us
    ppermute x3, waiting for transfers between devices, local(): lax.ppermute(slope, 'mod', pairs)  3.06 us
  transfers between devices with their start and end apart: 15, of which 9 were waited for; matrix products, arithmetic and copies ran while one was open for 0% of the time, Pallas kernels for 2%

profile of v18, /device:TPU:0, one launch (start us, length us, event | category | flops | bytes accessed | tf_op | source)
XLA Modules:
  0.0 64.1 jit_solution(8176624482974125200)
XLA Ops:
  0.6 0.0 copy-start
  0.6 0.0 copy-start.1
  0.6 1.0 %subtract_convert_fusion.free = f32[3,2,64,128]{3,2,1,0:T(8,128)S(1)} fusion(s32[3,2,64,128]{3,2,1,0:T(8,128)} %param.4), kind=kLoop, calls=%fused_computation | loop fusion | flops 98304 | bytes 393216 | tf_op jit(solution)/shard_map/convert_element_type | solution.py:582
  1.6 0.0 copy-done
  1.7 0.0 copy-done.1
  1.7 0.1 prepare.1
  1.7 0.5 collective-permute-start.4
  2.3 2.6 %collective-permute-start = (f32[4,64,128]{2,1,0:T(8,128)S(1)}, f32[4,64,128]{2,1,0:T(8,128)S(1)}, u32[]{:S(2)}, u32[]{:S(2)}) collective-permute-start(f32[4,64,128]{2,1,0:T(8,128)S(1)} %get-tuple-element.34), channel_id=1, source_target_pairs={{0,2},{1,31},{2,4},{3,1},{4,6},{5,3},{6,8},{7,5},{8,10},{9,7},{10,... | collective-permute-start | bytes 393224 | tf_op jit(solution)/shard_map/ppermute | solution.py:577
  4.9 4.1 %collective-permute-start.1 = (f32[4,64,128]{2,1,0:T(8,128)S(1)}, f32[4,64,128]{2,1,0:T(8,128)S(1)}, u32[]{:S(2)}, u32[]{:S(2)}) collective-permute-start(f32[4,64,128]{2,1,0:T(8,128)S(1)} %get-tuple-element.35), channel_id=1, source_target_pairs={{1,2},{0,31},{3,4},{2,1},{5,6},{4,3},{7,8},{6,5},{9,10},{8,7},{11,... | collective-permute-start | bytes 393224 | tf_op jit(solution)/shard_map/ppermute | solution.py:577
  9.0 0.0 collective-permute-start.2
  9.0 1.6 %collective-permute-start.3 = (f32[64,128]{1,0:T(8,128)S(1)}, f32[64,128]{1,0:T(8,128)S(1)}, u32[]{:S(2)}, u32[]{:S(2)}) collective-permute-start(f32[64,128]{1,0:T(8,128)S(1)} %get-tuple-element.37), channel_id=1, source_target_pairs={{0,2},{1,3},{2,4},{3,5},{4,6},{5,7},{6,0},{7,1},{8,10},{9,11},{10,... | collective-permute-start | bytes 98312 | tf_op jit(solution)/shard_map/ppermute | solution.py:577
  10.6 0.0 collective-permute-done.4.swap
  10.6 0.8 %start_inner.1 = (f32[3,128,128]{2,1,0:T(8,128)S(1)}, f32[3,128,128]{2,1,0:T(8,128)S(1)}, f32[3,128,128]{2,1,0:T(8,128)S(1)}, f32[12,128,128]{2,1,0:T(8,128)S(1)}, f32[3,128,128]{2,1,0:T(8,128)S(1)}) custom-call(f32[11,64,128]{2,1,0:T(8,128)S(1)} %get-tuple-element.38.own, f32[11,64,128]{2,1,0:T(8,128)S(1)} %collective-permute-done.4.swap), custom_call_target="tpu_custom_call" | custom-call | flops 10000000 | bytes 4000000 | tf_op jit(solution)/shard_map/start_inner/pallas_call | solution.py:597
  11.4 3.2 %collective-permute-done.2.refs_2_ = f32[64,128]{1,0:T(8,128)S(1)} collective-permute-done((f32[64,128]{1,0:T(8,128)S(1)}, f32[64,128]{1,0:T(8,128)S(1)}, u32[]{:S(2)}, u32[]{:S(2)}) %collective-permute-start.2) | collective-permute-done | bytes 32800 | tf_op jit(solution)/shard_map/ppermute | solution.py:577
  14.7 0.5 collective-permute-done.3.refs_3_
  15.2 0.0 collective-permute-done.refs_0_
  15.2 0.6 collective-permute-done.1.refs_1_
  15.8 1.0 %start_outer.1 = (f32[3,128,128]{2,1,0:T(8,128)S(1)}, f32[3,128,128]{2,1,0:T(8,128)S(1)}, f32[128,128]{1,0:T(8,128)S(1)}, f32[128,128]{1,0:T(8,128)S(1)}, f32[12...) custom-call(f32[4,64,128]{2,1,0:T(8,128)S(1)} %collective-permute-done.refs_0_, ...), custom_call_target="tpu_custom_call" | custom-call | tf_op jit(solution)/shard_map/start_outer/pallas_call | solution.py:604
  16.8 0.1 collective-permute-start.6
  16.9 0.7 %collective-permute-start.5 = (f32[3,128,128]{2,1,0:T(8,128)S(1)}, f32[3,128,128]{2,1,0:T(8,128)S(1)}, u32[]{:S(2)}, u32[]{:S(2)}) collective-permute-start(f32[3,128,128]{2,1,0:T(8,128)S(1)} %get-tuple-element.45.v1), channel_id=1, source_target_pairs={{1,2},{3,4},{2,1},{5,6},{4,3},{7,8},{6,5},{9,10},{8,7},{11,12},{10... | collective-permute-start | bytes 589832 | tf_op jit(solution)/shard_map/ppermute | solution.py:577
  17.6 0.7 %collective-permute-done.6.inner.v1_inner = f32[3,128,128]{2,1,0:T(8,128)S(1)} collective-permute-done((f32[3,128,128]{2,1,0:T(8,128)S(1)}, f32[3,128,128]{2,1,0:T(8,128)S(1)}, u32[]{:S(2)}, u32[]{:S(2)}) %collective-permute-start.6) | collective-permute-done | bytes 196640 | tf_op jit(solution)/shard_map/ppermute | solution.py:577
  18.3 0.0 collective-permute-done.5.outer
  18.3 1.2 %second.1 = (f32[3,128,128]{2,1,0:T(8,128)S(1)}, f32[3,128,128]{2,1,0:T(8,128)S(1)}, f32[8,128]{1,0:T(8,128)S(1)}) custom-call(f32[3,128,128]{2,1,0:T(8,128)S(1)} %get-tuple-element.45.v1, f32[3,128,128]{2,1,0:T(8,128)S(1)} %collective-permute-done.5.outer, f32[3,128,128]{2,1,0:T(8,128)S(1)} %collective-permute-done.6.inner.v1_inner, ...), custom_call_target="tpu_custom_call" | custom-call | tf_op jit(solution)/shard_map/second/pallas_call | solution.py:612
  19.5 6.3 %collective-permute-start.8 = (f32[3,128,128]{2,1,0:T(8,128)S(1)}, f32[3,128,128]{2,1,0:T(8,128)S(1)}, u32[]{:S(2)}, u32[]{:S(2)}) collective-permute-start(f32[3,128,128]{2,1,0:T(8,128)S(1)} %get-tuple-element.49.v2), channel_id=1, source_target_pairs={{0,1},{1,0},{2,3},{3,2},{4,5},{5,4},{6,7},{7,6},{8,9},{9,8},{10,11... | collective-permute-start | bytes 589832 | tf_op jit(solution)/shard_map/ppermute | solution.py:577
  25.8 0.7 %collective-permute-start.7 = (f32[3,128,128]{2,1,0:T(8,128)S(1)}, f32[3,128,128]{2,1,0:T(8,128)S(1)}, u32[]{:S(2)}, u32[]{:S(2)}) collective-permute-start(f32[3,128,128]{2,1,0:T(8,128)S(1)} %get-tuple-element.49.v2), channel_id=1, source_target_pairs={{2,1},{4,3},{6,5},{8,7},{10,9},{12,11},{14,13},{16,15},{18,17},{20... | collective-permute-start | bytes 589832 | tf_op jit(solution)/shard_map/ppermute | solution.py:577
  26.5 0.4 collective-permute-done.8.v2_inner
  26.9 0.0 collective-permute-done.7.v2_outer
  26.9 0.5 third.1
  27.4 23.1 %all_to_all.5.gathered = f32[32,8,128]{2,1,0:T(8,128)S(1)} all-to-all(f32[32,8,128]{2,1,0:T(8,128)S(1)} %broadcast_in_dim.3), channel_id=1, replica_groups=mesh['mod'=4,'slab'=4,'sub'=2] {'mod','slab','sub'}, dimensions={0} | all-to-all | bytes 262144 | tf_op jit(solution)/shard_map/all_to_all | solution.py:621
  50.6 0.7 %combine.1 = (f32[128,128]{1,0:T(8,128)S(1)}, f32[3,8,128]{2,1,0:T(8,128)S(1)}) custom-call(f32[32,8,128]{2,1,0:T(8,128)S(1)} %all_to_all.5.gathered, f32[3,128,128]{2,1,0:T(8,128)S(1)} %get-tuple-element.40.refs_4_.v0, f32[3,128,128]{2,1,0:T(8,128)S(1)} %get-tuple-element.53.v0_high, f32[3,128,128]{2,1,0:T(8,128)S(1)} %get-tuple-element.45.v1, ...), custom_call_target="tpu_custom_call" | custom-call | tf_op jit(solution)/shard_map/combine/pallas_call | solution.py:624
  51.3 1.0 %collective-permute-start.11 = (f32[128,128]{1,0:T(8,128)S(1)}, f32[128,128]{1,0:T(8,128)S(1)}, u32[]{:S(2)}, u32[]{:S(2)}) collective-permute-start(f32[128,128]{1,0:T(8,128)S(1)} %get-tuple-element.57.refs_0_), channel_id=1, source_target_pairs={{0,24},{8,16},{16,8},{24,0},{1,25},{9,17},{17,9},{25,1},{2,26},{10... | collective-permute-start | bytes 196616 | tf_op jit(solution)/shard_map/ppermute | solution.py:627
  52.3 1.3 %collective-permute-start.10 = (f32[128,128]{1,0:T(8,128)S(1)}, f32[128,128]{1,0:T(8,128)S(1)}, u32[]{:S(2)}, u32[]{:S(2)}) collective-permute-start(f32[128,128]{1,0:T(8,128)S(1)} %get-tuple-element.57.refs_0_), channel_id=1, source_target_pairs={{0,16},{8,24},{16,0},{24,8},{1,17},{9,25},{17,1},{25,9},{2,18},{10... | collective-permute-start | bytes 196616 | tf_op jit(solution)/shard_map/ppermute | solution.py:627
  53.6 1.2 %collective-permute-start.9 = (f32[128,128]{1,0:T(8,128)S(1)}, f32[128,128]{1,0:T(8,128)S(1)}, u32[]{:S(2)}, u32[]{:S(2)}) collective-permute-start(f32[128,128]{1,0:T(8,128)S(1)} %get-tuple-element.57.refs_0_), channel_id=1, source_target_pairs={{0,8},{8,0},{16,24},{24,16},{1,9},{9,1},{17,25},{25,17},{2,10},{10... | collective-permute-start | bytes 196616 | tf_op jit(solution)/shard_map/ppermute | solution.py:627
  54.8 2.3 %collective-permute-done.11.refs_3_ = f32[128,128]{1,0:T(8,128)S(1)} collective-permute-done((f32[128,128]{1,0:T(8,128)S(1)}, f32[128,128]{1,0:T(8,128)S(1)}, u32[]{:S(2)}, u32[]{:S(2)}) %collective-permute-start.11) | collective-permute-done | bytes 65568 | tf_op jit(solution)/shard_map/ppermute | solution.py:627
  57.2 0.2 collective-permute-done.10.refs_2_
  57.4 0.5 collective-permute-done.9.refs_1_
  57.9 0.1 collective-permute-start.12
  58.0 1.0 %collective-permute-start.13 = (f32[72,128]{1,0:T(8,128)S(1)}, f32[72,128]{1,0:T(8,128)S(1)}, u32[]{:S(2)}, u32[]{:S(2)}) collective-permute-start(f32[72,128]{1,0:T(8,128)S(1)} %get-tuple-element.64), channel_id=1, source_target_pairs={{0,6},{1,3},{2,0},{3,5},{4,2},{5,7},{6,4},{7,1},{8,14},{9,11},{10,... | collective-permute-start | bytes 110600 | tf_op jit(solution)/shard_map/ppermute | solution.py:577
  59.0 0.0 collective-permute-start.14
  59.0 0.8 %displace.1 = f32[3,2,64,128]{3,2,1,0:T(8,128)} custom-call(f32[3,8,128]{2,1,0:T(8,128)S(1)} %get-tuple-element.60.factors, f32[3,128,128]{2,1,0:T(8,128)S(1)} %get-tuple-element.40.refs_4_.v0, f32[3,128,128]{2,1,0:T(8,128)S(1)} %get-tuple-element.41.refs_5_.v0_inner, f32[3,128,128]{2,1,0:T(8,128)S(1)} %get-tuple-element.45.v1, ...), custom_call_target="tpu_custom_call" | custom-call | flops 10000000 | bytes 4000000 | tf_op jit(solution)/shard_map/displace/pallas_call | solution.py:628
  59.7 3.4 %collective-permute-done.12.outer = f32[72,128]{1,0:T(8,128)S(1)} collective-permute-done((f32[72,128]{1,0:T(8,128)S(1)}, f32[72,128]{1,0:T(8,128)S(1)}, u32[]{:S(2)}, u32[]{:S(2)}) %collective-permute-start.12) | collective-permute-done | bytes 36896 | tf_op jit(solution)/shard_map/ppermute | solution.py:577
  63.2 0.0 collective-permute-done.13.far
  63.2 0.0 collective-permute-done.14.partner
  63.2 0.9 %gradient.1 = f32[2,64,128]{2,1,0:T(8,128)} custom-call(f32[128,128]{1,0:T(8,128)S(1)} %get-tuple-element.62.scaled, f32[72,128]{1,0:T(8,128)S(1)} %collective-permute-done.12.outer, f32[72,128]{1,0:T(8,128)S(1)} %collective-permute-done.13.far, f32[72,128]{1,0:T(8,128)S(1)} %collective-permute-done.14.partner), custom_call_target="tpu_custom_call" | custom-call | tf_op jit(solution)/shard_map/gradient/pallas_call | solution.py:639
  (2 shorter events, 0.0 us)
Async XLA Ops:
  0.6 1.0 %copy-start = (s32[3,2,64,128]{3,2,1,0:T(8,128)S(1)}, s32[3,2,64,128]{3,2,1,0:T(8,128)}, u32[]{:S(2)}) copy-start(s32[3,2,64,128]{3,2,1,0:T(8,128)} %load.1) | copy-start | bytes 589828
  0.6 1.0 %copy-start.1 = (f32[2,64,128]{2,1,0:T(8,128)S(1)}, f32[2,64,128]{2,1,0:T(8,128)}, u32[]{:S(2)}) copy-start(f32[2,64,128]{2,1,0:T(8,128)} %design.1) | copy-start | bytes 196612
  1.7 8.9 %collective-permute-start.4 = (f32[11,64,128]{2,1,0:T(8,128)S(1)}, f32[11,64,128]{2,1,0:T(8,128)S(1)}, u32[]{:S(2)}, u32[]{:S(2)}) collective-permute-start(f32[11,64,128]{2,1,0:T(8,128)S(1)} %get-tuple-element.39), channel_id=1, source_target_pairs={{0,1},{1,0},{2,3},{3,2},{4,5},{5,4},{6,7},{7,6},{8,9},{9,8},{10,11... | collective-permute-start | bytes 1081352 | tf_op jit(solution)/shard_map/ppermute | solution.py:577
  2.3 12.9 %collective-permute-start = (f32[4,64,128]{2,1,0:T(8,128)S(1)}, f32[4,64,128]{2,1,0:T(8,128)S(1)}, u32[]{:S(2)}, u32[]{:S(2)}) collective-permute-start(f32[4,64,128]{2,1,0:T(8,128)S(1)} %get-tuple-element.34), channel_id=1, source_target_pairs={{0,2},{1,31},{2,4},{3,1},{4,6},{5,3},{6,8},{7,5},{8,10},{9,7},{10,... | collective-permute-start | bytes 393224 | tf_op jit(solution)/shard_map/ppermute | solution.py:577
  4.9 10.9 %collective-permute-start.1 = (f32[4,64,128]{2,1,0:T(8,128)S(1)}, f32[4,64,128]{2,1,0:T(8,128)S(1)}, u32[]{:S(2)}, u32[]{:S(2)}) collective-permute-start(f32[4,64,128]{2,1,0:T(8,128)S(1)} %get-tuple-element.35), channel_id=1, source_target_pairs={{1,2},{0,31},{3,4},{2,1},{5,6},{4,3},{7,8},{6,5},{9,10},{8,7},{11,... | collective-permute-start | bytes 393224 | tf_op jit(solution)/shard_map/ppermute | solution.py:577
  9.0 5.7 %collective-permute-start.2 = (f32[64,128]{1,0:T(8,128)S(1)}, f32[64,128]{1,0:T(8,128)S(1)}, u32[]{:S(2)}, u32[]{:S(2)}) collective-permute-start(f32[64,128]{1,0:T(8,128)S(1)} %get-tuple-element.36), channel_id=1, source_target_pairs={{0,3},{1,2},{2,5},{3,4},{4,7},{5,6},{6,1},{7,0},{8,11},{9,10},{10,... | collective-permute-start | bytes 98312 | tf_op jit(solution)/shard_map/ppermute | solution.py:577
  9.0 6.2 %collective-permute-start.3 = (f32[64,128]{1,0:T(8,128)S(1)}, f32[64,128]{1,0:T(8,128)S(1)}, u32[]{:S(2)}, u32[]{:S(2)}) collective-permute-start(f32[64,128]{1,0:T(8,128)S(1)} %get-tuple-element.37), channel_id=1, source_target_pairs={{0,2},{1,3},{2,4},{3,5},{4,6},{5,7},{6,0},{7,1},{8,10},{9,11},{10,... | collective-permute-start | bytes 98312 | tf_op jit(solution)/shard_map/ppermute | solution.py:577
  16.8 1.5 %collective-permute-start.6 = (f32[3,128,128]{2,1,0:T(8,128)S(1)}, f32[3,128,128]{2,1,0:T(8,128)S(1)}, u32[]{:S(2)}, u32[]{:S(2)}) collective-permute-start(f32[3,128,128]{2,1,0:T(8,128)S(1)} %get-tuple-element.45.v1), channel_id=1, source_target_pairs={{0,1},{1,0},{2,3},{3,2},{4,5},{5,4},{6,7},{7,6},{8,9},{9,8},{10,11... | collective-permute-start | bytes 589832 | tf_op jit(solution)/shard_map/ppermute | solution.py:577
  16.9 1.4 %collective-permute-start.5 = (f32[3,128,128]{2,1,0:T(8,128)S(1)}, f32[3,128,128]{2,1,0:T(8,128)S(1)}, u32[]{:S(2)}, u32[]{:S(2)}) collective-permute-start(f32[3,128,128]{2,1,0:T(8,128)S(1)} %get-tuple-element.45.v1), channel_id=1, source_target_pairs={{1,2},{3,4},{2,1},{5,6},{4,3},{7,8},{6,5},{9,10},{8,7},{11,12},{10... | collective-permute-start | bytes 589832 | tf_op jit(solution)/shard_map/ppermute | solution.py:577
  19.5 7.4 %collective-permute-start.8 = (f32[3,128,128]{2,1,0:T(8,128)S(1)}, f32[3,128,128]{2,1,0:T(8,128)S(1)}, u32[]{:S(2)}, u32[]{:S(2)}) collective-permute-start(f32[3,128,128]{2,1,0:T(8,128)S(1)} %get-tuple-element.49.v2), channel_id=1, source_target_pairs={{0,1},{1,0},{2,3},{3,2},{4,5},{5,4},{6,7},{7,6},{8,9},{9,8},{10,11... | collective-permute-start | bytes 589832 | tf_op jit(solution)/shard_map/ppermute | solution.py:577
  25.8 1.1 %collective-permute-start.7 = (f32[3,128,128]{2,1,0:T(8,128)S(1)}, f32[3,128,128]{2,1,0:T(8,128)S(1)}, u32[]{:S(2)}, u32[]{:S(2)}) collective-permute-start(f32[3,128,128]{2,1,0:T(8,128)S(1)} %get-tuple-element.49.v2), channel_id=1, source_target_pairs={{2,1},{4,3},{6,5},{8,7},{10,9},{12,11},{14,13},{16,15},{18,17},{20... | collective-permute-start | bytes 589832 | tf_op jit(solution)/shard_map/ppermute | solution.py:577
  51.3 5.9 %collective-permute-start.11 = (f32[128,128]{1,0:T(8,128)S(1)}, f32[128,128]{1,0:T(8,128)S(1)}, u32[]{:S(2)}, u32[]{:S(2)}) collective-permute-start(f32[128,128]{1,0:T(8,128)S(1)} %get-tuple-element.57.refs_0_), channel_id=1, source_target_pairs={{0,24},{8,16},{16,8},{24,0},{1,25},{9,17},{17,9},{25,1},{2,26},{10... | collective-permute-start | bytes 196616 | tf_op jit(solution)/shard_map/ppermute | solution.py:627
  52.3 5.1 %collective-permute-start.10 = (f32[128,128]{1,0:T(8,128)S(1)}, f32[128,128]{1,0:T(8,128)S(1)}, u32[]{:S(2)}, u32[]{:S(2)}) collective-permute-start(f32[128,128]{1,0:T(8,128)S(1)} %get-tuple-element.57.refs_0_), channel_id=1, source_target_pairs={{0,16},{8,24},{16,0},{24,8},{1,17},{9,25},{17,1},{25,9},{2,18},{10... | collective-permute-start | bytes 196616 | tf_op jit(solution)/shard_map/ppermute | solution.py:627
  53.6 4.3 %collective-permute-start.9 = (f32[128,128]{1,0:T(8,128)S(1)}, f32[128,128]{1,0:T(8,128)S(1)}, u32[]{:S(2)}, u32[]{:S(2)}) collective-permute-start(f32[128,128]{1,0:T(8,128)S(1)} %get-tuple-element.57.refs_0_), channel_id=1, source_target_pairs={{0,8},{8,0},{16,24},{24,16},{1,9},{9,1},{17,25},{25,17},{2,10},{10... | collective-permute-start | bytes 196616 | tf_op jit(solution)/shard_map/ppermute | solution.py:627
  57.9 5.2 %collective-permute-start.12 = (f32[72,128]{1,0:T(8,128)S(1)}, f32[72,128]{1,0:T(8,128)S(1)}, u32[]{:S(2)}, u32[]{:S(2)}) collective-permute-start(f32[72,128]{1,0:T(8,128)S(1)} %get-tuple-element.63), channel_id=1, source_target_pairs={{1,2},{0,7},{3,4},{2,1},{5,6},{4,3},{7,0},{6,5},{9,10},{8,15},{11,... | collective-permute-start | bytes 110600 | tf_op jit(solution)/shard_map/ppermute | solution.py:577
  58.0 5.2 %collective-permute-start.13 = (f32[72,128]{1,0:T(8,128)S(1)}, f32[72,128]{1,0:T(8,128)S(1)}, u32[]{:S(2)}, u32[]{:S(2)}) collective-permute-start(f32[72,128]{1,0:T(8,128)S(1)} %get-tuple-element.64), channel_id=1, source_target_pairs={{0,6},{1,3},{2,0},{3,5},{4,2},{5,7},{6,4},{7,1},{8,14},{9,11},{10,... | collective-permute-start | bytes 110600 | tf_op jit(solution)/shard_map/ppermute | solution.py:577
  59.0 4.2 %collective-permute-start.14 = (f32[72,128]{1,0:T(8,128)S(1)}, f32[72,128]{1,0:T(8,128)S(1)}, u32[]{:S(2)}, u32[]{:S(2)}) collective-permute-start(f32[72,128]{1,0:T(8,128)S(1)} %get-tuple-element.65), channel_id=1, source_target_pairs={{0,1},{1,0},{2,3},{3,2},{4,5},{5,4},{6,7},{7,6},{8,9},{9,8},{10,11... | collective-permute-start | bytes 110600 | tf_op jit(solution)/shard_map/ppermute | solution.py:577
